TPU v7x, 32 devices: a whole 2x2x4 slice. The times are simulated.
32 devices in a mesh: dp: 4 (over x, core), expert: 8 (over z, y).
Axes of the slice: x: 2, y: 2, z: 4, core: 2. Of those that a mesh axis runs over, the one named last changes fastest.
Arguments:
- out_grad: bfloat16 [2048, 7168], P('expert', 'dp'), may hold values from -6 to 6
- inputs: bfloat16 [2048, 7168], P('expert', 'dp'), may hold values from -2.5 to 2.5
- expert_ids: int32 [2048, 8], P('expert'), may hold values from 0 to 255, as said below
- gate_weights: float32 [2048, 8], P('expert'), may hold values from 0.1 to 1
- w_gate: bfloat16 [7168, 4096], P('dp', 'expert'), may hold values from -0.0625 to 0.0625
- w_up: bfloat16 [7168, 4096], P('dp', 'expert'), may hold values from -0.0625 to 0.0625
- w_down: bfloat16 [4096, 7168], P('expert', 'dp'), may hold values from -0.125 to 0.125
Outputs:
- in_grad: bfloat16 [2048, 7168], P('expert', 'dp')
- grad_gate: bfloat16 [7168, 4096], P('dp', 'expert')
- grad_up: bfloat16 [7168, 4096], P('dp', 'expert')
Inputs may be any that keep to these rules, and one draw needn't show every extreme that they name: `expert_ids`: each token names 8 different experts. Within one block of 256 consecutive tokens no expert is named by more than 12 tokens, and in every draw some expert below 2 is named by exactly 12 tokens of every block.
All inputs are finite; a program needn't handle non-finite values.
Results may differ from a plain program's by a relative error of at most 0.035.
Values may be sent and summed in bfloat16 or wider, within the bound.
No kernel may reach another device: no remote copies, remote signals or barrier semaphores. Data moves between devices by JAX's collectives and lax.ppermute only.
A program may use at most 64 MiB of HBM per device.

v0:
```python
import jax
import jax.numpy as jnp
from jax import lax
from jax.sharding import PartitionSpec as P

HSPLIT = 4
CAP = 12


def routes(block_ids, block_gates, experts):
    flat_ids = block_ids.reshape(-1)
    matches = (flat_ids[:, None] == jnp.arange(experts, dtype=jnp.int32)[None, :]).astype(jnp.int32)
    before = jnp.cumsum(matches, axis=0) - matches
    slot_index = jnp.sum(before * matches, axis=1)
    kept_mask = jnp.sum(matches, axis=1)
    target = jnp.where(kept_mask > 0, flat_ids * CAP + slot_index, -1)
    columns = jnp.arange(experts * CAP, dtype=jnp.int32)
    hits = target[:, None] == columns[None, :]
    slot_gate = jnp.sum(jnp.where(hits, block_gates.reshape(-1)[:, None], 0.0), axis=0)
    token_of = jnp.repeat(jnp.arange(block_ids.shape[0], dtype=jnp.int32), block_ids.shape[1])
    slot_token = jnp.sum(jnp.where(hits, token_of[:, None], 0), axis=0)
    slot_used = jnp.any(hits, axis=0)
    tokens_range = jnp.arange(block_ids.shape[0], dtype=jnp.int32)
    picker = ((slot_token[:, None] == tokens_range[None, :]) & slot_used[:, None]).astype(
        jnp.bfloat16
    )
    return (picker, slot_gate, target.reshape(block_ids.shape))


def activation_grads(hidden_grad, gate_pre, up_pre):
    sigma = jax.nn.sigmoid(gate_pre)
    grad_gate_pre = (hidden_grad * up_pre * sigma * (1.0 + gate_pre * (1.0 - sigma))).astype(
        jnp.bfloat16
    )
    grad_up_pre = (hidden_grad * gate_pre * sigma).astype(jnp.bfloat16)
    return (grad_gate_pre, grad_up_pre)


def contract(left, right, left_dim, right_dim):
    return lax.dot_general(
        left, right, (((left_dim,), (right_dim,)), ((), ())), preferred_element_type=jnp.float32
    )


def per_device(out_grad, inputs, expert_ids, gate_weights, w_gate, w_up, w_down):
    devices = lax.axis_size("expert")
    experts = devices // HSPLIT
    feature_width = out_grad.shape[1]
    picker, slot_gate, target = routes(expert_ids, gate_weights, experts)
    picked_grad = jnp.dot(picker, out_grad, preferred_element_type=jnp.float32)
    sent_grad = (slot_gate[:, None] * picked_grad).astype(jnp.bfloat16)
    sent_input = jnp.dot(picker, inputs, preferred_element_type=jnp.float32).astype(jnp.bfloat16)
    sent_grad = jnp.repeat(sent_grad.reshape(experts, CAP, feature_width), HSPLIT, axis=0)
    sent_input = jnp.repeat(sent_input.reshape(experts, CAP, feature_width), HSPLIT, axis=0)
    rows_grad, rows_input = (
        lax.all_to_all(sent_grad, "expert", split_axis=0, concat_axis=0, tiled=True),
        lax.all_to_all(sent_input, "expert", split_axis=0, concat_axis=0, tiled=True),
    )
    rows_grad = rows_grad.reshape(-1, feature_width)
    rows_input = rows_input.reshape(-1, feature_width)
    down_part = contract(rows_grad, w_down, 1, 1)
    gate_part = jnp.dot(rows_input, w_gate, preferred_element_type=jnp.float32)
    up_part = jnp.dot(rows_input, w_up, preferred_element_type=jnp.float32)
    hidden_grad, gate_pre, up_pre = (
        lax.psum(down_part.astype(jnp.bfloat16), "dp").astype(jnp.float32),
        lax.psum(gate_part.astype(jnp.bfloat16), "dp").astype(jnp.float32),
        lax.psum(up_part.astype(jnp.bfloat16), "dp").astype(jnp.float32),
    )
    grad_gate_pre, grad_up_pre = activation_grads(hidden_grad, gate_pre, up_pre)
    back_part = (contract(grad_gate_pre, w_gate, 1, 1) + contract(grad_up_pre, w_up, 1, 1)).astype(
        jnp.bfloat16
    )
    grad_gate = contract(rows_input, grad_gate_pre, 0, 0).astype(jnp.bfloat16)
    grad_up = contract(rows_input, grad_up_pre, 0, 0).astype(jnp.bfloat16)
    returned = lax.all_to_all(
        back_part.reshape(devices, CAP, feature_width),
        "expert",
        split_axis=0,
        concat_axis=0,
        tiled=True,
    )
    summed = jnp.sum(
        returned.astype(jnp.float32).reshape(experts, HSPLIT, CAP, feature_width), axis=1
    )
    summed = summed.reshape(experts * CAP, feature_width)
    kept = target >= 0
    fetched = jnp.take(summed, jnp.where(kept, target, 0), axis=0)
    in_grad = jnp.sum(jnp.where(kept[:, :, None], fetched, 0.0), axis=1).astype(jnp.bfloat16)
    return (in_grad, grad_gate, grad_up)


def solution(mesh):
    placed = (
        P("expert", "dp"),
        P("expert", "dp"),
        P("expert", None),
        P("expert", None),
        P("dp", "expert"),
        P("dp", "expert"),
        P("expert", "dp"),
    )
    return jax.shard_map(
        per_device,
        mesh=mesh,
        in_specs=placed,
        out_specs=(P("expert", "dp"), P("dp", "expert"), P("dp", "expert")),
        check_vma=False,
    )
```

profile of v0, /device:TPU:0, one launch (start us, length us, event | category | flops | bytes accessed | tf_op | source)
XLA Modules:
  0.0 134.4 jit_solution(2827062859766055841)
XLA Ops:
  7.2 1.0 copy.22
  8.4 0.6 reduce-window.6
  9.0 0.2 slice_reduce_fusion
  9.2 0.2 reduce-window.9
  9.6 0.1 fusion.13
  9.8 0.1 select_reduce_fusion
  9.9 1.5 %convolution_convert_fusion.2 = bf16[24,1792]{1,0:T(8,128)(2,1)S(1)} fusion(bf16[256,1792]{1,0:T(8,128)(2,1)} %param.8, s32[24]{0:T(128)S(1)} %select_reduce_fusion, pred[24]{0:T(512)(128)(4,1)S(1)} %fusion.13), kind=kOutput, calls=%fused_computation.10 | convolution fusion | flops 22075392 | bytes 1003640 | tf_op jit(solution)/shard_map/dot_general | solution.py:52
  11.4 0.8 broadcast_in_dim.89
  12.2 7.3 %all-to-all-start.1 = ((bf16[8,12,1792]{2,1,0:T(8,128)(2,1)}), bf16[8,12,1792]{2,1,0:T(8,128)(2,1)S(1)}, u32[]{:S(2)}, u32[]{:S(2)}) async-start(bf16[8,12,1792]{2,1,0:T(8,128)(2,1)} %bitcast.2), calls=%async_computation.1 | async-start | bytes 917504 | tf_op jit(solution)/shard_map/all_to_all | solution.py:57
  19.5 0.1 copy.28
  19.7 0.1 select_reduce_fusion.1
  19.9 0.3 fusion.3
  20.2 12.4 %all-to-all-done.1 = bf16[8,12,1792]{2,1,0:T(8,128)(2,1)S(1)} async-done(((bf16[8,12,1792]{2,1,0:T(8,128)(2,1)}), bf16[8,12,1792]{2,1,0:T(8,128)(2,1)S(1)}, u32[]{:S(2)}, u32[]{:S(2)}) %all-to-all-start.1) | async-done | bytes 344096 | tf_op jit(solution)/shard_map/all_to_all | solution.py:57
  32.6 0.8 broadcast_in_dim.88
  33.4 3.6 %all-to-all-start = ((bf16[8,12,1792]{2,1,0:T(8,128)(2,1)}), bf16[8,12,1792]{2,1,0:T(8,128)(2,1)S(1)}, u32[]{:S(2)}, u32[]{:S(2)}) async-start(bf16[8,12,1792]{2,1,0:T(8,128)(2,1)} %bitcast.1), calls=%async_computation | async-start | bytes 917504 | tf_op jit(solution)/shard_map/all_to_all | solution.py:56
  37.5 1.1 convolution_convert_fusion.3
  38.6 0.5 copy-done.1
  39.1 1.1 convolution_convert_fusion.4
  40.1 10.0 %all-to-all-done = bf16[8,12,1792]{2,1,0:T(8,128)(2,1)S(1)} async-done(((bf16[8,12,1792]{2,1,0:T(8,128)(2,1)}), bf16[8,12,1792]{2,1,0:T(8,128)(2,1)S(1)}, u32[]{:S(2)}, u32[]{:S(2)}) %all-to-all-start) | async-done | bytes 344096 | tf_op jit(solution)/shard_map/all_to_all | solution.py:56
  50.3 2.8 %convolution_convert_fusion.5 = bf16[96,512]{1,0:T(8,128)(2,1)} fusion(bf16[96,1792]{1,0:T(8,128)(2,1)S(1)} %reshape.85, bf16[512,1792]{1,0:T(8,128)(2,1)} %param.13), kind=kOutput, calls=%fused_computation.13 | convolution fusion | flops 176209920 | bytes 2277376 | tf_op jit(solution)/shard_map/dot_general | solution.py:40
  53.4 31.4 %all-reduce.3.cloned.1.call-done = (bf16[96,512]{1,0:T(8,128)(2,1)}, bf16[96,512]{1,0:T(8,128)(2,1)}, bf16[96,512]{1,0:T(8,128)(2,1)}) async-done(((bf16[96,512]{1,0:T(8,128)(2,1)}, bf16[96,512]{1,0:T(8,128)(2,1)}, bf16[96,512]{1,0:T(8,128)(2,1)}), (bf16[96,512]{1,0:T(8,128)(2,1)}, bf16[96,512]{1,0:T(8,128)(2,1)}, bf16[96,512]{1,0:T(8,128)(2,1)})) %all-reduce.3.cloned.1.call-update) | async-done | bytes 294928 | tf_op jit(solution)/shard_map/psum | solution.py:65
  84.8 1.8 %fusion.27 = f32[96,1792]{1,0:T(8,128)S(1)} fusion(bf16[1792,512]{1,0:T(8,128)(2,1)S(1)} %copy-done, bf16[96,512]{1,0:T(8,128)(2,1)} %get-tuple-element.5, bf16[96,512]{1,0:T(8,128)(2,1)} %get-tuple-element.6, bf16[96,512]{1,0:T(8,128)(2,1)} %get-tuple-element.7), kind=kOutput, calls=%fused_computation.55 | convolution fusion | flops 176799744 | bytes 2818048 | tf_op jit(solution)/shard_map/dot_general | solution.py:40
  86.6 0.7 fusion.2
  87.3 0.9 reshape.89
  88.1 5.6 %all-to-all-start.2 = ((bf16[8,12,1792]{2,1,0:T(8,128)(2,1)}), bf16[8,12,1792]{2,1,0:T(8,128)(2,1)S(1)}, u32[]{:S(2)}, u32[]{:S(2)}) async-start(bf16[8,12,1792]{2,1,0:T(8,128)(2,1)} %reshape.89), calls=%async_computation.2 | async-start | bytes 917504 | tf_op jit(solution)/shard_map/all_to_all | solution.py:75
  93.8 0.2 copy.26
  94.0 0.2 copy.27
  94.1 1.9 %convolution_convert_fusion = bf16[1792,512]{1,0:T(8,128)(2,1)} fusion(bf16[96,1792]{1,0:T(8,128)(2,1)S(1)} %reshape.88, bf16[96,512]{1,0:T(8,128)(2,1)S(1)} %copy-done.4, bf16[96,512]{1,0:T(8,128)(2,1)S(1)} %copy-done.3), kind=kOutput, calls=%fused_computation.4 | convolution fusion | flops 177471488 | bytes 2375680 | tf_op jit(solution)/shard_map/dot_general | solution.py:40
  96.1 1.9 %convolution_convert_fusion.1 = bf16[1792,512]{1,0:T(8,128)(2,1)} fusion(bf16[96,1792]{1,0:T(8,128)(2,1)S(1)} %reshape.88, bf16[96,512]{1,0:T(8,128)(2,1)S(1)} %copy-done.3, bf16[96,512]{1,0:T(8,128)(2,1)S(1)} %copy-done.4, bf16[96,512]{1,0:T(8,128)(2,1)S(1)} %copy-done.6), kind=kOutput, calls=%fused_computation.5 | convolution fusion | flops 177717248 | bytes 2473984 | tf_op jit(solution)/shard_map/dot_general | solution.py:40
  98.0 7.9 %all-to-all-done.2 = bf16[8,12,1792]{2,1,0:T(8,128)(2,1)S(1)} async-done(((bf16[8,12,1792]{2,1,0:T(8,128)(2,1)}), bf16[8,12,1792]{2,1,0:T(8,128)(2,1)S(1)}, u32[]{:S(2)}, u32[]{:S(2)}) %all-to-all-start.2) | async-done | bytes 344096 | tf_op jit(solution)/shard_map/all_to_all | solution.py:75
  106.0 12.4 %gather_fusion = f32[2048,1792]{1,0:T(8,128)} fusion(f32[24,1792]{1,0:T(8,128)S(1)} %reshape.92, s32[2048]{0:T(1024)S(1)} %broadcast_clamp_fusion), kind=kCustom, calls=%fused_computation | custom fusion | bytes 29368320 | tf_op jit(solution)/shard_map/jit(_take)/gather | solution.py:87
  118.4 9.2 %fusion.1 = bf16[256,1792]{1,0:T(8,128)(2,1)} fusion(f32[2048,1792]{1,0:T(8,128)} %gather_fusion, pred[256,8]{1,0:T(8,128)(4,1)S(1)} %copy.27, pred[256,8]{1,0:T(8,128)(4,1)S(1)} %copy.26), kind=kLoop, calls=%fused_computation.3 | loop fusion | flops 10551296 | bytes 15601664 | tf_op jit(solution)/shard_map/reduce_sum | solution.py:88
  (42 shorter events, 1.6 us)
Async XLA Ops:
  7.2 30.4 %copy-start = (bf16[1792,512]{1,0:T(8,128)(2,1)S(1)}, bf16[1792,512]{1,0:T(8,128)(2,1)}, u32[]{:S(2)}) copy-start(bf16[1792,512]{1,0:T(8,128)(2,1)} %param.11) | copy-start | bytes 5505028
  7.2 12.3 %copy-start.8 = (f32[256,8]{0,1:T(8,128)S(1)}, f32[256,8]{0,1:T(8,128)}, u32[]{:S(2)}) copy-start(f32[256,8]{0,1:T(8,128)} %param.10) | copy-start | bytes 24580
  8.3 11.6 %copy-start.5 = (bf16[256,1792]{1,0:T(8,128)(2,1)S(1)}, bf16[256,1792]{1,0:T(8,128)(2,1)}, u32[]{:S(2)}) copy-start(bf16[256,1792]{1,0:T(8,128)(2,1)} %param.7) | copy-start | bytes 2752516
  12.2 20.4 %all-to-all-start.1 = ((bf16[8,12,1792]{2,1,0:T(8,128)(2,1)}), bf16[8,12,1792]{2,1,0:T(8,128)(2,1)S(1)}, u32[]{:S(2)}, u32[]{:S(2)}) async-start(bf16[8,12,1792]{2,1,0:T(8,128)(2,1)} %bitcast.2), calls=%async_computation.1 | async-start | bytes 917504 | tf_op jit(solution)/shard_map/all_to_all | solution.py:57
  33.4 16.8 %all-to-all-start = ((bf16[8,12,1792]{2,1,0:T(8,128)(2,1)}), bf16[8,12,1792]{2,1,0:T(8,128)(2,1)S(1)}, u32[]{:S(2)}, u32[]{:S(2)}) async-start(bf16[8,12,1792]{2,1,0:T(8,128)(2,1)} %bitcast.1), calls=%async_computation | async-start | bytes 917504 | tf_op jit(solution)/shard_map/all_to_all | solution.py:56
  37.0 47.7 %all-reduce.3.cloned.1.call-start = ((), (), s32[]{:S(2)}) async-start(), calls=%async_computation.3 | async-start | bytes 589824 | tf_op jit(solution)/shard_map/psum | solution.py:65
  37.5 1.5 %copy-start.1 = (bf16[1792,512]{1,0:T(8,128)(2,1)S(1)}, bf16[1792,512]{1,0:T(8,128)(2,1)}, u32[]{:S(2)}) copy-start(bf16[1792,512]{1,0:T(8,128)(2,1)} %param.12) | copy-start | bytes 5505028
  40.1 13.0 %copy-start.7 = (s32[256,8]{0,1:T(8,128)S(1)}, s32[256,8]{0,1:T(8,128)}, u32[]{:S(2)}) copy-start(s32[256,8]{0,1:T(8,128)} %param.9) | copy-start | bytes 24580
  84.8 1.8 %copy-start.2 = (bf16[1792,512]{1,0:T(8,128)(2,1)S(1)}, bf16[1792,512]{1,0:T(8,128)(2,1)}, u32[]{:S(2)}) copy-start(bf16[1792,512]{1,0:T(8,128)(2,1)} %param.12) | copy-start | bytes 5505028
  84.8 1.8 %copy-start.3 = (bf16[96,512]{1,0:T(8,128)(2,1)S(1)}, bf16[96,512]{1,0:T(8,128)(2,1)}, u32[]{:S(2)}) copy-start(bf16[96,512]{1,0:T(8,128)(2,1)} %get-tuple-element.5) | copy-start | bytes 294916
  84.8 1.8 %copy-start.4 = (bf16[96,512]{1,0:T(8,128)(2,1)S(1)}, bf16[96,512]{1,0:T(8,128)(2,1)}, u32[]{:S(2)}) copy-start(bf16[96,512]{1,0:T(8,128)(2,1)} %get-tuple-element.6) | copy-start | bytes 294916
  88.1 7.9 %copy-start.6 = (bf16[96,512]{1,0:T(8,128)(2,1)S(1)}, bf16[96,512]{1,0:T(8,128)(2,1)}, u32[]{:S(2)}) copy-start(bf16[96,512]{1,0:T(8,128)(2,1)} %get-tuple-element.7) | copy-start | bytes 294916
  88.1 17.7 %all-to-all-start.2 = ((bf16[8,12,1792]{2,1,0:T(8,128)(2,1)}), bf16[8,12,1792]{2,1,0:T(8,128)(2,1)S(1)}, u32[]{:S(2)}, u32[]{:S(2)}) async-start(bf16[8,12,1792]{2,1,0:T(8,128)(2,1)} %reshape.89), calls=%async_computation.2 | async-start | bytes 917504 | tf_op jit(solution)/shard_map/all_to_all | solution.py:75
Sparse Core Ops, SparseCore 0:
  53.2 31.4 all-reduce.2
where the time goes:
time: 135 us; the launch traced here: 134 us
  waiting for transfers between devices  61.6 us (46%)
  local copies, waits for them, and re-layouts  18.2 us (13%)
  starting transfers between devices  16.6 us (12%)
  between operations  14.3 us (11%)
  matrix products  13.1 us (10%)
  other arithmetic  10.6 us (8%)
    psum x1, waiting for transfers between devices, per_device(): lax.psum(down_part.astype(jnp.bfloat16), 'dp').astype(jnp.float32)  31.4 us
    gather x1, local copies, waits for them, and re-layouts, per_device(): fetched = jnp.take(summed, jnp.where(kept, target, 0), axis=0)  12.4 us
    all_to_all x1, waiting for transfers between devices, per_device(): lax.all_to_all(sent_input, 'expert', split_axis=0, concat_axis=0, tiled=T...  12.4 us
    all_to_all x1, waiting for transfers between devices, per_device(): lax.all_to_all(sent_grad, 'expert', split_axis=0, concat_axis=0, tiled=True)  10 us
    dot_general x5, matrix products, contract(): lax.dot_general(left, right, (((left_dim,), (right_dim,)), ((), ())), pre...  9.18 us
    reduce_sum x1, other arithmetic, per_device(): jnp.sum(jnp.where(kept[:, :, None], fetched, 0.0), axis=1)  9.16 us
    all_to_all x1, waiting for transfers between devices, per_device(): lax.all_to_all(back_part.reshape(devices, CAP, feature_width), 'expert',...  7.86 us
    all_to_all x1, starting transfers between devices, per_device(): lax.all_to_all(sent_input, 'expert', split_axis=0, concat_axis=0, tiled=T...  7.28 us
  transfers between devices with their start and end apart: 4, of which 4 were waited for; matrix products, arithmetic and copies ran while one was open for 6% of the time, Pallas kernels for 0%

commit v1 on v0

v1 whole, which is shorter than its diff:
```python
import functools

import jax
import jax.numpy as jnp
from jax import lax
from jax.experimental import pallas as pl
from jax.experimental.pallas import tpu as pltpu
from jax.sharding import PartitionSpec as P

HSPLIT = 4
CAP = 12
F32 = jnp.float32
BF16 = jnp.bfloat16
VMEM = pl.BlockSpec(memory_space=pltpu.VMEM)
HBM = pl.BlockSpec(memory_space=pltpu.HBM)
ANY = pl.BlockSpec(memory_space=pl.ANY)


def shape(dims, dtype=BF16):
    return jax.ShapeDtypeStruct(dims, dtype)


def run(body, outs, specs, flops, nbytes, *args, out_spec=VMEM, scratch=()):
    return pl.pallas_call(
        body,
        out_shape=outs,
        in_specs=specs,
        out_specs=out_spec if isinstance(out_spec, tuple) else jax.tree.map(lambda _: out_spec, outs),
        scratch_shapes=scratch,
        compiler_params=pltpu.CompilerParams(vmem_limit_bytes=40 * 1024 * 1024),
        cost_estimate=pl.CostEstimate(flops=flops, bytes_accessed=nbytes, transcendentals=0),
    )(*args)


def in_hbm(value):
    return pltpu.with_memory_space_constraint(value, pltpu.HBM)


def dot(left, right, left_dim=1, right_dim=0):
    return lax.dot_general(
        left, right, (((left_dim,), (right_dim,)), ((), ())), preferred_element_type=F32
    )


def iota(dims, dim):
    return lax.broadcasted_iota(jnp.int32, dims, dim)


def over_cap(rows):
    return jnp.floor((rows.astype(F32) + 0.5) * (1.0 / CAP)).astype(jnp.int32)


def core_columns(width, far):
    side = lax.rem(lax.axis_index("dp"), 2)
    side = 1 - side if far else side
    return pl.ds(pl.multiple_of(side * width, width), width)


def fold_of(width):
    return 2 if width % 256 == 0 else 1


def pick_body(experts, fold, ids_hbm, gates_hbm, grads_hbm, inputs_hbm, *refs):
    picks, pieces = refs[:fold], refs[fold : fold + experts]
    ids, gates, grads, inputs, sems = refs[fold + experts :]
    loads = [
        pltpu.make_async_copy(source, target, sems.at[place])
        for place, (source, target) in enumerate(
            ((ids_hbm, ids), (gates_hbm, gates), (inputs_hbm, inputs), (grads_hbm, grads))
        )
    ]
    for load in loads:
        load.start()
    tokens = ids.shape[1]
    padded = max(8, experts)
    group = lax.div(lax.axis_index("expert"), HSPLIT)
    earlier = (iota((tokens, tokens), 0) < iota((tokens, tokens), 1)).astype(F32).astype(BF16)
    loads[0].wait()
    loads[1].wait()
    expert_ids = ids[...]
    route_gates = gates[...]
    match_rows = jnp.zeros((padded, tokens), F32)
    matches = []
    token_gates = []
    for step in range(experts):
        hits = expert_ids == lax.rem(group + step, experts)
        match = jnp.sum(hits.astype(F32), axis=0, keepdims=True)
        matches.append(match)
        token_gates.append(jnp.sum(jnp.where(hits, route_gates, 0.0), axis=0, keepdims=True))
        match_rows = jnp.where(iota((padded, tokens), 0) == step, match, match_rows)
    counts = dot(match_rows.astype(BF16), earlier)
    slots = [
        jnp.where(matches[step] > 0.0, counts[step : step + 1, :], -1.0e6)
        for step in range(experts)
    ]

    def chosen(rows, offset):
        places = (iota((rows, tokens), 0) - offset).astype(F32)
        return [(places == slots[step]).astype(F32) for step in range(experts)]

    input_picks = chosen(2 * CAP, 0)
    grad_picks = chosen(2 * CAP, CAP)
    slot_gates = [
        jnp.sum(hit * gate, axis=1, keepdims=True) for hit, gate in zip(grad_picks, token_gates)
    ]
    gate_column = jnp.concatenate(slot_gates, axis=0)
    input_picks = jnp.concatenate(input_picks, axis=0)
    grad_picks = jnp.concatenate(grad_picks, axis=0)
    if fold == 2:
        picks[0][...] = input_picks.astype(BF16)
        picks[1][...] = grad_picks.astype(BF16)
    else:
        picks[0][...] = jnp.concatenate(chosen(CAP, 0), axis=0).astype(BF16)
    loads[2].wait()
    total = dot(input_picks.astype(BF16), inputs[...])
    loads[3].wait()
    total = total + dot(grad_picks.astype(BF16), grads[...]) * gate_column
    for step in range(experts):
        pieces[step][...] = total[step * 2 * CAP : (step + 1) * 2 * CAP].astype(BF16)


def load_body(after, *refs):
    count = len(refs) // 2
    sems = refs[-1]
    loads = [
        pltpu.make_async_copy(refs[place], refs[count + place], sems.at[place])
        for place in range(count)
    ]
    for load in loads:
        load.start()
    for load in loads:
        load.wait()


def take_rows(offset, pieces, stack):
    place = 0
    for ref in pieces:
        stack[place : place + ref.shape[0], :] = ref[...].astype(F32)
        place += ref.shape[0]
    count = place // 2
    rows = iota((count, place), 0)
    mover = iota((count, place), 1) == rows + over_cap(rows) * CAP + offset
    return dot(mover.astype(F32).astype(BF16), stack[...].astype(BF16)).astype(BF16)


def forward_body(w_gate, w_up, *refs):
    pieces, (rows_out, keep, send, stack) = refs[:-4], refs[-4:]
    half = w_gate.shape[1] // 2
    rows = take_rows(0, pieces, stack)
    rows_out[...] = rows
    for target, far in ((send, True), (keep, False)):
        columns = core_columns(half, far)
        target[:, :half] = dot(rows, w_gate[:, columns]).astype(BF16)
        target[:, half:] = dot(rows, w_up[:, columns]).astype(BF16)


def hidden_body(w_down, *refs):
    pieces, (keep, send, stack) = refs[:-3], refs[-3:]
    half = w_down.shape[0] // 2
    rows = take_rows(CAP, pieces, stack)
    for target, far in ((send, True), (keep, False)):
        target[...] = dot(rows, w_down[core_columns(half, far), :], 1, 1).astype(BF16)


def activate_body(pre_own, pre_far, hid_own, hid_far, acts):
    half = hid_own.shape[1]
    pre = pre_own[...].astype(F32) + pre_far[...].astype(F32)
    hidden_grad = hid_own[...].astype(F32) + hid_far[...].astype(F32)
    gate_pre = pre[:, :half]
    up_pre = pre[:, half:]
    sigma = jax.nn.sigmoid(gate_pre)
    acts[:, :half] = (hidden_grad * up_pre * sigma * (1.0 + gate_pre * (1.0 - sigma))).astype(BF16)
    acts[:, half:] = (hidden_grad * gate_pre * sigma).astype(BF16)


def back_part(w_gate, w_up, acts, far):
    half = w_gate.shape[1] // 2
    columns = core_columns(half, far)
    part = dot(acts[:, :half], w_gate[:, columns], 1, 1)
    return part + dot(acts[:, half:], w_up[:, columns], 1, 1)


def back_own_body(w_gate, w_up, acts, total):
    total[...] = back_part(w_gate, w_up, acts, False)


def back_far_body(w_gate, w_up, acts, own, *outs):
    count = outs[0].shape[0]
    total = own[...] + back_part(w_gate, w_up, acts, True)
    for place, out in enumerate(outs):
        out[...] = total[place * count : (place + 1) * count].astype(BF16)


def weight_body(which, chunks, after, rows_ref, acts_own, acts_far, out, token, tile, sems):
    token[...] = jnp.zeros_like(token)
    half = out.shape[1] // 2
    depth = out.shape[0] // chunks
    stores = []
    for chunk in range(chunks):
        span = slice(chunk * depth, (chunk + 1) * depth)
        rows = rows_ref[:, span]
        for acts, far in ((acts_own, False), (acts_far, True)):
            part = dot(rows, acts[:, which * half : (which + 1) * half], 0, 0)
            tile[span, core_columns(half, far)] = part.astype(BF16)
        stores.append(pltpu.make_async_copy(tile.at[span], out.at[span], sems.at[chunk]))
        stores[-1].start()
    for store in stores:
        store.wait()


def gather_body(fold, experts, after, own, one, two, three, *outs):
    total = own[...].astype(F32) + one[...].astype(F32)
    total = (total + (two[...].astype(F32) + three[...].astype(F32))).astype(BF16)
    count = total.shape[0]
    width = total.shape[1] // fold
    piece = CAP * fold
    rows = iota((fold * count, count), 1)
    folded = None
    for part in range(fold):
        goal = rows + over_cap(rows) * (CAP * (fold - 1)) + part * CAP
        mover = (iota((fold * count, count), 0) == goal).astype(F32).astype(BF16)
        moved = dot(mover, total[:, part * width : (part + 1) * width])
        folded = moved if folded is None else folded + moved
    for step in range(experts):
        outs[step][...] = folded[step * piece : (step + 1) * piece].astype(BF16)


def scatter_body(fold, experts, *refs):
    picks, pieces = refs[:fold], refs[fold : fold + experts]
    out, stack, tile, sems = refs[-4:]
    width = out.shape[1] // fold
    piece = CAP * fold
    for step in range(experts):
        stack[step * piece : (step + 1) * piece, :] = pieces[step][...].astype(F32)
    returned = stack[...].astype(BF16)
    stores = []
    for part in range(fold):
        span = slice(part * width, (part + 1) * width)
        tile[:, span] = dot(picks[part][...], returned, 0, 0).astype(BF16)
        stores.append(pltpu.make_async_copy(tile.at[:, span], out.at[:, span], sems.at[part]))
        stores[-1].start()
    for store in stores:
        store.wait()


def per_device(out_grad, inputs, expert_ids, gate_weights, w_gate, w_up, w_down):
    devices = lax.axis_size("expert")
    spread = lax.axis_size("dp")
    experts = devices // HSPLIT
    tokens, features = out_grad.shape
    routed = expert_ids.shape[1]
    fold = fold_of(features)
    hidden = w_gate.shape[1]
    half = hidden // 2
    count = devices * CAP
    product = 2 * count * features * hidden
    dma = pltpu.SemaphoreType.DMA

    def to_expert(value, step):
        pairs = [(d, (d + step * HSPLIT) % devices) for d in range(devices)]
        return lax.ppermute(value, "expert", pairs)

    def to_peer(value, flip):
        return lax.ppermute(value, "expert", [(d, d ^ flip) for d in range(devices)])

    def to_dp(value, flip):
        return lax.ppermute(value, "dp", [(d, d ^ flip) for d in range(spread)])

    picked = run(
        functools.partial(pick_body, experts, fold),
        (shape((experts * fold * CAP, tokens)),) * fold
        + (shape((2 * CAP, features)),) * experts,
        [HBM] * 4,
        8 * experts * CAP * tokens * features,
        4 * tokens * features,
        *(in_hbm(array) for array in (expert_ids.T, gate_weights.T, out_grad, inputs)),
        scratch=(
            pltpu.VMEM((routed, tokens), jnp.int32),
            pltpu.VMEM((routed, tokens), F32),
            pltpu.VMEM((tokens, features), BF16),
            pltpu.VMEM((tokens, features), BF16),
            dma((4,)),
        ),
    )
    picks, own = picked[:fold], picked[fold:]
    weights = (w_gate, w_up, w_down)
    gate_here, up_here, down_here = run(
        load_body,
        tuple(pltpu.VMEM(weight.shape, weight.dtype) for weight in weights),
        [ANY] + [HBM] * 3,
        0,
        6 * features * hidden,
        picks[0],
        *(in_hbm(weight) for weight in weights),
        scratch=(dma((3,)),),
    )

    away = [to_expert(own[step], step) for step in range(1, experts)]
    pieces = [own[0]] + [to_peer(own[0], flip) for flip in range(1, HSPLIT)]
    if away:
        away = away[0] if len(away) == 1 else jnp.concatenate(away, axis=0)
        others = [away] + [to_peer(away, flip) for flip in range(1, HSPLIT)]
        pieces = [array for pair in zip(pieces, others) for array in pair]

    stack = pltpu.VMEM((2 * count, features), F32)
    rows_input, pre_keep, pre_send = run(
        forward_body,
        (shape((count, features)), shape((count, hidden)), shape((count, hidden))),
        [VMEM] * (2 + len(pieces)),
        2 * product,
        4 * features * hidden,
        gate_here,
        up_here,
        *pieces,
        scratch=(stack,),
    )

    def spread_sum(keep, send):
        near = (keep.astype(F32) + to_dp(send, 1).astype(F32)).astype(BF16)
        flip = 2
        far = jnp.zeros_like(near)
        while flip < spread:
            far = to_dp(near, flip)
            flip *= 2
            if flip < spread:
                near = (near.astype(F32) + far.astype(F32)).astype(BF16)
        return near, far

    pre_own, pre_far = spread_sum(pre_keep, pre_send)
    hid_keep, hid_send = run(
        hidden_body,
        (shape((count, half)), shape((count, half))),
        [VMEM] * (1 + len(pieces)),
        product,
        2 * features * hidden,
        down_here,
        *pieces,
        scratch=(stack,),
    )
    hid_own, hid_far = spread_sum(hid_keep, hid_send)
    acts = run(
        activate_body,
        shape((count, hidden)),
        [VMEM] * 4,
        20 * count * half,
        10 * count * half,
        pre_own,
        pre_far,
        hid_own,
        hid_far,
    )
    acts_far = to_dp(acts, 1)
    back_own = run(
        back_own_body,
        shape((count, features), F32),
        [VMEM] * 3,
        product,
        2 * features * hidden,
        gate_here,
        up_here,
        acts,
    )
    back = run(
        back_far_body,
        (shape((count // HSPLIT, features)),) * HSPLIT,
        [VMEM] * 4,
        product,
        2 * features * hidden,
        gate_here,
        up_here,
        acts_far,
        back_own,
    )
    back_far = [to_peer(back[flip], flip) for flip in range(1, HSPLIT)]

    def weight_grad(which, after):
        chunks = 2
        return run(
            functools.partial(weight_body, which, chunks),
            (shape((features, hidden)), shape((8, 128), F32)),
            [ANY] + [VMEM] * 3,
            product,
            4 * features * hidden,
            after,
            rows_input,
            acts,
            acts_far,
            out_spec=(HBM, VMEM),
            scratch=(pltpu.VMEM((features, hidden), BF16), dma((chunks,))),
        )

    grad_gate, token = weight_grad(0, back[0])
    summed = run(
        functools.partial(gather_body, fold, experts),
        (shape((CAP * fold, features // fold)),) * experts,
        [ANY] + [VMEM] * HSPLIT,
        4 * count * features,
        4 * count * features,
        token,
        back[0],
        *back_far,
    )
    grad_up, _ = weight_grad(1, summed[0])
    returned = [summed[0]] + [to_expert(summed[step], experts - step) for step in range(1, experts)]
    in_grad = run(
        functools.partial(scatter_body, fold, experts),
        shape((tokens, features)),
        [VMEM] * (fold + experts),
        4 * experts * CAP * tokens * features,
        2 * tokens * features,
        *picks,
        *returned,
        out_spec=HBM,
        scratch=(
            pltpu.VMEM((experts * fold * CAP, features // fold), F32),
            pltpu.VMEM((tokens, features), BF16),
            dma((fold,)),
        ),
    )
    return (in_grad, grad_gate, grad_up)


def solution(mesh):
    placed = (
        P("expert", "dp"),
        P("expert", "dp"),
        P("expert", None),
        P("expert", None),
        P("dp", "expert"),
        P("dp", "expert"),
        P("expert", "dp"),
    )
    return jax.shard_map(
        per_device,
        mesh=mesh,
        in_specs=placed,
        out_specs=(P("expert", "dp"), P("dp", "expert"), P("dp", "expert")),
        check_vma=False,
    )
```

time: 135 us -> 43.7 us (0.32)
  waiting for transfers between devices: 61.6 us -> 8.32 us
  local copies, waits for them, and re-layouts: 18.2 us -> 0 us
  between operations: 14.3 us -> 0.77 us
  matrix products: 13.1 us -> 0 us
  Pallas kernels: 0 us -> 13.1 us
  other arithmetic: 10.6 us -> 0.04 us
  starting transfers between devices: 16.6 us -> 21.2 us
    psum x1 -> x0, waiting for transfers between devices: 31.4 us -> none  [per_device(): lax.psum(down_part.astype(jnp.bfloat16), 'dp').astype(jnp.float32)]
    all_to_all x3 -> x0, waiting for transfers between devices: 30.3 us -> none  [the longest x1 12.4 us: per_device(): lax.all_to_all(sent_input, 'expert', split_axis=0, concat_axis=0, tiled=T...]
    ppermute x0 -> x16, starting transfers between devices: none -> 21.2 us  [the longest x9 10.9 us: to_peer(): lax.ppermute(value, 'expert', [(d, d ^ flip) for d in range(devices)])]
    all_to_all x3 -> x0, starting transfers between devices: 16.6 us -> none  [the longest x1 7.28 us: per_device(): lax.all_to_all(sent_input, 'expert', split_axis=0, concat_axis=0, tiled=T...]
    pallas_call x0 -> x11, Pallas kernels: none -> 13.1 us  [run(): pl.pallas_call(body, out_shape=outs, in_specs=specs, out_specs=out_spec i...]
    dot_general x9 -> x0, matrix products: 13.1 us -> none  [the longest x5 9.18 us: contract(): lax.dot_general(left, right, (((left_dim,), (right_dim,)), ((), ())), pre...]
    gather x1 -> x0, local copies, waits for them, and re-layouts: 12.4 us -> none  [per_device(): fetched = jnp.take(summed, jnp.where(kept, target, 0), axis=0)]
    reduce_sum x5 -> x0, other arithmetic: 9.57 us -> none  [the longest x1 9.16 us: per_device(): jnp.sum(jnp.where(kept[:, :, None], fetched, 0.0), axis=1)]
  transfers between devices with their start and end apart: 4 -> 16, of which waited for: 4 -> 7; matrix products, arithmetic and copies ran while one was open for 6% -> 0% of each run, Pallas kernels for 0% -> 18%
where the time goes in v1:
time: 43.7 us; the launch traced here: 43.4 us
  starting transfers between devices  21.2 us (49%)
  Pallas kernels  13.1 us (30%)
  waiting for transfers between devices  8.32 us (19%)
  between operations  0.77 us (2%)
    pallas_call x11, Pallas kernels, run(): pl.pallas_call(body, out_shape=outs, in_specs=specs, out_specs=out_spec i...  13.1 us
    ppermute x9, starting transfers between devices, to_peer(): lax.ppermute(value, 'expert', [(d, d ^ flip) for d in range(devices)])  10.9 us
    ppermute x2, starting transfers between devices, to_expert(): return lax.ppermute(value, 'expert', pairs)  7.23 us
    ppermute x5, waiting for transfers between devices, to_dp(): return lax.ppermute(value, 'dp', [(d, d ^ flip) for d in range(spread)])  4.11 us
    ppermute x9, waiting for transfers between devices, to_peer(): lax.ppermute(value, 'expert', [(d, d ^ flip) for d in range(devices)])  3.67 us
    ppermute x5, starting transfers between devices, to_dp(): return lax.ppermute(value, 'dp', [(d, d ^ flip) for d in range(spread)])  3.1 us
  transfers between devices with their start and end apart: 16, of which 7 were waited for; matrix products, arithmetic and copies ran while one was open for 0% of the time, Pallas kernels for 18%

profile of v1, /device:TPU:0, one launch (start us, length us, event | category | flops | bytes accessed | tf_op | source)
XLA Modules:
  0.0 43.4 jit_solution(8666961822462125391)
XLA Ops:
  0.6 2.0 %shard_map.94 = (bf16[48,256]{1,0:T(8,128)(2,1)S(1)}, bf16[48,256]{1,0:T(8,128)(2,1)S(1)}, bf16[24,1792]{1,0:T(8,128)(2,1)S(1)}, bf16[24,1792]{1,0:T(8,128)(2,1)S(1)}) custom-call(s32[8,256]{1,0:T(8,128)} %bitcast.2, f32[8,256]{1,0:T(8,128)} %bitcast.3, bf16[256,1792]{1,0:T(8,128)(2,1)} %grads_hbm.1, bf16[256,1792]{1,0:T(8,128)(2,1)} %inputs_hbm.1), custom_call_target="tpu_custom_call" | custom-call | flops 88080384 | bytes 1835008 | tf_op jit(solution)/shard_map/pallas_call | solution.py:24
  2.6 4.1 %collective-permute-start = (bf16[24,1792]{1,0:T(8,128)(2,1)S(1)}, bf16[24,1792]{1,0:T(8,128)(2,1)S(1)}, u32[]{:S(2)}, u32[]{:S(2)}) collective-permute-start(bf16[24,1792]{1,0:T(8,128)(2,1)S(1)} %get-tuple-element.29), channel_id=1, source_target_pairs={{0,4},{1,5},{2,6},{3,7},{4,0},{5,1},{6,2},{7,3},{8,12},{9,13},{10,... | collective-permute-start | bytes 258056 | tf_op jit(solution)/shard_map/ppermute | solution.py:261
  6.7 2.5 %collective-permute-start.5 = (bf16[24,1792]{1,0:T(8,128)(2,1)S(1)}, bf16[24,1792]{1,0:T(8,128)(2,1)S(1)}, u32[]{:S(2)}, u32[]{:S(2)}) collective-permute-start(bf16[24,1792]{1,0:T(8,128)(2,1)S(1)} %get-tuple-element.28.refs_0_), channel_id=1, source_target_pairs={{0,3},{1,2},{2,1},{3,0},{4,7},{5,6},{6,5},{7,4},{8,11},{9,10},{10,... | collective-permute-start | bytes 258056 | tf_op jit(solution)/shard_map/ppermute | solution.py:264
  9.3 0.4 %collective-permute-start.3 = (bf16[24,1792]{1,0:T(8,128)(2,1)S(1)}, bf16[24,1792]{1,0:T(8,128)(2,1)S(1)}, u32[]{:S(2)}, u32[]{:S(2)}) collective-permute-start(bf16[24,1792]{1,0:T(8,128)(2,1)S(1)} %get-tuple-element.28.refs_0_), channel_id=1, source_target_pairs={{0,2},{1,3},{2,0},{3,1},{4,6},{5,7},{6,4},{7,5},{8,10},{9,11},{10,... | collective-permute-start | bytes 258056 | tf_op jit(solution)/shard_map/ppermute | solution.py:264
  9.7 0.5 %collective-permute-start.1 = (bf16[24,1792]{1,0:T(8,128)(2,1)S(1)}, bf16[24,1792]{1,0:T(8,128)(2,1)S(1)}, u32[]{:S(2)}, u32[]{:S(2)}) collective-permute-start(bf16[24,1792]{1,0:T(8,128)(2,1)S(1)} %get-tuple-element.28.refs_0_), channel_id=1, source_target_pairs={{0,1},{1,0},{2,3},{3,2},{4,5},{5,4},{6,7},{7,6},{8,9},{9,8},{10,11... | collective-permute-start | bytes 258056 | tf_op jit(solution)/shard_map/ppermute | solution.py:264
  10.2 0.5 %collective-permute-done.refs_1_ = bf16[24,1792]{1,0:T(8,128)(2,1)S(1)} collective-permute-done((bf16[24,1792]{1,0:T(8,128)(2,1)S(1)}, bf16[24,1792]{1,0:T(8,128)(2,1)S(1)}, u32[]{:S(2)}, u32[]{:S(2)}) %collective-permute-start) | collective-permute-done | bytes 86048 | tf_op jit(solution)/shard_map/ppermute | solution.py:261
  10.8 2.2 %collective-permute-start.6 = (bf16[24,1792]{1,0:T(8,128)(2,1)S(1)}, bf16[24,1792]{1,0:T(8,128)(2,1)S(1)}, u32[]{:S(2)}, u32[]{:S(2)}) collective-permute-start(bf16[24,1792]{1,0:T(8,128)(2,1)S(1)} %collective-permute-done.refs_1_), channel_id=1, source_target_pairs={{0,3},{1,2},{2,1},{3,0},{4,7},{5,6},{6,5},{7,4},{8,11},{9,10},{10,... | collective-permute-start | bytes 258056 | tf_op jit(solution)/shard_map/ppermute | solution.py:264
  13.0 1.0 %collective-permute-start.4 = (bf16[24,1792]{1,0:T(8,128)(2,1)S(1)}, bf16[24,1792]{1,0:T(8,128)(2,1)S(1)}, u32[]{:S(2)}, u32[]{:S(2)}) collective-permute-start(bf16[24,1792]{1,0:T(8,128)(2,1)S(1)} %collective-permute-done.refs_1_), channel_id=1, source_target_pairs={{0,2},{1,3},{2,0},{3,1},{4,6},{5,7},{6,4},{7,5},{8,10},{9,11},{10,... | collective-permute-start | bytes 258056 | tf_op jit(solution)/shard_map/ppermute | solution.py:264
  14.0 0.6 %collective-permute-start.2 = (bf16[24,1792]{1,0:T(8,128)(2,1)S(1)}, bf16[24,1792]{1,0:T(8,128)(2,1)S(1)}, u32[]{:S(2)}, u32[]{:S(2)}) collective-permute-start(bf16[24,1792]{1,0:T(8,128)(2,1)S(1)} %collective-permute-done.refs_1_), channel_id=1, source_target_pairs={{0,1},{1,0},{2,3},{3,2},{4,5},{5,4},{6,7},{7,6},{8,9},{9,8},{10,11... | collective-permute-start | bytes 258056 | tf_op jit(solution)/shard_map/ppermute | solution.py:264
  14.6 2.6 %shard_map.95 = (bf16[1792,512]{1,0:T(8,128)(2,1)S(1)}, bf16[1792,512]{1,0:T(8,128)(2,1)S(1)}, bf16[512,1792]{1,0:T(8,128)(2,1)S(1)}) custom-call(bf16[48,256]{1,0:T(8,128)(2,1)S(1)} %get-tuple-element.24.after.refs_0_, bf16[1792,512]{1,0:T(8,128)(2,1)} %refs_0_.1, bf16[1792,512]{1,0:T(8,128)(2,1)} %refs_1_.1, bf16[512,1792]{1,0:T(8,128)(2,1)} %refs_2_.1), custom_call_target="tpu_custom_call" | custom-call | bytes 5505024 | tf_op jit(solution)/shard_map/pallas_call | solution.py:24
  17.3 0.4 collective-permute-done.4.refs_5_
  17.7 0.8 %collective-permute-done.2.refs_3_ = bf16[24,1792]{1,0:T(8,128)(2,1)S(1)} collective-permute-done((bf16[24,1792]{1,0:T(8,128)(2,1)S(1)}, bf16[24,1792]{1,0:T(8,128)(2,1)S(1)}, u32[]{:S(2)}, u32[]{:S(2)}) %collective-permute-start.2) | collective-permute-done | bytes 86048 | tf_op jit(solution)/shard_map/ppermute | solution.py:264
  18.5 0.9 %shard_map.96 = (bf16[96,1792]{1,0:T(8,128)(2,1)S(1)}, bf16[96,512]{1,0:T(8,128)(2,1)S(1)}, bf16[96,512]{1,0:T(8,128)(2,1)S(1)}) custom-call(bf16[1792,512]{1,0:T(8,128)(2,1)S(1)} %get-tuple-element.26.w_gate, bf16[1792,512]{1,0:T(8,128)(2,1)S(1)} %get-tuple-element.27.w_up, bf16[24,1792]{1,0:T(8,128)(2,1)S(1)} %get-tuple-element.28.refs_0_, ...), custom_call_target="tpu_custom_call" | custom-call | flops 352321536 | bytes 3670016 | tf_op jit(solution)/shard_map/pallas_call | solution.py:24
  19.4 0.8 %shard_map.97 = (bf16[96,256]{1,0:T(8,128)(2,1)S(1)}, bf16[96,256]{1,0:T(8,128)(2,1)S(1)}) custom-call(bf16[512,1792]{1,0:T(8,128)(2,1)S(1)} %get-tuple-element.32.w_down, bf16[24,1792]{1,0:T(8,128)(2,1)S(1)} %get-tuple-element.28.refs_0_, bf16[24,1792]{1,0:T(8,128)(2,1)S(1)} %collective-permute-done.refs_1_, ...), custom_call_target="tpu_custom_call" | custom-call | flops 176160768 | bytes 1835008 | tf_op jit(solution)/shard_map/pallas_call | solution.py:24
  20.2 0.6 %collective-permute-start.9 = (bf16[96,256]{1,0:T(8,128)(2,1)S(1)}, bf16[96,256]{1,0:T(8,128)(2,1)S(1)}, u32[]{:S(2)}, u32[]{:S(2)}) collective-permute-start(bf16[96,256]{1,0:T(8,128)(2,1)S(1)} %get-tuple-element.34), channel_id=1, source_target_pairs={{0,8},{8,0},{16,24},{24,16},{1,9},{9,1},{17,25},{25,17},{2,10},{10... | collective-permute-start | bytes 147464 | tf_op jit(solution)/shard_map/ppermute | solution.py:267
  20.8 1.6 %collective-permute-start.8 = (bf16[96,512]{1,0:T(8,128)(2,1)S(1)}, bf16[96,512]{1,0:T(8,128)(2,1)S(1)}, u32[]{:S(2)}, u32[]{:S(2)}) collective-permute-start(bf16[96,512]{1,0:T(8,128)(2,1)S(1)} %add_convert_fusion.pre_own), channel_id=1, source_target_pairs={{0,16},{8,24},{16,0},{24,8},{1,17},{9,25},{17,1},{25,9},{2,18},{10... | collective-permute-start | bytes 294920 | tf_op jit(solution)/shard_map/ppermute | solution.py:267
  22.4 0.8 %collective-permute-start.10 = (bf16[96,256]{1,0:T(8,128)(2,1)S(1)}, bf16[96,256]{1,0:T(8,128)(2,1)S(1)}, u32[]{:S(2)}, u32[]{:S(2)}) collective-permute-start(bf16[96,256]{1,0:T(8,128)(2,1)S(1)} %add_convert_fusion.1.hid_own), channel_id=1, source_target_pairs={{0,16},{8,24},{16,0},{24,8},{1,17},{9,25},{17,1},{25,9},{2,18},{10... | collective-permute-start | bytes 147464 | tf_op jit(solution)/shard_map/ppermute | solution.py:267
  23.2 3.5 %collective-permute-done.10.hid_far = bf16[96,256]{1,0:T(8,128)(2,1)S(1)} collective-permute-done((bf16[96,256]{1,0:T(8,128)(2,1)S(1)}, bf16[96,256]{1,0:T(8,128)(2,1)S(1)}, u32[]{:S(2)}, u32[]{:S(2)}) %collective-permute-start.10) | collective-permute-done | bytes 49184 | tf_op jit(solution)/shard_map/ppermute | solution.py:267
  26.8 0.1 collective-permute-start.11
  26.9 0.7 %shard_map.99.own = f32[96,1792]{1,0:T(8,128)S(1)} custom-call(bf16[1792,512]{1,0:T(8,128)(2,1)S(1)} %get-tuple-element.26.w_gate, bf16[1792,512]{1,0:T(8,128)(2,1)S(1)} %get-tuple-element.27.w_up, bf16[96,512]{1,0:T(8,128)(2,1)S(1)} %shard_map.98.acts.acts_own), custom_call_target="tpu_custom_call" | custom-call | flops 176160768 | bytes 1835008 | tf_op jit(solution)/shard_map/pallas_call | solution.py:24
  27.6 0.6 %collective-permute-done.11.acts.acts_far = bf16[96,512]{1,0:T(8,128)(2,1)S(1)} collective-permute-done((bf16[96,512]{1,0:T(8,128)(2,1)S(1)}, bf16[96,512]{1,0:T(8,128)(2,1)S(1)}, u32[]{:S(2)}, u32[]{:S(2)}) %collective-permute-start.11) | collective-permute-done | bytes 98336 | tf_op jit(solution)/shard_map/ppermute | solution.py:267
  28.2 0.7 %shard_map.100 = (bf16[24,1792]{1,0:T(8,128)(2,1)S(1)}, bf16[24,1792]{1,0:T(8,128)(2,1)S(1)}, bf16[24,1792]{1,0:T(8,128)(2,1)S(1)}, bf16[24,1792]{1,0:T(8,128)(2,1)S(1)}) custom-call(bf16[1792,512]{1,0:T(8,128)(2,1)S(1)} %get-tuple-element.26.w_gate, bf16[1792,512]{1,0:T(8,128)(2,1)S(1)} %get-tuple-element.27.w_up, ...), custom_call_target="tpu_custom_call" | custom-call | flops 176160768 | bytes 1835008 | tf_op jit(solution)/shard_map/pallas_call | solution.py:24
  28.9 0.7 %collective-permute-start.12 = (bf16[24,1792]{1,0:T(8,128)(2,1)S(1)}, bf16[24,1792]{1,0:T(8,128)(2,1)S(1)}, u32[]{:S(2)}, u32[]{:S(2)}) collective-permute-start(bf16[24,1792]{1,0:T(8,128)(2,1)S(1)} %get-tuple-element.38), channel_id=1, source_target_pairs={{0,1},{1,0},{2,3},{3,2},{4,5},{5,4},{6,7},{7,6},{8,9},{9,8},{10,11... | collective-permute-start | bytes 258056 | tf_op jit(solution)/shard_map/ppermute | solution.py:264
  29.6 1.1 %collective-permute-start.13 = (bf16[24,1792]{1,0:T(8,128)(2,1)S(1)}, bf16[24,1792]{1,0:T(8,128)(2,1)S(1)}, u32[]{:S(2)}, u32[]{:S(2)}) collective-permute-start(bf16[24,1792]{1,0:T(8,128)(2,1)S(1)} %get-tuple-element.39), channel_id=1, source_target_pairs={{0,2},{1,3},{2,0},{3,1},{4,6},{5,7},{6,4},{7,5},{8,10},{9,11},{10,... | collective-permute-start | bytes 258056 | tf_op jit(solution)/shard_map/ppermute | solution.py:264
  30.7 1.7 %collective-permute-start.14 = (bf16[24,1792]{1,0:T(8,128)(2,1)S(1)}, bf16[24,1792]{1,0:T(8,128)(2,1)S(1)}, u32[]{:S(2)}, u32[]{:S(2)}) collective-permute-start(bf16[24,1792]{1,0:T(8,128)(2,1)S(1)} %get-tuple-element.40), channel_id=1, source_target_pairs={{0,3},{1,2},{2,1},{3,0},{4,7},{5,6},{6,5},{7,4},{8,11},{9,10},{10,... | collective-permute-start | bytes 258056 | tf_op jit(solution)/shard_map/ppermute | solution.py:264
  32.4 1.7 %shard_map.101 = (bf16[1792,512]{1,0:T(8,128)(2,1)}, f32[8,128]{1,0:T(8,128)S(1)}) custom-call(bf16[24,1792]{1,0:T(8,128)(2,1)S(1)} %get-tuple-element.35.after.own, bf16[96,1792]{1,0:T(8,128)(2,1)S(1)} %get-tuple-element.36.rows_ref, bf16[96,512]{1,0:T(8,128)(2,1)S(1)} %shard_map.98.acts.acts_own, bf16[96,512]{1,0:T(8,128)(2,1)S(1)} %collective-permute-done.11.acts.acts_far), custom_call_target="tpu_custom_call" | custom-call | flops 176160768 | bytes 3670016 | tf_op jit(solution)/shard_map/pallas_call | solution.py:24
  34.1 0.5 %collective-permute-done.13.two = bf16[24,1792]{1,0:T(8,128)(2,1)S(1)} collective-permute-done((bf16[24,1792]{1,0:T(8,128)(2,1)S(1)}, bf16[24,1792]{1,0:T(8,128)(2,1)S(1)}, u32[]{:S(2)}, u32[]{:S(2)}) %collective-permute-start.13) | collective-permute-done | bytes 86048 | tf_op jit(solution)/shard_map/ppermute | solution.py:264
  34.6 2.0 %collective-permute-done.14.three = bf16[24,1792]{1,0:T(8,128)(2,1)S(1)} collective-permute-done((bf16[24,1792]{1,0:T(8,128)(2,1)S(1)}, bf16[24,1792]{1,0:T(8,128)(2,1)S(1)}, u32[]{:S(2)}, u32[]{:S(2)}) %collective-permute-start.14) | collective-permute-done | bytes 86048 | tf_op jit(solution)/shard_map/ppermute | solution.py:264
  36.6 0.2 shard_map.102
  36.8 3.1 %collective-permute-start.15 = (bf16[24,896]{1,0:T(8,128)(2,1)S(1)}, bf16[24,896]{1,0:T(8,128)(2,1)S(1)}, u32[]{:S(2)}, u32[]{:S(2)}) collective-permute-start(bf16[24,896]{1,0:T(8,128)(2,1)S(1)} %get-tuple-element.42), channel_id=1, source_target_pairs={{0,4},{1,5},{2,6},{3,7},{4,0},{5,1},{6,2},{7,3},{8,12},{9,13},{10,... | collective-permute-start | bytes 129032 | tf_op jit(solution)/shard_map/ppermute | solution.py:261
  39.9 2.3 %shard_map.104 = (bf16[1792,512]{1,0:T(8,128)(2,1)}, f32[8,128]{1,0:T(8,128)}) custom-call(bf16[24,896]{1,0:T(8,128)(2,1)S(1)} %get-tuple-element.41.refs_2_.after, bf16[96,1792]{1,0:T(8,128)(2,1)S(1)} %get-tuple-element.36.rows_ref, bf16[96,512]{1,0:T(8,128)(2,1)S(1)} %shard_map.98.acts.acts_own, bf16[96,512]{1,0:T(8,128)(2,1)S(1)} %collective-permute-done.11.acts.acts_far), custom_call_target="tpu_custom_call" | custom-call | flops 176160768 | bytes 3670016 | tf_op jit(solution)/shard_map/pallas_call | solution.py:24
  42.2 1.3 %shard_map.103 = bf16[256,1792]{1,0:T(8,128)(2,1)} custom-call(bf16[48,256]{1,0:T(8,128)(2,1)S(1)} %get-tuple-element.24.after.refs_0_, bf16[48,256]{1,0:T(8,128)(2,1)S(1)} %get-tuple-element.25.refs_1_, bf16[24,896]{1,0:T(8,128)(2,1)S(1)} %get-tuple-element.41.refs_2_.after, bf16[24,896]{1,0:T(8,128)(2,1)S(1)} %collective-permute-done.15.refs_3_), custom_call_target="tpu_custom_call" | custom-call | flops 44040192 | bytes 917504 | tf_op jit(solution)/shard_map/pallas_call | solution.py:24
  (13 shorter events, 0.2 us)
Async XLA Ops:
  2.6 8.1 %collective-permute-start = (bf16[24,1792]{1,0:T(8,128)(2,1)S(1)}, bf16[24,1792]{1,0:T(8,128)(2,1)S(1)}, u32[]{:S(2)}, u32[]{:S(2)}) collective-permute-start(bf16[24,1792]{1,0:T(8,128)(2,1)S(1)} %get-tuple-element.29), channel_id=1, source_target_pairs={{0,4},{1,5},{2,6},{3,7},{4,0},{5,1},{6,2},{7,3},{8,12},{9,13},{10,... | collective-permute-start | bytes 258056 | tf_op jit(solution)/shard_map/ppermute | solution.py:261
  6.7 7.3 %collective-permute-start.5 = (bf16[24,1792]{1,0:T(8,128)(2,1)S(1)}, bf16[24,1792]{1,0:T(8,128)(2,1)S(1)}, u32[]{:S(2)}, u32[]{:S(2)}) collective-permute-start(bf16[24,1792]{1,0:T(8,128)(2,1)S(1)} %get-tuple-element.28.refs_0_), channel_id=1, source_target_pairs={{0,3},{1,2},{2,1},{3,0},{4,7},{5,6},{6,5},{7,4},{8,11},{9,10},{10,... | collective-permute-start | bytes 258056 | tf_op jit(solution)/shard_map/ppermute | solution.py:264
  9.3 8.0 %collective-permute-start.3 = (bf16[24,1792]{1,0:T(8,128)(2,1)S(1)}, bf16[24,1792]{1,0:T(8,128)(2,1)S(1)}, u32[]{:S(2)}, u32[]{:S(2)}) collective-permute-start(bf16[24,1792]{1,0:T(8,128)(2,1)S(1)} %get-tuple-element.28.refs_0_), channel_id=1, source_target_pairs={{0,2},{1,3},{2,0},{3,1},{4,6},{5,7},{6,4},{7,5},{8,10},{9,11},{10,... | collective-permute-start | bytes 258056 | tf_op jit(solution)/shard_map/ppermute | solution.py:264
  9.7 7.6 %collective-permute-start.1 = (bf16[24,1792]{1,0:T(8,128)(2,1)S(1)}, bf16[24,1792]{1,0:T(8,128)(2,1)S(1)}, u32[]{:S(2)}, u32[]{:S(2)}) collective-permute-start(bf16[24,1792]{1,0:T(8,128)(2,1)S(1)} %get-tuple-element.28.refs_0_), channel_id=1, source_target_pairs={{0,1},{1,0},{2,3},{3,2},{4,5},{5,4},{6,7},{7,6},{8,9},{9,8},{10,11... | collective-permute-start | bytes 258056 | tf_op jit(solution)/shard_map/ppermute | solution.py:264
  10.8 6.5 %collective-permute-start.6 = (bf16[24,1792]{1,0:T(8,128)(2,1)S(1)}, bf16[24,1792]{1,0:T(8,128)(2,1)S(1)}, u32[]{:S(2)}, u32[]{:S(2)}) collective-permute-start(bf16[24,1792]{1,0:T(8,128)(2,1)S(1)} %collective-permute-done.refs_1_), channel_id=1, source_target_pairs={{0,3},{1,2},{2,1},{3,0},{4,7},{5,6},{6,5},{7,4},{8,11},{9,10},{10,... | collective-permute-start | bytes 258056 | tf_op jit(solution)/shard_map/ppermute | solution.py:264
  13.0 4.7 %collective-permute-start.4 = (bf16[24,1792]{1,0:T(8,128)(2,1)S(1)}, bf16[24,1792]{1,0:T(8,128)(2,1)S(1)}, u32[]{:S(2)}, u32[]{:S(2)}) collective-permute-start(bf16[24,1792]{1,0:T(8,128)(2,1)S(1)} %collective-permute-done.refs_1_), channel_id=1, source_target_pairs={{0,2},{1,3},{2,0},{3,1},{4,6},{5,7},{6,4},{7,5},{8,10},{9,11},{10,... | collective-permute-start | bytes 258056 | tf_op jit(solution)/shard_map/ppermute | solution.py:264
  14.0 4.5 %collective-permute-start.2 = (bf16[24,1792]{1,0:T(8,128)(2,1)S(1)}, bf16[24,1792]{1,0:T(8,128)(2,1)S(1)}, u32[]{:S(2)}, u32[]{:S(2)}) collective-permute-start(bf16[24,1792]{1,0:T(8,128)(2,1)S(1)} %collective-permute-done.refs_1_), channel_id=1, source_target_pairs={{0,1},{1,0},{2,3},{3,2},{4,5},{5,4},{6,7},{7,6},{8,9},{9,8},{10,11... | collective-permute-start | bytes 258056 | tf_op jit(solution)/shard_map/ppermute | solution.py:264
  19.4 1.4 %collective-permute-start.7 = (bf16[96,512]{1,0:T(8,128)(2,1)S(1)}, bf16[96,512]{1,0:T(8,128)(2,1)S(1)}, u32[]{:S(2)}, u32[]{:S(2)}) collective-permute-start(bf16[96,512]{1,0:T(8,128)(2,1)S(1)} %get-tuple-element.31), channel_id=1, source_target_pairs={{0,8},{8,0},{16,24},{24,16},{1,9},{9,1},{17,25},{25,17},{2,10},{10... | collective-permute-start | bytes 294920 | tf_op jit(solution)/shard_map/ppermute | solution.py:267
  20.2 2.2 %collective-permute-start.9 = (bf16[96,256]{1,0:T(8,128)(2,1)S(1)}, bf16[96,256]{1,0:T(8,128)(2,1)S(1)}, u32[]{:S(2)}, u32[]{:S(2)}) collective-permute-start(bf16[96,256]{1,0:T(8,128)(2,1)S(1)} %get-tuple-element.34), channel_id=1, source_target_pairs={{0,8},{8,0},{16,24},{24,16},{1,9},{9,1},{17,25},{25,17},{2,10},{10... | collective-permute-start | bytes 147464 | tf_op jit(solution)/shard_map/ppermute | solution.py:267
  20.8 5.9 %collective-permute-start.8 = (bf16[96,512]{1,0:T(8,128)(2,1)S(1)}, bf16[96,512]{1,0:T(8,128)(2,1)S(1)}, u32[]{:S(2)}, u32[]{:S(2)}) collective-permute-start(bf16[96,512]{1,0:T(8,128)(2,1)S(1)} %add_convert_fusion.pre_own), channel_id=1, source_target_pairs={{0,16},{8,24},{16,0},{24,8},{1,17},{9,25},{17,1},{25,9},{2,18},{10... | collective-permute-start | bytes 294920 | tf_op jit(solution)/shard_map/ppermute | solution.py:267
  22.4 4.4 %collective-permute-start.10 = (bf16[96,256]{1,0:T(8,128)(2,1)S(1)}, bf16[96,256]{1,0:T(8,128)(2,1)S(1)}, u32[]{:S(2)}, u32[]{:S(2)}) collective-permute-start(bf16[96,256]{1,0:T(8,128)(2,1)S(1)} %add_convert_fusion.1.hid_own), channel_id=1, source_target_pairs={{0,16},{8,24},{16,0},{24,8},{1,17},{9,25},{17,1},{25,9},{2,18},{10... | collective-permute-start | bytes 147464 | tf_op jit(solution)/shard_map/ppermute | solution.py:267
  26.8 1.4 %collective-permute-start.11 = (bf16[96,512]{1,0:T(8,128)(2,1)S(1)}, bf16[96,512]{1,0:T(8,128)(2,1)S(1)}, u32[]{:S(2)}, u32[]{:S(2)}) collective-permute-start(bf16[96,512]{1,0:T(8,128)(2,1)S(1)} %shard_map.98.acts.acts_own), channel_id=1, source_target_pairs={{0,8},{8,0},{16,24},{24,16},{1,9},{9,1},{17,25},{25,17},{2,10},{10... | collective-permute-start | bytes 294920 | tf_op jit(solution)/shard_map/ppermute | solution.py:267
  28.9 5.2 %collective-permute-start.12 = (bf16[24,1792]{1,0:T(8,128)(2,1)S(1)}, bf16[24,1792]{1,0:T(8,128)(2,1)S(1)}, u32[]{:S(2)}, u32[]{:S(2)}) collective-permute-start(bf16[24,1792]{1,0:T(8,128)(2,1)S(1)} %get-tuple-element.38), channel_id=1, source_target_pairs={{0,1},{1,0},{2,3},{3,2},{4,5},{5,4},{6,7},{7,6},{8,9},{9,8},{10,11... | collective-permute-start | bytes 258056 | tf_op jit(solution)/shard_map/ppermute | solution.py:264
  29.6 5.0 %collective-permute-start.13 = (bf16[24,1792]{1,0:T(8,128)(2,1)S(1)}, bf16[24,1792]{1,0:T(8,128)(2,1)S(1)}, u32[]{:S(2)}, u32[]{:S(2)}) collective-permute-start(bf16[24,1792]{1,0:T(8,128)(2,1)S(1)} %get-tuple-element.39), channel_id=1, source_target_pairs={{0,2},{1,3},{2,0},{3,1},{4,6},{5,7},{6,4},{7,5},{8,10},{9,11},{10,... | collective-permute-start | bytes 258056 | tf_op jit(solution)/shard_map/ppermute | solution.py:264
  30.7 5.8 %collective-permute-start.14 = (bf16[24,1792]{1,0:T(8,128)(2,1)S(1)}, bf16[24,1792]{1,0:T(8,128)(2,1)S(1)}, u32[]{:S(2)}, u32[]{:S(2)}) collective-permute-start(bf16[24,1792]{1,0:T(8,128)(2,1)S(1)} %get-tuple-element.40), channel_id=1, source_target_pairs={{0,3},{1,2},{2,1},{3,0},{4,7},{5,6},{6,5},{7,4},{8,11},{9,10},{10,... | collective-permute-start | bytes 258056 | tf_op jit(solution)/shard_map/ppermute | solution.py:264
  36.8 5.4 %collective-permute-start.15 = (bf16[24,896]{1,0:T(8,128)(2,1)S(1)}, bf16[24,896]{1,0:T(8,128)(2,1)S(1)}, u32[]{:S(2)}, u32[]{:S(2)}) collective-permute-start(bf16[24,896]{1,0:T(8,128)(2,1)S(1)} %get-tuple-element.42), channel_id=1, source_target_pairs={{0,4},{1,5},{2,6},{3,7},{4,0},{5,1},{6,2},{7,3},{8,12},{9,13},{10,... | collective-permute-start | bytes 129032 | tf_op jit(solution)/shard_map/ppermute | solution.py:261

commit v2 on v1

v2 whole, which is shorter than its diff:
```python
import functools

import jax
import jax.numpy as jnp
from jax import lax
from jax.experimental import pallas as pl
from jax.experimental.pallas import tpu as pltpu
from jax.sharding import PartitionSpec as P

HSPLIT = 4
CAP = 12
F32 = jnp.float32
BF16 = jnp.bfloat16
VMEM = pl.BlockSpec(memory_space=pltpu.VMEM)
HBM = pl.BlockSpec(memory_space=pltpu.HBM)
ANY = pl.BlockSpec(memory_space=pl.ANY)


NEAR_ORDER = (1, 3, 0, 2)
FAR_ORDER = (3, 2, 1, 0)


def shape(dims, dtype=BF16):
    return jax.ShapeDtypeStruct(dims, dtype)


def run(body, outs, specs, flops, nbytes, *args, out_spec=VMEM, scratch=()):
    return pl.pallas_call(
        body,
        out_shape=outs,
        in_specs=specs,
        out_specs=out_spec if isinstance(out_spec, tuple) else jax.tree.map(lambda _: out_spec, outs),
        scratch_shapes=scratch,
        compiler_params=pltpu.CompilerParams(vmem_limit_bytes=40 * 1024 * 1024),
        cost_estimate=pl.CostEstimate(flops=flops, bytes_accessed=nbytes, transcendentals=0),
    )(*args)


def in_hbm(value):
    return pltpu.with_memory_space_constraint(value, pltpu.HBM)


def dot(left, right, left_dim=1, right_dim=0):
    return lax.dot_general(
        left, right, (((left_dim,), (right_dim,)), ((), ())), preferred_element_type=F32
    )


def iota(dims, dim):
    return lax.broadcasted_iota(jnp.int32, dims, dim)


def over_cap(rows):
    return jnp.floor((rows.astype(F32) + 0.5) * (1.0 / CAP)).astype(jnp.int32)


def column_spans(width):
    whole = width // 128 * 128
    if whole != width or width < 512:
        return [slice(0, width)]
    middle = width // 256 * 128
    return [slice(0, middle), slice(middle, width)]


def core_columns(width, far):
    side = lax.rem(lax.axis_index("dp"), 2)
    side = 1 - side if far else side
    return pl.ds(pl.multiple_of(side * width, width), width)


def fold_of(width):
    return 2 if width % 256 == 0 else 1


def pick_body(experts, fold, ids_hbm, gates_hbm, grads_hbm, inputs_hbm, *refs):
    picks, pieces = refs[:fold], refs[fold : fold + experts]
    ids, gates, grads, inputs, sems = refs[fold + experts :]
    spans = column_spans(grads.shape[1])
    moves = [(ids_hbm, ids), (gates_hbm, gates)]
    for span in spans:
        moves.append((inputs_hbm.at[:, span], inputs.at[:, span]))
        moves.append((grads_hbm.at[:, span], grads.at[:, span]))
    loads = [
        pltpu.make_async_copy(source, target, sems.at[place])
        for place, (source, target) in enumerate(moves)
    ]
    for load in loads:
        load.start()
    tokens = ids.shape[1]
    padded = max(8, experts)
    group = lax.div(lax.axis_index("expert"), HSPLIT)
    earlier = (iota((tokens, tokens), 0) < iota((tokens, tokens), 1)).astype(F32).astype(BF16)
    loads[0].wait()
    loads[1].wait()
    expert_ids = ids[...]
    route_gates = gates[...]
    match_rows = jnp.zeros((padded, tokens), F32)
    matches = []
    token_gates = []
    for step in range(experts):
        hits = expert_ids == lax.rem(group + step, experts)
        match = jnp.sum(hits.astype(F32), axis=0, keepdims=True)
        matches.append(match)
        token_gates.append(jnp.sum(jnp.where(hits, route_gates, 0.0), axis=0, keepdims=True))
        match_rows = jnp.where(iota((padded, tokens), 0) == step, match, match_rows)
    counts = dot(match_rows.astype(BF16), earlier)
    slots = [
        jnp.where(matches[step] > 0.0, counts[step : step + 1, :], -1.0e6)
        for step in range(experts)
    ]

    def chosen(rows, offset):
        places = (iota((rows, tokens), 0) - offset).astype(F32)
        return [(places == slots[step]).astype(F32) for step in range(experts)]

    input_picks = chosen(2 * CAP, 0)
    grad_picks = chosen(2 * CAP, CAP)
    slot_gates = [
        jnp.sum(hit * gate, axis=1, keepdims=True) for hit, gate in zip(grad_picks, token_gates)
    ]
    gate_column = jnp.concatenate(slot_gates, axis=0)
    input_picks = jnp.concatenate(input_picks, axis=0)
    grad_picks = jnp.concatenate(grad_picks, axis=0)
    if fold == 2:
        picks[0][...] = input_picks.astype(BF16)
        picks[1][...] = grad_picks.astype(BF16)
    else:
        picks[0][...] = jnp.concatenate(chosen(CAP, 0), axis=0).astype(BF16)
    input_picks = input_picks.astype(BF16)
    grad_picks = grad_picks.astype(BF16)
    for place, span in enumerate(spans):
        loads[2 + 2 * place].wait()
        total = dot(input_picks, inputs[:, span])
        loads[3 + 2 * place].wait()
        total = total + dot(grad_picks, grads[:, span]) * gate_column
        for step in range(experts):
            rows = slice(step * 2 * CAP, (step + 1) * 2 * CAP)
            pieces[step][:, span] = total[rows].astype(BF16)


def take_rows(pieces, stack):
    place = 0
    for ref in pieces:
        stack[place : place + ref.shape[0], :] = ref[...].astype(F32)
        place += ref.shape[0]
    stacked = stack[...].astype(BF16)
    count = place // 2
    rows = iota((count, place), 0)
    source = rows + over_cap(rows) * CAP
    taken = []
    for offset in (0, CAP):
        mover = (iota((count, place), 1) == source + offset).astype(F32).astype(BF16)
        taken.append(dot(mover, stacked).astype(BF16))
    return taken


def pre_part(rows, weight, place, keep, send):
    half = weight.shape[1] // 2
    span = slice(place * half, (place + 1) * half)
    for target, far in ((send, True), (keep, False)):
        target[:, span] = dot(rows, weight[:, core_columns(half, far)]).astype(BF16)


def hidden_part(rows, weight, keep, send):
    half = weight.shape[0] // 2
    for target, far in ((send, True), (keep, False)):
        part = dot(rows, weight[core_columns(half, far), :], 1, 1)
        target[:, 2 * half :] = part.astype(BF16)


def near_body(after, w_gate, up_hbm, down_hbm, *refs):
    pieces = refs[:-7]
    w_up, w_down, rows_out, keep, send, stack, sems = refs[-7:]
    load_up = pltpu.make_async_copy(up_hbm, w_up, sems.at[0])
    load_down = pltpu.make_async_copy(down_hbm, w_down, sems.at[1])
    load_up.start()
    load_down.start()
    input_rows, grad_rows = take_rows(pieces, stack)
    rows_out[...] = input_rows
    pre_part(input_rows, w_gate, 0, keep, send)
    load_up.wait()
    pre_part(input_rows, w_up, 1, keep, send)
    load_down.wait()
    hidden_part(grad_rows, w_down, keep, send)


def far_body(w_gate, w_up, w_down, *refs):
    pieces = refs[:-4]
    rows_out, keep, send, stack = refs[-4:]
    input_rows, grad_rows = take_rows(pieces, stack)
    rows_out[...] = input_rows
    pre_part(input_rows, w_gate, 0, keep, send)
    pre_part(input_rows, w_up, 1, keep, send)
    hidden_part(grad_rows, w_down, keep, send)


def core_sum_body(own, other, *refs):
    refs[-1][...] = (own[...].astype(F32) + other[...].astype(F32)).astype(BF16)


def activate_body(own, other, *refs):
    acts = refs[-1]
    half = own.shape[1] // 3
    total = own[...].astype(F32) + other[...].astype(F32)
    gate_pre = total[:, :half]
    up_pre = total[:, half : 2 * half]
    hidden_grad = total[:, 2 * half :]
    sigma = jax.nn.sigmoid(gate_pre)
    acts[:, :half] = (hidden_grad * up_pre * sigma * (1.0 + gate_pre * (1.0 - sigma))).astype(BF16)
    acts[:, half:] = (hidden_grad * gate_pre * sigma).astype(BF16)


def fold_rows(total, fold):
    count = total.shape[0]
    width = total.shape[1] // fold
    rows = iota((fold * count, count), 1)
    folded = None
    for part in range(fold):
        goal = rows + over_cap(rows) * (CAP * (fold - 1)) + part * CAP
        mover = (iota((fold * count, count), 0) == goal).astype(F32).astype(BF16)
        moved = dot(mover, total[:, part * width : (part + 1) * width])
        folded = moved if folded is None else folded + moved
    return folded.astype(BF16)


def back_part(w_gate, w_up, acts, sibling):
    half = w_gate.shape[1] // 2
    columns = core_columns(half, sibling)
    part = dot(acts[:, :half], w_gate[:, columns], 1, 1)
    return part + dot(acts[:, half:], w_up[:, columns], 1, 1)


def back_own_body(w_gate, w_up, near, far, near_total, far_total):
    count = near.shape[0]
    acts = jnp.concatenate([near[...], far[...]], axis=0)
    total = back_part(w_gate, w_up, acts, False)
    near_total[...] = total[:count]
    far_total[...] = total[count:]


def back_far_body(fold, w_gate, w_up, far, own, *outs):
    total = (own[...] + back_part(w_gate, w_up, far[...], True)).astype(BF16)
    folded = fold_rows(total, fold)
    count = outs[0].shape[0]
    for place, out in enumerate(outs):
        out[...] = folded[place * count : (place + 1) * count]


def back_near_body(after, w_gate, w_up, near, own, send, keep):
    total = (own[...] + back_part(w_gate, w_up, near[...], True)).astype(BF16)
    count = send.shape[0]
    send[...] = total[:count]
    keep[...] = total[count:]


def weight_body(which, chunks, after, *refs):
    rows_near, rows_far, own_near, own_far, sib_near, sib_far = refs[:6]
    out, token, tile, rows_all, sems = refs[6:]
    token[...] = jnp.zeros_like(token)
    half = out.shape[1] // 2
    depth = out.shape[0] // chunks
    split = rows_near.shape[0]
    rows_all[:split, :] = rows_near[...]
    rows_all[split:, :] = rows_far[...]
    span = slice(which * half, (which + 1) * half)
    own = jnp.concatenate([own_near[:, span], own_far[:, span]], axis=0)
    sib = jnp.concatenate([sib_near[:, span], sib_far[:, span]], axis=0)
    stores = []
    for chunk in range(chunks):
        span = slice(chunk * depth, (chunk + 1) * depth)
        rows = rows_all[:, span]
        for acts, far in ((own, False), (sib, True)):
            tile[span, core_columns(half, far)] = dot(rows, acts, 0, 0).astype(BF16)
        stores.append(pltpu.make_async_copy(tile.at[span], out.at[span], sems.at[chunk]))
        stores[-1].start()
    for store in stores:
        store.wait()


def near_sum_body(fold, after, own, other, keep, send):
    total = (own[...].astype(F32) + other[...].astype(F32)).astype(BF16)
    folded = fold_rows(total, fold)
    keep[...] = folded[: keep.shape[0]]
    send[...] = folded[keep.shape[0] :]


def far_sum_body(after, own, one, two, three, *outs):
    total = own[...].astype(F32) + one[...].astype(F32)
    total = total + (two[...].astype(F32) + three[...].astype(F32))
    count = outs[0].shape[0]
    for place, out in enumerate(outs):
        out[...] = total[place * count : (place + 1) * count].astype(BF16)


def scatter_body(fold, *refs):
    picks, (near_own, near_other), pieces = refs[:fold], refs[fold : fold + 2], refs[fold + 2 : -4]
    out, stack, tile, sems = refs[-4:]
    width = out.shape[1] // fold
    piece = CAP * fold
    stack[:piece, :] = near_own[...].astype(F32) + near_other[...].astype(F32)
    for place, ref in enumerate(pieces):
        stack[(place + 1) * piece : (place + 2) * piece, :] = ref[...].astype(F32)
    returned = stack[...].astype(BF16)
    stores = []
    for part in range(fold):
        for span in column_spans(width):
            target = slice(part * width + span.start, part * width + span.stop)
            tile[:, target] = dot(picks[part][...], returned[:, span], 0, 0).astype(BF16)
            store = pltpu.make_async_copy(
                tile.at[:, target], out.at[:, target], sems.at[len(stores)]
            )
            store.start()
            stores.append(store)
    for store in stores:
        store.wait()


def per_device(out_grad, inputs, expert_ids, gate_weights, w_gate, w_up, w_down):
    devices = lax.axis_size("expert")
    spread = lax.axis_size("dp")
    experts = devices // HSPLIT
    tokens, features = out_grad.shape
    routed = expert_ids.shape[1]
    fold = fold_of(features)
    hidden = w_gate.shape[1]
    half = hidden // 2
    count = devices * CAP
    product = 2 * count * features * hidden
    dma = pltpu.SemaphoreType.DMA

    def to_expert(value, step):
        pairs = [(d, (d + step * HSPLIT) % devices) for d in range(devices)]
        return lax.ppermute(value, "expert", pairs)

    def to_peer(value, flip):
        return lax.ppermute(value, "expert", [(d, d ^ flip) for d in range(devices)])

    def to_dp(value, flip):
        return lax.ppermute(value, "dp", [(d, d ^ flip) for d in range(spread)])

    picked = run(
        functools.partial(pick_body, experts, fold),
        (shape((experts * fold * CAP, tokens)),) * fold
        + (shape((2 * CAP, features)),) * experts,
        [HBM] * 4,
        8 * experts * CAP * tokens * features,
        4 * tokens * features,
        *(in_hbm(array) for array in (expert_ids.T, gate_weights.T, out_grad, inputs)),
        scratch=(
            pltpu.VMEM((routed, tokens), jnp.int32),
            pltpu.VMEM((routed, tokens), F32),
            pltpu.VMEM((tokens, features), BF16),
            pltpu.VMEM((tokens, features), BF16),
            dma((2 + 2 * len(column_spans(features)),)),
        ),
    )
    picks, own = picked[:fold], picked[fold:]
    away = [to_expert(own[step], step) for step in range(1, experts)]
    near = [own[0]] + [to_peer(own[0], flip) for flip in range(1, HSPLIT)]
    away = away[0] if len(away) == 1 else jnp.concatenate(away, axis=0)
    far = [away] + [to_peer(away, flip) for flip in range(1, HSPLIT)]

    def rows_shapes(rows):
        return (shape((rows, features)), shape((rows, 3 * half)), shape((rows, 3 * half)))

    near_count = HSPLIT * CAP
    far_count = count - near_count
    up_here, down_here, rows_near, near_pre, near_send = run(
        near_body,
        tuple(pltpu.VMEM(weight.shape, weight.dtype) for weight in (w_up, w_down))
        + rows_shapes(near_count),
        [ANY, VMEM] + [HBM] * 2 + [VMEM] * HSPLIT,
        3 * product,
        6 * features * hidden,
        away,
        w_gate,
        in_hbm(w_up),
        in_hbm(w_down),
        *(near[peer] for peer in NEAR_ORDER),
        scratch=(pltpu.VMEM((2 * near_count, features), F32), dma((2,))),
    )
    rows_far, far_pre, far_send = run(
        far_body,
        rows_shapes(far_count),
        [VMEM] * (3 + HSPLIT),
        3 * product // 2,
        6 * features * hidden,
        w_gate,
        up_here,
        down_here,
        *(far[peer] for peer in FAR_ORDER),
        scratch=(pltpu.VMEM((2 * far_count, features), F32),),
    )

    def core_sum(keep, send, *after):
        return run(
            core_sum_body,
            shape(keep.shape),
            [VMEM] * 2 + [ANY] * len(after),
            0,
            0,
            keep,
            to_dp(send, 1),
            *after,
        )

    def activate(total, *after):
        flip = 2
        other = jnp.zeros_like(total)
        while flip < spread:
            other = to_dp(total, flip)
            flip *= 2
            if flip < spread:
                total = (total.astype(F32) + other.astype(F32)).astype(BF16)
        rows = total.shape[0]
        return run(
            activate_body,
            shape((rows, hidden)),
            [VMEM] * 2 + [ANY] * len(after),
            20 * rows * half,
            10 * rows * half,
            total,
            other,
            *after,
        )

    near_total = core_sum(near_pre, near_send)
    far_total = core_sum(far_pre, far_send, near_total)
    acts_near = activate(near_total)
    acts_far = activate(far_total, acts_near)
    sib_near = to_dp(acts_near, 1)
    sib_far = to_dp(acts_far, 1)
    near_total, far_total = run(
        back_own_body,
        (shape((near_count, features), F32), shape((far_count, features), F32)),
        [VMEM] * 4,
        product,
        2 * features * hidden,
        w_gate,
        up_here,
        acts_near,
        acts_far,
    )
    far_rows = shape((far_count // HSPLIT * fold, features // fold))
    far_out = run(
        functools.partial(back_far_body, fold),
        (far_rows,) * HSPLIT,
        [VMEM] * 4,
        product,
        2 * features * hidden,
        w_gate,
        up_here,
        sib_far,
        far_total,
    )
    near_out, near_keep = run(
        back_near_body,
        (shape((2 * CAP, features)),) * 2,
        [ANY] + [VMEM] * 4,
        product,
        2 * features * hidden,
        far_out[-1],
        w_gate,
        up_here,
        sib_near,
        near_total,
    )

    def weight_grad(which, after):
        chunks = 4 if features % 512 == 0 else 2
        return run(
            functools.partial(weight_body, which, chunks),
            (shape((features, hidden)), shape((8, 128), F32)),
            [ANY] + [VMEM] * 6,
            0,
            0,
            after,
            rows_near,
            rows_far,
            acts_near,
            acts_far,
            sib_near,
            sib_far,
            out_spec=(HBM, VMEM),
            scratch=(
                pltpu.VMEM((features, hidden), BF16),
                pltpu.VMEM((count, features), BF16),
                dma((chunks,)),
            ),
        )

    grad_gate, token = weight_grad(0, far_out[-1])
    piece = shape((CAP * fold, features // fold))
    summed = run(
        far_sum_body,
        (piece,) * (experts - 1),
        [ANY] + [VMEM] * HSPLIT,
        4 * product,
        0,
        token,
        *(to_peer(out, peer) for out, peer in zip(far_out, FAR_ORDER) if peer),
        far_out[FAR_ORDER.index(0)],
    )
    near_own, near_last = run(
        functools.partial(near_sum_body, fold),
        (piece,) * 2,
        [ANY] + [VMEM] * 2,
        0,
        0,
        summed[0],
        near_keep,
        to_peer(near_out, 1),
    )
    near_other = to_peer(near_last, 2)
    grad_up, _ = weight_grad(1, near_last)
    returned = [to_expert(summed[step - 1], experts - step) for step in range(1, experts)]
    in_grad = run(
        functools.partial(scatter_body, fold),
        shape((tokens, features)),
        [VMEM] * (fold + 2 + len(returned)),
        4 * experts * CAP * tokens * features,
        2 * tokens * features,
        *picks,
        near_own,
        near_other,
        *returned,
        out_spec=HBM,
        scratch=(
            pltpu.VMEM((experts * fold * CAP, features // fold), F32),
            pltpu.VMEM((tokens, features), BF16),
            dma((fold * len(column_spans(features // fold)),)),
        ),
    )
    return (in_grad, grad_gate, grad_up)


def solution(mesh):
    placed = (
        P("expert", "dp"),
        P("expert", "dp"),
        P("expert", None),
        P("expert", None),
        P("dp", "expert"),
        P("dp", "expert"),
        P("expert", "dp"),
    )
    return jax.shard_map(
        per_device,
        mesh=mesh,
        in_specs=placed,
        out_specs=(P("expert", "dp"), P("dp", "expert"), P("dp", "expert")),
        check_vma=False,
    )
```

time: 43.7 us -> 44 us (level)
  waiting for transfers between devices: 8.32 us -> 5.6 us
  starting transfers between devices: 21.2 us -> 23.1 us
  Pallas kernels: 13.1 us -> 14.3 us
    ppermute x9 -> x11, starting transfers between devices: 10.9 us -> 14.1 us  [to_peer(): lax.ppermute(value, 'expert', [(d, d ^ flip) for d in range(devices)])]
    ppermute x9 -> x11, waiting for transfers between devices: 3.67 us -> 1.32 us  [to_peer(): lax.ppermute(value, 'expert', [(d, d ^ flip) for d in range(devices)])]
    ppermute x2, starting transfers between devices: 7.23 us -> 5.51 us  [to_expert(): return lax.ppermute(value, 'expert', pairs)]
    pallas_call x11 -> x15, Pallas kernels: 13.1 us -> 14.3 us  [run(): pl.pallas_call(body, out_shape=outs, in_specs=specs, out_specs=out_spec i...]
    ppermute x5 -> x6, waiting for transfers between devices: 4.11 us -> 3.51 us  [to_dp(): return lax.ppermute(value, 'dp', [(d, d ^ flip) for d in range(spread)])]
    ppermute x5 -> x6, starting transfers between devices: 3.1 us -> 3.48 us  [to_dp(): return lax.ppermute(value, 'dp', [(d, d ^ flip) for d in range(spread)])]
  transfers between devices with their start and end apart: 16 -> 19, of which waited for: 7 -> 6; matrix products, arithmetic and copies ran while one was open for 0% -> 0% of each run, Pallas kernels for 18% -> 25%
where the time goes in v2:
time: 44 us; the launch traced here: 43.8 us
  starting transfers between devices  23.1 us (52%)
  Pallas kernels  14.3 us (32%)
  waiting for transfers between devices  5.6 us (13%)
  between operations  0.82 us (2%)
    pallas_call x15, Pallas kernels, run(): pl.pallas_call(body, out_shape=outs, in_specs=specs, out_specs=out_spec i...  14.3 us
    ppermute x11, starting transfers between devices, to_peer(): lax.ppermute(value, 'expert', [(d, d ^ flip) for d in range(devices)])  14.1 us
    ppermute x2, starting transfers between devices, to_expert(): return lax.ppermute(value, 'expert', pairs)  5.51 us
    ppermute x6, waiting for transfers between devices, to_dp(): return lax.ppermute(value, 'dp', [(d, d ^ flip) for d in range(spread)])  3.51 us
    ppermute x6, starting transfers between devices, to_dp(): return lax.ppermute(value, 'dp', [(d, d ^ flip) for d in range(spread)])  3.48 us
    ppermute x11, waiting for transfers between devices, to_peer(): lax.ppermute(value, 'expert', [(d, d ^ flip) for d in range(devices)])  1.32 us
  transfers between devices with their start and end apart: 19, of which 6 were waited for; matrix products, arithmetic and copies ran while one was open for 0% of the time, Pallas kernels for 25%

profile of v2, /device:TPU:0, one launch (start us, length us, event | category | flops | bytes accessed | tf_op | source)
XLA Modules:
  0.0 43.8 jit_solution(10779878655125375025)
XLA Ops:
  0.6 1.9 %shard_map.94 = (bf16[48,256]{1,0:T(8,128)(2,1)S(1)}, bf16[48,256]{1,0:T(8,128)(2,1)S(1)}, bf16[24,1792]{1,0:T(8,128)(2,1)S(1)}, bf16[24,1792]{1,0:T(8,128)(2,1)S(1)}) custom-call(s32[8,256]{1,0:T(8,128)} %bitcast.2, f32[8,256]{1,0:T(8,128)} %bitcast.3, bf16[256,1792]{1,0:T(8,128)(2,1)} %grads_hbm.1, bf16[256,1792]{1,0:T(8,128)(2,1)} %inputs_hbm.1), custom_call_target="tpu_custom_call" | custom-call | flops 88080384 | bytes 1835008 | tf_op jit(solution)/shard_map/pallas_call | solution.py:28
  2.6 4.1 %collective-permute-start = (bf16[24,1792]{1,0:T(8,128)(2,1)S(1)}, bf16[24,1792]{1,0:T(8,128)(2,1)S(1)}, u32[]{:S(2)}, u32[]{:S(2)}) collective-permute-start(bf16[24,1792]{1,0:T(8,128)(2,1)S(1)} %get-tuple-element.30), channel_id=1, source_target_pairs={{0,4},{1,5},{2,6},{3,7},{4,0},{5,1},{6,2},{7,3},{8,12},{9,13},{10,... | collective-permute-start | bytes 258056 | tf_op jit(solution)/shard_map/ppermute | solution.py:333
  6.7 1.5 %collective-permute-start.1 = (bf16[24,1792]{1,0:T(8,128)(2,1)S(1)}, bf16[24,1792]{1,0:T(8,128)(2,1)S(1)}, u32[]{:S(2)}, u32[]{:S(2)}) collective-permute-start(bf16[24,1792]{1,0:T(8,128)(2,1)S(1)} %get-tuple-element.31.refs_2_), channel_id=1, source_target_pairs={{0,1},{1,0},{2,3},{3,2},{4,5},{5,4},{6,7},{7,6},{8,9},{9,8},{10,11... | collective-permute-start | bytes 258056 | tf_op jit(solution)/shard_map/ppermute | solution.py:336
  8.2 1.5 %collective-permute-start.2 = (bf16[24,1792]{1,0:T(8,128)(2,1)S(1)}, bf16[24,1792]{1,0:T(8,128)(2,1)S(1)}, u32[]{:S(2)}, u32[]{:S(2)}) collective-permute-start(bf16[24,1792]{1,0:T(8,128)(2,1)S(1)} %get-tuple-element.31.refs_2_), channel_id=1, source_target_pairs={{0,3},{1,2},{2,1},{3,0},{4,7},{5,6},{6,5},{7,4},{8,11},{9,10},{10,... | collective-permute-start | bytes 258056 | tf_op jit(solution)/shard_map/ppermute | solution.py:336
  9.7 0.4 %collective-permute-start.3 = (bf16[24,1792]{1,0:T(8,128)(2,1)S(1)}, bf16[24,1792]{1,0:T(8,128)(2,1)S(1)}, u32[]{:S(2)}, u32[]{:S(2)}) collective-permute-start(bf16[24,1792]{1,0:T(8,128)(2,1)S(1)} %get-tuple-element.31.refs_2_), channel_id=1, source_target_pairs={{0,2},{1,3},{2,0},{3,1},{4,6},{5,7},{6,4},{7,5},{8,10},{9,11},{10,... | collective-permute-start | bytes 258056 | tf_op jit(solution)/shard_map/ppermute | solution.py:336
  10.2 0.8 %collective-permute-done.after.refs_3_ = bf16[24,1792]{1,0:T(8,128)(2,1)S(1)} collective-permute-done((bf16[24,1792]{1,0:T(8,128)(2,1)S(1)}, bf16[24,1792]{1,0:T(8,128)(2,1)S(1)}, u32[]{:S(2)}, u32[]{:S(2)}) %collective-permute-start) | collective-permute-done | bytes 86048 | tf_op jit(solution)/shard_map/ppermute | solution.py:333
  10.9 1.8 %collective-permute-start.4 = (bf16[24,1792]{1,0:T(8,128)(2,1)S(1)}, bf16[24,1792]{1,0:T(8,128)(2,1)S(1)}, u32[]{:S(2)}, u32[]{:S(2)}) collective-permute-start(bf16[24,1792]{1,0:T(8,128)(2,1)S(1)} %collective-permute-done.after.refs_3_), channel_id=1, source_target_pairs={{0,3},{1,2},{2,1},{3,0},{4,7},{5,6},{6,5},{7,4},{8,11},{9,10},{10,... | collective-permute-start | bytes 258056 | tf_op jit(solution)/shard_map/ppermute | solution.py:336
  12.8 1.5 %collective-permute-start.5 = (bf16[24,1792]{1,0:T(8,128)(2,1)S(1)}, bf16[24,1792]{1,0:T(8,128)(2,1)S(1)}, u32[]{:S(2)}, u32[]{:S(2)}) collective-permute-start(bf16[24,1792]{1,0:T(8,128)(2,1)S(1)} %collective-permute-done.after.refs_3_), channel_id=1, source_target_pairs={{0,2},{1,3},{2,0},{3,1},{4,6},{5,7},{6,4},{7,5},{8,10},{9,11},{10,... | collective-permute-start | bytes 258056 | tf_op jit(solution)/shard_map/ppermute | solution.py:336
  14.3 0.1 collective-permute-start.6
  14.4 0.1 collective-permute-done.2.refs_1_
  14.6 0.5 %collective-permute-done.3.refs_3_ = bf16[24,1792]{1,0:T(8,128)(2,1)S(1)} collective-permute-done((bf16[24,1792]{1,0:T(8,128)(2,1)S(1)}, bf16[24,1792]{1,0:T(8,128)(2,1)S(1)}, u32[]{:S(2)}, u32[]{:S(2)}) %collective-permute-start.3) | collective-permute-done | bytes 86048 | tf_op jit(solution)/shard_map/ppermute | solution.py:336
  15.1 3.1 %shard_map.95 = (bf16[1792,512]{1,0:T(8,128)(2,1)S(1)}, bf16[512,1792]{1,0:T(8,128)(2,1)S(1)}, bf16[48,1792]{1,0:T(8,128)(2,1)S(1)}, bf16[48,768]{1,0:T(8,128)(2,1)S(1)}, bf16[48,768]{1,0:T(8,128)(2,1)S(1)}) custom-call(bf16[24,1792]{1,0:T(8,128)(2,1)S(1)} %collective-permute-done.after.refs_3_, bf16[1792,512]{1,0:T(8,128)(2,1)S(1)} %copy-done, ...), custom_call_target="tpu_custom_call" | custom-call | flops 528482304 | bytes 5505024 | tf_op jit(solution)/shard_map/pallas_call | solution.py:28
  18.4 0.6 %collective-permute-done.6.refs_2_ = bf16[24,1792]{1,0:T(8,128)(2,1)S(1)} collective-permute-done((bf16[24,1792]{1,0:T(8,128)(2,1)S(1)}, bf16[24,1792]{1,0:T(8,128)(2,1)S(1)}, u32[]{:S(2)}, u32[]{:S(2)}) %collective-permute-start.6) | collective-permute-done | bytes 86048 | tf_op jit(solution)/shard_map/ppermute | solution.py:336
  19.0 1.4 %shard_map.96 = (bf16[48,1792]{1,0:T(8,128)(2,1)S(1)}, bf16[48,768]{1,0:T(8,128)(2,1)S(1)}, bf16[48,768]{1,0:T(8,128)(2,1)S(1)}) custom-call(bf16[1792,512]{1,0:T(8,128)(2,1)S(1)} %copy-done, bf16[1792,512]{1,0:T(8,128)(2,1)S(1)} %get-tuple-element.32.w_up, bf16[512,1792]{1,0:T(8,128)(2,1)S(1)} %get-tuple-element.33.w_down, ...), custom_call_target="tpu_custom_call" | custom-call | flops 264241152 | bytes 5505024 | tf_op jit(solution)/shard_map/pallas_call | solution.py:28
  20.5 1.7 %collective-permute-start.10 = (bf16[48,768]{1,0:T(8,128)(2,1)S(1)}, bf16[48,768]{1,0:T(8,128)(2,1)S(1)}, u32[]{:S(2)}, u32[]{:S(2)}) collective-permute-start(bf16[48,768]{1,0:T(8,128)(2,1)S(1)} %shard_map.97.refs_0_.own), channel_id=1, source_target_pairs={{0,16},{8,24},{16,0},{24,8},{1,17},{9,25},{17,1},{25,9},{2,18},{10... | collective-permute-start | bytes 221192 | tf_op jit(solution)/shard_map/ppermute | solution.py:339
  22.3 1.0 %collective-permute-start.9 = (bf16[48,768]{1,0:T(8,128)(2,1)S(1)}, bf16[48,768]{1,0:T(8,128)(2,1)S(1)}, u32[]{:S(2)}, u32[]{:S(2)}) collective-permute-start(bf16[48,768]{1,0:T(8,128)(2,1)S(1)} %shard_map.98.own), channel_id=1, source_target_pairs={{0,16},{8,24},{16,0},{24,8},{1,17},{9,25},{17,1},{25,9},{2,18},{10... | collective-permute-start | bytes 221192 | tf_op jit(solution)/shard_map/ppermute | solution.py:339
  23.3 2.2 %collective-permute-done.10.other = bf16[48,768]{1,0:T(8,128)(2,1)S(1)} collective-permute-done((bf16[48,768]{1,0:T(8,128)(2,1)S(1)}, bf16[48,768]{1,0:T(8,128)(2,1)S(1)}, u32[]{:S(2)}, u32[]{:S(2)}) %collective-permute-start.10) | collective-permute-done | bytes 73760 | tf_op jit(solution)/shard_map/ppermute | solution.py:339
  25.6 1.2 %collective-permute-done.9.other = bf16[48,768]{1,0:T(8,128)(2,1)S(1)} collective-permute-done((bf16[48,768]{1,0:T(8,128)(2,1)S(1)}, bf16[48,768]{1,0:T(8,128)(2,1)S(1)}, u32[]{:S(2)}, u32[]{:S(2)}) %collective-permute-start.9) | collective-permute-done | bytes 73760 | tf_op jit(solution)/shard_map/ppermute | solution.py:339
  26.9 0.5 %collective-permute-start.12 = (bf16[48,512]{1,0:T(8,128)(2,1)S(1)}, bf16[48,512]{1,0:T(8,128)(2,1)S(1)}, u32[]{:S(2)}, u32[]{:S(2)}) collective-permute-start(bf16[48,512]{1,0:T(8,128)(2,1)S(1)} %shard_map.99.refs_0_.near.refs_2_), channel_id=1, source_target_pairs={{0,8},{8,0},{16,24},{24,16},{1,9},{9,1},{17,25},{25,17},{2,10},{10... | collective-permute-start | bytes 147464 | tf_op jit(solution)/shard_map/ppermute | solution.py:339
  27.4 0.7 %shard_map.101 = (f32[48,1792]{1,0:T(8,128)S(1)}, f32[48,1792]{1,0:T(8,128)S(1)}) custom-call(bf16[1792,512]{1,0:T(8,128)(2,1)S(1)} %copy-done, bf16[1792,512]{1,0:T(8,128)(2,1)S(1)} %get-tuple-element.32.w_up, bf16[48,512]{1,0:T(8,128)(2,1)S(1)} %shard_map.99.refs_0_.near.refs_2_, bf16[48,512]{1,0:T(8,128)(2,1)S(1)} %shard_map.100.far.refs_3_), custom_call_target="tpu_custom_call" | custom-call | flops 176160768 | bytes 1835008 | tf_op jit(solution)/shard_map/pallas_call | solution.py:28
  28.1 1.0 %shard_map.102 = (bf16[24,896]{1,0:T(8,128)(2,1)S(1)}, bf16[24,896]{1,0:T(8,128)(2,1)S(1)}, bf16[24,896]{1,0:T(8,128)(2,1)S(1)}, bf16[24,896]{1,0:T(8,128)(2,1)S(1)}) custom-call(bf16[1792,512]{1,0:T(8,128)(2,1)S(1)} %copy-done, bf16[1792,512]{1,0:T(8,128)(2,1)S(1)} %get-tuple-element.32.w_up, bf16[48,512]{1,0:T(8,128)(2,1)S(1)} %collective-permute-done.11.far.refs_5_, ...), custom_call_target="tpu_custom_call" | custom-call | flops 176160768 | bytes 1835008 | tf_op jit(solution)/shard_map/pallas_call | solution.py:28
  29.1 1.8 %collective-permute-start.13 = (bf16[24,896]{1,0:T(8,128)(2,1)S(1)}, bf16[24,896]{1,0:T(8,128)(2,1)S(1)}, u32[]{:S(2)}, u32[]{:S(2)}) collective-permute-start(bf16[24,896]{1,0:T(8,128)(2,1)S(1)} %get-tuple-element.43), channel_id=1, source_target_pairs={{0,3},{1,2},{2,1},{3,0},{4,7},{5,6},{6,5},{7,4},{8,11},{9,10},{10,... | collective-permute-start | bytes 129032 | tf_op jit(solution)/shard_map/ppermute | solution.py:336
  30.9 1.2 %collective-permute-start.14 = (bf16[24,896]{1,0:T(8,128)(2,1)S(1)}, bf16[24,896]{1,0:T(8,128)(2,1)S(1)}, u32[]{:S(2)}, u32[]{:S(2)}) collective-permute-start(bf16[24,896]{1,0:T(8,128)(2,1)S(1)} %get-tuple-element.44), channel_id=1, source_target_pairs={{0,2},{1,3},{2,0},{3,1},{4,6},{5,7},{6,4},{7,5},{8,10},{9,11},{10,... | collective-permute-start | bytes 129032 | tf_op jit(solution)/shard_map/ppermute | solution.py:336
  32.1 0.6 %collective-permute-start.15 = (bf16[24,896]{1,0:T(8,128)(2,1)S(1)}, bf16[24,896]{1,0:T(8,128)(2,1)S(1)}, u32[]{:S(2)}, u32[]{:S(2)}) collective-permute-start(bf16[24,896]{1,0:T(8,128)(2,1)S(1)} %get-tuple-element.45), channel_id=1, source_target_pairs={{0,1},{1,0},{2,3},{3,2},{4,5},{5,4},{6,7},{7,6},{8,9},{9,8},{10,11... | collective-permute-start | bytes 129032 | tf_op jit(solution)/shard_map/ppermute | solution.py:336
  32.7 0.6 %shard_map.105 = (bf16[24,1792]{1,0:T(8,128)(2,1)S(1)}, bf16[24,1792]{1,0:T(8,128)(2,1)S(1)}) custom-call(bf16[24,896]{1,0:T(8,128)(2,1)S(1)} %get-tuple-element.39.after.three, bf16[1792,512]{1,0:T(8,128)(2,1)S(1)} %copy-done, bf16[1792,512]{1,0:T(8,128)(2,1)S(1)} %get-tuple-element.32.w_up, bf16[48,512]{1,0:T(8,128)(2,1)S(1)} %collective-permute-done.12.refs_4_.near, ...), custom_call_target="tpu_custom_call" | custom-call | flops 176160768 | bytes 1835008 | tf_op jit(solution)/shard_map/pallas_call | solution.py:28
  33.3 1.5 %collective-permute-start.16 = (bf16[24,1792]{1,0:T(8,128)(2,1)S(1)}, bf16[24,1792]{1,0:T(8,128)(2,1)S(1)}, u32[]{:S(2)}, u32[]{:S(2)}) collective-permute-start(bf16[24,1792]{1,0:T(8,128)(2,1)S(1)} %get-tuple-element.48), channel_id=1, source_target_pairs={{0,1},{1,0},{2,3},{3,2},{4,5},{5,4},{6,7},{7,6},{8,9},{9,8},{10,11... | collective-permute-start | bytes 258056 | tf_op jit(solution)/shard_map/ppermute | solution.py:336
  34.8 1.7 %shard_map.103 = (bf16[1792,512]{1,0:T(8,128)(2,1)}, f32[8,128]{1,0:T(8,128)S(1)}) custom-call(bf16[24,896]{1,0:T(8,128)(2,1)S(1)} %get-tuple-element.39.after.three, bf16[48,1792]{1,0:T(8,128)(2,1)S(1)} %get-tuple-element.40.refs_0_, bf16[48,1792]{1,0:T(8,128)(2,1)S(1)} %get-tuple-element.41.refs_1_, bf16[48,512]{1,0:T(8,128)(2,1)S(1)} %shard_map.99.refs_0_.near.refs_2_, ...), custom_call_target="tpu_custom_call" | custom-call | tf_op jit(solution)/shard_map/pallas_call | solution.py:28
  36.6 1.4 %collective-permute-start.18 = (bf16[24,896]{1,0:T(8,128)(2,1)S(1)}, bf16[24,896]{1,0:T(8,128)(2,1)S(1)}, u32[]{:S(2)}, u32[]{:S(2)}) collective-permute-start(bf16[24,896]{1,0:T(8,128)(2,1)S(1)} %shard_map.104.after), channel_id=1, source_target_pairs={{0,4},{1,5},{2,6},{3,7},{4,0},{5,1},{6,2},{7,3},{8,12},{9,13},{10,... | collective-permute-start | bytes 129032 | tf_op jit(solution)/shard_map/ppermute | solution.py:333
  38.0 0.2 shard_map.106
  38.2 2.1 %collective-permute-start.17 = (bf16[24,896]{1,0:T(8,128)(2,1)S(1)}, bf16[24,896]{1,0:T(8,128)(2,1)S(1)}, u32[]{:S(2)}, u32[]{:S(2)}) collective-permute-start(bf16[24,896]{1,0:T(8,128)(2,1)S(1)} %get-tuple-element.50.after), channel_id=1, source_target_pairs={{0,2},{1,3},{2,0},{3,1},{4,6},{5,7},{6,4},{7,5},{8,10},{9,11},{10,... | collective-permute-start | bytes 129032 | tf_op jit(solution)/shard_map/ppermute | solution.py:336
  40.3 2.3 %shard_map.108 = (bf16[1792,512]{1,0:T(8,128)(2,1)}, f32[8,128]{1,0:T(8,128)}) custom-call(bf16[24,896]{1,0:T(8,128)(2,1)S(1)} %get-tuple-element.50.after, bf16[48,1792]{1,0:T(8,128)(2,1)S(1)} %get-tuple-element.40.refs_0_, bf16[48,1792]{1,0:T(8,128)(2,1)S(1)} %get-tuple-element.41.refs_1_, bf16[48,512]{1,0:T(8,128)(2,1)S(1)} %shard_map.99.refs_0_.near.refs_2_, ...), custom_call_target="tpu_custom_call" | custom-call | tf_op jit(solution)/shard_map/pallas_call | solution.py:28
  42.6 1.2 %shard_map.107 = bf16[256,1792]{1,0:T(8,128)(2,1)} custom-call(bf16[48,256]{1,0:T(8,128)(2,1)S(1)} %get-tuple-element.28.refs_0_, bf16[48,256]{1,0:T(8,128)(2,1)S(1)} %get-tuple-element.29.refs_1_, bf16[24,896]{1,0:T(8,128)(2,1)S(1)} %get-tuple-element.49.refs_2_, bf16[24,896]{1,0:T(8,128)(2,1)S(1)} %collective-permute-done.17.refs_3_, ...), custom_call_target="tpu_custom_call" | custom-call | flops 44040192 | bytes 917504 | tf_op jit(solution)/shard_map/pallas_call | solution.py:28
  (23 shorter events, 0.5 us)
Async XLA Ops:
  0.6 14.5 %copy-start = (bf16[1792,512]{1,0:T(8,128)(2,1)S(1)}, bf16[1792,512]{1,0:T(8,128)(2,1)}, u32[]{:S(2)}) copy-start(bf16[1792,512]{1,0:T(8,128)(2,1)} %w_gate.9) | copy-start | bytes 5505028
  2.6 8.4 %collective-permute-start = (bf16[24,1792]{1,0:T(8,128)(2,1)S(1)}, bf16[24,1792]{1,0:T(8,128)(2,1)S(1)}, u32[]{:S(2)}, u32[]{:S(2)}) collective-permute-start(bf16[24,1792]{1,0:T(8,128)(2,1)S(1)} %get-tuple-element.30), channel_id=1, source_target_pairs={{0,4},{1,5},{2,6},{3,7},{4,0},{5,1},{6,2},{7,3},{8,12},{9,13},{10,... | collective-permute-start | bytes 258056 | tf_op jit(solution)/shard_map/ppermute | solution.py:333
  6.7 7.6 %collective-permute-start.1 = (bf16[24,1792]{1,0:T(8,128)(2,1)S(1)}, bf16[24,1792]{1,0:T(8,128)(2,1)S(1)}, u32[]{:S(2)}, u32[]{:S(2)}) collective-permute-start(bf16[24,1792]{1,0:T(8,128)(2,1)S(1)} %get-tuple-element.31.refs_2_), channel_id=1, source_target_pairs={{0,1},{1,0},{2,3},{3,2},{4,5},{5,4},{6,7},{7,6},{8,9},{9,8},{10,11... | collective-permute-start | bytes 258056 | tf_op jit(solution)/shard_map/ppermute | solution.py:336
  8.2 6.4 %collective-permute-start.2 = (bf16[24,1792]{1,0:T(8,128)(2,1)S(1)}, bf16[24,1792]{1,0:T(8,128)(2,1)S(1)}, u32[]{:S(2)}, u32[]{:S(2)}) collective-permute-start(bf16[24,1792]{1,0:T(8,128)(2,1)S(1)} %get-tuple-element.31.refs_2_), channel_id=1, source_target_pairs={{0,3},{1,2},{2,1},{3,0},{4,7},{5,6},{6,5},{7,4},{8,11},{9,10},{10,... | collective-permute-start | bytes 258056 | tf_op jit(solution)/shard_map/ppermute | solution.py:336
  9.7 5.4 %collective-permute-start.3 = (bf16[24,1792]{1,0:T(8,128)(2,1)S(1)}, bf16[24,1792]{1,0:T(8,128)(2,1)S(1)}, u32[]{:S(2)}, u32[]{:S(2)}) collective-permute-start(bf16[24,1792]{1,0:T(8,128)(2,1)S(1)} %get-tuple-element.31.refs_2_), channel_id=1, source_target_pairs={{0,2},{1,3},{2,0},{3,1},{4,6},{5,7},{6,4},{7,5},{8,10},{9,11},{10,... | collective-permute-start | bytes 258056 | tf_op jit(solution)/shard_map/ppermute | solution.py:336
  10.9 7.4 %collective-permute-start.4 = (bf16[24,1792]{1,0:T(8,128)(2,1)S(1)}, bf16[24,1792]{1,0:T(8,128)(2,1)S(1)}, u32[]{:S(2)}, u32[]{:S(2)}) collective-permute-start(bf16[24,1792]{1,0:T(8,128)(2,1)S(1)} %collective-permute-done.after.refs_3_), channel_id=1, source_target_pairs={{0,3},{1,2},{2,1},{3,0},{4,7},{5,6},{6,5},{7,4},{8,11},{9,10},{10,... | collective-permute-start | bytes 258056 | tf_op jit(solution)/shard_map/ppermute | solution.py:336
  12.8 5.6 %collective-permute-start.5 = (bf16[24,1792]{1,0:T(8,128)(2,1)S(1)}, bf16[24,1792]{1,0:T(8,128)(2,1)S(1)}, u32[]{:S(2)}, u32[]{:S(2)}) collective-permute-start(bf16[24,1792]{1,0:T(8,128)(2,1)S(1)} %collective-permute-done.after.refs_3_), channel_id=1, source_target_pairs={{0,2},{1,3},{2,0},{3,1},{4,6},{5,7},{6,4},{7,5},{8,10},{9,11},{10,... | collective-permute-start | bytes 258056 | tf_op jit(solution)/shard_map/ppermute | solution.py:336
  14.3 4.7 %collective-permute-start.6 = (bf16[24,1792]{1,0:T(8,128)(2,1)S(1)}, bf16[24,1792]{1,0:T(8,128)(2,1)S(1)}, u32[]{:S(2)}, u32[]{:S(2)}) collective-permute-start(bf16[24,1792]{1,0:T(8,128)(2,1)S(1)} %collective-permute-done.after.refs_3_), channel_id=1, source_target_pairs={{0,1},{1,0},{2,3},{3,2},{4,5},{5,4},{6,7},{7,6},{8,9},{9,8},{10,11... | collective-permute-start | bytes 258056 | tf_op jit(solution)/shard_map/ppermute | solution.py:336
  18.3 2.2 %collective-permute-start.8 = (bf16[48,768]{1,0:T(8,128)(2,1)S(1)}, bf16[48,768]{1,0:T(8,128)(2,1)S(1)}, u32[]{:S(2)}, u32[]{:S(2)}) collective-permute-start(bf16[48,768]{1,0:T(8,128)(2,1)S(1)} %get-tuple-element.37), channel_id=1, source_target_pairs={{0,8},{8,0},{16,24},{24,16},{1,9},{9,1},{17,25},{25,17},{2,10},{10... | collective-permute-start | bytes 221192 | tf_op jit(solution)/shard_map/ppermute | solution.py:339
  20.4 1.8 %collective-permute-start.7 = (bf16[48,768]{1,0:T(8,128)(2,1)S(1)}, bf16[48,768]{1,0:T(8,128)(2,1)S(1)}, u32[]{:S(2)}, u32[]{:S(2)}) collective-permute-start(bf16[48,768]{1,0:T(8,128)(2,1)S(1)} %get-tuple-element.35), channel_id=1, source_target_pairs={{0,8},{8,0},{16,24},{24,16},{1,9},{9,1},{17,25},{25,17},{2,10},{10... | collective-permute-start | bytes 221192 | tf_op jit(solution)/shard_map/ppermute | solution.py:339
  20.5 5.0 %collective-permute-start.10 = (bf16[48,768]{1,0:T(8,128)(2,1)S(1)}, bf16[48,768]{1,0:T(8,128)(2,1)S(1)}, u32[]{:S(2)}, u32[]{:S(2)}) collective-permute-start(bf16[48,768]{1,0:T(8,128)(2,1)S(1)} %shard_map.97.refs_0_.own), channel_id=1, source_target_pairs={{0,16},{8,24},{16,0},{24,8},{1,17},{9,25},{17,1},{25,9},{2,18},{10... | collective-permute-start | bytes 221192 | tf_op jit(solution)/shard_map/ppermute | solution.py:339
  22.3 4.5 %collective-permute-start.9 = (bf16[48,768]{1,0:T(8,128)(2,1)S(1)}, bf16[48,768]{1,0:T(8,128)(2,1)S(1)}, u32[]{:S(2)}, u32[]{:S(2)}) collective-permute-start(bf16[48,768]{1,0:T(8,128)(2,1)S(1)} %shard_map.98.own), channel_id=1, source_target_pairs={{0,16},{8,24},{16,0},{24,8},{1,17},{9,25},{17,1},{25,9},{2,18},{10... | collective-permute-start | bytes 221192 | tf_op jit(solution)/shard_map/ppermute | solution.py:339
  26.8 1.3 %collective-permute-start.11 = (bf16[48,512]{1,0:T(8,128)(2,1)S(1)}, bf16[48,512]{1,0:T(8,128)(2,1)S(1)}, u32[]{:S(2)}, u32[]{:S(2)}) collective-permute-start(bf16[48,512]{1,0:T(8,128)(2,1)S(1)} %shard_map.100.far.refs_3_), channel_id=1, source_target_pairs={{0,8},{8,0},{16,24},{24,16},{1,9},{9,1},{17,25},{25,17},{2,10},{10... | collective-permute-start | bytes 147464 | tf_op jit(solution)/shard_map/ppermute | solution.py:339
  26.9 5.7 %collective-permute-start.12 = (bf16[48,512]{1,0:T(8,128)(2,1)S(1)}, bf16[48,512]{1,0:T(8,128)(2,1)S(1)}, u32[]{:S(2)}, u32[]{:S(2)}) collective-permute-start(bf16[48,512]{1,0:T(8,128)(2,1)S(1)} %shard_map.99.refs_0_.near.refs_2_), channel_id=1, source_target_pairs={{0,8},{8,0},{16,24},{24,16},{1,9},{9,1},{17,25},{25,17},{2,10},{10... | collective-permute-start | bytes 147464 | tf_op jit(solution)/shard_map/ppermute | solution.py:339
  29.1 7.4 %collective-permute-start.13 = (bf16[24,896]{1,0:T(8,128)(2,1)S(1)}, bf16[24,896]{1,0:T(8,128)(2,1)S(1)}, u32[]{:S(2)}, u32[]{:S(2)}) collective-permute-start(bf16[24,896]{1,0:T(8,128)(2,1)S(1)} %get-tuple-element.43), channel_id=1, source_target_pairs={{0,3},{1,2},{2,1},{3,0},{4,7},{5,6},{6,5},{7,4},{8,11},{9,10},{10,... | collective-permute-start | bytes 129032 | tf_op jit(solution)/shard_map/ppermute | solution.py:336
  30.9 5.6 %collective-permute-start.14 = (bf16[24,896]{1,0:T(8,128)(2,1)S(1)}, bf16[24,896]{1,0:T(8,128)(2,1)S(1)}, u32[]{:S(2)}, u32[]{:S(2)}) collective-permute-start(bf16[24,896]{1,0:T(8,128)(2,1)S(1)} %get-tuple-element.44), channel_id=1, source_target_pairs={{0,2},{1,3},{2,0},{3,1},{4,6},{5,7},{6,4},{7,5},{8,10},{9,11},{10,... | collective-permute-start | bytes 129032 | tf_op jit(solution)/shard_map/ppermute | solution.py:336
  32.1 4.5 %collective-permute-start.15 = (bf16[24,896]{1,0:T(8,128)(2,1)S(1)}, bf16[24,896]{1,0:T(8,128)(2,1)S(1)}, u32[]{:S(2)}, u32[]{:S(2)}) collective-permute-start(bf16[24,896]{1,0:T(8,128)(2,1)S(1)} %get-tuple-element.45), channel_id=1, source_target_pairs={{0,1},{1,0},{2,3},{3,2},{4,5},{5,4},{6,7},{7,6},{8,9},{9,8},{10,11... | collective-permute-start | bytes 129032 | tf_op jit(solution)/shard_map/ppermute | solution.py:336
  33.3 4.7 %collective-permute-start.16 = (bf16[24,1792]{1,0:T(8,128)(2,1)S(1)}, bf16[24,1792]{1,0:T(8,128)(2,1)S(1)}, u32[]{:S(2)}, u32[]{:S(2)}) collective-permute-start(bf16[24,1792]{1,0:T(8,128)(2,1)S(1)} %get-tuple-element.48), channel_id=1, source_target_pairs={{0,1},{1,0},{2,3},{3,2},{4,5},{5,4},{6,7},{7,6},{8,9},{9,8},{10,11... | collective-permute-start | bytes 258056 | tf_op jit(solution)/shard_map/ppermute | solution.py:336
  36.6 6.0 %collective-permute-start.18 = (bf16[24,896]{1,0:T(8,128)(2,1)S(1)}, bf16[24,896]{1,0:T(8,128)(2,1)S(1)}, u32[]{:S(2)}, u32[]{:S(2)}) collective-permute-start(bf16[24,896]{1,0:T(8,128)(2,1)S(1)} %shard_map.104.after), channel_id=1, source_target_pairs={{0,4},{1,5},{2,6},{3,7},{4,0},{5,1},{6,2},{7,3},{8,12},{9,13},{10,... | collective-permute-start | bytes 129032 | tf_op jit(solution)/shard_map/ppermute | solution.py:333
  38.2 4.4 %collective-permute-start.17 = (bf16[24,896]{1,0:T(8,128)(2,1)S(1)}, bf16[24,896]{1,0:T(8,128)(2,1)S(1)}, u32[]{:S(2)}, u32[]{:S(2)}) collective-permute-start(bf16[24,896]{1,0:T(8,128)(2,1)S(1)} %get-tuple-element.50.after), channel_id=1, source_target_pairs={{0,2},{1,3},{2,0},{3,1},{4,6},{5,7},{6,4},{7,5},{8,10},{9,11},{10,... | collective-permute-start | bytes 129032 | tf_op jit(solution)/shard_map/ppermute | solution.py:336

commit v3 on v1

--- a/solution.py
+++ b/solution.py
@@ -50,6 +50,14 @@
     return jnp.floor((rows.astype(F32) + 0.5) * (1.0 / CAP)).astype(jnp.int32)
 
 
+def column_spans(width):
+    whole = width // 128 * 128
+    if whole != width or width < 512:
+        return [slice(0, width)]
+    middle = width // 256 * 128
+    return [slice(0, middle), slice(middle, width)]
+
+
 def core_columns(width, far):
     side = lax.rem(lax.axis_index("dp"), 2)
     side = 1 - side if far else side
@@ -63,11 +71,14 @@
 def pick_body(experts, fold, ids_hbm, gates_hbm, grads_hbm, inputs_hbm, *refs):
     picks, pieces = refs[:fold], refs[fold : fold + experts]
     ids, gates, grads, inputs, sems = refs[fold + experts :]
+    spans = column_spans(grads.shape[1])
+    moves = [(ids_hbm, ids), (gates_hbm, gates)]
+    for span in spans:
+        moves.append((inputs_hbm.at[:, span], inputs.at[:, span]))
+        moves.append((grads_hbm.at[:, span], grads.at[:, span]))
     loads = [
         pltpu.make_async_copy(source, target, sems.at[place])
-        for place, (source, target) in enumerate(
-            ((ids_hbm, ids), (gates_hbm, gates), (inputs_hbm, inputs), (grads_hbm, grads))
-        )
+        for place, (source, target) in enumerate(moves)
     ]
     for load in loads:
         load.start()
@@ -111,21 +122,28 @@
         picks[1][...] = grad_picks.astype(BF16)
     else:
         picks[0][...] = jnp.concatenate(chosen(CAP, 0), axis=0).astype(BF16)
-    loads[2].wait()
-    total = dot(input_picks.astype(BF16), inputs[...])
-    loads[3].wait()
-    total = total + dot(grad_picks.astype(BF16), grads[...]) * gate_column
-    for step in range(experts):
-        pieces[step][...] = total[step * 2 * CAP : (step + 1) * 2 * CAP].astype(BF16)
-
-
-def load_body(after, *refs):
+    input_picks = input_picks.astype(BF16)
+    grad_picks = grad_picks.astype(BF16)
+    for place, span in enumerate(spans):
+        loads[2 + 2 * place].wait()
+        total = dot(input_picks, inputs[:, span])
+        loads[3 + 2 * place].wait()
+        total = total + dot(grad_picks, grads[:, span]) * gate_column
+        for step in range(experts):
+            rows = slice(step * 2 * CAP, (step + 1) * 2 * CAP)
+            pieces[step][:, span] = total[rows].astype(BF16)
+
+
+def load_body(parts, after, *refs):
     count = len(refs) // 2
     sems = refs[-1]
-    loads = [
-        pltpu.make_async_copy(refs[place], refs[count + place], sems.at[place])
-        for place in range(count)
-    ]
+    loads = []
+    for place in range(count):
+        depth = refs[place].shape[0] // parts
+        for part in range(parts):
+            rows = slice(part * depth, (part + 1) * depth)
+            source, target = refs[place].at[rows], refs[count + place].at[rows]
+            loads.append(pltpu.make_async_copy(source, target, sems.at[len(loads)]))
     for load in loads:
         load.start()
     for load in loads:
@@ -162,7 +180,14 @@
         target[...] = dot(rows, w_down[core_columns(half, far), :], 1, 1).astype(BF16)
 
 
-def activate_body(pre_own, pre_far, hid_own, hid_far, acts):
+def transpose_body(after, rows_ref, out):
+    rows = rows_ref[...]
+    count = rows.shape[0]
+    same = (iota((count, count), 0) == iota((count, count), 1)).astype(F32).astype(BF16)
+    out[...] = dot(rows, same, 0, 0).astype(BF16)
+
+
+def activate_body(after, pre_own, pre_far, hid_own, hid_far, acts):
     half = hid_own.shape[1]
     pre = pre_own[...].astype(F32) + pre_far[...].astype(F32)
     hidden_grad = hid_own[...].astype(F32) + hid_far[...].astype(F32)
@@ -173,9 +198,20 @@
     acts[:, half:] = (hidden_grad * gate_pre * sigma).astype(BF16)
 
 
-def back_part(w_gate, w_up, acts, far):
+def fold_rows(rows, fold):
+    width = rows.shape[1] // fold
+    return [
+        jnp.concatenate(
+            [rows[place : place + CAP, part * width : (part + 1) * width] for part in range(fold)],
+            axis=0,
+        )
+        for place in range(0, rows.shape[0], CAP)
+    ]
+
+
+def back_part(w_gate, w_up, acts, sibling):
     half = w_gate.shape[1] // 2
-    columns = core_columns(half, far)
+    columns = core_columns(half, sibling)
     part = dot(acts[:, :half], w_gate[:, columns], 1, 1)
     return part + dot(acts[:, half:], w_up[:, columns], 1, 1)
 
@@ -195,50 +231,45 @@
     token[...] = jnp.zeros_like(token)
     half = out.shape[1] // 2
     depth = out.shape[0] // chunks
+    columns = slice(which * half, (which + 1) * half)
     stores = []
     for chunk in range(chunks):
         span = slice(chunk * depth, (chunk + 1) * depth)
-        rows = rows_ref[:, span]
+        rows = rows_ref[span, :]
         for acts, far in ((acts_own, False), (acts_far, True)):
-            part = dot(rows, acts[:, which * half : (which + 1) * half], 0, 0)
-            tile[span, core_columns(half, far)] = part.astype(BF16)
+            tile[span, core_columns(half, far)] = dot(rows, acts[:, columns]).astype(BF16)
         stores.append(pltpu.make_async_copy(tile.at[span], out.at[span], sems.at[chunk]))
         stores[-1].start()
     for store in stores:
         store.wait()
 
 
-def gather_body(fold, experts, after, own, one, two, three, *outs):
-    total = own[...].astype(F32) + one[...].astype(F32)
-    total = (total + (two[...].astype(F32) + three[...].astype(F32))).astype(BF16)
-    count = total.shape[0]
-    width = total.shape[1] // fold
-    piece = CAP * fold
-    rows = iota((fold * count, count), 1)
-    folded = None
-    for part in range(fold):
-        goal = rows + over_cap(rows) * (CAP * (fold - 1)) + part * CAP
-        mover = (iota((fold * count, count), 0) == goal).astype(F32).astype(BF16)
-        moved = dot(mover, total[:, part * width : (part + 1) * width])
-        folded = moved if folded is None else folded + moved
-    for step in range(experts):
-        outs[step][...] = folded[step * piece : (step + 1) * piece].astype(BF16)
-
-
-def scatter_body(fold, experts, *refs):
-    picks, pieces = refs[:fold], refs[fold : fold + experts]
+def gather_body(fold, experts, after, *refs):
+    parts, outs = refs[:HSPLIT], refs[HSPLIT:]
+    total = parts[0][...].astype(F32) + parts[1][...].astype(F32)
+    total = total + (parts[2][...].astype(F32) + parts[3][...].astype(F32))
+    for out, rows in zip(outs, fold_rows(total, fold)):
+        out[...] = rows.astype(BF16)
+
+
+def scatter_body(fold, *refs):
+    picks, pieces = refs[:fold], refs[fold:-4]
     out, stack, tile, sems = refs[-4:]
     width = out.shape[1] // fold
     piece = CAP * fold
-    for step in range(experts):
-        stack[step * piece : (step + 1) * piece, :] = pieces[step][...].astype(F32)
+    for place, ref in enumerate(pieces):
+        stack[place * piece : (place + 1) * piece, :] = ref[...].astype(F32)
     returned = stack[...].astype(BF16)
     stores = []
     for part in range(fold):
-        span = slice(part * width, (part + 1) * width)
-        tile[:, span] = dot(picks[part][...], returned, 0, 0).astype(BF16)
-        stores.append(pltpu.make_async_copy(tile.at[:, span], out.at[:, span], sems.at[part]))
-        stores[-1].start()
+        for span in column_spans(width):
+            target = slice(part * width + span.start, part * width + span.stop)
+            tile[:, target] = dot(picks[part][...], returned[:, span], 0, 0).astype(BF16)
+            store = pltpu.make_async_copy(
+                tile.at[:, target], out.at[:, target], sems.at[len(stores)]
+            )
+            store.start()
+            stores.append(store)
     for store in stores:
         store.wait()
 
@@ -279,28 +310,27 @@
             pltpu.VMEM((routed, tokens), F32),
             pltpu.VMEM((tokens, features), BF16),
             pltpu.VMEM((tokens, features), BF16),
-            dma((4,)),
+            dma((2 + 2 * len(column_spans(features)),)),
         ),
     )
     picks, own = picked[:fold], picked[fold:]
     weights = (w_gate, w_up, w_down)
     gate_here, up_here, down_here = run(
-        load_body,
+        functools.partial(load_body, 4),
         tuple(pltpu.VMEM(weight.shape, weight.dtype) for weight in weights),
         [ANY] + [HBM] * 3,
         0,
         6 * features * hidden,
         picks[0],
         *(in_hbm(weight) for weight in weights),
-        scratch=(dma((3,)),),
+        scratch=(dma((12,)),),
     )
 
     away = [to_expert(own[step], step) for step in range(1, experts)]
-    pieces = [own[0]] + [to_peer(own[0], flip) for flip in range(1, HSPLIT)]
-    if away:
-        away = away[0] if len(away) == 1 else jnp.concatenate(away, axis=0)
-        others = [away] + [to_peer(away, flip) for flip in range(1, HSPLIT)]
-        pieces = [array for pair in zip(pieces, others) for array in pair]
+    near = [own[0]] + [to_peer(own[0], flip) for flip in range(1, HSPLIT)]
+    away = away[0] if len(away) == 1 else jnp.concatenate(away, axis=0)
+    far = [away] + [to_peer(away, flip) for flip in range(1, HSPLIT)]
+    pieces = [array for pair in zip(near, far) for array in pair]
 
     stack = pltpu.VMEM((2 * count, features), F32)
     rows_input, pre_keep, pre_send = run(
@@ -338,12 +368,22 @@
         scratch=(stack,),
     )
     hid_own, hid_far = spread_sum(hid_keep, hid_send)
+    rows_across = run(
+        transpose_body,
+        shape((features, count)),
+        [ANY, VMEM],
+        0,
+        0,
+        hid_own,
+        rows_input,
+    )
     acts = run(
         activate_body,
         shape((count, hidden)),
-        [VMEM] * 4,
+        [ANY] + [VMEM] * 4,
         20 * count * half,
         10 * count * half,
+        rows_across,
         pre_own,
         pre_far,
         hid_own,
@@ -371,18 +411,17 @@
         acts_far,
         back_own,
     )
-    back_far = [to_peer(back[flip], flip) for flip in range(1, HSPLIT)]
 
     def weight_grad(which, after):
-        chunks = 2
+        chunks = features // 256 if features % 256 == 0 else 2
         return run(
             functools.partial(weight_body, which, chunks),
             (shape((features, hidden)), shape((8, 128), F32)),
             [ANY] + [VMEM] * 3,
-            product,
-            4 * features * hidden,
+            0,
+            0,
             after,
-            rows_input,
+            rows_across,
             acts,
             acts_far,
             out_spec=(HBM, VMEM),
@@ -394,16 +433,16 @@
         functools.partial(gather_body, fold, experts),
         (shape((CAP * fold, features // fold)),) * experts,
         [ANY] + [VMEM] * HSPLIT,
-        4 * count * features,
-        4 * count * features,
+        0,
+        0,
         token,
+        *(to_peer(back[flip], flip) for flip in range(HSPLIT - 1, 0, -1)),
         back[0],
-        *back_far,
     )
     grad_up, _ = weight_grad(1, summed[0])
     returned = [summed[0]] + [to_expert(summed[step], experts - step) for step in range(1, experts)]
     in_grad = run(
-        functools.partial(scatter_body, fold, experts),
+        functools.partial(scatter_body, fold),
         shape((tokens, features)),
         [VMEM] * (fold + experts),
         4 * experts * CAP * tokens * features,
@@ -414,7 +453,7 @@
         scratch=(
             pltpu.VMEM((experts * fold * CAP, features // fold), F32),
             pltpu.VMEM((tokens, features), BF16),
-            dma((fold,)),
+            dma((fold * len(column_spans(features // fold)),)),
         ),
     )
     return (in_grad, grad_gate, grad_up)

time: 43.7 us -> 42.6 us (0.975)
  starting transfers between devices: 21.2 us -> 20.3 us
    ppermute x2, starting transfers between devices: 7.23 us -> 6.34 us  [to_expert(): return lax.ppermute(value, 'expert', pairs)]
    ppermute x2, waiting for transfers between devices: 0.54 us -> 1.2 us  [to_expert(): return lax.ppermute(value, 'expert', pairs)]
    pallas_call x11 -> x12, Pallas kernels: 13.1 us -> 12.7 us  [run(): pl.pallas_call(body, out_shape=outs, in_specs=specs, out_specs=out_spec i...]
  transfers between devices with their start and end apart: 16 -> 16, of which waited for: 7 -> 9; matrix products, arithmetic and copies ran while one was open for 0% -> 0% of each run, Pallas kernels for 18% -> 19%
where the time goes in v3:
time: 42.6 us; the launch traced here: 42.3 us
  starting transfers between devices  20.3 us (48%)
  Pallas kernels  12.7 us (30%)
  waiting for transfers between devices  8.53 us (20%)
  between operations  0.76 us (2%)
    pallas_call x12, Pallas kernels, run(): pl.pallas_call(body, out_shape=outs, in_specs=specs, out_specs=out_spec i...  12.7 us
    ppermute x9, starting transfers between devices, to_peer(): lax.ppermute(value, 'expert', [(d, d ^ flip) for d in range(devices)])  10.9 us
    ppermute x2, starting transfers between devices, to_expert(): return lax.ppermute(value, 'expert', pairs)  6.34 us
    ppermute x5, waiting for transfers between devices, to_dp(): return lax.ppermute(value, 'dp', [(d, d ^ flip) for d in range(spread)])  3.8 us
    ppermute x9, waiting for transfers between devices, to_peer(): lax.ppermute(value, 'expert', [(d, d ^ flip) for d in range(devices)])  3.53 us
    ppermute x5, starting transfers between devices, to_dp(): return lax.ppermute(value, 'dp', [(d, d ^ flip) for d in range(spread)])  3.09 us
    ppermute x2, waiting for transfers between devices, to_expert(): return lax.ppermute(value, 'expert', pairs)  1.2 us
  transfers between devices with their start and end apart: 16, of which 9 were waited for; matrix products, arithmetic and copies ran while one was open for 0% of the time, Pallas kernels for 19%

profile of v3, /device:TPU:0, one launch (start us, length us, event | category | flops | bytes accessed | tf_op | source)
XLA Modules:
  0.0 42.3 jit_solution(16380188154073283736)
XLA Ops:
  0.6 1.8 %shard_map.94 = (bf16[48,256]{1,0:T(8,128)(2,1)S(1)}, bf16[48,256]{1,0:T(8,128)(2,1)S(1)}, bf16[24,1792]{1,0:T(8,128)(2,1)S(1)}, bf16[24,1792]{1,0:T(8,128)(2,1)S(1)}) custom-call(s32[8,256]{1,0:T(8,128)} %bitcast.2, f32[8,256]{1,0:T(8,128)} %bitcast.3, bf16[256,1792]{1,0:T(8,128)(2,1)} %grads_hbm.1, bf16[256,1792]{1,0:T(8,128)(2,1)} %inputs_hbm.1), custom_call_target="tpu_custom_call" | custom-call | flops 88080384 | bytes 1835008 | tf_op jit(solution)/shard_map/pallas_call | solution.py:24
  2.4 4.1 %collective-permute-start = (bf16[24,1792]{1,0:T(8,128)(2,1)S(1)}, bf16[24,1792]{1,0:T(8,128)(2,1)S(1)}, u32[]{:S(2)}, u32[]{:S(2)}) collective-permute-start(bf16[24,1792]{1,0:T(8,128)(2,1)S(1)} %get-tuple-element.30), channel_id=1, source_target_pairs={{0,4},{1,5},{2,6},{3,7},{4,0},{5,1},{6,2},{7,3},{8,12},{9,13},{10,... | collective-permute-start | bytes 258056 | tf_op jit(solution)/shard_map/ppermute | solution.py:292
  6.5 2.5 %collective-permute-start.5 = (bf16[24,1792]{1,0:T(8,128)(2,1)S(1)}, bf16[24,1792]{1,0:T(8,128)(2,1)S(1)}, u32[]{:S(2)}, u32[]{:S(2)}) collective-permute-start(bf16[24,1792]{1,0:T(8,128)(2,1)S(1)} %get-tuple-element.29.refs_0_), channel_id=1, source_target_pairs={{0,3},{1,2},{2,1},{3,0},{4,7},{5,6},{6,5},{7,4},{8,11},{9,10},{10,... | collective-permute-start | bytes 258056 | tf_op jit(solution)/shard_map/ppermute | solution.py:295
  9.1 0.4 %collective-permute-start.3 = (bf16[24,1792]{1,0:T(8,128)(2,1)S(1)}, bf16[24,1792]{1,0:T(8,128)(2,1)S(1)}, u32[]{:S(2)}, u32[]{:S(2)}) collective-permute-start(bf16[24,1792]{1,0:T(8,128)(2,1)S(1)} %get-tuple-element.29.refs_0_), channel_id=1, source_target_pairs={{0,2},{1,3},{2,0},{3,1},{4,6},{5,7},{6,4},{7,5},{8,10},{9,11},{10,... | collective-permute-start | bytes 258056 | tf_op jit(solution)/shard_map/ppermute | solution.py:295
  9.5 0.5 %collective-permute-start.1 = (bf16[24,1792]{1,0:T(8,128)(2,1)S(1)}, bf16[24,1792]{1,0:T(8,128)(2,1)S(1)}, u32[]{:S(2)}, u32[]{:S(2)}) collective-permute-start(bf16[24,1792]{1,0:T(8,128)(2,1)S(1)} %get-tuple-element.29.refs_0_), channel_id=1, source_target_pairs={{0,1},{1,0},{2,3},{3,2},{4,5},{5,4},{6,7},{7,6},{8,9},{9,8},{10,11... | collective-permute-start | bytes 258056 | tf_op jit(solution)/shard_map/ppermute | solution.py:295
  10.0 0.5 %collective-permute-done.refs_1_ = bf16[24,1792]{1,0:T(8,128)(2,1)S(1)} collective-permute-done((bf16[24,1792]{1,0:T(8,128)(2,1)S(1)}, bf16[24,1792]{1,0:T(8,128)(2,1)S(1)}, u32[]{:S(2)}, u32[]{:S(2)}) %collective-permute-start) | collective-permute-done | bytes 86048 | tf_op jit(solution)/shard_map/ppermute | solution.py:292
  10.6 2.2 %collective-permute-start.6 = (bf16[24,1792]{1,0:T(8,128)(2,1)S(1)}, bf16[24,1792]{1,0:T(8,128)(2,1)S(1)}, u32[]{:S(2)}, u32[]{:S(2)}) collective-permute-start(bf16[24,1792]{1,0:T(8,128)(2,1)S(1)} %collective-permute-done.refs_1_), channel_id=1, source_target_pairs={{0,3},{1,2},{2,1},{3,0},{4,7},{5,6},{6,5},{7,4},{8,11},{9,10},{10,... | collective-permute-start | bytes 258056 | tf_op jit(solution)/shard_map/ppermute | solution.py:295
  12.8 1.0 %collective-permute-start.4 = (bf16[24,1792]{1,0:T(8,128)(2,1)S(1)}, bf16[24,1792]{1,0:T(8,128)(2,1)S(1)}, u32[]{:S(2)}, u32[]{:S(2)}) collective-permute-start(bf16[24,1792]{1,0:T(8,128)(2,1)S(1)} %collective-permute-done.refs_1_), channel_id=1, source_target_pairs={{0,2},{1,3},{2,0},{3,1},{4,6},{5,7},{6,4},{7,5},{8,10},{9,11},{10,... | collective-permute-start | bytes 258056 | tf_op jit(solution)/shard_map/ppermute | solution.py:295
  13.8 0.6 %collective-permute-start.2 = (bf16[24,1792]{1,0:T(8,128)(2,1)S(1)}, bf16[24,1792]{1,0:T(8,128)(2,1)S(1)}, u32[]{:S(2)}, u32[]{:S(2)}) collective-permute-start(bf16[24,1792]{1,0:T(8,128)(2,1)S(1)} %collective-permute-done.refs_1_), channel_id=1, source_target_pairs={{0,1},{1,0},{2,3},{3,2},{4,5},{5,4},{6,7},{7,6},{8,9},{9,8},{10,11... | collective-permute-start | bytes 258056 | tf_op jit(solution)/shard_map/ppermute | solution.py:295
  14.4 2.6 %shard_map.95 = (bf16[1792,512]{1,0:T(8,128)(2,1)S(1)}, bf16[1792,512]{1,0:T(8,128)(2,1)S(1)}, bf16[512,1792]{1,0:T(8,128)(2,1)S(1)}) custom-call(bf16[48,256]{1,0:T(8,128)(2,1)S(1)} %get-tuple-element.24.after.refs_0_, bf16[1792,512]{1,0:T(8,128)(2,1)} %refs_0_.1, bf16[1792,512]{1,0:T(8,128)(2,1)} %refs_1_.1, bf16[512,1792]{1,0:T(8,128)(2,1)} %refs_2_.1), custom_call_target="tpu_custom_call" | custom-call | bytes 5505024 | tf_op jit(solution)/shard_map/pallas_call | solution.py:24
  17.1 0.4 collective-permute-done.4.refs_5_
  17.5 0.8 %collective-permute-done.2.refs_3_ = bf16[24,1792]{1,0:T(8,128)(2,1)S(1)} collective-permute-done((bf16[24,1792]{1,0:T(8,128)(2,1)S(1)}, bf16[24,1792]{1,0:T(8,128)(2,1)S(1)}, u32[]{:S(2)}, u32[]{:S(2)}) %collective-permute-start.2) | collective-permute-done | bytes 86048 | tf_op jit(solution)/shard_map/ppermute | solution.py:295
  18.3 0.9 %shard_map.97 = (bf16[96,1792]{1,0:T(8,128)(2,1)S(1)}, bf16[96,512]{1,0:T(8,128)(2,1)S(1)}, bf16[96,512]{1,0:T(8,128)(2,1)S(1)}) custom-call(bf16[1792,512]{1,0:T(8,128)(2,1)S(1)} %get-tuple-element.26.w_gate, bf16[1792,512]{1,0:T(8,128)(2,1)S(1)} %get-tuple-element.27.w_up, bf16[24,1792]{1,0:T(8,128)(2,1)S(1)} %get-tuple-element.29.refs_0_, ...), custom_call_target="tpu_custom_call" | custom-call | flops 352321536 | bytes 3670016 | tf_op jit(solution)/shard_map/pallas_call | solution.py:24
  19.3 0.8 %shard_map.96 = (bf16[96,256]{1,0:T(8,128)(2,1)S(1)}, bf16[96,256]{1,0:T(8,128)(2,1)S(1)}) custom-call(bf16[512,1792]{1,0:T(8,128)(2,1)S(1)} %get-tuple-element.28.w_down, bf16[24,1792]{1,0:T(8,128)(2,1)S(1)} %get-tuple-element.29.refs_0_, bf16[24,1792]{1,0:T(8,128)(2,1)S(1)} %collective-permute-done.refs_1_, ...), custom_call_target="tpu_custom_call" | custom-call | flops 176160768 | bytes 1835008 | tf_op jit(solution)/shard_map/pallas_call | solution.py:24
  20.0 0.6 %collective-permute-start.7 = (bf16[96,256]{1,0:T(8,128)(2,1)S(1)}, bf16[96,256]{1,0:T(8,128)(2,1)S(1)}, u32[]{:S(2)}, u32[]{:S(2)}) collective-permute-start(bf16[96,256]{1,0:T(8,128)(2,1)S(1)} %get-tuple-element.32), channel_id=1, source_target_pairs={{0,8},{8,0},{16,24},{24,16},{1,9},{9,1},{17,25},{25,17},{2,10},{10... | collective-permute-start | bytes 147464 | tf_op jit(solution)/shard_map/ppermute | solution.py:298
  20.6 1.6 %collective-permute-start.9 = (bf16[96,512]{1,0:T(8,128)(2,1)S(1)}, bf16[96,512]{1,0:T(8,128)(2,1)S(1)}, u32[]{:S(2)}, u32[]{:S(2)}) collective-permute-start(bf16[96,512]{1,0:T(8,128)(2,1)S(1)} %add_convert_fusion.pre_own), channel_id=1, source_target_pairs={{0,16},{8,24},{16,0},{24,8},{1,17},{9,25},{17,1},{25,9},{2,18},{10... | collective-permute-start | bytes 294920 | tf_op jit(solution)/shard_map/ppermute | solution.py:298
  22.2 0.8 %collective-permute-start.10 = (bf16[96,256]{1,0:T(8,128)(2,1)S(1)}, bf16[96,256]{1,0:T(8,128)(2,1)S(1)}, u32[]{:S(2)}, u32[]{:S(2)}) collective-permute-start(bf16[96,256]{1,0:T(8,128)(2,1)S(1)} %add_convert_fusion.1.after.hid_own), channel_id=1, source_target_pairs={{0,16},{8,24},{16,0},{24,8},{1,17},{9,25},{17,1},{25,9},{2,18},{10... | collective-permute-start | bytes 147464 | tf_op jit(solution)/shard_map/ppermute | solution.py:298
  23.0 0.3 shard_map.98.after.rows_ref
  23.3 3.2 %collective-permute-done.10.hid_far = bf16[96,256]{1,0:T(8,128)(2,1)S(1)} collective-permute-done((bf16[96,256]{1,0:T(8,128)(2,1)S(1)}, bf16[96,256]{1,0:T(8,128)(2,1)S(1)}, u32[]{:S(2)}, u32[]{:S(2)}) %collective-permute-start.10) | collective-permute-done | bytes 49184 | tf_op jit(solution)/shard_map/ppermute | solution.py:298
  26.7 0.7 %shard_map.100.own = f32[96,1792]{1,0:T(8,128)S(1)} custom-call(bf16[1792,512]{1,0:T(8,128)(2,1)S(1)} %get-tuple-element.26.w_gate, bf16[1792,512]{1,0:T(8,128)(2,1)S(1)} %get-tuple-element.27.w_up, bf16[96,512]{1,0:T(8,128)(2,1)S(1)} %shard_map.99.acts.acts_own), custom_call_target="tpu_custom_call" | custom-call | flops 176160768 | bytes 1835008 | tf_op jit(solution)/shard_map/pallas_call | solution.py:24
  27.4 0.6 %collective-permute-done.11.acts.acts_far = bf16[96,512]{1,0:T(8,128)(2,1)S(1)} collective-permute-done((bf16[96,512]{1,0:T(8,128)(2,1)S(1)}, bf16[96,512]{1,0:T(8,128)(2,1)S(1)}, u32[]{:S(2)}, u32[]{:S(2)}) %collective-permute-start.11) | collective-permute-done | bytes 98336 | tf_op jit(solution)/shard_map/ppermute | solution.py:298
  28.0 0.7 %shard_map.101 = (bf16[24,1792]{1,0:T(8,128)(2,1)S(1)}, bf16[24,1792]{1,0:T(8,128)(2,1)S(1)}, bf16[24,1792]{1,0:T(8,128)(2,1)S(1)}, bf16[24,1792]{1,0:T(8,128)(2,1)S(1)}) custom-call(bf16[1792,512]{1,0:T(8,128)(2,1)S(1)} %get-tuple-element.26.w_gate, bf16[1792,512]{1,0:T(8,128)(2,1)S(1)} %get-tuple-element.27.w_up, ...), custom_call_target="tpu_custom_call" | custom-call | flops 176160768 | bytes 1835008 | tf_op jit(solution)/shard_map/pallas_call | solution.py:24
  28.7 1.3 %collective-permute-start.12 = (bf16[24,1792]{1,0:T(8,128)(2,1)S(1)}, bf16[24,1792]{1,0:T(8,128)(2,1)S(1)}, u32[]{:S(2)}, u32[]{:S(2)}) collective-permute-start(bf16[24,1792]{1,0:T(8,128)(2,1)S(1)} %get-tuple-element.38), channel_id=1, source_target_pairs={{0,3},{1,2},{2,1},{3,0},{4,7},{5,6},{6,5},{7,4},{8,11},{9,10},{10,... | collective-permute-start | bytes 258056 | tf_op jit(solution)/shard_map/ppermute | solution.py:295
  30.0 0.9 %collective-permute-start.13 = (bf16[24,1792]{1,0:T(8,128)(2,1)S(1)}, bf16[24,1792]{1,0:T(8,128)(2,1)S(1)}, u32[]{:S(2)}, u32[]{:S(2)}) collective-permute-start(bf16[24,1792]{1,0:T(8,128)(2,1)S(1)} %get-tuple-element.39), channel_id=1, source_target_pairs={{0,2},{1,3},{2,0},{3,1},{4,6},{5,7},{6,4},{7,5},{8,10},{9,11},{10,... | collective-permute-start | bytes 258056 | tf_op jit(solution)/shard_map/ppermute | solution.py:295
  30.9 1.4 %collective-permute-start.14 = (bf16[24,1792]{1,0:T(8,128)(2,1)S(1)}, bf16[24,1792]{1,0:T(8,128)(2,1)S(1)}, u32[]{:S(2)}, u32[]{:S(2)}) collective-permute-start(bf16[24,1792]{1,0:T(8,128)(2,1)S(1)} %get-tuple-element.40), channel_id=1, source_target_pairs={{0,1},{1,0},{2,3},{3,2},{4,5},{5,4},{6,7},{7,6},{8,9},{9,8},{10,11... | collective-permute-start | bytes 258056 | tf_op jit(solution)/shard_map/ppermute | solution.py:295
  32.2 1.5 %shard_map.102 = (bf16[1792,512]{1,0:T(8,128)(2,1)}, f32[8,128]{1,0:T(8,128)S(1)}) custom-call(bf16[24,1792]{1,0:T(8,128)(2,1)S(1)} %get-tuple-element.36.after.refs_3_, bf16[1792,96]{1,0:T(8,128)(2,1)S(1)} %shard_map.98.after.rows_ref, bf16[96,512]{1,0:T(8,128)(2,1)S(1)} %shard_map.99.acts.acts_own, bf16[96,512]{1,0:T(8,128)(2,1)S(1)} %collective-permute-done.11.acts.acts_far), custom_call_target="tpu_custom_call" | custom-call | tf_op jit(solution)/shard_map/pallas_call | solution.py:24
  33.7 1.3 %collective-permute-done.12.refs_0_ = bf16[24,1792]{1,0:T(8,128)(2,1)S(1)} collective-permute-done((bf16[24,1792]{1,0:T(8,128)(2,1)S(1)}, bf16[24,1792]{1,0:T(8,128)(2,1)S(1)}, u32[]{:S(2)}, u32[]{:S(2)}) %collective-permute-start.12) | collective-permute-done | bytes 86048 | tf_op jit(solution)/shard_map/ppermute | solution.py:295
  35.3 0.8 %collective-permute-done.14.refs_2_ = bf16[24,1792]{1,0:T(8,128)(2,1)S(1)} collective-permute-done((bf16[24,1792]{1,0:T(8,128)(2,1)S(1)}, bf16[24,1792]{1,0:T(8,128)(2,1)S(1)}, u32[]{:S(2)}, u32[]{:S(2)}) %collective-permute-start.14) | collective-permute-done | bytes 86048 | tf_op jit(solution)/shard_map/ppermute | solution.py:295
  36.1 2.2 %collective-permute-start.15 = (bf16[24,896]{1,0:T(8,128)(2,1)S(1)}, bf16[24,896]{1,0:T(8,128)(2,1)S(1)}, u32[]{:S(2)}, u32[]{:S(2)}) collective-permute-start(bf16[24,896]{1,0:T(8,128)(2,1)S(1)} %get-tuple-element.42), channel_id=1, source_target_pairs={{0,4},{1,5},{2,6},{3,7},{4,0},{5,1},{6,2},{7,3},{8,12},{9,13},{10,... | collective-permute-start | bytes 129032 | tf_op jit(solution)/shard_map/ppermute | solution.py:292
  38.4 2.1 %shard_map.105 = (bf16[1792,512]{1,0:T(8,128)(2,1)}, f32[8,128]{1,0:T(8,128)}) custom-call(bf16[24,896]{1,0:T(8,128)(2,1)S(1)} %get-tuple-element.41.refs_2_.after, bf16[1792,96]{1,0:T(8,128)(2,1)S(1)} %shard_map.98.after.rows_ref, bf16[96,512]{1,0:T(8,128)(2,1)S(1)} %shard_map.99.acts.acts_own, bf16[96,512]{1,0:T(8,128)(2,1)S(1)} %collective-permute-done.11.acts.acts_far), custom_call_target="tpu_custom_call" | custom-call | tf_op jit(solution)/shard_map/pallas_call | solution.py:24
  40.5 0.7 %collective-permute-done.15.refs_3_ = bf16[24,896]{1,0:T(8,128)(2,1)S(1)} collective-permute-done((bf16[24,896]{1,0:T(8,128)(2,1)S(1)}, bf16[24,896]{1,0:T(8,128)(2,1)S(1)}, u32[]{:S(2)}, u32[]{:S(2)}) %collective-permute-start.15) | collective-permute-done | bytes 43040 | tf_op jit(solution)/shard_map/ppermute | solution.py:292
  41.1 1.2 %shard_map.104 = bf16[256,1792]{1,0:T(8,128)(2,1)} custom-call(bf16[48,256]{1,0:T(8,128)(2,1)S(1)} %get-tuple-element.24.after.refs_0_, bf16[48,256]{1,0:T(8,128)(2,1)S(1)} %get-tuple-element.25.refs_1_, bf16[24,896]{1,0:T(8,128)(2,1)S(1)} %get-tuple-element.41.refs_2_.after, bf16[24,896]{1,0:T(8,128)(2,1)S(1)} %collective-permute-done.15.refs_3_), custom_call_target="tpu_custom_call" | custom-call | flops 44040192 | bytes 917504 | tf_op jit(solution)/shard_map/pallas_call | solution.py:24
  (14 shorter events, 0.6 us)
Async XLA Ops:
  2.4 8.1 %collective-permute-start = (bf16[24,1792]{1,0:T(8,128)(2,1)S(1)}, bf16[24,1792]{1,0:T(8,128)(2,1)S(1)}, u32[]{:S(2)}, u32[]{:S(2)}) collective-permute-start(bf16[24,1792]{1,0:T(8,128)(2,1)S(1)} %get-tuple-element.30), channel_id=1, source_target_pairs={{0,4},{1,5},{2,6},{3,7},{4,0},{5,1},{6,2},{7,3},{8,12},{9,13},{10,... | collective-permute-start | bytes 258056 | tf_op jit(solution)/shard_map/ppermute | solution.py:292
  6.5 7.3 %collective-permute-start.5 = (bf16[24,1792]{1,0:T(8,128)(2,1)S(1)}, bf16[24,1792]{1,0:T(8,128)(2,1)S(1)}, u32[]{:S(2)}, u32[]{:S(2)}) collective-permute-start(bf16[24,1792]{1,0:T(8,128)(2,1)S(1)} %get-tuple-element.29.refs_0_), channel_id=1, source_target_pairs={{0,3},{1,2},{2,1},{3,0},{4,7},{5,6},{6,5},{7,4},{8,11},{9,10},{10,... | collective-permute-start | bytes 258056 | tf_op jit(solution)/shard_map/ppermute | solution.py:295
  9.1 8.0 %collective-permute-start.3 = (bf16[24,1792]{1,0:T(8,128)(2,1)S(1)}, bf16[24,1792]{1,0:T(8,128)(2,1)S(1)}, u32[]{:S(2)}, u32[]{:S(2)}) collective-permute-start(bf16[24,1792]{1,0:T(8,128)(2,1)S(1)} %get-tuple-element.29.refs_0_), channel_id=1, source_target_pairs={{0,2},{1,3},{2,0},{3,1},{4,6},{5,7},{6,4},{7,5},{8,10},{9,11},{10,... | collective-permute-start | bytes 258056 | tf_op jit(solution)/shard_map/ppermute | solution.py:295
  9.5 7.6 %collective-permute-start.1 = (bf16[24,1792]{1,0:T(8,128)(2,1)S(1)}, bf16[24,1792]{1,0:T(8,128)(2,1)S(1)}, u32[]{:S(2)}, u32[]{:S(2)}) collective-permute-start(bf16[24,1792]{1,0:T(8,128)(2,1)S(1)} %get-tuple-element.29.refs_0_), channel_id=1, source_target_pairs={{0,1},{1,0},{2,3},{3,2},{4,5},{5,4},{6,7},{7,6},{8,9},{9,8},{10,11... | collective-permute-start | bytes 258056 | tf_op jit(solution)/shard_map/ppermute | solution.py:295
  10.6 6.5 %collective-permute-start.6 = (bf16[24,1792]{1,0:T(8,128)(2,1)S(1)}, bf16[24,1792]{1,0:T(8,128)(2,1)S(1)}, u32[]{:S(2)}, u32[]{:S(2)}) collective-permute-start(bf16[24,1792]{1,0:T(8,128)(2,1)S(1)} %collective-permute-done.refs_1_), channel_id=1, source_target_pairs={{0,3},{1,2},{2,1},{3,0},{4,7},{5,6},{6,5},{7,4},{8,11},{9,10},{10,... | collective-permute-start | bytes 258056 | tf_op jit(solution)/shard_map/ppermute | solution.py:295
  12.8 4.7 %collective-permute-start.4 = (bf16[24,1792]{1,0:T(8,128)(2,1)S(1)}, bf16[24,1792]{1,0:T(8,128)(2,1)S(1)}, u32[]{:S(2)}, u32[]{:S(2)}) collective-permute-start(bf16[24,1792]{1,0:T(8,128)(2,1)S(1)} %collective-permute-done.refs_1_), channel_id=1, source_target_pairs={{0,2},{1,3},{2,0},{3,1},{4,6},{5,7},{6,4},{7,5},{8,10},{9,11},{10,... | collective-permute-start | bytes 258056 | tf_op jit(solution)/shard_map/ppermute | solution.py:295
  13.8 4.5 %collective-permute-start.2 = (bf16[24,1792]{1,0:T(8,128)(2,1)S(1)}, bf16[24,1792]{1,0:T(8,128)(2,1)S(1)}, u32[]{:S(2)}, u32[]{:S(2)}) collective-permute-start(bf16[24,1792]{1,0:T(8,128)(2,1)S(1)} %collective-permute-done.refs_1_), channel_id=1, source_target_pairs={{0,1},{1,0},{2,3},{3,2},{4,5},{5,4},{6,7},{7,6},{8,9},{9,8},{10,11... | collective-permute-start | bytes 258056 | tf_op jit(solution)/shard_map/ppermute | solution.py:295
  19.2 1.4 %collective-permute-start.8 = (bf16[96,512]{1,0:T(8,128)(2,1)S(1)}, bf16[96,512]{1,0:T(8,128)(2,1)S(1)}, u32[]{:S(2)}, u32[]{:S(2)}) collective-permute-start(bf16[96,512]{1,0:T(8,128)(2,1)S(1)} %get-tuple-element.35), channel_id=1, source_target_pairs={{0,8},{8,0},{16,24},{24,16},{1,9},{9,1},{17,25},{25,17},{2,10},{10... | collective-permute-start | bytes 294920 | tf_op jit(solution)/shard_map/ppermute | solution.py:298
  20.0 2.2 %collective-permute-start.7 = (bf16[96,256]{1,0:T(8,128)(2,1)S(1)}, bf16[96,256]{1,0:T(8,128)(2,1)S(1)}, u32[]{:S(2)}, u32[]{:S(2)}) collective-permute-start(bf16[96,256]{1,0:T(8,128)(2,1)S(1)} %get-tuple-element.32), channel_id=1, source_target_pairs={{0,8},{8,0},{16,24},{24,16},{1,9},{9,1},{17,25},{25,17},{2,10},{10... | collective-permute-start | bytes 147464 | tf_op jit(solution)/shard_map/ppermute | solution.py:298
  20.6 5.9 %collective-permute-start.9 = (bf16[96,512]{1,0:T(8,128)(2,1)S(1)}, bf16[96,512]{1,0:T(8,128)(2,1)S(1)}, u32[]{:S(2)}, u32[]{:S(2)}) collective-permute-start(bf16[96,512]{1,0:T(8,128)(2,1)S(1)} %add_convert_fusion.pre_own), channel_id=1, source_target_pairs={{0,16},{8,24},{16,0},{24,8},{1,17},{9,25},{17,1},{25,9},{2,18},{10... | collective-permute-start | bytes 294920 | tf_op jit(solution)/shard_map/ppermute | solution.py:298
  22.2 4.4 %collective-permute-start.10 = (bf16[96,256]{1,0:T(8,128)(2,1)S(1)}, bf16[96,256]{1,0:T(8,128)(2,1)S(1)}, u32[]{:S(2)}, u32[]{:S(2)}) collective-permute-start(bf16[96,256]{1,0:T(8,128)(2,1)S(1)} %add_convert_fusion.1.after.hid_own), channel_id=1, source_target_pairs={{0,16},{8,24},{16,0},{24,8},{1,17},{9,25},{17,1},{25,9},{2,18},{10... | collective-permute-start | bytes 147464 | tf_op jit(solution)/shard_map/ppermute | solution.py:298
  26.6 1.4 %collective-permute-start.11 = (bf16[96,512]{1,0:T(8,128)(2,1)S(1)}, bf16[96,512]{1,0:T(8,128)(2,1)S(1)}, u32[]{:S(2)}, u32[]{:S(2)}) collective-permute-start(bf16[96,512]{1,0:T(8,128)(2,1)S(1)} %shard_map.99.acts.acts_own), channel_id=1, source_target_pairs={{0,8},{8,0},{16,24},{24,16},{1,9},{9,1},{17,25},{25,17},{2,10},{10... | collective-permute-start | bytes 294920 | tf_op jit(solution)/shard_map/ppermute | solution.py:298
  28.7 6.3 %collective-permute-start.12 = (bf16[24,1792]{1,0:T(8,128)(2,1)S(1)}, bf16[24,1792]{1,0:T(8,128)(2,1)S(1)}, u32[]{:S(2)}, u32[]{:S(2)}) collective-permute-start(bf16[24,1792]{1,0:T(8,128)(2,1)S(1)} %get-tuple-element.38), channel_id=1, source_target_pairs={{0,3},{1,2},{2,1},{3,0},{4,7},{5,6},{6,5},{7,4},{8,11},{9,10},{10,... | collective-permute-start | bytes 258056 | tf_op jit(solution)/shard_map/ppermute | solution.py:295
  30.0 5.3 %collective-permute-start.13 = (bf16[24,1792]{1,0:T(8,128)(2,1)S(1)}, bf16[24,1792]{1,0:T(8,128)(2,1)S(1)}, u32[]{:S(2)}, u32[]{:S(2)}) collective-permute-start(bf16[24,1792]{1,0:T(8,128)(2,1)S(1)} %get-tuple-element.39), channel_id=1, source_target_pairs={{0,2},{1,3},{2,0},{3,1},{4,6},{5,7},{6,4},{7,5},{8,10},{9,11},{10,... | collective-permute-start | bytes 258056 | tf_op jit(solution)/shard_map/ppermute | solution.py:295
  30.9 5.2 %collective-permute-start.14 = (bf16[24,1792]{1,0:T(8,128)(2,1)S(1)}, bf16[24,1792]{1,0:T(8,128)(2,1)S(1)}, u32[]{:S(2)}, u32[]{:S(2)}) collective-permute-start(bf16[24,1792]{1,0:T(8,128)(2,1)S(1)} %get-tuple-element.40), channel_id=1, source_target_pairs={{0,1},{1,0},{2,3},{3,2},{4,5},{5,4},{6,7},{7,6},{8,9},{9,8},{10,11... | collective-permute-start | bytes 258056 | tf_op jit(solution)/shard_map/ppermute | solution.py:295
  36.1 5.0 %collective-permute-start.15 = (bf16[24,896]{1,0:T(8,128)(2,1)S(1)}, bf16[24,896]{1,0:T(8,128)(2,1)S(1)}, u32[]{:S(2)}, u32[]{:S(2)}) collective-permute-start(bf16[24,896]{1,0:T(8,128)(2,1)S(1)} %get-tuple-element.42), channel_id=1, source_target_pairs={{0,4},{1,5},{2,6},{3,7},{4,0},{5,1},{6,2},{7,3},{8,12},{9,13},{10,... | collective-permute-start | bytes 129032 | tf_op jit(solution)/shard_map/ppermute | solution.py:292

commit v4 on v3

--- a/solution.py
+++ b/solution.py
@@ -135,8 +135,9 @@
 
 
 def load_body(parts, after, *refs):
-    count = len(refs) // 2
-    sems = refs[-1]
+    count = len(refs) // 2 - 1
+    token, sems = refs[-2:]
+    token[...] = jnp.zeros_like(token)
     loads = []
     for place in range(count):
         depth = refs[place].shape[0] // parts
@@ -150,49 +151,64 @@
         load.wait()
 
 
-def take_rows(offset, pieces, stack):
+def take_rows(pieces, stack):
     place = 0
     for ref in pieces:
         stack[place : place + ref.shape[0], :] = ref[...].astype(F32)
         place += ref.shape[0]
+    stacked = stack[...].astype(BF16)
     count = place // 2
     rows = iota((count, place), 0)
-    mover = iota((count, place), 1) == rows + over_cap(rows) * CAP + offset
-    return dot(mover.astype(F32).astype(BF16), stack[...].astype(BF16)).astype(BF16)
-
-
-def forward_body(w_gate, w_up, *refs):
-    pieces, (rows_out, keep, send, stack) = refs[:-4], refs[-4:]
-    half = w_gate.shape[1] // 2
-    rows = take_rows(0, pieces, stack)
-    rows_out[...] = rows
+    source = rows + over_cap(rows) * CAP
+    taken = []
+    for offset in (0, CAP):
+        mover = (iota((count, place), 1) == source + offset).astype(F32).astype(BF16)
+        taken.append(dot(mover, stacked).astype(BF16))
+    return taken
+
+
+def pre_part(rows, weight, place, keep, send):
+    half = weight.shape[1] // 2
+    span = slice(place * half, (place + 1) * half)
     for target, far in ((send, True), (keep, False)):
-        columns = core_columns(half, far)
-        target[:, :half] = dot(rows, w_gate[:, columns]).astype(BF16)
-        target[:, half:] = dot(rows, w_up[:, columns]).astype(BF16)
-
-
-def hidden_body(w_down, *refs):
-    pieces, (keep, send, stack) = refs[:-3], refs[-3:]
-    half = w_down.shape[0] // 2
-    rows = take_rows(CAP, pieces, stack)
+        target[:, span] = dot(rows, weight[:, core_columns(half, far)]).astype(BF16)
+
+
+def hidden_part(rows, weight, keep, send):
+    half = weight.shape[0] // 2
     for target, far in ((send, True), (keep, False)):
-        target[...] = dot(rows, w_down[core_columns(half, far), :], 1, 1).astype(BF16)
-
-
-def transpose_body(after, rows_ref, out):
-    rows = rows_ref[...]
+        part = dot(rows, weight[core_columns(half, far), :], 1, 1)
+        target[:, 2 * half :] = part.astype(BF16)
+
+
+def rows_body(after, w_gate, w_up, w_down, *refs):
+    pieces = refs[:-4][::-1]
+    rows_out, keep, send, stack = refs[-4:]
+    input_rows, grad_rows = take_rows(pieces, stack)
+    rows_out[...] = input_rows
+    pre_part(input_rows, w_gate, 0, keep, send)
+    pre_part(input_rows, w_up, 1, keep, send)
+    hidden_part(grad_rows, w_down, keep, send)
+
+
+def transpose_body(after, near, far, out):
+    rows = jnp.concatenate([near[...], far[...]], axis=0)
     count = rows.shape[0]
     same = (iota((count, count), 0) == iota((count, count), 1)).astype(F32).astype(BF16)
     out[...] = dot(rows, same, 0, 0).astype(BF16)
 
 
-def activate_body(after, pre_own, pre_far, hid_own, hid_far, acts):
-    half = hid_own.shape[1]
-    pre = pre_own[...].astype(F32) + pre_far[...].astype(F32)
-    hidden_grad = hid_own[...].astype(F32) + hid_far[...].astype(F32)
-    gate_pre = pre[:, :half]
-    up_pre = pre[:, half:]
+def core_sum_body(own, other, *refs):
+    refs[-1][...] = (own[...].astype(F32) + other[...].astype(F32)).astype(BF16)
+
+
+def activate_body(own, other, *refs):
+    acts = refs[-1]
+    half = own.shape[1] // 3
+    total = own[...].astype(F32) + other[...].astype(F32)
+    gate_pre = total[:, :half]
+    up_pre = total[:, half : 2 * half]
+    hidden_grad = total[:, 2 * half :]
     sigma = jax.nn.sigmoid(gate_pre)
     acts[:, :half] = (hidden_grad * up_pre * sigma * (1.0 + gate_pre * (1.0 - sigma))).astype(BF16)
     acts[:, half:] = (hidden_grad * gate_pre * sigma).astype(BF16)
@@ -209,35 +225,52 @@
     ]
 
 
-def back_part(w_gate, w_up, acts, sibling):
+def back_part(experts, w_gate, w_up, near, far, sibling):
     half = w_gate.shape[1] // 2
+    acts = jnp.concatenate([near[...], far[...]], axis=0)
+    count = acts.shape[0]
+    rows = iota((count, count), 0)
+    group = CAP * experts
+    peer = jnp.floor((rows.astype(F32) + 0.5) * (1.0 / group)).astype(jnp.int32)
+    inner = rows - peer * group
+    source = jnp.where(
+        inner < CAP,
+        peer * CAP + inner,
+        HSPLIT * CAP + peer * (group - CAP) + inner - CAP,
+    )
+    mover = (iota((count, count), 1) == source).astype(F32).astype(BF16)
+    acts = dot(mover, acts).astype(BF16)
     columns = core_columns(half, sibling)
     part = dot(acts[:, :half], w_gate[:, columns], 1, 1)
     return part + dot(acts[:, half:], w_up[:, columns], 1, 1)
 
 
-def back_own_body(w_gate, w_up, acts, total):
-    total[...] = back_part(w_gate, w_up, acts, False)
-
-
-def back_far_body(w_gate, w_up, acts, own, *outs):
+def back_own_body(experts, w_gate, w_up, near, far, total):
+    total[...] = back_part(experts, w_gate, w_up, near, far, False)
+
+
+def back_far_body(experts, w_gate, w_up, near, far, own, *outs):
     count = outs[0].shape[0]
-    total = own[...] + back_part(w_gate, w_up, acts, True)
+    total = own[...] + back_part(experts, w_gate, w_up, near, far, True)
     for place, out in enumerate(outs):
         out[...] = total[place * count : (place + 1) * count].astype(BF16)
 
 
-def weight_body(which, chunks, after, rows_ref, acts_own, acts_far, out, token, tile, sems):
+def weight_body(
+    which, chunks, after, rows_ref, own_near, own_far, sib_near, sib_far, out, token, tile, sems
+):
     token[...] = jnp.zeros_like(token)
     half = out.shape[1] // 2
     depth = out.shape[0] // chunks
     columns = slice(which * half, (which + 1) * half)
+    own = jnp.concatenate([own_near[:, columns], own_far[:, columns]], axis=0)
+    sib = jnp.concatenate([sib_near[:, columns], sib_far[:, columns]], axis=0)
     stores = []
     for chunk in range(chunks):
         span = slice(chunk * depth, (chunk + 1) * depth)
         rows = rows_ref[span, :]
-        for acts, far in ((acts_own, False), (acts_far, True)):
-            tile[span, core_columns(half, far)] = dot(rows, acts[:, columns]).astype(BF16)
+        for acts, far in ((own, False), (sib, True)):
+            tile[span, core_columns(half, far)] = dot(rows, acts).astype(BF16)
         stores.append(pltpu.make_async_copy(tile.at[span], out.at[span], sems.at[chunk]))
         stores[-1].start()
     for store in stores:
@@ -314,101 +347,112 @@
         ),
     )
     picks, own = picked[:fold], picked[fold:]
-    weights = (w_gate, w_up, w_down)
-    gate_here, up_here, down_here = run(
+    weights = (w_up, w_down)
+    up_here, down_here, loaded = run(
         functools.partial(load_body, 4),
-        tuple(pltpu.VMEM(weight.shape, weight.dtype) for weight in weights),
-        [ANY] + [HBM] * 3,
+        tuple(pltpu.VMEM(weight.shape, weight.dtype) for weight in weights)
+        + (shape((8, 128), F32),),
+        [ANY] + [HBM] * 2,
         0,
-        6 * features * hidden,
+        4 * features * hidden,
         picks[0],
         *(in_hbm(weight) for weight in weights),
-        scratch=(dma((12,)),),
+        scratch=(dma((8,)),),
     )
 
     away = [to_expert(own[step], step) for step in range(1, experts)]
     near = [own[0]] + [to_peer(own[0], flip) for flip in range(1, HSPLIT)]
     away = away[0] if len(away) == 1 else jnp.concatenate(away, axis=0)
+    away, loaded = lax.optimization_barrier((away, loaded))
     far = [away] + [to_peer(away, flip) for flip in range(1, HSPLIT)]
-    pieces = [array for pair in zip(near, far) for array in pair]
-
-    stack = pltpu.VMEM((2 * count, features), F32)
-    rows_input, pre_keep, pre_send = run(
-        forward_body,
-        (shape((count, features)), shape((count, hidden)), shape((count, hidden))),
-        [VMEM] * (2 + len(pieces)),
-        2 * product,
-        4 * features * hidden,
-        gate_here,
-        up_here,
-        *pieces,
-        scratch=(stack,),
-    )
-
-    def spread_sum(keep, send):
-        near = (keep.astype(F32) + to_dp(send, 1).astype(F32)).astype(BF16)
+
+    def multiply(after, pieces, flops):
+        rows = sum(piece.shape[0] for piece in pieces) // 2
+        return run(
+            rows_body,
+            (shape((rows, features)), shape((rows, 3 * half)), shape((rows, 3 * half))),
+            [ANY] + [VMEM] * (3 + len(pieces)),
+            flops,
+            0,
+            after,
+            w_gate,
+            up_here,
+            down_here,
+            *pieces[::-1],
+            scratch=(pltpu.VMEM((2 * rows, features), F32),),
+        )
+
+    def core_sum(keep, send, after):
+        return run(
+            core_sum_body,
+            shape(keep.shape),
+            [VMEM] * 2 + [ANY],
+            0,
+            0,
+            keep,
+            to_dp(send, 1),
+            after,
+        )
+
+    def activate(total, after):
         flip = 2
-        far = jnp.zeros_like(near)
+        other = jnp.zeros_like(total)
         while flip < spread:
-            far = to_dp(near, flip)
+            other = to_dp(total, flip)
             flip *= 2
             if flip < spread:
-                near = (near.astype(F32) + far.astype(F32)).astype(BF16)
-        return near, far
-
-    pre_own, pre_far = spread_sum(pre_keep, pre_send)
-    hid_keep, hid_send = run(
-        hidden_body,
-        (shape((count, half)), shape((count, half))),
-        [VMEM] * (1 + len(pieces)),
-        product,
-        2 * features * hidden,
-        down_here,
-        *pieces,
-        scratch=(stack,),
-    )
-    hid_own, hid_far = spread_sum(hid_keep, hid_send)
+                total = (total.astype(F32) + other.astype(F32)).astype(BF16)
+        rows = total.shape[0]
+        return run(
+            activate_body,
+            shape((rows, hidden)),
+            [VMEM] * 2 + [ANY],
+            20 * rows * half,
+            10 * rows * half,
+            total,
+            other,
+            after,
+        )
+
+    rows_near, near_keep, near_send = multiply(away, near, 3 * product)
+    near_sum = core_sum(near_keep, near_send, away)
+    rows_far, far_keep, far_send = multiply(near_sum, far, 0)
+    acts_near = activate(near_sum, away)
+    far_sum = core_sum(far_keep, far_send, acts_near)
     rows_across = run(
         transpose_body,
         shape((features, count)),
-        [ANY, VMEM],
+        [ANY] + [VMEM] * 2,
         0,
         0,
-        hid_own,
-        rows_input,
-    )
-    acts = run(
-        activate_body,
-        shape((count, hidden)),
-        [ANY] + [VMEM] * 4,
-        20 * count * half,
-        10 * count * half,
-        rows_across,
-        pre_own,
-        pre_far,
-        hid_own,
-        hid_far,
-    )
-    acts_far = to_dp(acts, 1)
+        far_sum,
+        rows_near,
+        rows_far,
+    )
+    acts_far = activate(far_sum, rows_across)
+    sib_near = to_dp(acts_near, 1)
+    sib_far = to_dp(acts_far, 1)
     back_own = run(
-        back_own_body,
+        functools.partial(back_own_body, experts),
         shape((count, features), F32),
-        [VMEM] * 3,
-        product,
-        2 * features * hidden,
-        gate_here,
-        up_here,
-        acts,
-    )
-    back = run(
-        back_far_body,
-        (shape((count // HSPLIT, features)),) * HSPLIT,
         [VMEM] * 4,
         product,
         2 * features * hidden,
-        gate_here,
+        w_gate,
         up_here,
+        acts_near,
         acts_far,
+    )
+    back = run(
+        functools.partial(back_far_body, experts),
+        (shape((count // HSPLIT, features)),) * HSPLIT,
+        [VMEM] * 5,
+        product,
+        2 * features * hidden,
+        w_gate,
+        up_here,
+        sib_near,
+        sib_far,
         back_own,
     )
 
@@ -417,13 +461,15 @@
         return run(
             functools.partial(weight_body, which, chunks),
             (shape((features, hidden)), shape((8, 128), F32)),
-            [ANY] + [VMEM] * 3,
+            [ANY] + [VMEM] * 5,
             0,
             0,
             after,
             rows_across,
-            acts,
+            acts_near,
             acts_far,
+            sib_near,
+            sib_far,
             out_spec=(HBM, VMEM),
             scratch=(pltpu.VMEM((features, hidden), BF16), dma((chunks,))),
         )

time: 42.6 us -> 44.3 us (1.040)
  waiting for transfers between devices: 8.53 us -> 10.7 us
  starting transfers between devices: 20.3 us -> 18.4 us
  Pallas kernels: 12.7 us -> 14.2 us
    ppermute x2, starting transfers between devices: 6.34 us -> 4.47 us  [to_expert(): return lax.ppermute(value, 'expert', pairs)]
    ppermute x5 -> x6, waiting for transfers between devices: 3.8 us -> 5.59 us  [to_dp(): return lax.ppermute(value, 'dp', [(d, d ^ flip) for d in range(spread)])]
    pallas_call x12 -> x15, Pallas kernels: 12.7 us -> 14.2 us  [run(): pl.pallas_call(body, out_shape=outs, in_specs=specs, out_specs=out_spec i...]
    ppermute x2, waiting for transfers between devices: 1.2 us -> 2.53 us  [to_expert(): return lax.ppermute(value, 'expert', pairs)]
    ppermute x9, waiting for transfers between devices: 3.53 us -> 2.53 us  [to_peer(): lax.ppermute(value, 'expert', [(d, d ^ flip) for d in range(devices)])]
    ppermute x5 -> x6, starting transfers between devices: 3.09 us -> 3.32 us  [to_dp(): return lax.ppermute(value, 'dp', [(d, d ^ flip) for d in range(spread)])]
  transfers between devices with their start and end apart: 16 -> 17, of which waited for: 9 -> 8; matrix products, arithmetic and copies ran while one was open for 0% -> 0% of each run, Pallas kernels for 19% -> 24%
where the time goes in v4:
time: 44.3 us; the launch traced here: 44 us
  starting transfers between devices  18.4 us (42%)
  Pallas kernels  14.2 us (32%)
  waiting for transfers between devices  10.7 us (24%)
  between operations  0.78 us (2%)
    pallas_call x15, Pallas kernels, run(): pl.pallas_call(body, out_shape=outs, in_specs=specs, out_specs=out_spec i...  14.2 us
    ppermute x9, starting transfers between devices, to_peer(): lax.ppermute(value, 'expert', [(d, d ^ flip) for d in range(devices)])  10.6 us
    ppermute x6, waiting for transfers between devices, to_dp(): return lax.ppermute(value, 'dp', [(d, d ^ flip) for d in range(spread)])  5.59 us
    ppermute x2, starting transfers between devices, to_expert(): return lax.ppermute(value, 'expert', pairs)  4.47 us
    ppermute x6, starting transfers between devices, to_dp(): return lax.ppermute(value, 'dp', [(d, d ^ flip) for d in range(spread)])  3.32 us
    ppermute x2, waiting for transfers between devices, to_expert(): return lax.ppermute(value, 'expert', pairs)  2.53 us
    ppermute x9, waiting for transfers between devices, to_peer(): lax.ppermute(value, 'expert', [(d, d ^ flip) for d in range(devices)])  2.53 us
  transfers between devices with their start and end apart: 17, of which 8 were waited for; matrix products, arithmetic and copies ran while one was open for 0% of the time, Pallas kernels for 24%

profile of v4, /device:TPU:0, one launch (start us, length us, event | category | flops | bytes accessed | tf_op | source)
XLA Modules:
  0.0 44.0 jit_solution(15606489357809959095)
XLA Ops:
  0.6 1.8 %shard_map.94 = (bf16[48,256]{1,0:T(8,128)(2,1)S(1)}, bf16[48,256]{1,0:T(8,128)(2,1)S(1)}, bf16[24,1792]{1,0:T(8,128)(2,1)S(1)}, bf16[24,1792]{1,0:T(8,128)(2,1)S(1)}) custom-call(s32[8,256]{1,0:T(8,128)} %bitcast.2, f32[8,256]{1,0:T(8,128)} %bitcast.3, bf16[256,1792]{1,0:T(8,128)(2,1)} %grads_hbm.1, bf16[256,1792]{1,0:T(8,128)(2,1)} %inputs_hbm.1), custom_call_target="tpu_custom_call" | custom-call | flops 88080384 | bytes 1835008 | tf_op jit(solution)/shard_map/pallas_call | solution.py:24
  2.4 4.1 %collective-permute-start = (bf16[24,1792]{1,0:T(8,128)(2,1)S(1)}, bf16[24,1792]{1,0:T(8,128)(2,1)S(1)}, u32[]{:S(2)}, u32[]{:S(2)}) collective-permute-start(bf16[24,1792]{1,0:T(8,128)(2,1)S(1)} %get-tuple-element.27), channel_id=1, source_target_pairs={{0,4},{1,5},{2,6},{3,7},{4,0},{5,1},{6,2},{7,3},{8,12},{9,13},{10,... | collective-permute-start | bytes 258056 | tf_op jit(solution)/shard_map/ppermute | solution.py:325
  6.5 2.5 %collective-permute-start.1 = (bf16[24,1792]{1,0:T(8,128)(2,1)S(1)}, bf16[24,1792]{1,0:T(8,128)(2,1)S(1)}, u32[]{:S(2)}, u32[]{:S(2)}) collective-permute-start(bf16[24,1792]{1,0:T(8,128)(2,1)S(1)} %get-tuple-element.29.refs_3_), channel_id=1, source_target_pairs={{0,3},{1,2},{2,1},{3,0},{4,7},{5,6},{6,5},{7,4},{8,11},{9,10},{10,... | collective-permute-start | bytes 258056 | tf_op jit(solution)/shard_map/ppermute | solution.py:328
  9.1 0.4 %collective-permute-start.2 = (bf16[24,1792]{1,0:T(8,128)(2,1)S(1)}, bf16[24,1792]{1,0:T(8,128)(2,1)S(1)}, u32[]{:S(2)}, u32[]{:S(2)}) collective-permute-start(bf16[24,1792]{1,0:T(8,128)(2,1)S(1)} %get-tuple-element.29.refs_3_), channel_id=1, source_target_pairs={{0,2},{1,3},{2,0},{3,1},{4,6},{5,7},{6,4},{7,5},{8,10},{9,11},{10,... | collective-permute-start | bytes 258056 | tf_op jit(solution)/shard_map/ppermute | solution.py:328
  9.5 0.5 %collective-permute-start.3 = (bf16[24,1792]{1,0:T(8,128)(2,1)S(1)}, bf16[24,1792]{1,0:T(8,128)(2,1)S(1)}, u32[]{:S(2)}, u32[]{:S(2)}) collective-permute-start(bf16[24,1792]{1,0:T(8,128)(2,1)S(1)} %get-tuple-element.29.refs_3_), channel_id=1, source_target_pairs={{0,1},{1,0},{2,3},{3,2},{4,5},{5,4},{6,7},{7,6},{8,9},{9,8},{10,11... | collective-permute-start | bytes 258056 | tf_op jit(solution)/shard_map/ppermute | solution.py:328
  10.0 2.8 %shard_map.95 = (bf16[1792,512]{1,0:T(8,128)(2,1)S(1)}, bf16[512,1792]{1,0:T(8,128)(2,1)S(1)}, f32[8,128]{1,0:T(8,128)}) custom-call(bf16[48,256]{1,0:T(8,128)(2,1)S(1)} %get-tuple-element.24.after.refs_0_, bf16[1792,512]{1,0:T(8,128)(2,1)} %refs_0_.1, bf16[512,1792]{1,0:T(8,128)(2,1)} %refs_1_.1), custom_call_target="tpu_custom_call" | custom-call | bytes 3670016 | tf_op jit(solution)/shard_map/pallas_call | solution.py:24
  12.8 2.6 %collective-permute-start.7 = (bf16[24,1792]{1,0:T(8,128)(2,1)S(1)}, bf16[24,1792]{1,0:T(8,128)(2,1)S(1)}, u32[]{:S(2)}, u32[]{:S(2)}) collective-permute-start(bf16[24,1792]{1,0:T(8,128)(2,1)S(1)} %collective-permute-done.after.refs_0_.refs_3_), channel_id=1, source_target_pairs={{0,3},{1,2},{2,1},{3,0},{4,7},{5,6},{6,5},{7,4},{8,11},{9,10},{10,... | collective-permute-start | bytes 258056 | tf_op jit(solution)/shard_map/ppermute | solution.py:328
  15.4 0.4 %collective-permute-start.8 = (bf16[24,1792]{1,0:T(8,128)(2,1)S(1)}, bf16[24,1792]{1,0:T(8,128)(2,1)S(1)}, u32[]{:S(2)}, u32[]{:S(2)}) collective-permute-start(bf16[24,1792]{1,0:T(8,128)(2,1)S(1)} %collective-permute-done.after.refs_0_.refs_3_), channel_id=1, source_target_pairs={{0,2},{1,3},{2,0},{3,1},{4,6},{5,7},{6,4},{7,5},{8,10},{9,11},{10,... | collective-permute-start | bytes 258056 | tf_op jit(solution)/shard_map/ppermute | solution.py:328
  15.9 0.5 %collective-permute-start.9 = (bf16[24,1792]{1,0:T(8,128)(2,1)S(1)}, bf16[24,1792]{1,0:T(8,128)(2,1)S(1)}, u32[]{:S(2)}, u32[]{:S(2)}) collective-permute-start(bf16[24,1792]{1,0:T(8,128)(2,1)S(1)} %collective-permute-done.after.refs_0_.refs_3_), channel_id=1, source_target_pairs={{0,1},{1,0},{2,3},{3,2},{4,5},{5,4},{6,7},{7,6},{8,9},{9,8},{10,11... | collective-permute-start | bytes 258056 | tf_op jit(solution)/shard_map/ppermute | solution.py:328
  16.4 1.4 %shard_map.96 = (bf16[48,1792]{1,0:T(8,128)(2,1)S(1)}, bf16[48,768]{1,0:T(8,128)(2,1)S(1)}, bf16[48,768]{1,0:T(8,128)(2,1)S(1)}) custom-call(bf16[24,1792]{1,0:T(8,128)(2,1)S(1)} %collective-permute-done.after.refs_0_.refs_3_, bf16[1792,512]{1,0:T(8,128)(2,1)S(1)} %copy-done, bf16[1792,512]{1,0:T(8,128)(2,1)S(1)} %get-tuple-element.26.w_up, ...), custom_call_target="tpu_custom_call" | custom-call | flops 528482304 | tf_op jit(solution)/shard_map/pallas_call | solution.py:24
  17.9 1.3 %collective-permute-done.4.other = bf16[48,768]{1,0:T(8,128)(2,1)S(1)} collective-permute-done((bf16[48,768]{1,0:T(8,128)(2,1)S(1)}, bf16[48,768]{1,0:T(8,128)(2,1)S(1)}, u32[]{:S(2)}, u32[]{:S(2)}) %collective-permute-start.4) | collective-permute-done | bytes 73760 | tf_op jit(solution)/shard_map/ppermute | solution.py:331
  19.2 1.6 %collective-permute-start.5 = (bf16[48,768]{1,0:T(8,128)(2,1)S(1)}, bf16[48,768]{1,0:T(8,128)(2,1)S(1)}, u32[]{:S(2)}, u32[]{:S(2)}) collective-permute-start(bf16[48,768]{1,0:T(8,128)(2,1)S(1)} %shard_map.97.own.after), channel_id=1, source_target_pairs={{0,16},{8,24},{16,0},{24,8},{1,17},{9,25},{17,1},{25,9},{2,18},{10... | collective-permute-start | bytes 221192 | tf_op jit(solution)/shard_map/ppermute | solution.py:331
  20.8 1.4 %shard_map.99 = (bf16[48,1792]{1,0:T(8,128)(2,1)S(1)}, bf16[48,768]{1,0:T(8,128)(2,1)S(1)}, bf16[48,768]{1,0:T(8,128)(2,1)S(1)}) custom-call(bf16[48,768]{1,0:T(8,128)(2,1)S(1)} %shard_map.97.own.after, bf16[1792,512]{1,0:T(8,128)(2,1)S(1)} %copy-done, bf16[1792,512]{1,0:T(8,128)(2,1)S(1)} %get-tuple-element.26.w_up, ...), custom_call_target="tpu_custom_call" | custom-call | tf_op jit(solution)/shard_map/pallas_call | solution.py:24
  22.3 1.3 %collective-permute-done.5.other = bf16[48,768]{1,0:T(8,128)(2,1)S(1)} collective-permute-done((bf16[48,768]{1,0:T(8,128)(2,1)S(1)}, bf16[48,768]{1,0:T(8,128)(2,1)S(1)}, u32[]{:S(2)}, u32[]{:S(2)}) %collective-permute-start.5) | collective-permute-done | bytes 73760 | tf_op jit(solution)/shard_map/ppermute | solution.py:331
  23.7 1.6 %collective-permute-start.11 = (bf16[48,768]{1,0:T(8,128)(2,1)S(1)}, bf16[48,768]{1,0:T(8,128)(2,1)S(1)}, u32[]{:S(2)}, u32[]{:S(2)}) collective-permute-start(bf16[48,768]{1,0:T(8,128)(2,1)S(1)} %shard_map.100.after.own), channel_id=1, source_target_pairs={{0,16},{8,24},{16,0},{24,8},{1,17},{9,25},{17,1},{25,9},{2,18},{10... | collective-permute-start | bytes 221192 | tf_op jit(solution)/shard_map/ppermute | solution.py:331
  25.2 0.3 shard_map.101.refs_0_.rows_ref
  25.6 2.5 %collective-permute-done.11.other = bf16[48,768]{1,0:T(8,128)(2,1)S(1)} collective-permute-done((bf16[48,768]{1,0:T(8,128)(2,1)S(1)}, bf16[48,768]{1,0:T(8,128)(2,1)S(1)}, u32[]{:S(2)}, u32[]{:S(2)}) %collective-permute-start.11) | collective-permute-done | bytes 73760 | tf_op jit(solution)/shard_map/ppermute | solution.py:331
  28.1 0.1 collective-permute-start.12
  28.2 0.8 %shard_map.103.own = f32[96,1792]{1,0:T(8,128)S(1)} custom-call(bf16[1792,512]{1,0:T(8,128)(2,1)S(1)} %copy-done, bf16[1792,512]{1,0:T(8,128)(2,1)S(1)} %get-tuple-element.26.w_up, bf16[48,512]{1,0:T(8,128)(2,1)S(1)} %shard_map.98.refs_0_.near.own_near, bf16[48,512]{1,0:T(8,128)(2,1)S(1)} %shard_map.102.far.own_far), custom_call_target="tpu_custom_call" | custom-call | flops 176160768 | bytes 1835008 | tf_op jit(solution)/shard_map/pallas_call | solution.py:24
  29.0 0.4 %collective-permute-done.12.far.sib_far = bf16[48,512]{1,0:T(8,128)(2,1)S(1)} collective-permute-done((bf16[48,512]{1,0:T(8,128)(2,1)S(1)}, bf16[48,512]{1,0:T(8,128)(2,1)S(1)}, u32[]{:S(2)}, u32[]{:S(2)}) %collective-permute-start.12) | collective-permute-done | bytes 49184 | tf_op jit(solution)/shard_map/ppermute | solution.py:331
  29.4 0.8 %shard_map.104 = (bf16[24,1792]{1,0:T(8,128)(2,1)S(1)}, bf16[24,1792]{1,0:T(8,128)(2,1)S(1)}, bf16[24,1792]{1,0:T(8,128)(2,1)S(1)}, bf16[24,1792]{1,0:T(8,128)(2,1)S(1)}) custom-call(bf16[1792,512]{1,0:T(8,128)(2,1)S(1)} %copy-done, bf16[1792,512]{1,0:T(8,128)(2,1)S(1)} %get-tuple-element.26.w_up, bf16[48,512]{1,0:T(8,128)(2,1)S(1)} %collective-permute-done.6.near.sib_near, ...), custom_call_target="tpu_custom_call" | custom-call | flops 176160768 | bytes 1835008 | tf_op jit(solution)/shard_map/pallas_call | solution.py:24
  30.2 2.6 %collective-permute-start.13 = (bf16[24,1792]{1,0:T(8,128)(2,1)S(1)}, bf16[24,1792]{1,0:T(8,128)(2,1)S(1)}, u32[]{:S(2)}, u32[]{:S(2)}) collective-permute-start(bf16[24,1792]{1,0:T(8,128)(2,1)S(1)} %get-tuple-element.38), channel_id=1, source_target_pairs={{0,3},{1,2},{2,1},{3,0},{4,7},{5,6},{6,5},{7,4},{8,11},{9,10},{10,... | collective-permute-start | bytes 258056 | tf_op jit(solution)/shard_map/ppermute | solution.py:328
  32.8 0.5 %collective-permute-start.14 = (bf16[24,1792]{1,0:T(8,128)(2,1)S(1)}, bf16[24,1792]{1,0:T(8,128)(2,1)S(1)}, u32[]{:S(2)}, u32[]{:S(2)}) collective-permute-start(bf16[24,1792]{1,0:T(8,128)(2,1)S(1)} %get-tuple-element.39), channel_id=1, source_target_pairs={{0,2},{1,3},{2,0},{3,1},{4,6},{5,7},{6,4},{7,5},{8,10},{9,11},{10,... | collective-permute-start | bytes 258056 | tf_op jit(solution)/shard_map/ppermute | solution.py:328
  33.3 0.5 %collective-permute-start.15 = (bf16[24,1792]{1,0:T(8,128)(2,1)S(1)}, bf16[24,1792]{1,0:T(8,128)(2,1)S(1)}, u32[]{:S(2)}, u32[]{:S(2)}) collective-permute-start(bf16[24,1792]{1,0:T(8,128)(2,1)S(1)} %get-tuple-element.40), channel_id=1, source_target_pairs={{0,1},{1,0},{2,3},{3,2},{4,5},{5,4},{6,7},{7,6},{8,9},{9,8},{10,11... | collective-permute-start | bytes 258056 | tf_op jit(solution)/shard_map/ppermute | solution.py:328
  33.8 1.5 %shard_map.105 = (bf16[1792,512]{1,0:T(8,128)(2,1)}, f32[8,128]{1,0:T(8,128)S(1)}) custom-call(bf16[24,1792]{1,0:T(8,128)(2,1)S(1)} %get-tuple-element.36.after.refs_3_, bf16[1792,96]{1,0:T(8,128)(2,1)S(1)} %shard_map.101.refs_0_.rows_ref, bf16[48,512]{1,0:T(8,128)(2,1)S(1)} %shard_map.98.refs_0_.near.own_near, bf16[48,512]{1,0:T(8,128)(2,1)S(1)} %shard_map.102.far.own_far, ...), custom_call_target="tpu_custom_call" | custom-call | tf_op jit(solution)/shard_map/pallas_call | solution.py:24
  35.3 1.1 %collective-permute-done.13.refs_0_ = bf16[24,1792]{1,0:T(8,128)(2,1)S(1)} collective-permute-done((bf16[24,1792]{1,0:T(8,128)(2,1)S(1)}, bf16[24,1792]{1,0:T(8,128)(2,1)S(1)}, u32[]{:S(2)}, u32[]{:S(2)}) %collective-permute-start.13) | collective-permute-done | bytes 86048 | tf_op jit(solution)/shard_map/ppermute | solution.py:328
  36.4 1.3 %collective-permute-done.14.refs_1_ = bf16[24,1792]{1,0:T(8,128)(2,1)S(1)} collective-permute-done((bf16[24,1792]{1,0:T(8,128)(2,1)S(1)}, bf16[24,1792]{1,0:T(8,128)(2,1)S(1)}, u32[]{:S(2)}, u32[]{:S(2)}) %collective-permute-start.14) | collective-permute-done | bytes 86048 | tf_op jit(solution)/shard_map/ppermute | solution.py:328
  37.7 0.1 collective-permute-done.15.refs_2_
  37.8 0.4 collective-permute-start.16
  38.2 2.1 %shard_map.108 = (bf16[1792,512]{1,0:T(8,128)(2,1)}, f32[8,128]{1,0:T(8,128)}) custom-call(bf16[24,896]{1,0:T(8,128)(2,1)S(1)} %get-tuple-element.41.refs_2_.after, bf16[1792,96]{1,0:T(8,128)(2,1)S(1)} %shard_map.101.refs_0_.rows_ref, bf16[48,512]{1,0:T(8,128)(2,1)S(1)} %shard_map.98.refs_0_.near.own_near, bf16[48,512]{1,0:T(8,128)(2,1)S(1)} %shard_map.102.far.own_far, ...), custom_call_target="tpu_custom_call" | custom-call | tf_op jit(solution)/shard_map/pallas_call | solution.py:24
  40.3 2.5 %collective-permute-done.16.refs_3_ = bf16[24,896]{1,0:T(8,128)(2,1)S(1)} collective-permute-done((bf16[24,896]{1,0:T(8,128)(2,1)S(1)}, bf16[24,896]{1,0:T(8,128)(2,1)S(1)}, u32[]{:S(2)}, u32[]{:S(2)}) %collective-permute-start.16) | collective-permute-done | bytes 43040 | tf_op jit(solution)/shard_map/ppermute | solution.py:325
  42.8 1.2 %shard_map.107 = bf16[256,1792]{1,0:T(8,128)(2,1)} custom-call(bf16[48,256]{1,0:T(8,128)(2,1)S(1)} %get-tuple-element.24.after.refs_0_, bf16[48,256]{1,0:T(8,128)(2,1)S(1)} %get-tuple-element.25.refs_1_, bf16[24,896]{1,0:T(8,128)(2,1)S(1)} %get-tuple-element.41.refs_2_.after, bf16[24,896]{1,0:T(8,128)(2,1)S(1)} %collective-permute-done.16.refs_3_), custom_call_target="tpu_custom_call" | custom-call | flops 44040192 | bytes 917504 | tf_op jit(solution)/shard_map/pallas_call | solution.py:24
  (19 shorter events, 0.3 us)
Async XLA Ops:
  2.4 10.4 %collective-permute-start = (bf16[24,1792]{1,0:T(8,128)(2,1)S(1)}, bf16[24,1792]{1,0:T(8,128)(2,1)S(1)}, u32[]{:S(2)}, u32[]{:S(2)}) collective-permute-start(bf16[24,1792]{1,0:T(8,128)(2,1)S(1)} %get-tuple-element.27), channel_id=1, source_target_pairs={{0,4},{1,5},{2,6},{3,7},{4,0},{5,1},{6,2},{7,3},{8,12},{9,13},{10,... | collective-permute-start | bytes 258056 | tf_op jit(solution)/shard_map/ppermute | solution.py:325
  6.5 9.3 %collective-permute-start.1 = (bf16[24,1792]{1,0:T(8,128)(2,1)S(1)}, bf16[24,1792]{1,0:T(8,128)(2,1)S(1)}, u32[]{:S(2)}, u32[]{:S(2)}) collective-permute-start(bf16[24,1792]{1,0:T(8,128)(2,1)S(1)} %get-tuple-element.29.refs_3_), channel_id=1, source_target_pairs={{0,3},{1,2},{2,1},{3,0},{4,7},{5,6},{6,5},{7,4},{8,11},{9,10},{10,... | collective-permute-start | bytes 258056 | tf_op jit(solution)/shard_map/ppermute | solution.py:328
  9.1 7.3 %collective-permute-start.2 = (bf16[24,1792]{1,0:T(8,128)(2,1)S(1)}, bf16[24,1792]{1,0:T(8,128)(2,1)S(1)}, u32[]{:S(2)}, u32[]{:S(2)}) collective-permute-start(bf16[24,1792]{1,0:T(8,128)(2,1)S(1)} %get-tuple-element.29.refs_3_), channel_id=1, source_target_pairs={{0,2},{1,3},{2,0},{3,1},{4,6},{5,7},{6,4},{7,5},{8,10},{9,11},{10,... | collective-permute-start | bytes 258056 | tf_op jit(solution)/shard_map/ppermute | solution.py:328
  9.5 6.9 %collective-permute-start.3 = (bf16[24,1792]{1,0:T(8,128)(2,1)S(1)}, bf16[24,1792]{1,0:T(8,128)(2,1)S(1)}, u32[]{:S(2)}, u32[]{:S(2)}) collective-permute-start(bf16[24,1792]{1,0:T(8,128)(2,1)S(1)} %get-tuple-element.29.refs_3_), channel_id=1, source_target_pairs={{0,1},{1,0},{2,3},{3,2},{4,5},{5,4},{6,7},{7,6},{8,9},{9,8},{10,11... | collective-permute-start | bytes 258056 | tf_op jit(solution)/shard_map/ppermute | solution.py:328
  10.0 6.4 %copy-start = (bf16[1792,512]{1,0:T(8,128)(2,1)S(1)}, bf16[1792,512]{1,0:T(8,128)(2,1)}, u32[]{:S(2)}) copy-start(bf16[1792,512]{1,0:T(8,128)(2,1)} %w_gate.7) | copy-start | bytes 5505028
  12.8 7.9 %collective-permute-start.7 = (bf16[24,1792]{1,0:T(8,128)(2,1)S(1)}, bf16[24,1792]{1,0:T(8,128)(2,1)S(1)}, u32[]{:S(2)}, u32[]{:S(2)}) collective-permute-start(bf16[24,1792]{1,0:T(8,128)(2,1)S(1)} %collective-permute-done.after.refs_0_.refs_3_), channel_id=1, source_target_pairs={{0,3},{1,2},{2,1},{3,0},{4,7},{5,6},{6,5},{7,4},{8,11},{9,10},{10,... | collective-permute-start | bytes 258056 | tf_op jit(solution)/shard_map/ppermute | solution.py:328
  15.4 5.3 %collective-permute-start.8 = (bf16[24,1792]{1,0:T(8,128)(2,1)S(1)}, bf16[24,1792]{1,0:T(8,128)(2,1)S(1)}, u32[]{:S(2)}, u32[]{:S(2)}) collective-permute-start(bf16[24,1792]{1,0:T(8,128)(2,1)S(1)} %collective-permute-done.after.refs_0_.refs_3_), channel_id=1, source_target_pairs={{0,2},{1,3},{2,0},{3,1},{4,6},{5,7},{6,4},{7,5},{8,10},{9,11},{10,... | collective-permute-start | bytes 258056 | tf_op jit(solution)/shard_map/ppermute | solution.py:328
  15.9 4.9 %collective-permute-start.9 = (bf16[24,1792]{1,0:T(8,128)(2,1)S(1)}, bf16[24,1792]{1,0:T(8,128)(2,1)S(1)}, u32[]{:S(2)}, u32[]{:S(2)}) collective-permute-start(bf16[24,1792]{1,0:T(8,128)(2,1)S(1)} %collective-permute-done.after.refs_0_.refs_3_), channel_id=1, source_target_pairs={{0,1},{1,0},{2,3},{3,2},{4,5},{5,4},{6,7},{7,6},{8,9},{9,8},{10,11... | collective-permute-start | bytes 258056 | tf_op jit(solution)/shard_map/ppermute | solution.py:328
  17.8 1.3 %collective-permute-start.4 = (bf16[48,768]{1,0:T(8,128)(2,1)S(1)}, bf16[48,768]{1,0:T(8,128)(2,1)S(1)}, u32[]{:S(2)}, u32[]{:S(2)}) collective-permute-start(bf16[48,768]{1,0:T(8,128)(2,1)S(1)} %get-tuple-element.31), channel_id=1, source_target_pairs={{0,8},{8,0},{16,24},{24,16},{1,9},{9,1},{17,25},{25,17},{2,10},{10... | collective-permute-start | bytes 221192 | tf_op jit(solution)/shard_map/ppermute | solution.py:331
  19.2 4.4 %collective-permute-start.5 = (bf16[48,768]{1,0:T(8,128)(2,1)S(1)}, bf16[48,768]{1,0:T(8,128)(2,1)S(1)}, u32[]{:S(2)}, u32[]{:S(2)}) collective-permute-start(bf16[48,768]{1,0:T(8,128)(2,1)S(1)} %shard_map.97.own.after), channel_id=1, source_target_pairs={{0,16},{8,24},{16,0},{24,8},{1,17},{9,25},{17,1},{25,9},{2,18},{10... | collective-permute-start | bytes 221192 | tf_op jit(solution)/shard_map/ppermute | solution.py:331
  22.2 1.5 %collective-permute-start.10 = (bf16[48,768]{1,0:T(8,128)(2,1)S(1)}, bf16[48,768]{1,0:T(8,128)(2,1)S(1)}, u32[]{:S(2)}, u32[]{:S(2)}) collective-permute-start(bf16[48,768]{1,0:T(8,128)(2,1)S(1)} %get-tuple-element.33), channel_id=1, source_target_pairs={{0,8},{8,0},{16,24},{24,16},{1,9},{9,1},{17,25},{25,17},{2,10},{10... | collective-permute-start | bytes 221192 | tf_op jit(solution)/shard_map/ppermute | solution.py:331
  23.7 4.4 %collective-permute-start.11 = (bf16[48,768]{1,0:T(8,128)(2,1)S(1)}, bf16[48,768]{1,0:T(8,128)(2,1)S(1)}, u32[]{:S(2)}, u32[]{:S(2)}) collective-permute-start(bf16[48,768]{1,0:T(8,128)(2,1)S(1)} %shard_map.100.after.own), channel_id=1, source_target_pairs={{0,16},{8,24},{16,0},{24,8},{1,17},{9,25},{17,1},{25,9},{2,18},{10... | collective-permute-start | bytes 221192 | tf_op jit(solution)/shard_map/ppermute | solution.py:331
  25.2 3.7 %collective-permute-start.6 = (bf16[48,512]{1,0:T(8,128)(2,1)S(1)}, bf16[48,512]{1,0:T(8,128)(2,1)S(1)}, u32[]{:S(2)}, u32[]{:S(2)}) collective-permute-start(bf16[48,512]{1,0:T(8,128)(2,1)S(1)} %shard_map.98.refs_0_.near.own_near), channel_id=1, source_target_pairs={{0,8},{8,0},{16,24},{24,16},{1,9},{9,1},{17,25},{25,17},{2,10},{10... | collective-permute-start | bytes 147464 | tf_op jit(solution)/shard_map/ppermute | solution.py:331
  28.1 1.3 %collective-permute-start.12 = (bf16[48,512]{1,0:T(8,128)(2,1)S(1)}, bf16[48,512]{1,0:T(8,128)(2,1)S(1)}, u32[]{:S(2)}, u32[]{:S(2)}) collective-permute-start(bf16[48,512]{1,0:T(8,128)(2,1)S(1)} %shard_map.102.far.own_far), channel_id=1, source_target_pairs={{0,8},{8,0},{16,24},{24,16},{1,9},{9,1},{17,25},{25,17},{2,10},{10... | collective-permute-start | bytes 147464 | tf_op jit(solution)/shard_map/ppermute | solution.py:331
  30.2 6.2 %collective-permute-start.13 = (bf16[24,1792]{1,0:T(8,128)(2,1)S(1)}, bf16[24,1792]{1,0:T(8,128)(2,1)S(1)}, u32[]{:S(2)}, u32[]{:S(2)}) collective-permute-start(bf16[24,1792]{1,0:T(8,128)(2,1)S(1)} %get-tuple-element.38), channel_id=1, source_target_pairs={{0,3},{1,2},{2,1},{3,0},{4,7},{5,6},{6,5},{7,4},{8,11},{9,10},{10,... | collective-permute-start | bytes 258056 | tf_op jit(solution)/shard_map/ppermute | solution.py:328
  32.8 4.9 %collective-permute-start.14 = (bf16[24,1792]{1,0:T(8,128)(2,1)S(1)}, bf16[24,1792]{1,0:T(8,128)(2,1)S(1)}, u32[]{:S(2)}, u32[]{:S(2)}) collective-permute-start(bf16[24,1792]{1,0:T(8,128)(2,1)S(1)} %get-tuple-element.39), channel_id=1, source_target_pairs={{0,2},{1,3},{2,0},{3,1},{4,6},{5,7},{6,4},{7,5},{8,10},{9,11},{10,... | collective-permute-start | bytes 258056 | tf_op jit(solution)/shard_map/ppermute | solution.py:328
  33.3 4.5 %collective-permute-start.15 = (bf16[24,1792]{1,0:T(8,128)(2,1)S(1)}, bf16[24,1792]{1,0:T(8,128)(2,1)S(1)}, u32[]{:S(2)}, u32[]{:S(2)}) collective-permute-start(bf16[24,1792]{1,0:T(8,128)(2,1)S(1)} %get-tuple-element.40), channel_id=1, source_target_pairs={{0,1},{1,0},{2,3},{3,2},{4,5},{5,4},{6,7},{7,6},{8,9},{9,8},{10,11... | collective-permute-start | bytes 258056 | tf_op jit(solution)/shard_map/ppermute | solution.py:328
  37.8 5.0 %collective-permute-start.16 = (bf16[24,896]{1,0:T(8,128)(2,1)S(1)}, bf16[24,896]{1,0:T(8,128)(2,1)S(1)}, u32[]{:S(2)}, u32[]{:S(2)}) collective-permute-start(bf16[24,896]{1,0:T(8,128)(2,1)S(1)} %get-tuple-element.42), channel_id=1, source_target_pairs={{0,4},{1,5},{2,6},{3,7},{4,0},{5,1},{6,2},{7,3},{8,12},{9,13},{10,... | collective-permute-start | bytes 129032 | tf_op jit(solution)/shard_map/ppermute | solution.py:325

commit v5 on v3

--- a/solution.py
+++ b/solution.py
@@ -135,36 +135,37 @@
 
 
 def load_body(parts, after, *refs):
-    count = len(refs) // 2
-    sems = refs[-1]
+    hbm, (w_gate, w_up, down_across, w_down, sems) = refs[:3], refs[3:]
     loads = []
-    for place in range(count):
-        depth = refs[place].shape[0] // parts
+    for source, target in zip((hbm[2], hbm[0], hbm[1]), (w_down, w_gate, w_up)):
+        depth = source.shape[0] // parts
         for part in range(parts):
             rows = slice(part * depth, (part + 1) * depth)
-            source, target = refs[place].at[rows], refs[count + place].at[rows]
-            loads.append(pltpu.make_async_copy(source, target, sems.at[len(loads)]))
+            loads.append(
+                pltpu.make_async_copy(source.at[rows], target.at[rows], sems.at[len(loads)])
+            )
     for load in loads:
         load.start()
-    for load in loads:
+    for load in loads[:parts]:
         load.wait()
-
-
-def take_rows(offset, pieces, stack):
-    place = 0
-    for ref in pieces:
-        stack[place : place + ref.shape[0], :] = ref[...].astype(F32)
-        place += ref.shape[0]
-    count = place // 2
-    rows = iota((count, place), 0)
-    mover = iota((count, place), 1) == rows + over_cap(rows) * CAP + offset
-    return dot(mover.astype(F32).astype(BF16), stack[...].astype(BF16)).astype(BF16)
+    down_across[...] = w_down[...].T
+    for load in loads[parts:]:
+        load.wait()
+
+
+def take_rows(offset, pieces):
+    rows = []
+    for ref in pieces[::-1]:
+        piece = ref[...].astype(F32)
+        for place in range(offset, piece.shape[0], 2 * CAP):
+            rows.append(piece[place : place + CAP])
+    return jnp.concatenate(rows, axis=0).astype(BF16)
 
 
 def forward_body(w_gate, w_up, *refs):
-    pieces, (rows_out, keep, send, stack) = refs[:-4], refs[-4:]
+    pieces, (rows_out, keep, send) = refs[:-3], refs[-3:]
     half = w_gate.shape[1] // 2
-    rows = take_rows(0, pieces, stack)
+    rows = take_rows(0, pieces)
     rows_out[...] = rows
     for target, far in ((send, True), (keep, False)):
         columns = core_columns(half, far)
@@ -172,19 +173,21 @@
         target[:, half:] = dot(rows, w_up[:, columns]).astype(BF16)
 
 
-def hidden_body(w_down, *refs):
-    pieces, (keep, send, stack) = refs[:-3], refs[-3:]
-    half = w_down.shape[0] // 2
-    rows = take_rows(CAP, pieces, stack)
+def hidden_body(down_across, *refs):
+    pieces, (keep, send) = refs[:-2], refs[-2:]
+    half = down_across.shape[1] // 2
+    rows = take_rows(CAP, pieces)
     for target, far in ((send, True), (keep, False)):
-        target[...] = dot(rows, w_down[core_columns(half, far), :], 1, 1).astype(BF16)
-
-
-def transpose_body(after, rows_ref, out):
+        target[...] = dot(rows, down_across[:, core_columns(half, far)]).astype(BF16)
+
+
+def transpose_body(after, rows_ref, w_gate, w_up, rows_across, gate_across, up_across):
     rows = rows_ref[...]
     count = rows.shape[0]
     same = (iota((count, count), 0) == iota((count, count), 1)).astype(F32).astype(BF16)
-    out[...] = dot(rows, same, 0, 0).astype(BF16)
+    rows_across[...] = dot(rows, same, 0, 0).astype(BF16)
+    gate_across[...] = w_gate[...].T
+    up_across[...] = w_up[...].T
 
 
 def activate_body(after, pre_own, pre_far, hid_own, hid_far, acts):
@@ -209,20 +212,20 @@
     ]
 
 
-def back_part(w_gate, w_up, acts, sibling):
-    half = w_gate.shape[1] // 2
-    columns = core_columns(half, sibling)
-    part = dot(acts[:, :half], w_gate[:, columns], 1, 1)
-    return part + dot(acts[:, half:], w_up[:, columns], 1, 1)
-
-
-def back_own_body(w_gate, w_up, acts, total):
-    total[...] = back_part(w_gate, w_up, acts, False)
-
-
-def back_far_body(w_gate, w_up, acts, own, *outs):
+def back_part(gate_across, up_across, acts, sibling):
+    half = gate_across.shape[0] // 2
+    units = core_columns(half, sibling)
+    part = dot(acts[:, :half], gate_across[units, :])
+    return part + dot(acts[:, half:], up_across[units, :])
+
+
+def back_own_body(gate_across, up_across, acts, total):
+    total[...] = back_part(gate_across, up_across, acts, False)
+
+
+def back_far_body(gate_across, up_across, acts, own, *outs):
     count = outs[0].shape[0]
-    total = own[...] + back_part(w_gate, w_up, acts, True)
+    total = own[...] + back_part(gate_across, up_across, acts, True)
     for place, out in enumerate(outs):
         out[...] = total[place * count : (place + 1) * count].astype(BF16)
 
@@ -314,25 +317,23 @@
         ),
     )
     picks, own = picked[:fold], picked[fold:]
-    weights = (w_gate, w_up, w_down)
-    gate_here, up_here, down_here = run(
+    gate_here, up_here, down_across = run(
         functools.partial(load_body, 4),
-        tuple(pltpu.VMEM(weight.shape, weight.dtype) for weight in weights),
+        tuple(pltpu.VMEM(dims, BF16) for dims in (w_gate.shape, w_up.shape, w_down.shape[::-1])),
         [ANY] + [HBM] * 3,
         0,
         6 * features * hidden,
         picks[0],
-        *(in_hbm(weight) for weight in weights),
-        scratch=(dma((12,)),),
+        *(in_hbm(weight) for weight in (w_gate, w_up, w_down)),
+        scratch=(pltpu.VMEM(w_down.shape, BF16), dma((12,))),
     )
 
     away = [to_expert(own[step], step) for step in range(1, experts)]
     near = [own[0]] + [to_peer(own[0], flip) for flip in range(1, HSPLIT)]
     away = away[0] if len(away) == 1 else jnp.concatenate(away, axis=0)
     far = [away] + [to_peer(away, flip) for flip in range(1, HSPLIT)]
-    pieces = [array for pair in zip(near, far) for array in pair]
-
-    stack = pltpu.VMEM((2 * count, features), F32)
+    pieces = [array for pair in zip(near, far) for array in pair][::-1]
+
     rows_input, pre_keep, pre_send = run(
         forward_body,
         (shape((count, features)), shape((count, hidden)), shape((count, hidden))),
@@ -342,7 +343,6 @@
         gate_here,
         up_here,
         *pieces,
-        scratch=(stack,),
     )
 
     def spread_sum(keep, send):
@@ -363,19 +363,20 @@
         [VMEM] * (1 + len(pieces)),
         product,
         2 * features * hidden,
-        down_here,
+        down_across,
         *pieces,
-        scratch=(stack,),
     )
     hid_own, hid_far = spread_sum(hid_keep, hid_send)
-    rows_across = run(
+    rows_across, gate_across, up_across = run(
         transpose_body,
-        shape((features, count)),
-        [ANY, VMEM],
+        (shape((features, count)),) + (shape((hidden, features)),) * 2,
+        [ANY] + [VMEM] * 3,
         0,
         0,
         hid_own,
         rows_input,
+        gate_here,
+        up_here,
     )
     acts = run(
         activate_body,
@@ -396,8 +397,8 @@
         [VMEM] * 3,
         product,
         2 * features * hidden,
-        gate_here,
-        up_here,
+        gate_across,
+        up_across,
         acts,
     )
     back = run(
@@ -406,8 +407,8 @@
         [VMEM] * 4,
         product,
         2 * features * hidden,
-        gate_here,
-        up_here,
+        gate_across,
+        up_across,
         acts_far,
         back_own,
     )

time: 42.6 us -> 42.2 us (level)
  transfers between devices with their start and end apart: 16 -> 16, of which waited for: 9 -> 10; matrix products, arithmetic and copies ran while one was open for 0% -> 0% of each run, Pallas kernels for 19% -> 20%
where the time goes in v5:
time: 42.2 us; the launch traced here: 41.9 us
  starting transfers between devices  20.1 us (48%)
  Pallas kernels  12.6 us (30%)
  waiting for transfers between devices  8.51 us (20%)
  between operations  0.74 us (2%)
    pallas_call x12, Pallas kernels, run(): pl.pallas_call(body, out_shape=outs, in_specs=specs, out_specs=out_spec i...  12.6 us
    ppermute x9, starting transfers between devices, to_peer(): lax.ppermute(value, 'expert', [(d, d ^ flip) for d in range(devices)])  10.9 us
    ppermute x2, starting transfers between devices, to_expert(): return lax.ppermute(value, 'expert', pairs)  6.34 us
    ppermute x5, waiting for transfers between devices, to_dp(): return lax.ppermute(value, 'dp', [(d, d ^ flip) for d in range(spread)])  3.78 us
    ppermute x9, waiting for transfers between devices, to_peer(): lax.ppermute(value, 'expert', [(d, d ^ flip) for d in range(devices)])  3.53 us
    ppermute x5, starting transfers between devices, to_dp(): return lax.ppermute(value, 'dp', [(d, d ^ flip) for d in range(spread)])  2.84 us
    ppermute x2, waiting for transfers between devices, to_expert(): return lax.ppermute(value, 'expert', pairs)  1.2 us
  transfers between devices with their start and end apart: 16, of which 10 were waited for; matrix products, arithmetic and copies ran while one was open for 0% of the time, Pallas kernels for 20%

profile of v5, /device:TPU:0, one launch (start us, length us, event | category | flops | bytes accessed | tf_op | source)
XLA Modules:
  0.0 41.9 jit_solution(18234262191754235934)
XLA Ops:
  0.6 1.8 %shard_map.94 = (bf16[48,256]{1,0:T(8,128)(2,1)S(1)}, bf16[48,256]{1,0:T(8,128)(2,1)S(1)}, bf16[24,1792]{1,0:T(8,128)(2,1)S(1)}, bf16[24,1792]{1,0:T(8,128)(2,1)S(1)}) custom-call(s32[8,256]{1,0:T(8,128)} %bitcast.2, f32[8,256]{1,0:T(8,128)} %bitcast.3, bf16[256,1792]{1,0:T(8,128)(2,1)} %grads_hbm.1, bf16[256,1792]{1,0:T(8,128)(2,1)} %inputs_hbm.1), custom_call_target="tpu_custom_call" | custom-call | flops 88080384 | bytes 1835008 | tf_op jit(solution)/shard_map/pallas_call | solution.py:24
  2.4 4.1 %collective-permute-start = (bf16[24,1792]{1,0:T(8,128)(2,1)S(1)}, bf16[24,1792]{1,0:T(8,128)(2,1)S(1)}, u32[]{:S(2)}, u32[]{:S(2)}) collective-permute-start(bf16[24,1792]{1,0:T(8,128)(2,1)S(1)} %get-tuple-element.30), channel_id=1, source_target_pairs={{0,4},{1,5},{2,6},{3,7},{4,0},{5,1},{6,2},{7,3},{8,12},{9,13},{10,... | collective-permute-start | bytes 258056 | tf_op jit(solution)/shard_map/ppermute | solution.py:295
  6.5 2.5 %collective-permute-start.2 = (bf16[24,1792]{1,0:T(8,128)(2,1)S(1)}, bf16[24,1792]{1,0:T(8,128)(2,1)S(1)}, u32[]{:S(2)}, u32[]{:S(2)}) collective-permute-start(bf16[24,1792]{1,0:T(8,128)(2,1)S(1)} %get-tuple-element.31.refs_7_), channel_id=1, source_target_pairs={{0,3},{1,2},{2,1},{3,0},{4,7},{5,6},{6,5},{7,4},{8,11},{9,10},{10,... | collective-permute-start | bytes 258056 | tf_op jit(solution)/shard_map/ppermute | solution.py:298
  9.1 0.4 %collective-permute-start.4 = (bf16[24,1792]{1,0:T(8,128)(2,1)S(1)}, bf16[24,1792]{1,0:T(8,128)(2,1)S(1)}, u32[]{:S(2)}, u32[]{:S(2)}) collective-permute-start(bf16[24,1792]{1,0:T(8,128)(2,1)S(1)} %get-tuple-element.31.refs_7_), channel_id=1, source_target_pairs={{0,2},{1,3},{2,0},{3,1},{4,6},{5,7},{6,4},{7,5},{8,10},{9,11},{10,... | collective-permute-start | bytes 258056 | tf_op jit(solution)/shard_map/ppermute | solution.py:298
  9.5 0.5 %collective-permute-start.6 = (bf16[24,1792]{1,0:T(8,128)(2,1)S(1)}, bf16[24,1792]{1,0:T(8,128)(2,1)S(1)}, u32[]{:S(2)}, u32[]{:S(2)}) collective-permute-start(bf16[24,1792]{1,0:T(8,128)(2,1)S(1)} %get-tuple-element.31.refs_7_), channel_id=1, source_target_pairs={{0,1},{1,0},{2,3},{3,2},{4,5},{5,4},{6,7},{7,6},{8,9},{9,8},{10,11... | collective-permute-start | bytes 258056 | tf_op jit(solution)/shard_map/ppermute | solution.py:298
  10.0 0.5 %collective-permute-done.refs_6_ = bf16[24,1792]{1,0:T(8,128)(2,1)S(1)} collective-permute-done((bf16[24,1792]{1,0:T(8,128)(2,1)S(1)}, bf16[24,1792]{1,0:T(8,128)(2,1)S(1)}, u32[]{:S(2)}, u32[]{:S(2)}) %collective-permute-start) | collective-permute-done | bytes 86048 | tf_op jit(solution)/shard_map/ppermute | solution.py:295
  10.6 2.2 %collective-permute-start.1 = (bf16[24,1792]{1,0:T(8,128)(2,1)S(1)}, bf16[24,1792]{1,0:T(8,128)(2,1)S(1)}, u32[]{:S(2)}, u32[]{:S(2)}) collective-permute-start(bf16[24,1792]{1,0:T(8,128)(2,1)S(1)} %collective-permute-done.refs_6_), channel_id=1, source_target_pairs={{0,3},{1,2},{2,1},{3,0},{4,7},{5,6},{6,5},{7,4},{8,11},{9,10},{10,... | collective-permute-start | bytes 258056 | tf_op jit(solution)/shard_map/ppermute | solution.py:298
  12.8 1.0 %collective-permute-start.3 = (bf16[24,1792]{1,0:T(8,128)(2,1)S(1)}, bf16[24,1792]{1,0:T(8,128)(2,1)S(1)}, u32[]{:S(2)}, u32[]{:S(2)}) collective-permute-start(bf16[24,1792]{1,0:T(8,128)(2,1)S(1)} %collective-permute-done.refs_6_), channel_id=1, source_target_pairs={{0,2},{1,3},{2,0},{3,1},{4,6},{5,7},{6,4},{7,5},{8,10},{9,11},{10,... | collective-permute-start | bytes 258056 | tf_op jit(solution)/shard_map/ppermute | solution.py:298
  13.8 0.6 %collective-permute-start.5 = (bf16[24,1792]{1,0:T(8,128)(2,1)S(1)}, bf16[24,1792]{1,0:T(8,128)(2,1)S(1)}, u32[]{:S(2)}, u32[]{:S(2)}) collective-permute-start(bf16[24,1792]{1,0:T(8,128)(2,1)S(1)} %collective-permute-done.refs_6_), channel_id=1, source_target_pairs={{0,1},{1,0},{2,3},{3,2},{4,5},{5,4},{6,7},{7,6},{8,9},{9,8},{10,11... | collective-permute-start | bytes 258056 | tf_op jit(solution)/shard_map/ppermute | solution.py:298
  14.4 2.6 %shard_map.95 = (bf16[1792,512]{1,0:T(8,128)(2,1)S(1)}, bf16[1792,512]{1,0:T(8,128)(2,1)S(1)}, bf16[1792,512]{1,0:T(8,128)(2,1)S(1)}) custom-call(bf16[48,256]{1,0:T(8,128)(2,1)S(1)} %get-tuple-element.27.after.refs_0_, bf16[1792,512]{1,0:T(8,128)(2,1)} %refs_0_.1, bf16[1792,512]{1,0:T(8,128)(2,1)} %refs_1_.1, bf16[512,1792]{1,0:T(8,128)(2,1)} %refs_2_.1), custom_call_target="tpu_custom_call" | custom-call | bytes 5505024 | tf_op jit(solution)/shard_map/pallas_call | solution.py:24
  17.1 0.4 collective-permute-done.3.refs_2_
  17.5 0.8 %collective-permute-done.5.refs_4_ = bf16[24,1792]{1,0:T(8,128)(2,1)S(1)} collective-permute-done((bf16[24,1792]{1,0:T(8,128)(2,1)S(1)}, bf16[24,1792]{1,0:T(8,128)(2,1)S(1)}, u32[]{:S(2)}, u32[]{:S(2)}) %collective-permute-start.5) | collective-permute-done | bytes 86048 | tf_op jit(solution)/shard_map/ppermute | solution.py:298
  18.3 0.7 %shard_map.97 = (bf16[96,1792]{1,0:T(8,128)(2,1)S(1)}, bf16[96,512]{1,0:T(8,128)(2,1)S(1)}, bf16[96,512]{1,0:T(8,128)(2,1)S(1)}) custom-call(bf16[1792,512]{1,0:T(8,128)(2,1)S(1)} %get-tuple-element.34.w_gate, bf16[1792,512]{1,0:T(8,128)(2,1)S(1)} %get-tuple-element.35.w_up, bf16[24,1792]{1,0:T(8,128)(2,1)S(1)} %collective-permute-done.1.refs_0_, ...), custom_call_target="tpu_custom_call" | custom-call | flops 352321536 | bytes 3670016 | tf_op jit(solution)/shard_map/pallas_call | solution.py:24
  19.1 0.5 %shard_map.96 = (bf16[96,256]{1,0:T(8,128)(2,1)S(1)}, bf16[96,256]{1,0:T(8,128)(2,1)S(1)}) custom-call(bf16[1792,512]{1,0:T(8,128)(2,1)S(1)} %get-tuple-element.29.down_across, bf16[24,1792]{1,0:T(8,128)(2,1)S(1)} %collective-permute-done.1.refs_0_, bf16[24,1792]{1,0:T(8,128)(2,1)S(1)} %collective-permute-done.2.refs_1_, ...), custom_call_target="tpu_custom_call" | custom-call | flops 176160768 | bytes 1835008 | tf_op jit(solution)/shard_map/pallas_call | solution.py:24
  19.6 0.5 %collective-permute-start.7 = (bf16[96,256]{1,0:T(8,128)(2,1)S(1)}, bf16[96,256]{1,0:T(8,128)(2,1)S(1)}, u32[]{:S(2)}, u32[]{:S(2)}) collective-permute-start(bf16[96,256]{1,0:T(8,128)(2,1)S(1)} %get-tuple-element.33), channel_id=1, source_target_pairs={{0,8},{8,0},{16,24},{24,16},{1,9},{9,1},{17,25},{25,17},{2,10},{10... | collective-permute-start | bytes 147464 | tf_op jit(solution)/shard_map/ppermute | solution.py:301
  20.4 1.6 %collective-permute-start.9 = (bf16[96,512]{1,0:T(8,128)(2,1)S(1)}, bf16[96,512]{1,0:T(8,128)(2,1)S(1)}, u32[]{:S(2)}, u32[]{:S(2)}) collective-permute-start(bf16[96,512]{1,0:T(8,128)(2,1)S(1)} %add_convert_fusion.pre_own), channel_id=1, source_target_pairs={{0,16},{8,24},{16,0},{24,8},{1,17},{9,25},{17,1},{25,9},{2,18},{10... | collective-permute-start | bytes 294920 | tf_op jit(solution)/shard_map/ppermute | solution.py:301
  22.0 0.6 %collective-permute-start.10 = (bf16[96,256]{1,0:T(8,128)(2,1)S(1)}, bf16[96,256]{1,0:T(8,128)(2,1)S(1)}, u32[]{:S(2)}, u32[]{:S(2)}) collective-permute-start(bf16[96,256]{1,0:T(8,128)(2,1)S(1)} %add_convert_fusion.1.after.hid_own), channel_id=1, source_target_pairs={{0,16},{8,24},{16,0},{24,8},{1,17},{9,25},{17,1},{25,9},{2,18},{10... | collective-permute-start | bytes 147464 | tf_op jit(solution)/shard_map/ppermute | solution.py:301
  22.6 1.1 %shard_map.98 = (bf16[1792,96]{1,0:T(8,128)(2,1)S(1)}, bf16[512,1792]{1,0:T(8,128)(2,1)S(1)}, bf16[512,1792]{1,0:T(8,128)(2,1)S(1)}) custom-call(bf16[96,256]{1,0:T(8,128)(2,1)S(1)} %add_convert_fusion.1.after.hid_own, bf16[96,1792]{1,0:T(8,128)(2,1)S(1)} %get-tuple-element.36.rows_ref, bf16[1792,512]{1,0:T(8,128)(2,1)S(1)} %get-tuple-element.34.w_gate, ...), custom_call_target="tpu_custom_call" | custom-call | tf_op jit(solution)/shard_map/pallas_call | solution.py:24
  23.8 2.6 %collective-permute-done.10.hid_far = bf16[96,256]{1,0:T(8,128)(2,1)S(1)} collective-permute-done((bf16[96,256]{1,0:T(8,128)(2,1)S(1)}, bf16[96,256]{1,0:T(8,128)(2,1)S(1)}, u32[]{:S(2)}, u32[]{:S(2)}) %collective-permute-start.10) | collective-permute-done | bytes 49184 | tf_op jit(solution)/shard_map/ppermute | solution.py:301
  26.6 0.4 %shard_map.100.own = f32[96,1792]{1,0:T(8,128)S(1)} custom-call(bf16[512,1792]{1,0:T(8,128)(2,1)S(1)} %get-tuple-element.37.gate_across, bf16[512,1792]{1,0:T(8,128)(2,1)S(1)} %get-tuple-element.38.up_across, bf16[96,512]{1,0:T(8,128)(2,1)S(1)} %shard_map.99.acts.acts_own), custom_call_target="tpu_custom_call" | custom-call | flops 176160768 | bytes 1835008 | tf_op jit(solution)/shard_map/pallas_call | solution.py:24
  27.0 0.8 %collective-permute-done.11.acts.acts_far = bf16[96,512]{1,0:T(8,128)(2,1)S(1)} collective-permute-done((bf16[96,512]{1,0:T(8,128)(2,1)S(1)}, bf16[96,512]{1,0:T(8,128)(2,1)S(1)}, u32[]{:S(2)}, u32[]{:S(2)}) %collective-permute-start.11) | collective-permute-done | bytes 98336 | tf_op jit(solution)/shard_map/ppermute | solution.py:301
  27.9 0.4 %shard_map.101 = (bf16[24,1792]{1,0:T(8,128)(2,1)S(1)}, bf16[24,1792]{1,0:T(8,128)(2,1)S(1)}, bf16[24,1792]{1,0:T(8,128)(2,1)S(1)}, bf16[24,1792]{1,0:T(8,128)(2,1)S(1)}) custom-call(bf16[512,1792]{1,0:T(8,128)(2,1)S(1)} %get-tuple-element.37.gate_across, bf16[512,1792]{1,0:T(8,128)(2,1)S(1)} %get-tuple-element.38.up_across, ...), custom_call_target="tpu_custom_call" | custom-call | flops 176160768 | bytes 1835008 | tf_op jit(solution)/shard_map/pallas_call | solution.py:24
  28.3 1.3 %collective-permute-start.12 = (bf16[24,1792]{1,0:T(8,128)(2,1)S(1)}, bf16[24,1792]{1,0:T(8,128)(2,1)S(1)}, u32[]{:S(2)}, u32[]{:S(2)}) collective-permute-start(bf16[24,1792]{1,0:T(8,128)(2,1)S(1)} %get-tuple-element.44), channel_id=1, source_target_pairs={{0,3},{1,2},{2,1},{3,0},{4,7},{5,6},{6,5},{7,4},{8,11},{9,10},{10,... | collective-permute-start | bytes 258056 | tf_op jit(solution)/shard_map/ppermute | solution.py:298
  29.6 0.9 %collective-permute-start.13 = (bf16[24,1792]{1,0:T(8,128)(2,1)S(1)}, bf16[24,1792]{1,0:T(8,128)(2,1)S(1)}, u32[]{:S(2)}, u32[]{:S(2)}) collective-permute-start(bf16[24,1792]{1,0:T(8,128)(2,1)S(1)} %get-tuple-element.45), channel_id=1, source_target_pairs={{0,2},{1,3},{2,0},{3,1},{4,6},{5,7},{6,4},{7,5},{8,10},{9,11},{10,... | collective-permute-start | bytes 258056 | tf_op jit(solution)/shard_map/ppermute | solution.py:298
  30.5 1.4 %collective-permute-start.14 = (bf16[24,1792]{1,0:T(8,128)(2,1)S(1)}, bf16[24,1792]{1,0:T(8,128)(2,1)S(1)}, u32[]{:S(2)}, u32[]{:S(2)}) collective-permute-start(bf16[24,1792]{1,0:T(8,128)(2,1)S(1)} %get-tuple-element.46), channel_id=1, source_target_pairs={{0,1},{1,0},{2,3},{3,2},{4,5},{5,4},{6,7},{7,6},{8,9},{9,8},{10,11... | collective-permute-start | bytes 258056 | tf_op jit(solution)/shard_map/ppermute | solution.py:298
  31.8 1.5 %shard_map.102 = (bf16[1792,512]{1,0:T(8,128)(2,1)}, f32[8,128]{1,0:T(8,128)S(1)}) custom-call(bf16[24,1792]{1,0:T(8,128)(2,1)S(1)} %get-tuple-element.42.after.refs_3_, bf16[1792,96]{1,0:T(8,128)(2,1)S(1)} %get-tuple-element.39.after.rows_ref, bf16[96,512]{1,0:T(8,128)(2,1)S(1)} %shard_map.99.acts.acts_own, ...), custom_call_target="tpu_custom_call" | custom-call | tf_op jit(solution)/shard_map/pallas_call | solution.py:24
  33.3 1.3 %collective-permute-done.12.refs_0_ = bf16[24,1792]{1,0:T(8,128)(2,1)S(1)} collective-permute-done((bf16[24,1792]{1,0:T(8,128)(2,1)S(1)}, bf16[24,1792]{1,0:T(8,128)(2,1)S(1)}, u32[]{:S(2)}, u32[]{:S(2)}) %collective-permute-start.12) | collective-permute-done | bytes 86048 | tf_op jit(solution)/shard_map/ppermute | solution.py:298
  34.9 0.8 %collective-permute-done.14.refs_2_ = bf16[24,1792]{1,0:T(8,128)(2,1)S(1)} collective-permute-done((bf16[24,1792]{1,0:T(8,128)(2,1)S(1)}, bf16[24,1792]{1,0:T(8,128)(2,1)S(1)}, u32[]{:S(2)}, u32[]{:S(2)}) %collective-permute-start.14) | collective-permute-done | bytes 86048 | tf_op jit(solution)/shard_map/ppermute | solution.py:298
  35.7 2.2 %collective-permute-start.15 = (bf16[24,896]{1,0:T(8,128)(2,1)S(1)}, bf16[24,896]{1,0:T(8,128)(2,1)S(1)}, u32[]{:S(2)}, u32[]{:S(2)}) collective-permute-start(bf16[24,896]{1,0:T(8,128)(2,1)S(1)} %get-tuple-element.48), channel_id=1, source_target_pairs={{0,4},{1,5},{2,6},{3,7},{4,0},{5,1},{6,2},{7,3},{8,12},{9,13},{10,... | collective-permute-start | bytes 129032 | tf_op jit(solution)/shard_map/ppermute | solution.py:295
  38.0 2.1 %shard_map.105 = (bf16[1792,512]{1,0:T(8,128)(2,1)}, f32[8,128]{1,0:T(8,128)}) custom-call(bf16[24,896]{1,0:T(8,128)(2,1)S(1)} %get-tuple-element.47.refs_2_.after, bf16[1792,96]{1,0:T(8,128)(2,1)S(1)} %get-tuple-element.39.after.rows_ref, bf16[96,512]{1,0:T(8,128)(2,1)S(1)} %shard_map.99.acts.acts_own, bf16[96,512]{1,0:T(8,128)(2,1)S(1)} %collective-permute-done.11.acts.acts_far), custom_call_target="tpu_custom_call" | custom-call | tf_op jit(solution)/shard_map/pallas_call | solution.py:24
  40.1 0.7 %collective-permute-done.15.refs_3_ = bf16[24,896]{1,0:T(8,128)(2,1)S(1)} collective-permute-done((bf16[24,896]{1,0:T(8,128)(2,1)S(1)}, bf16[24,896]{1,0:T(8,128)(2,1)S(1)}, u32[]{:S(2)}, u32[]{:S(2)}) %collective-permute-start.15) | collective-permute-done | bytes 43040 | tf_op jit(solution)/shard_map/ppermute | solution.py:295
  40.7 1.2 %shard_map.104 = bf16[256,1792]{1,0:T(8,128)(2,1)} custom-call(bf16[48,256]{1,0:T(8,128)(2,1)S(1)} %get-tuple-element.27.after.refs_0_, bf16[48,256]{1,0:T(8,128)(2,1)S(1)} %get-tuple-element.28.refs_1_, bf16[24,896]{1,0:T(8,128)(2,1)S(1)} %get-tuple-element.47.refs_2_.after, bf16[24,896]{1,0:T(8,128)(2,1)S(1)} %collective-permute-done.15.refs_3_), custom_call_target="tpu_custom_call" | custom-call | flops 44040192 | bytes 917504 | tf_op jit(solution)/shard_map/pallas_call | solution.py:24
  (14 shorter events, 0.8 us)
Async XLA Ops:
  2.4 8.1 %collective-permute-start = (bf16[24,1792]{1,0:T(8,128)(2,1)S(1)}, bf16[24,1792]{1,0:T(8,128)(2,1)S(1)}, u32[]{:S(2)}, u32[]{:S(2)}) collective-permute-start(bf16[24,1792]{1,0:T(8,128)(2,1)S(1)} %get-tuple-element.30), channel_id=1, source_target_pairs={{0,4},{1,5},{2,6},{3,7},{4,0},{5,1},{6,2},{7,3},{8,12},{9,13},{10,... | collective-permute-start | bytes 258056 | tf_op jit(solution)/shard_map/ppermute | solution.py:295
  6.5 7.3 %collective-permute-start.2 = (bf16[24,1792]{1,0:T(8,128)(2,1)S(1)}, bf16[24,1792]{1,0:T(8,128)(2,1)S(1)}, u32[]{:S(2)}, u32[]{:S(2)}) collective-permute-start(bf16[24,1792]{1,0:T(8,128)(2,1)S(1)} %get-tuple-element.31.refs_7_), channel_id=1, source_target_pairs={{0,3},{1,2},{2,1},{3,0},{4,7},{5,6},{6,5},{7,4},{8,11},{9,10},{10,... | collective-permute-start | bytes 258056 | tf_op jit(solution)/shard_map/ppermute | solution.py:298
  9.1 8.0 %collective-permute-start.4 = (bf16[24,1792]{1,0:T(8,128)(2,1)S(1)}, bf16[24,1792]{1,0:T(8,128)(2,1)S(1)}, u32[]{:S(2)}, u32[]{:S(2)}) collective-permute-start(bf16[24,1792]{1,0:T(8,128)(2,1)S(1)} %get-tuple-element.31.refs_7_), channel_id=1, source_target_pairs={{0,2},{1,3},{2,0},{3,1},{4,6},{5,7},{6,4},{7,5},{8,10},{9,11},{10,... | collective-permute-start | bytes 258056 | tf_op jit(solution)/shard_map/ppermute | solution.py:298
  9.5 7.6 %collective-permute-start.6 = (bf16[24,1792]{1,0:T(8,128)(2,1)S(1)}, bf16[24,1792]{1,0:T(8,128)(2,1)S(1)}, u32[]{:S(2)}, u32[]{:S(2)}) collective-permute-start(bf16[24,1792]{1,0:T(8,128)(2,1)S(1)} %get-tuple-element.31.refs_7_), channel_id=1, source_target_pairs={{0,1},{1,0},{2,3},{3,2},{4,5},{5,4},{6,7},{7,6},{8,9},{9,8},{10,11... | collective-permute-start | bytes 258056 | tf_op jit(solution)/shard_map/ppermute | solution.py:298
  10.6 6.5 %collective-permute-start.1 = (bf16[24,1792]{1,0:T(8,128)(2,1)S(1)}, bf16[24,1792]{1,0:T(8,128)(2,1)S(1)}, u32[]{:S(2)}, u32[]{:S(2)}) collective-permute-start(bf16[24,1792]{1,0:T(8,128)(2,1)S(1)} %collective-permute-done.refs_6_), channel_id=1, source_target_pairs={{0,3},{1,2},{2,1},{3,0},{4,7},{5,6},{6,5},{7,4},{8,11},{9,10},{10,... | collective-permute-start | bytes 258056 | tf_op jit(solution)/shard_map/ppermute | solution.py:298
  12.8 4.7 %collective-permute-start.3 = (bf16[24,1792]{1,0:T(8,128)(2,1)S(1)}, bf16[24,1792]{1,0:T(8,128)(2,1)S(1)}, u32[]{:S(2)}, u32[]{:S(2)}) collective-permute-start(bf16[24,1792]{1,0:T(8,128)(2,1)S(1)} %collective-permute-done.refs_6_), channel_id=1, source_target_pairs={{0,2},{1,3},{2,0},{3,1},{4,6},{5,7},{6,4},{7,5},{8,10},{9,11},{10,... | collective-permute-start | bytes 258056 | tf_op jit(solution)/shard_map/ppermute | solution.py:298
  13.8 4.5 %collective-permute-start.5 = (bf16[24,1792]{1,0:T(8,128)(2,1)S(1)}, bf16[24,1792]{1,0:T(8,128)(2,1)S(1)}, u32[]{:S(2)}, u32[]{:S(2)}) collective-permute-start(bf16[24,1792]{1,0:T(8,128)(2,1)S(1)} %collective-permute-done.refs_6_), channel_id=1, source_target_pairs={{0,1},{1,0},{2,3},{3,2},{4,5},{5,4},{6,7},{7,6},{8,9},{9,8},{10,11... | collective-permute-start | bytes 258056 | tf_op jit(solution)/shard_map/ppermute | solution.py:298
  19.0 1.4 %collective-permute-start.8 = (bf16[96,512]{1,0:T(8,128)(2,1)S(1)}, bf16[96,512]{1,0:T(8,128)(2,1)S(1)}, u32[]{:S(2)}, u32[]{:S(2)}) collective-permute-start(bf16[96,512]{1,0:T(8,128)(2,1)S(1)} %get-tuple-element.41), channel_id=1, source_target_pairs={{0,8},{8,0},{16,24},{24,16},{1,9},{9,1},{17,25},{25,17},{2,10},{10... | collective-permute-start | bytes 294920 | tf_op jit(solution)/shard_map/ppermute | solution.py:301
  19.6 2.4 %collective-permute-start.7 = (bf16[96,256]{1,0:T(8,128)(2,1)S(1)}, bf16[96,256]{1,0:T(8,128)(2,1)S(1)}, u32[]{:S(2)}, u32[]{:S(2)}) collective-permute-start(bf16[96,256]{1,0:T(8,128)(2,1)S(1)} %get-tuple-element.33), channel_id=1, source_target_pairs={{0,8},{8,0},{16,24},{24,16},{1,9},{9,1},{17,25},{25,17},{2,10},{10... | collective-permute-start | bytes 147464 | tf_op jit(solution)/shard_map/ppermute | solution.py:301
  20.4 6.0 %collective-permute-start.9 = (bf16[96,512]{1,0:T(8,128)(2,1)S(1)}, bf16[96,512]{1,0:T(8,128)(2,1)S(1)}, u32[]{:S(2)}, u32[]{:S(2)}) collective-permute-start(bf16[96,512]{1,0:T(8,128)(2,1)S(1)} %add_convert_fusion.pre_own), channel_id=1, source_target_pairs={{0,16},{8,24},{16,0},{24,8},{1,17},{9,25},{17,1},{25,9},{2,18},{10... | collective-permute-start | bytes 294920 | tf_op jit(solution)/shard_map/ppermute | solution.py:301
  22.0 4.4 %collective-permute-start.10 = (bf16[96,256]{1,0:T(8,128)(2,1)S(1)}, bf16[96,256]{1,0:T(8,128)(2,1)S(1)}, u32[]{:S(2)}, u32[]{:S(2)}) collective-permute-start(bf16[96,256]{1,0:T(8,128)(2,1)S(1)} %add_convert_fusion.1.after.hid_own), channel_id=1, source_target_pairs={{0,16},{8,24},{16,0},{24,8},{1,17},{9,25},{17,1},{25,9},{2,18},{10... | collective-permute-start | bytes 147464 | tf_op jit(solution)/shard_map/ppermute | solution.py:301
  26.5 1.4 %collective-permute-start.11 = (bf16[96,512]{1,0:T(8,128)(2,1)S(1)}, bf16[96,512]{1,0:T(8,128)(2,1)S(1)}, u32[]{:S(2)}, u32[]{:S(2)}) collective-permute-start(bf16[96,512]{1,0:T(8,128)(2,1)S(1)} %shard_map.99.acts.acts_own), channel_id=1, source_target_pairs={{0,8},{8,0},{16,24},{24,16},{1,9},{9,1},{17,25},{25,17},{2,10},{10... | collective-permute-start | bytes 294920 | tf_op jit(solution)/shard_map/ppermute | solution.py:301
  28.3 6.3 %collective-permute-start.12 = (bf16[24,1792]{1,0:T(8,128)(2,1)S(1)}, bf16[24,1792]{1,0:T(8,128)(2,1)S(1)}, u32[]{:S(2)}, u32[]{:S(2)}) collective-permute-start(bf16[24,1792]{1,0:T(8,128)(2,1)S(1)} %get-tuple-element.44), channel_id=1, source_target_pairs={{0,3},{1,2},{2,1},{3,0},{4,7},{5,6},{6,5},{7,4},{8,11},{9,10},{10,... | collective-permute-start | bytes 258056 | tf_op jit(solution)/shard_map/ppermute | solution.py:298
  29.6 5.3 %collective-permute-start.13 = (bf16[24,1792]{1,0:T(8,128)(2,1)S(1)}, bf16[24,1792]{1,0:T(8,128)(2,1)S(1)}, u32[]{:S(2)}, u32[]{:S(2)}) collective-permute-start(bf16[24,1792]{1,0:T(8,128)(2,1)S(1)} %get-tuple-element.45), channel_id=1, source_target_pairs={{0,2},{1,3},{2,0},{3,1},{4,6},{5,7},{6,4},{7,5},{8,10},{9,11},{10,... | collective-permute-start | bytes 258056 | tf_op jit(solution)/shard_map/ppermute | solution.py:298
  30.5 5.2 %collective-permute-start.14 = (bf16[24,1792]{1,0:T(8,128)(2,1)S(1)}, bf16[24,1792]{1,0:T(8,128)(2,1)S(1)}, u32[]{:S(2)}, u32[]{:S(2)}) collective-permute-start(bf16[24,1792]{1,0:T(8,128)(2,1)S(1)} %get-tuple-element.46), channel_id=1, source_target_pairs={{0,1},{1,0},{2,3},{3,2},{4,5},{5,4},{6,7},{7,6},{8,9},{9,8},{10,11... | collective-permute-start | bytes 258056 | tf_op jit(solution)/shard_map/ppermute | solution.py:298
  35.7 5.0 %collective-permute-start.15 = (bf16[24,896]{1,0:T(8,128)(2,1)S(1)}, bf16[24,896]{1,0:T(8,128)(2,1)S(1)}, u32[]{:S(2)}, u32[]{:S(2)}) collective-permute-start(bf16[24,896]{1,0:T(8,128)(2,1)S(1)} %get-tuple-element.48), channel_id=1, source_target_pairs={{0,4},{1,5},{2,6},{3,7},{4,0},{5,1},{6,2},{7,3},{8,12},{9,13},{10,... | collective-permute-start | bytes 129032 | tf_op jit(solution)/shard_map/ppermute | solution.py:295

commit v6 on v5

--- a/solution.py
+++ b/solution.py
@@ -50,12 +50,10 @@
     return jnp.floor((rows.astype(F32) + 0.5) * (1.0 / CAP)).astype(jnp.int32)
 
 
-def column_spans(width):
-    whole = width // 128 * 128
-    if whole != width or width < 512:
+def column_spans(width, size):
+    if width % 128:
         return [slice(0, width)]
-    middle = width // 256 * 128
-    return [slice(0, middle), slice(middle, width)]
+    return [slice(start, min(start + size, width)) for start in range(0, width, size)]
 
 
 def core_columns(width, far):
@@ -71,7 +69,7 @@
 def pick_body(experts, fold, ids_hbm, gates_hbm, grads_hbm, inputs_hbm, *refs):
     picks, pieces = refs[:fold], refs[fold : fold + experts]
     ids, gates, grads, inputs, sems = refs[fold + experts :]
-    spans = column_spans(grads.shape[1])
+    spans = column_spans(grads.shape[1], 512)
     moves = [(ids_hbm, ids), (gates_hbm, gates)]
     for span in spans:
         moves.append((inputs_hbm.at[:, span], inputs.at[:, span]))
@@ -162,23 +160,24 @@
     return jnp.concatenate(rows, axis=0).astype(BF16)
 
 
-def forward_body(w_gate, w_up, *refs):
+def gate_body(w_gate, *refs):
     pieces, (rows_out, keep, send) = refs[:-3], refs[-3:]
     half = w_gate.shape[1] // 2
     rows = take_rows(0, pieces)
     rows_out[...] = rows
     for target, far in ((send, True), (keep, False)):
+        target[...] = dot(rows, w_gate[:, core_columns(half, far)]).astype(BF16)
+
+
+def rest_body(w_up, down_across, rows_ref, *refs):
+    pieces, (keep, send) = refs[:-2], refs[-2:]
+    half = w_up.shape[1] // 2
+    rows = rows_ref[...]
+    grads = take_rows(CAP, pieces)
+    for target, far in ((send, True), (keep, False)):
         columns = core_columns(half, far)
-        target[:, :half] = dot(rows, w_gate[:, columns]).astype(BF16)
-        target[:, half:] = dot(rows, w_up[:, columns]).astype(BF16)
-
-
-def hidden_body(down_across, *refs):
-    pieces, (keep, send) = refs[:-2], refs[-2:]
-    half = down_across.shape[1] // 2
-    rows = take_rows(CAP, pieces)
-    for target, far in ((send, True), (keep, False)):
-        target[...] = dot(rows, down_across[:, core_columns(half, far)]).astype(BF16)
+        target[:, :half] = dot(rows, w_up[:, columns]).astype(BF16)
+        target[:, half:] = dot(grads, down_across[:, columns]).astype(BF16)
 
 
 def transpose_body(after, rows_ref, w_gate, w_up, rows_across, gate_across, up_across):
@@ -190,15 +189,24 @@
     up_across[...] = w_up[...].T
 
 
-def activate_body(after, pre_own, pre_far, hid_own, hid_far, acts):
-    half = hid_own.shape[1]
-    pre = pre_own[...].astype(F32) + pre_far[...].astype(F32)
-    hidden_grad = hid_own[...].astype(F32) + hid_far[...].astype(F32)
-    gate_pre = pre[:, :half]
-    up_pre = pre[:, half:]
+def core_sum_body(own, other, *refs):
+    refs[-1][...] = (own[...].astype(F32) + other[...].astype(F32)).astype(BF16)
+
+
+def slope_body(own, other, slope, value):
+    gate_pre = own[...].astype(F32) + other[...].astype(F32)
     sigma = jax.nn.sigmoid(gate_pre)
-    acts[:, :half] = (hidden_grad * up_pre * sigma * (1.0 + gate_pre * (1.0 - sigma))).astype(BF16)
-    acts[:, half:] = (hidden_grad * gate_pre * sigma).astype(BF16)
+    slope[...] = sigma * (1.0 + gate_pre * (1.0 - sigma))
+    value[...] = gate_pre * sigma
+
+
+def activate_body(after, slope, value, rest_own, rest_far, acts):
+    half = slope.shape[1]
+    rest = rest_own[...].astype(F32) + rest_far[...].astype(F32)
+    up_pre = rest[:, :half]
+    hidden_grad = rest[:, half:]
+    acts[:, :half] = (hidden_grad * up_pre * slope[...]).astype(BF16)
+    acts[:, half:] = (hidden_grad * value[...]).astype(BF16)
 
 
 def fold_rows(rows, fold):
@@ -265,7 +273,7 @@
     returned = stack[...].astype(BF16)
     stores = []
     for part in range(fold):
-        for span in column_spans(width):
+        for span in column_spans(width, 384):
             target = slice(part * width + span.start, part * width + span.stop)
             tile[:, target] = dot(picks[part][...], returned[:, span], 0, 0).astype(BF16)
             store = pltpu.make_async_copy(
@@ -313,7 +321,7 @@
             pltpu.VMEM((routed, tokens), F32),
             pltpu.VMEM((tokens, features), BF16),
             pltpu.VMEM((tokens, features), BF16),
-            dma((2 + 2 * len(column_spans(features)),)),
+            dma((2 + 2 * len(column_spans(features, 512)),)),
         ),
     )
     picks, own = picked[:fold], picked[fold:]
@@ -334,46 +342,68 @@
     far = [away] + [to_peer(away, flip) for flip in range(1, HSPLIT)]
     pieces = [array for pair in zip(near, far) for array in pair][::-1]
 
-    rows_input, pre_keep, pre_send = run(
-        forward_body,
-        (shape((count, features)), shape((count, hidden)), shape((count, hidden))),
-        [VMEM] * (2 + len(pieces)),
-        2 * product,
-        4 * features * hidden,
-        gate_here,
-        up_here,
-        *pieces,
-    )
-
-    def spread_sum(keep, send):
-        near = (keep.astype(F32) + to_dp(send, 1).astype(F32)).astype(BF16)
-        flip = 2
-        far = jnp.zeros_like(near)
-        while flip < spread:
-            far = to_dp(near, flip)
-            flip *= 2
-            if flip < spread:
-                near = (near.astype(F32) + far.astype(F32)).astype(BF16)
-        return near, far
-
-    pre_own, pre_far = spread_sum(pre_keep, pre_send)
-    hid_keep, hid_send = run(
-        hidden_body,
-        (shape((count, half)), shape((count, half))),
+    rows_input, gate_keep, gate_send = run(
+        gate_body,
+        (shape((count, features)), shape((count, half)), shape((count, half))),
         [VMEM] * (1 + len(pieces)),
         product,
         2 * features * hidden,
+        gate_here,
+        *pieces,
+    )
+
+    rest_keep, rest_send = run(
+        rest_body,
+        (shape((count, hidden)),) * 2,
+        [VMEM] * (3 + len(pieces)),
+        0,
+        0,
+        up_here,
         down_across,
+        rows_input,
         *pieces,
     )
-    hid_own, hid_far = spread_sum(hid_keep, hid_send)
+    def core_sum(keep, send, flops, *after):
+        return run(
+            core_sum_body,
+            shape(keep.shape),
+            [VMEM] * 2 + [ANY] * len(after),
+            flops,
+            0,
+            keep,
+            to_dp(send, 1),
+            *after,
+        )
+
+    def spread_sum(total):
+        flip = 2
+        other = jnp.zeros_like(total)
+        while flip < spread:
+            other = to_dp(total, flip)
+            flip *= 2
+            if flip < spread:
+                total = (total.astype(F32) + other.astype(F32)).astype(BF16)
+        return total, other
+
+    gate_sum = core_sum(gate_keep, gate_send, 8 * product)
+    gate_own, gate_far = spread_sum(gate_sum)
+    slope, value = run(
+        slope_body,
+        (shape((count, half), F32),) * 2,
+        [VMEM] * 2,
+        8 * product,
+        0,
+        gate_own,
+        gate_far,
+    )
+    rest_own, rest_far = spread_sum(core_sum(rest_keep, rest_send, 0, gate_sum))
     rows_across, gate_across, up_across = run(
         transpose_body,
         (shape((features, count)),) + (shape((hidden, features)),) * 2,
         [ANY] + [VMEM] * 3,
         0,
         0,
-        hid_own,
+        slope,
         rows_input,
         gate_here,
         up_here,
@@ -385,10 +415,10 @@
         20 * count * half,
         10 * count * half,
         rows_across,
-        pre_own,
-        pre_far,
-        hid_own,
-        hid_far,
+        slope,
+        value,
+        rest_own,
+        rest_far,
     )
     acts_far = to_dp(acts, 1)
     back_own = run(
@@ -454,7 +484,7 @@
         scratch=(
             pltpu.VMEM((experts * fold * CAP, features // fold), F32),
             pltpu.VMEM((tokens, features), BF16),
-            dma((fold * len(column_spans(features // fold)),)),
+            dma((fold * len(column_spans(features // fold, 384)),)),
         ),
     )
     return (in_grad, grad_gate, grad_up)

time: 42.2 us -> 43.5 us (1.031)
  starting transfers between devices: 20.1 us -> 21.3 us
    ppermute x2, starting transfers between devices: 6.34 us -> 7.34 us  [to_expert(): return lax.ppermute(value, 'expert', pairs)]
    ppermute x5, starting transfers between devices: 2.84 us -> 3.33 us  [to_dp(): return lax.ppermute(value, 'dp', [(d, d ^ flip) for d in range(spread)])]
    pallas_call x12 -> x15, Pallas kernels: 12.6 us -> 12.8 us  [run(): pl.pallas_call(body, out_shape=outs, in_specs=specs, out_specs=out_spec i...]
  transfers between devices with their start and end apart: 16 -> 16, of which waited for: 10 -> 9; matrix products, arithmetic and copies ran while one was open for 0% -> 0% of each run, Pallas kernels for 20% -> 20%
where the time goes in v6:
time: 43.5 us; the launch traced here: 43.3 us
  starting transfers between devices  21.3 us (49%)
  Pallas kernels  12.8 us (29%)
  waiting for transfers between devices  8.4 us (19%)
  between operations  0.75 us (2%)
    pallas_call x15, Pallas kernels, run(): pl.pallas_call(body, out_shape=outs, in_specs=specs, out_specs=out_spec i...  12.8 us
    ppermute x9, starting transfers between devices, to_peer(): lax.ppermute(value, 'expert', [(d, d ^ flip) for d in range(devices)])  10.7 us
    ppermute x2, starting transfers between devices, to_expert(): return lax.ppermute(value, 'expert', pairs)  7.34 us
    ppermute x9, waiting for transfers between devices, to_peer(): lax.ppermute(value, 'expert', [(d, d ^ flip) for d in range(devices)])  3.8 us
    ppermute x5, waiting for transfers between devices, to_dp(): return lax.ppermute(value, 'dp', [(d, d ^ flip) for d in range(spread)])  3.41 us
    ppermute x5, starting transfers between devices, to_dp(): return lax.ppermute(value, 'dp', [(d, d ^ flip) for d in range(spread)])  3.33 us
    ppermute x2, waiting for transfers between devices, to_expert(): return lax.ppermute(value, 'expert', pairs)  1.2 us
  transfers between devices with their start and end apart: 16, of which 9 were waited for; matrix products, arithmetic and copies ran while one was open for 0% of the time, Pallas kernels for 20%

profile of v6, /device:TPU:0, one launch (start us, length us, event | category | flops | bytes accessed | tf_op | source)
XLA Modules:
  0.0 43.3 jit_solution(1622643920567495902)
XLA Ops:
  0.6 2.0 %shard_map.94 = (bf16[48,256]{1,0:T(8,128)(2,1)S(1)}, bf16[48,256]{1,0:T(8,128)(2,1)S(1)}, bf16[24,1792]{1,0:T(8,128)(2,1)S(1)}, bf16[24,1792]{1,0:T(8,128)(2,1)S(1)}) custom-call(s32[8,256]{1,0:T(8,128)} %bitcast.2, f32[8,256]{1,0:T(8,128)} %bitcast.3, bf16[256,1792]{1,0:T(8,128)(2,1)} %grads_hbm.1, bf16[256,1792]{1,0:T(8,128)(2,1)} %inputs_hbm.1), custom_call_target="tpu_custom_call" | custom-call | flops 88080384 | bytes 1835008 | tf_op jit(solution)/shard_map/pallas_call | solution.py:24
  2.6 4.1 %collective-permute-start = (bf16[24,1792]{1,0:T(8,128)(2,1)S(1)}, bf16[24,1792]{1,0:T(8,128)(2,1)S(1)}, u32[]{:S(2)}, u32[]{:S(2)}) collective-permute-start(bf16[24,1792]{1,0:T(8,128)(2,1)S(1)} %get-tuple-element.32), channel_id=1, source_target_pairs={{0,4},{1,5},{2,6},{3,7},{4,0},{5,1},{6,2},{7,3},{8,12},{9,13},{10,... | collective-permute-start | bytes 258056 | tf_op jit(solution)/shard_map/ppermute | solution.py:303
  6.7 1.5 %collective-permute-start.6 = (bf16[24,1792]{1,0:T(8,128)(2,1)S(1)}, bf16[24,1792]{1,0:T(8,128)(2,1)S(1)}, u32[]{:S(2)}, u32[]{:S(2)}) collective-permute-start(bf16[24,1792]{1,0:T(8,128)(2,1)S(1)} %get-tuple-element.33.refs_7_), channel_id=1, source_target_pairs={{0,1},{1,0},{2,3},{3,2},{4,5},{5,4},{6,7},{7,6},{8,9},{9,8},{10,11... | collective-permute-start | bytes 258056 | tf_op jit(solution)/shard_map/ppermute | solution.py:306
  8.3 1.6 %collective-permute-start.4 = (bf16[24,1792]{1,0:T(8,128)(2,1)S(1)}, bf16[24,1792]{1,0:T(8,128)(2,1)S(1)}, u32[]{:S(2)}, u32[]{:S(2)}) collective-permute-start(bf16[24,1792]{1,0:T(8,128)(2,1)S(1)} %get-tuple-element.33.refs_7_), channel_id=1, source_target_pairs={{0,2},{1,3},{2,0},{3,1},{4,6},{5,7},{6,4},{7,5},{8,10},{9,11},{10,... | collective-permute-start | bytes 258056 | tf_op jit(solution)/shard_map/ppermute | solution.py:306
  9.8 0.4 collective-permute-start.2
  10.2 0.8 %collective-permute-done.refs_6_ = bf16[24,1792]{1,0:T(8,128)(2,1)S(1)} collective-permute-done((bf16[24,1792]{1,0:T(8,128)(2,1)S(1)}, bf16[24,1792]{1,0:T(8,128)(2,1)S(1)}, u32[]{:S(2)}, u32[]{:S(2)}) %collective-permute-start) | collective-permute-done | bytes 86048 | tf_op jit(solution)/shard_map/ppermute | solution.py:303
  11.1 1.5 %collective-permute-start.5 = (bf16[24,1792]{1,0:T(8,128)(2,1)S(1)}, bf16[24,1792]{1,0:T(8,128)(2,1)S(1)}, u32[]{:S(2)}, u32[]{:S(2)}) collective-permute-start(bf16[24,1792]{1,0:T(8,128)(2,1)S(1)} %collective-permute-done.refs_6_), channel_id=1, source_target_pairs={{0,1},{1,0},{2,3},{3,2},{4,5},{5,4},{6,7},{7,6},{8,9},{9,8},{10,11... | collective-permute-start | bytes 258056 | tf_op jit(solution)/shard_map/ppermute | solution.py:306
  12.6 0.8 %collective-permute-start.3 = (bf16[24,1792]{1,0:T(8,128)(2,1)S(1)}, bf16[24,1792]{1,0:T(8,128)(2,1)S(1)}, u32[]{:S(2)}, u32[]{:S(2)}) collective-permute-start(bf16[24,1792]{1,0:T(8,128)(2,1)S(1)} %collective-permute-done.refs_6_), channel_id=1, source_target_pairs={{0,2},{1,3},{2,0},{3,1},{4,6},{5,7},{6,4},{7,5},{8,10},{9,11},{10,... | collective-permute-start | bytes 258056 | tf_op jit(solution)/shard_map/ppermute | solution.py:306
  13.4 1.3 %collective-permute-start.1 = (bf16[24,1792]{1,0:T(8,128)(2,1)S(1)}, bf16[24,1792]{1,0:T(8,128)(2,1)S(1)}, u32[]{:S(2)}, u32[]{:S(2)}) collective-permute-start(bf16[24,1792]{1,0:T(8,128)(2,1)S(1)} %collective-permute-done.refs_6_), channel_id=1, source_target_pairs={{0,3},{1,2},{2,1},{3,0},{4,7},{5,6},{6,5},{7,4},{8,11},{9,10},{10,... | collective-permute-start | bytes 258056 | tf_op jit(solution)/shard_map/ppermute | solution.py:306
  14.7 2.6 %shard_map.95 = (bf16[1792,512]{1,0:T(8,128)(2,1)S(1)}, bf16[1792,512]{1,0:T(8,128)(2,1)S(1)}, bf16[1792,512]{1,0:T(8,128)(2,1)S(1)}) custom-call(bf16[48,256]{1,0:T(8,128)(2,1)S(1)} %get-tuple-element.29.after.refs_0_, bf16[1792,512]{1,0:T(8,128)(2,1)} %refs_0_.1, bf16[1792,512]{1,0:T(8,128)(2,1)} %refs_1_.1, bf16[512,1792]{1,0:T(8,128)(2,1)} %refs_2_.1), custom_call_target="tpu_custom_call" | custom-call | bytes 5505024 | tf_op jit(solution)/shard_map/pallas_call | solution.py:24
  17.4 1.4 %collective-permute-done.1.refs_0_ = bf16[24,1792]{1,0:T(8,128)(2,1)S(1)} collective-permute-done((bf16[24,1792]{1,0:T(8,128)(2,1)S(1)}, bf16[24,1792]{1,0:T(8,128)(2,1)S(1)}, u32[]{:S(2)}, u32[]{:S(2)}) %collective-permute-start.1) | collective-permute-done | bytes 86048 | tf_op jit(solution)/shard_map/ppermute | solution.py:306
  18.8 0.4 %shard_map.96 = (bf16[96,1792]{1,0:T(8,128)(2,1)S(1)}, bf16[96,256]{1,0:T(8,128)(2,1)S(1)}, bf16[96,256]{1,0:T(8,128)(2,1)S(1)}) custom-call(bf16[1792,512]{1,0:T(8,128)(2,1)S(1)} %get-tuple-element.31.w_gate, bf16[24,1792]{1,0:T(8,128)(2,1)S(1)} %collective-permute-done.1.refs_0_, bf16[24,1792]{1,0:T(8,128)(2,1)S(1)} %collective-permute-done.2.refs_1_, ...), custom_call_target="tpu_custom_call" | custom-call | flops 176160768 | bytes 1835008 | tf_op jit(solution)/shard_map/pallas_call | solution.py:24
  19.3 0.7 %shard_map.100 = (bf16[96,512]{1,0:T(8,128)(2,1)S(1)}, bf16[96,512]{1,0:T(8,128)(2,1)S(1)}) custom-call(bf16[1792,512]{1,0:T(8,128)(2,1)S(1)} %get-tuple-element.38.w_up, bf16[1792,512]{1,0:T(8,128)(2,1)S(1)} %get-tuple-element.43.down_across, bf16[96,1792]{1,0:T(8,128)(2,1)S(1)} %get-tuple-element.37.rows_ref, ...), custom_call_target="tpu_custom_call" | custom-call | tf_op jit(solution)/shard_map/pallas_call | solution.py:24
  20.1 0.6 %collective-permute-start.9 = (bf16[96,512]{1,0:T(8,128)(2,1)S(1)}, bf16[96,512]{1,0:T(8,128)(2,1)S(1)}, u32[]{:S(2)}, u32[]{:S(2)}) collective-permute-start(bf16[96,512]{1,0:T(8,128)(2,1)S(1)} %get-tuple-element.45), channel_id=1, source_target_pairs={{0,8},{8,0},{16,24},{24,16},{1,9},{9,1},{17,25},{25,17},{2,10},{10... | collective-permute-start | bytes 294920 | tf_op jit(solution)/shard_map/ppermute | solution.py:309
  20.7 1.7 %collective-permute-start.8 = (bf16[96,256]{1,0:T(8,128)(2,1)S(1)}, bf16[96,256]{1,0:T(8,128)(2,1)S(1)}, u32[]{:S(2)}, u32[]{:S(2)}) collective-permute-start(bf16[96,256]{1,0:T(8,128)(2,1)S(1)} %shard_map.97.own.refs_0_), channel_id=1, source_target_pairs={{0,16},{8,24},{16,0},{24,8},{1,17},{9,25},{17,1},{25,9},{2,18},{10... | collective-permute-start | bytes 147464 | tf_op jit(solution)/shard_map/ppermute | solution.py:309
  22.4 0.9 %collective-permute-start.10 = (bf16[96,512]{1,0:T(8,128)(2,1)S(1)}, bf16[96,512]{1,0:T(8,128)(2,1)S(1)}, u32[]{:S(2)}, u32[]{:S(2)}) collective-permute-start(bf16[96,512]{1,0:T(8,128)(2,1)S(1)} %shard_map.101.rest_own), channel_id=1, source_target_pairs={{0,16},{8,24},{16,0},{24,8},{1,17},{9,25},{17,1},{25,9},{2,18},{10... | collective-permute-start | bytes 294920 | tf_op jit(solution)/shard_map/ppermute | solution.py:309
  23.3 1.5 %collective-permute-done.8.other = bf16[96,256]{1,0:T(8,128)(2,1)S(1)} collective-permute-done((bf16[96,256]{1,0:T(8,128)(2,1)S(1)}, bf16[96,256]{1,0:T(8,128)(2,1)S(1)}, u32[]{:S(2)}, u32[]{:S(2)}) %collective-permute-start.8) | collective-permute-done | bytes 49184 | tf_op jit(solution)/shard_map/ppermute | solution.py:309
  24.9 1.1 %shard_map.99 = (bf16[1792,96]{1,0:T(8,128)(2,1)S(1)}, bf16[512,1792]{1,0:T(8,128)(2,1)S(1)}, bf16[512,1792]{1,0:T(8,128)(2,1)S(1)}) custom-call(f32[96,256]{1,0:T(8,128)S(1)} %get-tuple-element.36.after.slope, bf16[96,1792]{1,0:T(8,128)(2,1)S(1)} %get-tuple-element.37.rows_ref, bf16[1792,512]{1,0:T(8,128)(2,1)S(1)} %get-tuple-element.31.w_gate, ...), custom_call_target="tpu_custom_call" | custom-call | tf_op jit(solution)/shard_map/pallas_call | solution.py:24
  26.0 1.1 %collective-permute-done.10.rest_far = bf16[96,512]{1,0:T(8,128)(2,1)S(1)} collective-permute-done((bf16[96,512]{1,0:T(8,128)(2,1)S(1)}, bf16[96,512]{1,0:T(8,128)(2,1)S(1)}, u32[]{:S(2)}, u32[]{:S(2)}) %collective-permute-start.10) | collective-permute-done | bytes 98336 | tf_op jit(solution)/shard_map/ppermute | solution.py:309
  27.2 0.4 %shard_map.103.own = f32[96,1792]{1,0:T(8,128)S(1)} custom-call(bf16[512,1792]{1,0:T(8,128)(2,1)S(1)} %get-tuple-element.39.gate_across, bf16[512,1792]{1,0:T(8,128)(2,1)S(1)} %get-tuple-element.40.up_across, bf16[96,512]{1,0:T(8,128)(2,1)S(1)} %shard_map.102.acts.acts_own), custom_call_target="tpu_custom_call" | custom-call | flops 176160768 | bytes 1835008 | tf_op jit(solution)/shard_map/pallas_call | solution.py:24
  27.7 0.8 %collective-permute-done.11.acts.acts_far = bf16[96,512]{1,0:T(8,128)(2,1)S(1)} collective-permute-done((bf16[96,512]{1,0:T(8,128)(2,1)S(1)}, bf16[96,512]{1,0:T(8,128)(2,1)S(1)}, u32[]{:S(2)}, u32[]{:S(2)}) %collective-permute-start.11) | collective-permute-done | bytes 98336 | tf_op jit(solution)/shard_map/ppermute | solution.py:309
  28.5 0.4 shard_map.104
  28.9 1.3 %collective-permute-start.12 = (bf16[24,1792]{1,0:T(8,128)(2,1)S(1)}, bf16[24,1792]{1,0:T(8,128)(2,1)S(1)}, u32[]{:S(2)}, u32[]{:S(2)}) collective-permute-start(bf16[24,1792]{1,0:T(8,128)(2,1)S(1)} %get-tuple-element.48), channel_id=1, source_target_pairs={{0,3},{1,2},{2,1},{3,0},{4,7},{5,6},{6,5},{7,4},{8,11},{9,10},{10,... | collective-permute-start | bytes 258056 | tf_op jit(solution)/shard_map/ppermute | solution.py:306
  30.3 0.8 %collective-permute-start.13 = (bf16[24,1792]{1,0:T(8,128)(2,1)S(1)}, bf16[24,1792]{1,0:T(8,128)(2,1)S(1)}, u32[]{:S(2)}, u32[]{:S(2)}) collective-permute-start(bf16[24,1792]{1,0:T(8,128)(2,1)S(1)} %get-tuple-element.49), channel_id=1, source_target_pairs={{0,2},{1,3},{2,0},{3,1},{4,6},{5,7},{6,4},{7,5},{8,10},{9,11},{10,... | collective-permute-start | bytes 258056 | tf_op jit(solution)/shard_map/ppermute | solution.py:306
  31.1 1.4 %collective-permute-start.14 = (bf16[24,1792]{1,0:T(8,128)(2,1)S(1)}, bf16[24,1792]{1,0:T(8,128)(2,1)S(1)}, u32[]{:S(2)}, u32[]{:S(2)}) collective-permute-start(bf16[24,1792]{1,0:T(8,128)(2,1)S(1)} %get-tuple-element.50), channel_id=1, source_target_pairs={{0,1},{1,0},{2,3},{3,2},{4,5},{5,4},{6,7},{7,6},{8,9},{9,8},{10,11... | collective-permute-start | bytes 258056 | tf_op jit(solution)/shard_map/ppermute | solution.py:306
  32.5 1.5 %shard_map.105 = (bf16[1792,512]{1,0:T(8,128)(2,1)}, f32[8,128]{1,0:T(8,128)S(1)}) custom-call(bf16[24,1792]{1,0:T(8,128)(2,1)S(1)} %get-tuple-element.46.after.refs_3_, bf16[1792,96]{1,0:T(8,128)(2,1)S(1)} %get-tuple-element.41.after.rows_ref, bf16[96,512]{1,0:T(8,128)(2,1)S(1)} %shard_map.102.acts.acts_own, ...), custom_call_target="tpu_custom_call" | custom-call | tf_op jit(solution)/shard_map/pallas_call | solution.py:24
  34.0 1.3 %collective-permute-done.12.refs_0_ = bf16[24,1792]{1,0:T(8,128)(2,1)S(1)} collective-permute-done((bf16[24,1792]{1,0:T(8,128)(2,1)S(1)}, bf16[24,1792]{1,0:T(8,128)(2,1)S(1)}, u32[]{:S(2)}, u32[]{:S(2)}) %collective-permute-start.12) | collective-permute-done | bytes 86048 | tf_op jit(solution)/shard_map/ppermute | solution.py:306
  35.5 0.9 %collective-permute-done.14.refs_2_ = bf16[24,1792]{1,0:T(8,128)(2,1)S(1)} collective-permute-done((bf16[24,1792]{1,0:T(8,128)(2,1)S(1)}, bf16[24,1792]{1,0:T(8,128)(2,1)S(1)}, u32[]{:S(2)}, u32[]{:S(2)}) %collective-permute-start.14) | collective-permute-done | bytes 86048 | tf_op jit(solution)/shard_map/ppermute | solution.py:306
  36.4 3.2 %collective-permute-start.15 = (bf16[24,896]{1,0:T(8,128)(2,1)S(1)}, bf16[24,896]{1,0:T(8,128)(2,1)S(1)}, u32[]{:S(2)}, u32[]{:S(2)}) collective-permute-start(bf16[24,896]{1,0:T(8,128)(2,1)S(1)} %get-tuple-element.52), channel_id=1, source_target_pairs={{0,4},{1,5},{2,6},{3,7},{4,0},{5,1},{6,2},{7,3},{8,12},{9,13},{10,... | collective-permute-start | bytes 129032 | tf_op jit(solution)/shard_map/ppermute | solution.py:303
  39.6 2.1 %shard_map.108 = (bf16[1792,512]{1,0:T(8,128)(2,1)}, f32[8,128]{1,0:T(8,128)}) custom-call(bf16[24,896]{1,0:T(8,128)(2,1)S(1)} %get-tuple-element.51.refs_2_.after, bf16[1792,96]{1,0:T(8,128)(2,1)S(1)} %get-tuple-element.41.after.rows_ref, bf16[96,512]{1,0:T(8,128)(2,1)S(1)} %shard_map.102.acts.acts_own, ...), custom_call_target="tpu_custom_call" | custom-call | tf_op jit(solution)/shard_map/pallas_call | solution.py:24
  41.7 0.4 collective-permute-done.15.refs_3_
  42.1 1.2 %shard_map.107 = bf16[256,1792]{1,0:T(8,128)(2,1)} custom-call(bf16[48,256]{1,0:T(8,128)(2,1)S(1)} %get-tuple-element.29.after.refs_0_, bf16[48,256]{1,0:T(8,128)(2,1)S(1)} %get-tuple-element.30.refs_1_, bf16[24,896]{1,0:T(8,128)(2,1)S(1)} %get-tuple-element.51.refs_2_.after, bf16[24,896]{1,0:T(8,128)(2,1)S(1)} %collective-permute-done.15.refs_3_), custom_call_target="tpu_custom_call" | custom-call | flops 44040192 | bytes 917504 | tf_op jit(solution)/shard_map/pallas_call | solution.py:24
  (15 shorter events, 0.5 us)
Async XLA Ops:
  2.6 8.4 %collective-permute-start = (bf16[24,1792]{1,0:T(8,128)(2,1)S(1)}, bf16[24,1792]{1,0:T(8,128)(2,1)S(1)}, u32[]{:S(2)}, u32[]{:S(2)}) collective-permute-start(bf16[24,1792]{1,0:T(8,128)(2,1)S(1)} %get-tuple-element.32), channel_id=1, source_target_pairs={{0,4},{1,5},{2,6},{3,7},{4,0},{5,1},{6,2},{7,3},{8,12},{9,13},{10,... | collective-permute-start | bytes 258056 | tf_op jit(solution)/shard_map/ppermute | solution.py:303
  6.7 6.6 %collective-permute-start.6 = (bf16[24,1792]{1,0:T(8,128)(2,1)S(1)}, bf16[24,1792]{1,0:T(8,128)(2,1)S(1)}, u32[]{:S(2)}, u32[]{:S(2)}) collective-permute-start(bf16[24,1792]{1,0:T(8,128)(2,1)S(1)} %get-tuple-element.33.refs_7_), channel_id=1, source_target_pairs={{0,1},{1,0},{2,3},{3,2},{4,5},{5,4},{6,7},{7,6},{8,9},{9,8},{10,11... | collective-permute-start | bytes 258056 | tf_op jit(solution)/shard_map/ppermute | solution.py:306
  8.3 9.1 %collective-permute-start.4 = (bf16[24,1792]{1,0:T(8,128)(2,1)S(1)}, bf16[24,1792]{1,0:T(8,128)(2,1)S(1)}, u32[]{:S(2)}, u32[]{:S(2)}) collective-permute-start(bf16[24,1792]{1,0:T(8,128)(2,1)S(1)} %get-tuple-element.33.refs_7_), channel_id=1, source_target_pairs={{0,2},{1,3},{2,0},{3,1},{4,6},{5,7},{6,4},{7,5},{8,10},{9,11},{10,... | collective-permute-start | bytes 258056 | tf_op jit(solution)/shard_map/ppermute | solution.py:306
  9.8 7.5 %collective-permute-start.2 = (bf16[24,1792]{1,0:T(8,128)(2,1)S(1)}, bf16[24,1792]{1,0:T(8,128)(2,1)S(1)}, u32[]{:S(2)}, u32[]{:S(2)}) collective-permute-start(bf16[24,1792]{1,0:T(8,128)(2,1)S(1)} %get-tuple-element.33.refs_7_), channel_id=1, source_target_pairs={{0,3},{1,2},{2,1},{3,0},{4,7},{5,6},{6,5},{7,4},{8,11},{9,10},{10,... | collective-permute-start | bytes 258056 | tf_op jit(solution)/shard_map/ppermute | solution.py:306
  11.1 6.3 %collective-permute-start.5 = (bf16[24,1792]{1,0:T(8,128)(2,1)S(1)}, bf16[24,1792]{1,0:T(8,128)(2,1)S(1)}, u32[]{:S(2)}, u32[]{:S(2)}) collective-permute-start(bf16[24,1792]{1,0:T(8,128)(2,1)S(1)} %collective-permute-done.refs_6_), channel_id=1, source_target_pairs={{0,1},{1,0},{2,3},{3,2},{4,5},{5,4},{6,7},{7,6},{8,9},{9,8},{10,11... | collective-permute-start | bytes 258056 | tf_op jit(solution)/shard_map/ppermute | solution.py:306
  12.6 4.8 %collective-permute-start.3 = (bf16[24,1792]{1,0:T(8,128)(2,1)S(1)}, bf16[24,1792]{1,0:T(8,128)(2,1)S(1)}, u32[]{:S(2)}, u32[]{:S(2)}) collective-permute-start(bf16[24,1792]{1,0:T(8,128)(2,1)S(1)} %collective-permute-done.refs_6_), channel_id=1, source_target_pairs={{0,2},{1,3},{2,0},{3,1},{4,6},{5,7},{6,4},{7,5},{8,10},{9,11},{10,... | collective-permute-start | bytes 258056 | tf_op jit(solution)/shard_map/ppermute | solution.py:306
  13.4 5.4 %collective-permute-start.1 = (bf16[24,1792]{1,0:T(8,128)(2,1)S(1)}, bf16[24,1792]{1,0:T(8,128)(2,1)S(1)}, u32[]{:S(2)}, u32[]{:S(2)}) collective-permute-start(bf16[24,1792]{1,0:T(8,128)(2,1)S(1)} %collective-permute-done.refs_6_), channel_id=1, source_target_pairs={{0,3},{1,2},{2,1},{3,0},{4,7},{5,6},{6,5},{7,4},{8,11},{9,10},{10,... | collective-permute-start | bytes 258056 | tf_op jit(solution)/shard_map/ppermute | solution.py:306
  19.3 1.4 %collective-permute-start.7 = (bf16[96,256]{1,0:T(8,128)(2,1)S(1)}, bf16[96,256]{1,0:T(8,128)(2,1)S(1)}, u32[]{:S(2)}, u32[]{:S(2)}) collective-permute-start(bf16[96,256]{1,0:T(8,128)(2,1)S(1)} %get-tuple-element.35), channel_id=1, source_target_pairs={{0,8},{8,0},{16,24},{24,16},{1,9},{9,1},{17,25},{25,17},{2,10},{10... | collective-permute-start | bytes 147464 | tf_op jit(solution)/shard_map/ppermute | solution.py:309
  20.1 2.3 %collective-permute-start.9 = (bf16[96,512]{1,0:T(8,128)(2,1)S(1)}, bf16[96,512]{1,0:T(8,128)(2,1)S(1)}, u32[]{:S(2)}, u32[]{:S(2)}) collective-permute-start(bf16[96,512]{1,0:T(8,128)(2,1)S(1)} %get-tuple-element.45), channel_id=1, source_target_pairs={{0,8},{8,0},{16,24},{24,16},{1,9},{9,1},{17,25},{25,17},{2,10},{10... | collective-permute-start | bytes 294920 | tf_op jit(solution)/shard_map/ppermute | solution.py:309
  20.7 4.2 %collective-permute-start.8 = (bf16[96,256]{1,0:T(8,128)(2,1)S(1)}, bf16[96,256]{1,0:T(8,128)(2,1)S(1)}, u32[]{:S(2)}, u32[]{:S(2)}) collective-permute-start(bf16[96,256]{1,0:T(8,128)(2,1)S(1)} %shard_map.97.own.refs_0_), channel_id=1, source_target_pairs={{0,16},{8,24},{16,0},{24,8},{1,17},{9,25},{17,1},{25,9},{2,18},{10... | collective-permute-start | bytes 147464 | tf_op jit(solution)/shard_map/ppermute | solution.py:309
  22.4 4.7 %collective-permute-start.10 = (bf16[96,512]{1,0:T(8,128)(2,1)S(1)}, bf16[96,512]{1,0:T(8,128)(2,1)S(1)}, u32[]{:S(2)}, u32[]{:S(2)}) collective-permute-start(bf16[96,512]{1,0:T(8,128)(2,1)S(1)} %shard_map.101.rest_own), channel_id=1, source_target_pairs={{0,16},{8,24},{16,0},{24,8},{1,17},{9,25},{17,1},{25,9},{2,18},{10... | collective-permute-start | bytes 294920 | tf_op jit(solution)/shard_map/ppermute | solution.py:309
  27.1 1.4 %collective-permute-start.11 = (bf16[96,512]{1,0:T(8,128)(2,1)S(1)}, bf16[96,512]{1,0:T(8,128)(2,1)S(1)}, u32[]{:S(2)}, u32[]{:S(2)}) collective-permute-start(bf16[96,512]{1,0:T(8,128)(2,1)S(1)} %shard_map.102.acts.acts_own), channel_id=1, source_target_pairs={{0,8},{8,0},{16,24},{24,16},{1,9},{9,1},{17,25},{25,17},{2,10},{10... | collective-permute-start | bytes 294920 | tf_op jit(solution)/shard_map/ppermute | solution.py:309
  28.9 6.3 %collective-permute-start.12 = (bf16[24,1792]{1,0:T(8,128)(2,1)S(1)}, bf16[24,1792]{1,0:T(8,128)(2,1)S(1)}, u32[]{:S(2)}, u32[]{:S(2)}) collective-permute-start(bf16[24,1792]{1,0:T(8,128)(2,1)S(1)} %get-tuple-element.48), channel_id=1, source_target_pairs={{0,3},{1,2},{2,1},{3,0},{4,7},{5,6},{6,5},{7,4},{8,11},{9,10},{10,... | collective-permute-start | bytes 258056 | tf_op jit(solution)/shard_map/ppermute | solution.py:306
  30.3 5.2 %collective-permute-start.13 = (bf16[24,1792]{1,0:T(8,128)(2,1)S(1)}, bf16[24,1792]{1,0:T(8,128)(2,1)S(1)}, u32[]{:S(2)}, u32[]{:S(2)}) collective-permute-start(bf16[24,1792]{1,0:T(8,128)(2,1)S(1)} %get-tuple-element.49), channel_id=1, source_target_pairs={{0,2},{1,3},{2,0},{3,1},{4,6},{5,7},{6,4},{7,5},{8,10},{9,11},{10,... | collective-permute-start | bytes 258056 | tf_op jit(solution)/shard_map/ppermute | solution.py:306
  31.1 5.3 %collective-permute-start.14 = (bf16[24,1792]{1,0:T(8,128)(2,1)S(1)}, bf16[24,1792]{1,0:T(8,128)(2,1)S(1)}, u32[]{:S(2)}, u32[]{:S(2)}) collective-permute-start(bf16[24,1792]{1,0:T(8,128)(2,1)S(1)} %get-tuple-element.50), channel_id=1, source_target_pairs={{0,1},{1,0},{2,3},{3,2},{4,5},{5,4},{6,7},{7,6},{8,9},{9,8},{10,11... | collective-permute-start | bytes 258056 | tf_op jit(solution)/shard_map/ppermute | solution.py:306
  36.4 5.7 %collective-permute-start.15 = (bf16[24,896]{1,0:T(8,128)(2,1)S(1)}, bf16[24,896]{1,0:T(8,128)(2,1)S(1)}, u32[]{:S(2)}, u32[]{:S(2)}) collective-permute-start(bf16[24,896]{1,0:T(8,128)(2,1)S(1)} %get-tuple-element.52), channel_id=1, source_target_pairs={{0,4},{1,5},{2,6},{3,7},{4,0},{5,1},{6,2},{7,3},{8,12},{9,13},{10,... | collective-permute-start | bytes 129032 | tf_op jit(solution)/shard_map/ppermute | solution.py:303

commit v7 on v5

--- a/solution.py
+++ b/solution.py
@@ -430,6 +430,7 @@
         )
 
     grad_gate, token = weight_grad(0, back[0])
+    grad_up, token = weight_grad(1, token)
     summed = run(
         functools.partial(gather_body, fold, experts),
         (shape((CAP * fold, features // fold)),) * experts,
@@ -440,7 +441,6 @@
         *(to_peer(back[flip], flip) for flip in range(HSPLIT - 1, 0, -1)),
         back[0],
     )
-    grad_up, _ = weight_grad(1, summed[0])
     returned = [summed[0]] + [to_expert(summed[step], experts - step) for step in range(1, experts)]
     in_grad = run(
         functools.partial(scatter_body, fold),

time: 42.2 us -> 42.2 us (level)
  Pallas kernels: 12.6 us -> 12 us
  waiting for transfers between devices: 8.51 us -> 9.1 us
    ppermute x2, waiting for transfers between devices: 1.2 us -> 3.29 us  [to_expert(): return lax.ppermute(value, 'expert', pairs)]
    ppermute x9, waiting for transfers between devices: 3.53 us -> 2.02 us  [to_peer(): lax.ppermute(value, 'expert', [(d, d ^ flip) for d in range(devices)])]
    pallas_call x12, Pallas kernels: 12.6 us -> 12 us  [run(): pl.pallas_call(body, out_shape=outs, in_specs=specs, out_specs=out_spec i...]
  transfers between devices with their start and end apart: 16 -> 16, of which waited for: 10 -> 8; matrix products, arithmetic and copies ran while one was open for 0% -> 0% of each run, Pallas kernels for 20% -> 18%
where the time goes in v7:
time: 42.2 us; the launch traced here: 41.9 us
  starting transfers between devices  20.1 us (48%)
  Pallas kernels  12 us (28%)
  waiting for transfers between devices  9.1 us (22%)
  between operations  0.75 us (2%)
    pallas_call x12, Pallas kernels, run(): pl.pallas_call(body, out_shape=outs, in_specs=specs, out_specs=out_spec i...  12 us
    ppermute x9, starting transfers between devices, to_peer(): lax.ppermute(value, 'expert', [(d, d ^ flip) for d in range(devices)])  10.9 us
    ppermute x2, starting transfers between devices, to_expert(): return lax.ppermute(value, 'expert', pairs)  6.34 us
    ppermute x5, waiting for transfers between devices, to_dp(): return lax.ppermute(value, 'dp', [(d, d ^ flip) for d in range(spread)])  3.78 us
    ppermute x2, waiting for transfers between devices, to_expert(): return lax.ppermute(value, 'expert', pairs)  3.29 us
    ppermute x5, starting transfers between devices, to_dp(): return lax.ppermute(value, 'dp', [(d, d ^ flip) for d in range(spread)])  2.84 us
    ppermute x9, waiting for transfers between devices, to_peer(): lax.ppermute(value, 'expert', [(d, d ^ flip) for d in range(devices)])  2.02 us
  transfers between devices with their start and end apart: 16, of which 8 were waited for; matrix products, arithmetic and copies ran while one was open for 0% of the time, Pallas kernels for 18%

profile of v7, /device:TPU:0, one launch (start us, length us, event | category | flops | bytes accessed | tf_op | source)
XLA Modules:
  0.0 41.9 jit_solution(9794238891428983481)
XLA Ops:
  0.6 1.8 %shard_map.94 = (bf16[48,256]{1,0:T(8,128)(2,1)S(1)}, bf16[48,256]{1,0:T(8,128)(2,1)S(1)}, bf16[24,1792]{1,0:T(8,128)(2,1)S(1)}, bf16[24,1792]{1,0:T(8,128)(2,1)S(1)}) custom-call(s32[8,256]{1,0:T(8,128)} %bitcast.2, f32[8,256]{1,0:T(8,128)} %bitcast.3, bf16[256,1792]{1,0:T(8,128)(2,1)} %grads_hbm.1, bf16[256,1792]{1,0:T(8,128)(2,1)} %inputs_hbm.1), custom_call_target="tpu_custom_call" | custom-call | flops 88080384 | bytes 1835008 | tf_op jit(solution)/shard_map/pallas_call | solution.py:24
  2.4 4.1 %collective-permute-start = (bf16[24,1792]{1,0:T(8,128)(2,1)S(1)}, bf16[24,1792]{1,0:T(8,128)(2,1)S(1)}, u32[]{:S(2)}, u32[]{:S(2)}) collective-permute-start(bf16[24,1792]{1,0:T(8,128)(2,1)S(1)} %get-tuple-element.31), channel_id=1, source_target_pairs={{0,4},{1,5},{2,6},{3,7},{4,0},{5,1},{6,2},{7,3},{8,12},{9,13},{10,... | collective-permute-start | bytes 258056 | tf_op jit(solution)/shard_map/ppermute | solution.py:295
  6.5 2.5 %collective-permute-start.2 = (bf16[24,1792]{1,0:T(8,128)(2,1)S(1)}, bf16[24,1792]{1,0:T(8,128)(2,1)S(1)}, u32[]{:S(2)}, u32[]{:S(2)}) collective-permute-start(bf16[24,1792]{1,0:T(8,128)(2,1)S(1)} %get-tuple-element.32.refs_7_), channel_id=1, source_target_pairs={{0,3},{1,2},{2,1},{3,0},{4,7},{5,6},{6,5},{7,4},{8,11},{9,10},{10,... | collective-permute-start | bytes 258056 | tf_op jit(solution)/shard_map/ppermute | solution.py:298
  9.1 0.4 %collective-permute-start.4 = (bf16[24,1792]{1,0:T(8,128)(2,1)S(1)}, bf16[24,1792]{1,0:T(8,128)(2,1)S(1)}, u32[]{:S(2)}, u32[]{:S(2)}) collective-permute-start(bf16[24,1792]{1,0:T(8,128)(2,1)S(1)} %get-tuple-element.32.refs_7_), channel_id=1, source_target_pairs={{0,2},{1,3},{2,0},{3,1},{4,6},{5,7},{6,4},{7,5},{8,10},{9,11},{10,... | collective-permute-start | bytes 258056 | tf_op jit(solution)/shard_map/ppermute | solution.py:298
  9.5 0.5 %collective-permute-start.6 = (bf16[24,1792]{1,0:T(8,128)(2,1)S(1)}, bf16[24,1792]{1,0:T(8,128)(2,1)S(1)}, u32[]{:S(2)}, u32[]{:S(2)}) collective-permute-start(bf16[24,1792]{1,0:T(8,128)(2,1)S(1)} %get-tuple-element.32.refs_7_), channel_id=1, source_target_pairs={{0,1},{1,0},{2,3},{3,2},{4,5},{5,4},{6,7},{7,6},{8,9},{9,8},{10,11... | collective-permute-start | bytes 258056 | tf_op jit(solution)/shard_map/ppermute | solution.py:298
  10.0 0.5 %collective-permute-done.refs_6_ = bf16[24,1792]{1,0:T(8,128)(2,1)S(1)} collective-permute-done((bf16[24,1792]{1,0:T(8,128)(2,1)S(1)}, bf16[24,1792]{1,0:T(8,128)(2,1)S(1)}, u32[]{:S(2)}, u32[]{:S(2)}) %collective-permute-start) | collective-permute-done | bytes 86048 | tf_op jit(solution)/shard_map/ppermute | solution.py:295
  10.6 2.2 %collective-permute-start.1 = (bf16[24,1792]{1,0:T(8,128)(2,1)S(1)}, bf16[24,1792]{1,0:T(8,128)(2,1)S(1)}, u32[]{:S(2)}, u32[]{:S(2)}) collective-permute-start(bf16[24,1792]{1,0:T(8,128)(2,1)S(1)} %collective-permute-done.refs_6_), channel_id=1, source_target_pairs={{0,3},{1,2},{2,1},{3,0},{4,7},{5,6},{6,5},{7,4},{8,11},{9,10},{10,... | collective-permute-start | bytes 258056 | tf_op jit(solution)/shard_map/ppermute | solution.py:298
  12.8 1.0 %collective-permute-start.3 = (bf16[24,1792]{1,0:T(8,128)(2,1)S(1)}, bf16[24,1792]{1,0:T(8,128)(2,1)S(1)}, u32[]{:S(2)}, u32[]{:S(2)}) collective-permute-start(bf16[24,1792]{1,0:T(8,128)(2,1)S(1)} %collective-permute-done.refs_6_), channel_id=1, source_target_pairs={{0,2},{1,3},{2,0},{3,1},{4,6},{5,7},{6,4},{7,5},{8,10},{9,11},{10,... | collective-permute-start | bytes 258056 | tf_op jit(solution)/shard_map/ppermute | solution.py:298
  13.8 0.6 %collective-permute-start.5 = (bf16[24,1792]{1,0:T(8,128)(2,1)S(1)}, bf16[24,1792]{1,0:T(8,128)(2,1)S(1)}, u32[]{:S(2)}, u32[]{:S(2)}) collective-permute-start(bf16[24,1792]{1,0:T(8,128)(2,1)S(1)} %collective-permute-done.refs_6_), channel_id=1, source_target_pairs={{0,1},{1,0},{2,3},{3,2},{4,5},{5,4},{6,7},{7,6},{8,9},{9,8},{10,11... | collective-permute-start | bytes 258056 | tf_op jit(solution)/shard_map/ppermute | solution.py:298
  14.4 2.6 %shard_map.95 = (bf16[1792,512]{1,0:T(8,128)(2,1)S(1)}, bf16[1792,512]{1,0:T(8,128)(2,1)S(1)}, bf16[1792,512]{1,0:T(8,128)(2,1)S(1)}) custom-call(bf16[48,256]{1,0:T(8,128)(2,1)S(1)} %get-tuple-element.28.after.refs_0_, bf16[1792,512]{1,0:T(8,128)(2,1)} %refs_0_.1, bf16[1792,512]{1,0:T(8,128)(2,1)} %refs_1_.1, bf16[512,1792]{1,0:T(8,128)(2,1)} %refs_2_.1), custom_call_target="tpu_custom_call" | custom-call | bytes 5505024 | tf_op jit(solution)/shard_map/pallas_call | solution.py:24
  17.1 0.4 collective-permute-done.3.refs_2_
  17.5 0.8 %collective-permute-done.5.refs_4_ = bf16[24,1792]{1,0:T(8,128)(2,1)S(1)} collective-permute-done((bf16[24,1792]{1,0:T(8,128)(2,1)S(1)}, bf16[24,1792]{1,0:T(8,128)(2,1)S(1)}, u32[]{:S(2)}, u32[]{:S(2)}) %collective-permute-start.5) | collective-permute-done | bytes 86048 | tf_op jit(solution)/shard_map/ppermute | solution.py:298
  18.3 0.7 %shard_map.97 = (bf16[96,1792]{1,0:T(8,128)(2,1)S(1)}, bf16[96,512]{1,0:T(8,128)(2,1)S(1)}, bf16[96,512]{1,0:T(8,128)(2,1)S(1)}) custom-call(bf16[1792,512]{1,0:T(8,128)(2,1)S(1)} %get-tuple-element.35.w_gate, bf16[1792,512]{1,0:T(8,128)(2,1)S(1)} %get-tuple-element.36.w_up, bf16[24,1792]{1,0:T(8,128)(2,1)S(1)} %collective-permute-done.1.refs_0_, ...), custom_call_target="tpu_custom_call" | custom-call | flops 352321536 | bytes 3670016 | tf_op jit(solution)/shard_map/pallas_call | solution.py:24
  19.1 0.5 %shard_map.96 = (bf16[96,256]{1,0:T(8,128)(2,1)S(1)}, bf16[96,256]{1,0:T(8,128)(2,1)S(1)}) custom-call(bf16[1792,512]{1,0:T(8,128)(2,1)S(1)} %get-tuple-element.30.down_across, bf16[24,1792]{1,0:T(8,128)(2,1)S(1)} %collective-permute-done.1.refs_0_, bf16[24,1792]{1,0:T(8,128)(2,1)S(1)} %collective-permute-done.2.refs_1_, ...), custom_call_target="tpu_custom_call" | custom-call | flops 176160768 | bytes 1835008 | tf_op jit(solution)/shard_map/pallas_call | solution.py:24
  19.6 0.5 %collective-permute-start.7 = (bf16[96,256]{1,0:T(8,128)(2,1)S(1)}, bf16[96,256]{1,0:T(8,128)(2,1)S(1)}, u32[]{:S(2)}, u32[]{:S(2)}) collective-permute-start(bf16[96,256]{1,0:T(8,128)(2,1)S(1)} %get-tuple-element.34), channel_id=1, source_target_pairs={{0,8},{8,0},{16,24},{24,16},{1,9},{9,1},{17,25},{25,17},{2,10},{10... | collective-permute-start | bytes 147464 | tf_op jit(solution)/shard_map/ppermute | solution.py:301
  20.1 0.3 collective-permute-done.8
  20.4 1.6 %collective-permute-start.9 = (bf16[96,512]{1,0:T(8,128)(2,1)S(1)}, bf16[96,512]{1,0:T(8,128)(2,1)S(1)}, u32[]{:S(2)}, u32[]{:S(2)}) collective-permute-start(bf16[96,512]{1,0:T(8,128)(2,1)S(1)} %add_convert_fusion.pre_own), channel_id=1, source_target_pairs={{0,16},{8,24},{16,0},{24,8},{1,17},{9,25},{17,1},{25,9},{2,18},{10... | collective-permute-start | bytes 294920 | tf_op jit(solution)/shard_map/ppermute | solution.py:301
  22.0 0.6 %collective-permute-start.10 = (bf16[96,256]{1,0:T(8,128)(2,1)S(1)}, bf16[96,256]{1,0:T(8,128)(2,1)S(1)}, u32[]{:S(2)}, u32[]{:S(2)}) collective-permute-start(bf16[96,256]{1,0:T(8,128)(2,1)S(1)} %add_convert_fusion.1.after.hid_own), channel_id=1, source_target_pairs={{0,16},{8,24},{16,0},{24,8},{1,17},{9,25},{17,1},{25,9},{2,18},{10... | collective-permute-start | bytes 147464 | tf_op jit(solution)/shard_map/ppermute | solution.py:301
  22.6 1.1 %shard_map.98 = (bf16[1792,96]{1,0:T(8,128)(2,1)S(1)}, bf16[512,1792]{1,0:T(8,128)(2,1)S(1)}, bf16[512,1792]{1,0:T(8,128)(2,1)S(1)}) custom-call(bf16[96,256]{1,0:T(8,128)(2,1)S(1)} %add_convert_fusion.1.after.hid_own, bf16[96,1792]{1,0:T(8,128)(2,1)S(1)} %get-tuple-element.37.rows_ref, bf16[1792,512]{1,0:T(8,128)(2,1)S(1)} %get-tuple-element.35.w_gate, ...), custom_call_target="tpu_custom_call" | custom-call | tf_op jit(solution)/shard_map/pallas_call | solution.py:24
  23.8 2.6 %collective-permute-done.10.hid_far = bf16[96,256]{1,0:T(8,128)(2,1)S(1)} collective-permute-done((bf16[96,256]{1,0:T(8,128)(2,1)S(1)}, bf16[96,256]{1,0:T(8,128)(2,1)S(1)}, u32[]{:S(2)}, u32[]{:S(2)}) %collective-permute-start.10) | collective-permute-done | bytes 49184 | tf_op jit(solution)/shard_map/ppermute | solution.py:301
  26.6 0.4 %shard_map.100.own = f32[96,1792]{1,0:T(8,128)S(1)} custom-call(bf16[512,1792]{1,0:T(8,128)(2,1)S(1)} %get-tuple-element.38.gate_across, bf16[512,1792]{1,0:T(8,128)(2,1)S(1)} %get-tuple-element.39.up_across, bf16[96,512]{1,0:T(8,128)(2,1)S(1)} %shard_map.99.acts.acts_own), custom_call_target="tpu_custom_call" | custom-call | flops 176160768 | bytes 1835008 | tf_op jit(solution)/shard_map/pallas_call | solution.py:24
  27.0 0.8 %collective-permute-done.11.acts.acts_far = bf16[96,512]{1,0:T(8,128)(2,1)S(1)} collective-permute-done((bf16[96,512]{1,0:T(8,128)(2,1)S(1)}, bf16[96,512]{1,0:T(8,128)(2,1)S(1)}, u32[]{:S(2)}, u32[]{:S(2)}) %collective-permute-start.11) | collective-permute-done | bytes 98336 | tf_op jit(solution)/shard_map/ppermute | solution.py:301
  27.9 0.4 %shard_map.101 = (bf16[24,1792]{1,0:T(8,128)(2,1)S(1)}, bf16[24,1792]{1,0:T(8,128)(2,1)S(1)}, bf16[24,1792]{1,0:T(8,128)(2,1)S(1)}, bf16[24,1792]{1,0:T(8,128)(2,1)S(1)}) custom-call(bf16[512,1792]{1,0:T(8,128)(2,1)S(1)} %get-tuple-element.38.gate_across, bf16[512,1792]{1,0:T(8,128)(2,1)S(1)} %get-tuple-element.39.up_across, ...), custom_call_target="tpu_custom_call" | custom-call | flops 176160768 | bytes 1835008 | tf_op jit(solution)/shard_map/pallas_call | solution.py:24
  28.3 1.3 %collective-permute-start.12 = (bf16[24,1792]{1,0:T(8,128)(2,1)S(1)}, bf16[24,1792]{1,0:T(8,128)(2,1)S(1)}, u32[]{:S(2)}, u32[]{:S(2)}) collective-permute-start(bf16[24,1792]{1,0:T(8,128)(2,1)S(1)} %get-tuple-element.46), channel_id=1, source_target_pairs={{0,3},{1,2},{2,1},{3,0},{4,7},{5,6},{6,5},{7,4},{8,11},{9,10},{10,... | collective-permute-start | bytes 258056 | tf_op jit(solution)/shard_map/ppermute | solution.py:298
  29.6 0.9 %collective-permute-start.13 = (bf16[24,1792]{1,0:T(8,128)(2,1)S(1)}, bf16[24,1792]{1,0:T(8,128)(2,1)S(1)}, u32[]{:S(2)}, u32[]{:S(2)}) collective-permute-start(bf16[24,1792]{1,0:T(8,128)(2,1)S(1)} %get-tuple-element.47), channel_id=1, source_target_pairs={{0,2},{1,3},{2,0},{3,1},{4,6},{5,7},{6,4},{7,5},{8,10},{9,11},{10,... | collective-permute-start | bytes 258056 | tf_op jit(solution)/shard_map/ppermute | solution.py:298
  30.5 1.4 %collective-permute-start.14 = (bf16[24,1792]{1,0:T(8,128)(2,1)S(1)}, bf16[24,1792]{1,0:T(8,128)(2,1)S(1)}, u32[]{:S(2)}, u32[]{:S(2)}) collective-permute-start(bf16[24,1792]{1,0:T(8,128)(2,1)S(1)} %get-tuple-element.48), channel_id=1, source_target_pairs={{0,1},{1,0},{2,3},{3,2},{4,5},{5,4},{6,7},{7,6},{8,9},{9,8},{10,11... | collective-permute-start | bytes 258056 | tf_op jit(solution)/shard_map/ppermute | solution.py:298
  31.8 1.5 %shard_map.102 = (bf16[1792,512]{1,0:T(8,128)(2,1)}, f32[8,128]{1,0:T(8,128)S(1)}) custom-call(bf16[24,1792]{1,0:T(8,128)(2,1)S(1)} %get-tuple-element.43.after.refs_3_, bf16[1792,96]{1,0:T(8,128)(2,1)S(1)} %get-tuple-element.40.after.rows_ref, bf16[96,512]{1,0:T(8,128)(2,1)S(1)} %shard_map.99.acts.acts_own, ...), custom_call_target="tpu_custom_call" | custom-call | tf_op jit(solution)/shard_map/pallas_call | solution.py:24
  33.3 1.5 %shard_map.103 = (bf16[1792,512]{1,0:T(8,128)(2,1)}, f32[8,128]{1,0:T(8,128)S(1)}) custom-call(f32[8,128]{1,0:T(8,128)S(1)} %get-tuple-element.44.after, bf16[1792,96]{1,0:T(8,128)(2,1)S(1)} %get-tuple-element.40.after.rows_ref, bf16[96,512]{1,0:T(8,128)(2,1)S(1)} %shard_map.99.acts.acts_own, bf16[96,512]{1,0:T(8,128)(2,1)S(1)} %collective-permute-done.11.acts.acts_far), custom_call_target="tpu_custom_call" | custom-call | tf_op jit(solution)/shard_map/pallas_call | solution.py:24
  34.9 0.8 %collective-permute-done.14.refs_2_ = bf16[24,1792]{1,0:T(8,128)(2,1)S(1)} collective-permute-done((bf16[24,1792]{1,0:T(8,128)(2,1)S(1)}, bf16[24,1792]{1,0:T(8,128)(2,1)S(1)}, u32[]{:S(2)}, u32[]{:S(2)}) %collective-permute-start.14) | collective-permute-done | bytes 86048 | tf_op jit(solution)/shard_map/ppermute | solution.py:298
  35.7 2.2 %collective-permute-start.15 = (bf16[24,896]{1,0:T(8,128)(2,1)S(1)}, bf16[24,896]{1,0:T(8,128)(2,1)S(1)}, u32[]{:S(2)}, u32[]{:S(2)}) collective-permute-start(bf16[24,896]{1,0:T(8,128)(2,1)S(1)} %get-tuple-element.50), channel_id=1, source_target_pairs={{0,4},{1,5},{2,6},{3,7},{4,0},{5,1},{6,2},{7,3},{8,12},{9,13},{10,... | collective-permute-start | bytes 129032 | tf_op jit(solution)/shard_map/ppermute | solution.py:295
  38.0 2.8 %collective-permute-done.15.refs_3_ = bf16[24,896]{1,0:T(8,128)(2,1)S(1)} collective-permute-done((bf16[24,896]{1,0:T(8,128)(2,1)S(1)}, bf16[24,896]{1,0:T(8,128)(2,1)S(1)}, u32[]{:S(2)}, u32[]{:S(2)}) %collective-permute-start.15) | collective-permute-done | bytes 43040 | tf_op jit(solution)/shard_map/ppermute | solution.py:295
  40.7 1.2 %shard_map.105 = bf16[256,1792]{1,0:T(8,128)(2,1)} custom-call(bf16[48,256]{1,0:T(8,128)(2,1)S(1)} %get-tuple-element.28.after.refs_0_, bf16[48,256]{1,0:T(8,128)(2,1)S(1)} %get-tuple-element.29.refs_1_, bf16[24,896]{1,0:T(8,128)(2,1)S(1)} %get-tuple-element.49.refs_2_, bf16[24,896]{1,0:T(8,128)(2,1)S(1)} %collective-permute-done.15.refs_3_), custom_call_target="tpu_custom_call" | custom-call | flops 44040192 | bytes 917504 | tf_op jit(solution)/shard_map/pallas_call | solution.py:24
  (14 shorter events, 0.3 us)
Async XLA Ops:
  2.4 8.1 %collective-permute-start = (bf16[24,1792]{1,0:T(8,128)(2,1)S(1)}, bf16[24,1792]{1,0:T(8,128)(2,1)S(1)}, u32[]{:S(2)}, u32[]{:S(2)}) collective-permute-start(bf16[24,1792]{1,0:T(8,128)(2,1)S(1)} %get-tuple-element.31), channel_id=1, source_target_pairs={{0,4},{1,5},{2,6},{3,7},{4,0},{5,1},{6,2},{7,3},{8,12},{9,13},{10,... | collective-permute-start | bytes 258056 | tf_op jit(solution)/shard_map/ppermute | solution.py:295
  6.5 7.3 %collective-permute-start.2 = (bf16[24,1792]{1,0:T(8,128)(2,1)S(1)}, bf16[24,1792]{1,0:T(8,128)(2,1)S(1)}, u32[]{:S(2)}, u32[]{:S(2)}) collective-permute-start(bf16[24,1792]{1,0:T(8,128)(2,1)S(1)} %get-tuple-element.32.refs_7_), channel_id=1, source_target_pairs={{0,3},{1,2},{2,1},{3,0},{4,7},{5,6},{6,5},{7,4},{8,11},{9,10},{10,... | collective-permute-start | bytes 258056 | tf_op jit(solution)/shard_map/ppermute | solution.py:298
  9.1 8.0 %collective-permute-start.4 = (bf16[24,1792]{1,0:T(8,128)(2,1)S(1)}, bf16[24,1792]{1,0:T(8,128)(2,1)S(1)}, u32[]{:S(2)}, u32[]{:S(2)}) collective-permute-start(bf16[24,1792]{1,0:T(8,128)(2,1)S(1)} %get-tuple-element.32.refs_7_), channel_id=1, source_target_pairs={{0,2},{1,3},{2,0},{3,1},{4,6},{5,7},{6,4},{7,5},{8,10},{9,11},{10,... | collective-permute-start | bytes 258056 | tf_op jit(solution)/shard_map/ppermute | solution.py:298
  9.5 7.6 %collective-permute-start.6 = (bf16[24,1792]{1,0:T(8,128)(2,1)S(1)}, bf16[24,1792]{1,0:T(8,128)(2,1)S(1)}, u32[]{:S(2)}, u32[]{:S(2)}) collective-permute-start(bf16[24,1792]{1,0:T(8,128)(2,1)S(1)} %get-tuple-element.32.refs_7_), channel_id=1, source_target_pairs={{0,1},{1,0},{2,3},{3,2},{4,5},{5,4},{6,7},{7,6},{8,9},{9,8},{10,11... | collective-permute-start | bytes 258056 | tf_op jit(solution)/shard_map/ppermute | solution.py:298
  10.6 6.5 %collective-permute-start.1 = (bf16[24,1792]{1,0:T(8,128)(2,1)S(1)}, bf16[24,1792]{1,0:T(8,128)(2,1)S(1)}, u32[]{:S(2)}, u32[]{:S(2)}) collective-permute-start(bf16[24,1792]{1,0:T(8,128)(2,1)S(1)} %collective-permute-done.refs_6_), channel_id=1, source_target_pairs={{0,3},{1,2},{2,1},{3,0},{4,7},{5,6},{6,5},{7,4},{8,11},{9,10},{10,... | collective-permute-start | bytes 258056 | tf_op jit(solution)/shard_map/ppermute | solution.py:298
  12.8 4.7 %collective-permute-start.3 = (bf16[24,1792]{1,0:T(8,128)(2,1)S(1)}, bf16[24,1792]{1,0:T(8,128)(2,1)S(1)}, u32[]{:S(2)}, u32[]{:S(2)}) collective-permute-start(bf16[24,1792]{1,0:T(8,128)(2,1)S(1)} %collective-permute-done.refs_6_), channel_id=1, source_target_pairs={{0,2},{1,3},{2,0},{3,1},{4,6},{5,7},{6,4},{7,5},{8,10},{9,11},{10,... | collective-permute-start | bytes 258056 | tf_op jit(solution)/shard_map/ppermute | solution.py:298
  13.8 4.5 %collective-permute-start.5 = (bf16[24,1792]{1,0:T(8,128)(2,1)S(1)}, bf16[24,1792]{1,0:T(8,128)(2,1)S(1)}, u32[]{:S(2)}, u32[]{:S(2)}) collective-permute-start(bf16[24,1792]{1,0:T(8,128)(2,1)S(1)} %collective-permute-done.refs_6_), channel_id=1, source_target_pairs={{0,1},{1,0},{2,3},{3,2},{4,5},{5,4},{6,7},{7,6},{8,9},{9,8},{10,11... | collective-permute-start | bytes 258056 | tf_op jit(solution)/shard_map/ppermute | solution.py:298
  19.0 1.4 %collective-permute-start.8 = (bf16[96,512]{1,0:T(8,128)(2,1)S(1)}, bf16[96,512]{1,0:T(8,128)(2,1)S(1)}, u32[]{:S(2)}, u32[]{:S(2)}) collective-permute-start(bf16[96,512]{1,0:T(8,128)(2,1)S(1)} %get-tuple-element.42), channel_id=1, source_target_pairs={{0,8},{8,0},{16,24},{24,16},{1,9},{9,1},{17,25},{25,17},{2,10},{10... | collective-permute-start | bytes 294920 | tf_op jit(solution)/shard_map/ppermute | solution.py:301
  19.6 2.4 %collective-permute-start.7 = (bf16[96,256]{1,0:T(8,128)(2,1)S(1)}, bf16[96,256]{1,0:T(8,128)(2,1)S(1)}, u32[]{:S(2)}, u32[]{:S(2)}) collective-permute-start(bf16[96,256]{1,0:T(8,128)(2,1)S(1)} %get-tuple-element.34), channel_id=1, source_target_pairs={{0,8},{8,0},{16,24},{24,16},{1,9},{9,1},{17,25},{25,17},{2,10},{10... | collective-permute-start | bytes 147464 | tf_op jit(solution)/shard_map/ppermute | solution.py:301
  20.4 6.0 %collective-permute-start.9 = (bf16[96,512]{1,0:T(8,128)(2,1)S(1)}, bf16[96,512]{1,0:T(8,128)(2,1)S(1)}, u32[]{:S(2)}, u32[]{:S(2)}) collective-permute-start(bf16[96,512]{1,0:T(8,128)(2,1)S(1)} %add_convert_fusion.pre_own), channel_id=1, source_target_pairs={{0,16},{8,24},{16,0},{24,8},{1,17},{9,25},{17,1},{25,9},{2,18},{10... | collective-permute-start | bytes 294920 | tf_op jit(solution)/shard_map/ppermute | solution.py:301
  22.0 4.4 %collective-permute-start.10 = (bf16[96,256]{1,0:T(8,128)(2,1)S(1)}, bf16[96,256]{1,0:T(8,128)(2,1)S(1)}, u32[]{:S(2)}, u32[]{:S(2)}) collective-permute-start(bf16[96,256]{1,0:T(8,128)(2,1)S(1)} %add_convert_fusion.1.after.hid_own), channel_id=1, source_target_pairs={{0,16},{8,24},{16,0},{24,8},{1,17},{9,25},{17,1},{25,9},{2,18},{10... | collective-permute-start | bytes 147464 | tf_op jit(solution)/shard_map/ppermute | solution.py:301
  26.5 1.4 %collective-permute-start.11 = (bf16[96,512]{1,0:T(8,128)(2,1)S(1)}, bf16[96,512]{1,0:T(8,128)(2,1)S(1)}, u32[]{:S(2)}, u32[]{:S(2)}) collective-permute-start(bf16[96,512]{1,0:T(8,128)(2,1)S(1)} %shard_map.99.acts.acts_own), channel_id=1, source_target_pairs={{0,8},{8,0},{16,24},{24,16},{1,9},{9,1},{17,25},{25,17},{2,10},{10... | collective-permute-start | bytes 294920 | tf_op jit(solution)/shard_map/ppermute | solution.py:301
  28.3 6.6 %collective-permute-start.12 = (bf16[24,1792]{1,0:T(8,128)(2,1)S(1)}, bf16[24,1792]{1,0:T(8,128)(2,1)S(1)}, u32[]{:S(2)}, u32[]{:S(2)}) collective-permute-start(bf16[24,1792]{1,0:T(8,128)(2,1)S(1)} %get-tuple-element.46), channel_id=1, source_target_pairs={{0,3},{1,2},{2,1},{3,0},{4,7},{5,6},{6,5},{7,4},{8,11},{9,10},{10,... | collective-permute-start | bytes 258056 | tf_op jit(solution)/shard_map/ppermute | solution.py:298
  29.6 5.3 %collective-permute-start.13 = (bf16[24,1792]{1,0:T(8,128)(2,1)S(1)}, bf16[24,1792]{1,0:T(8,128)(2,1)S(1)}, u32[]{:S(2)}, u32[]{:S(2)}) collective-permute-start(bf16[24,1792]{1,0:T(8,128)(2,1)S(1)} %get-tuple-element.47), channel_id=1, source_target_pairs={{0,2},{1,3},{2,0},{3,1},{4,6},{5,7},{6,4},{7,5},{8,10},{9,11},{10,... | collective-permute-start | bytes 258056 | tf_op jit(solution)/shard_map/ppermute | solution.py:298
  30.5 5.2 %collective-permute-start.14 = (bf16[24,1792]{1,0:T(8,128)(2,1)S(1)}, bf16[24,1792]{1,0:T(8,128)(2,1)S(1)}, u32[]{:S(2)}, u32[]{:S(2)}) collective-permute-start(bf16[24,1792]{1,0:T(8,128)(2,1)S(1)} %get-tuple-element.48), channel_id=1, source_target_pairs={{0,1},{1,0},{2,3},{3,2},{4,5},{5,4},{6,7},{7,6},{8,9},{9,8},{10,11... | collective-permute-start | bytes 258056 | tf_op jit(solution)/shard_map/ppermute | solution.py:298
  35.7 5.0 %collective-permute-start.15 = (bf16[24,896]{1,0:T(8,128)(2,1)S(1)}, bf16[24,896]{1,0:T(8,128)(2,1)S(1)}, u32[]{:S(2)}, u32[]{:S(2)}) collective-permute-start(bf16[24,896]{1,0:T(8,128)(2,1)S(1)} %get-tuple-element.50), channel_id=1, source_target_pairs={{0,4},{1,5},{2,6},{3,7},{4,0},{5,1},{6,2},{7,3},{8,12},{9,13},{10,... | collective-permute-start | bytes 129032 | tf_op jit(solution)/shard_map/ppermute | solution.py:295

commit v8 on v7

--- a/solution.py
+++ b/solution.py
@@ -162,23 +162,35 @@
     return jnp.concatenate(rows, axis=0).astype(BF16)
 
 
-def forward_body(w_gate, w_up, *refs):
-    pieces, (rows_out, keep, send) = refs[:-3], refs[-3:]
+def pre_part(rows, w_gate, w_up, out, far):
     half = w_gate.shape[1] // 2
+    columns = core_columns(half, far)
+    out[:, :half] = dot(rows, w_gate[:, columns]).astype(BF16)
+    out[:, half:] = dot(rows, w_up[:, columns]).astype(BF16)
+
+
+def pre_send_body(w_gate, w_up, *refs):
+    pieces, (rows_out, send) = refs[:-2], refs[-2:]
     rows = take_rows(0, pieces)
     rows_out[...] = rows
-    for target, far in ((send, True), (keep, False)):
-        columns = core_columns(half, far)
-        target[:, :half] = dot(rows, w_gate[:, columns]).astype(BF16)
-        target[:, half:] = dot(rows, w_up[:, columns]).astype(BF16)
-
-
-def hidden_body(down_across, *refs):
-    pieces, (keep, send) = refs[:-2], refs[-2:]
+    pre_part(rows, w_gate, w_up, send, True)
+
+
+def pre_keep_body(after, w_gate, w_up, rows_ref, keep):
+    pre_part(rows_ref[...], w_gate, w_up, keep, False)
+
+
+def hidden_send_body(down_across, *refs):
+    pieces, (rows_out, send) = refs[:-2], refs[-2:]
     half = down_across.shape[1] // 2
     rows = take_rows(CAP, pieces)
-    for target, far in ((send, True), (keep, False)):
-        target[...] = dot(rows, down_across[:, core_columns(half, far)]).astype(BF16)
+    rows_out[...] = rows
+    send[...] = dot(rows, down_across[:, core_columns(half, True)]).astype(BF16)
+
+
+def hidden_keep_body(down_across, rows_ref, keep):
+    half = down_across.shape[1] // 2
+    keep[...] = dot(rows_ref[...], down_across[:, core_columns(half, False)]).astype(BF16)
 
 
 def transpose_body(after, rows_ref, w_gate, w_up, rows_across, gate_across, up_across):
@@ -190,15 +202,15 @@
     up_across[...] = w_up[...].T
 
 
-def activate_body(after, pre_own, pre_far, hid_own, hid_far, acts):
+def activate_body(after, pre_own, pre_far, hid_own, hid_far, gate_acts, up_acts):
     half = hid_own.shape[1]
     pre = pre_own[...].astype(F32) + pre_far[...].astype(F32)
     hidden_grad = hid_own[...].astype(F32) + hid_far[...].astype(F32)
     gate_pre = pre[:, :half]
     up_pre = pre[:, half:]
     sigma = jax.nn.sigmoid(gate_pre)
-    acts[:, :half] = (hidden_grad * up_pre * sigma * (1.0 + gate_pre * (1.0 - sigma))).astype(BF16)
-    acts[:, half:] = (hidden_grad * gate_pre * sigma).astype(BF16)
+    gate_acts[...] = (hidden_grad * up_pre * sigma * (1.0 + gate_pre * (1.0 - sigma))).astype(BF16)
+    up_acts[...] = (hidden_grad * gate_pre * sigma).astype(BF16)
 
 
 def fold_rows(rows, fold):
@@ -212,35 +224,35 @@
     ]
 
 
-def back_part(gate_across, up_across, acts, sibling):
-    half = gate_across.shape[0] // 2
-    units = core_columns(half, sibling)
-    part = dot(acts[:, :half], gate_across[units, :])
-    return part + dot(acts[:, half:], up_across[units, :])
-
-
-def back_own_body(gate_across, up_across, acts, total):
-    total[...] = back_part(gate_across, up_across, acts, False)
-
-
-def back_far_body(gate_across, up_across, acts, own, *outs):
+def back_part(across, acts, sibling):
+    return dot(acts[...], across[core_columns(across.shape[0] // 2, sibling), :])
+
+
+def back_own_body(gate_across, up_across, gate_acts, up_acts, total):
+    total[...] = back_part(gate_across, gate_acts, False) + back_part(up_across, up_acts, False)
+
+
+def back_gate_body(gate_across, gate_acts, own, total):
+    total[...] = own[...] + back_part(gate_across, gate_acts, True)
+
+
+def back_up_body(up_across, up_acts, own, *outs):
     count = outs[0].shape[0]
-    total = own[...] + back_part(gate_across, up_across, acts, True)
+    total = own[...] + back_part(up_across, up_acts, True)
     for place, out in enumerate(outs):
         out[...] = total[place * count : (place + 1) * count].astype(BF16)
 
 
-def weight_body(which, chunks, after, rows_ref, acts_own, acts_far, out, token, tile, sems):
+def weight_body(chunks, after, rows_ref, acts_own, acts_far, out, token, tile, sems):
     token[...] = jnp.zeros_like(token)
     half = out.shape[1] // 2
     depth = out.shape[0] // chunks
-    columns = slice(which * half, (which + 1) * half)
     stores = []
     for chunk in range(chunks):
         span = slice(chunk * depth, (chunk + 1) * depth)
         rows = rows_ref[span, :]
         for acts, far in ((acts_own, False), (acts_far, True)):
-            tile[span, core_columns(half, far)] = dot(rows, acts[:, columns]).astype(BF16)
+            tile[span, core_columns(half, far)] = dot(rows, acts[...]).astype(BF16)
         stores.append(pltpu.make_async_copy(tile.at[span], out.at[span], sems.at[chunk]))
         stores[-1].start()
     for store in stores:
@@ -334,15 +346,44 @@
     far = [away] + [to_peer(away, flip) for flip in range(1, HSPLIT)]
     pieces = [array for pair in zip(near, far) for array in pair][::-1]
 
-    rows_input, pre_keep, pre_send = run(
-        forward_body,
-        (shape((count, features)), shape((count, hidden)), shape((count, hidden))),
+    rows_input, pre_send = run(
+        pre_send_body,
+        (shape((count, features)), shape((count, hidden))),
         [VMEM] * (2 + len(pieces)),
-        2 * product,
+        product,
         4 * features * hidden,
         gate_here,
         up_here,
         *pieces,
+    )
+    rows_grad, hid_send = run(
+        hidden_send_body,
+        (shape((count, features)), shape((count, half))),
+        [VMEM] * (1 + len(pieces)),
+        product // 2,
+        2 * features * hidden,
+        down_across,
+        *pieces,
+    )
+    pre_keep = run(
+        pre_keep_body,
+        shape((count, hidden)),
+        [ANY] + [VMEM] * 3,
+        0,
+        0,
+        hid_send,
+        gate_here,
+        up_here,
+        rows_input,
+    )
+    hid_keep = run(
+        hidden_keep_body,
+        shape((count, half)),
+        [VMEM] * 2,
+        0,
+        0,
+        down_across,
+        rows_grad,
     )
 
     def spread_sum(keep, send):
@@ -357,15 +398,6 @@
         return near, far
 
     pre_own, pre_far = spread_sum(pre_keep, pre_send)
-    hid_keep, hid_send = run(
-        hidden_body,
-        (shape((count, half)), shape((count, half))),
-        [VMEM] * (1 + len(pieces)),
-        product,
-        2 * features * hidden,
-        down_across,
-        *pieces,
-    )
     hid_own, hid_far = spread_sum(hid_keep, hid_send)
     rows_across, gate_across, up_across = run(
         transpose_body,
@@ -378,9 +410,9 @@
         gate_here,
         up_here,
     )
-    acts = run(
+    gate_acts, up_acts = run(
         activate_body,
-        shape((count, hidden)),
+        (shape((count, half)),) * 2,
         [ANY] + [VMEM] * 4,
         20 * count * half,
         10 * count * half,
@@ -390,33 +422,44 @@
         hid_own,
         hid_far,
     )
-    acts_far = to_dp(acts, 1)
+    gate_other = to_dp(gate_acts, 1)
+    up_other = to_dp(up_acts, 1)
     back_own = run(
         back_own_body,
         shape((count, features), F32),
-        [VMEM] * 3,
-        product,
-        2 * features * hidden,
-        gate_across,
-        up_across,
-        acts,
-    )
-    back = run(
-        back_far_body,
-        (shape((count // HSPLIT, features)),) * HSPLIT,
         [VMEM] * 4,
         product,
         2 * features * hidden,
         gate_across,
         up_across,
-        acts_far,
+        gate_acts,
+        up_acts,
+    )
+    back_gate = run(
+        back_gate_body,
+        shape((count, features), F32),
+        [VMEM] * 3,
+        product // 2,
+        features * hidden,
+        gate_across,
+        gate_other,
         back_own,
     )
-
-    def weight_grad(which, after):
+    back = run(
+        back_up_body,
+        (shape((count // HSPLIT, features)),) * HSPLIT,
+        [VMEM] * 3,
+        product // 2,
+        features * hidden,
+        up_across,
+        up_other,
+        back_gate,
+    )
+
+    def weight_grad(acts, other, after):
         chunks = features // 256 if features % 256 == 0 else 2
         return run(
-            functools.partial(weight_body, which, chunks),
+            functools.partial(weight_body, chunks),
             (shape((features, hidden)), shape((8, 128), F32)),
             [ANY] + [VMEM] * 3,
             0,
@@ -424,13 +467,12 @@
             after,
             rows_across,
             acts,
-            acts_far,
+            other,
             out_spec=(HBM, VMEM),
             scratch=(pltpu.VMEM((features, hidden), BF16), dma((chunks,))),
         )
 
-    grad_gate, token = weight_grad(0, back[0])
-    grad_up, token = weight_grad(1, token)
+    grad_gate, token = weight_grad(gate_acts, gate_other, back[0])
     summed = run(
         functools.partial(gather_body, fold, experts),
         (shape((CAP * fold, features // fold)),) * experts,
@@ -441,6 +483,7 @@
         *(to_peer(back[flip], flip) for flip in range(HSPLIT - 1, 0, -1)),
         back[0],
     )
+    grad_up, _ = weight_grad(up_acts, up_other, summed[0])
     returned = [summed[0]] + [to_expert(summed[step], experts - step) for step in range(1, experts)]
     in_grad = run(
         functools.partial(scatter_body, fold),

time: 42.2 us -> 42.3 us (level)
  waiting for transfers between devices: 9.1 us -> 7.6 us
  Pallas kernels: 12 us -> 13 us
  starting transfers between devices: 20.1 us -> 20.6 us
    ppermute x2, waiting for transfers between devices: 3.29 us -> 1.2 us  [to_expert(): return lax.ppermute(value, 'expert', pairs)]
    ppermute x9, waiting for transfers between devices: 2.02 us -> 3.57 us  [to_peer(): lax.ppermute(value, 'expert', [(d, d ^ flip) for d in range(devices)])]
    pallas_call x12 -> x15, Pallas kernels: 12 us -> 13 us  [run(): pl.pallas_call(body, out_shape=outs, in_specs=specs, out_specs=out_spec i...]
    ppermute x5 -> x6, waiting for transfers between devices: 3.78 us -> 2.83 us  [to_dp(): return lax.ppermute(value, 'dp', [(d, d ^ flip) for d in range(spread)])]
    ppermute x5 -> x6, starting transfers between devices: 2.84 us -> 3.35 us  [to_dp(): return lax.ppermute(value, 'dp', [(d, d ^ flip) for d in range(spread)])]
  transfers between devices with their start and end apart: 16 -> 17, of which waited for: 8 -> 9; matrix products, arithmetic and copies ran while one was open for 0% -> 0% of each run, Pallas kernels for 18% -> 22%
where the time goes in v8:
time: 42.3 us; the launch traced here: 42 us
  starting transfers between devices  20.6 us (49%)
  Pallas kernels  13 us (31%)
  waiting for transfers between devices  7.6 us (18%)
  between operations  0.8 us (2%)
    pallas_call x15, Pallas kernels, run(): pl.pallas_call(body, out_shape=outs, in_specs=specs, out_specs=out_spec i...  13 us
    ppermute x9, starting transfers between devices, to_peer(): lax.ppermute(value, 'expert', [(d, d ^ flip) for d in range(devices)])  10.9 us
    ppermute x2, starting transfers between devices, to_expert(): return lax.ppermute(value, 'expert', pairs)  6.33 us
    ppermute x9, waiting for transfers between devices, to_peer(): lax.ppermute(value, 'expert', [(d, d ^ flip) for d in range(devices)])  3.57 us
    ppermute x6, starting transfers between devices, to_dp(): return lax.ppermute(value, 'dp', [(d, d ^ flip) for d in range(spread)])  3.35 us
    ppermute x6, waiting for transfers between devices, to_dp(): return lax.ppermute(value, 'dp', [(d, d ^ flip) for d in range(spread)])  2.83 us
    ppermute x2, waiting for transfers between devices, to_expert(): return lax.ppermute(value, 'expert', pairs)  1.2 us
  transfers between devices with their start and end apart: 17, of which 9 were waited for; matrix products, arithmetic and copies ran while one was open for 0% of the time, Pallas kernels for 22%

profile of v8, /device:TPU:0, one launch (start us, length us, event | category | flops | bytes accessed | tf_op | source)
XLA Modules:
  0.0 42.0 jit_solution(6340244000745156685)
XLA Ops:
  0.6 1.8 %shard_map.94 = (bf16[48,256]{1,0:T(8,128)(2,1)S(1)}, bf16[48,256]{1,0:T(8,128)(2,1)S(1)}, bf16[24,1792]{1,0:T(8,128)(2,1)S(1)}, bf16[24,1792]{1,0:T(8,128)(2,1)S(1)}) custom-call(s32[8,256]{1,0:T(8,128)} %bitcast.2, f32[8,256]{1,0:T(8,128)} %bitcast.3, bf16[256,1792]{1,0:T(8,128)(2,1)} %grads_hbm.1, bf16[256,1792]{1,0:T(8,128)(2,1)} %inputs_hbm.1), custom_call_target="tpu_custom_call" | custom-call | flops 88080384 | bytes 1835008 | tf_op jit(solution)/shard_map/pallas_call | solution.py:24
  2.4 4.1 %collective-permute-start = (bf16[24,1792]{1,0:T(8,128)(2,1)S(1)}, bf16[24,1792]{1,0:T(8,128)(2,1)S(1)}, u32[]{:S(2)}, u32[]{:S(2)}) collective-permute-start(bf16[24,1792]{1,0:T(8,128)(2,1)S(1)} %get-tuple-element.31), channel_id=1, source_target_pairs={{0,4},{1,5},{2,6},{3,7},{4,0},{5,1},{6,2},{7,3},{8,12},{9,13},{10,... | collective-permute-start | bytes 258056 | tf_op jit(solution)/shard_map/ppermute | solution.py:307
  6.5 2.5 %collective-permute-start.2 = (bf16[24,1792]{1,0:T(8,128)(2,1)S(1)}, bf16[24,1792]{1,0:T(8,128)(2,1)S(1)}, u32[]{:S(2)}, u32[]{:S(2)}) collective-permute-start(bf16[24,1792]{1,0:T(8,128)(2,1)S(1)} %get-tuple-element.32.refs_7_), channel_id=1, source_target_pairs={{0,3},{1,2},{2,1},{3,0},{4,7},{5,6},{6,5},{7,4},{8,11},{9,10},{10,... | collective-permute-start | bytes 258056 | tf_op jit(solution)/shard_map/ppermute | solution.py:310
  9.1 0.4 %collective-permute-start.4 = (bf16[24,1792]{1,0:T(8,128)(2,1)S(1)}, bf16[24,1792]{1,0:T(8,128)(2,1)S(1)}, u32[]{:S(2)}, u32[]{:S(2)}) collective-permute-start(bf16[24,1792]{1,0:T(8,128)(2,1)S(1)} %get-tuple-element.32.refs_7_), channel_id=1, source_target_pairs={{0,2},{1,3},{2,0},{3,1},{4,6},{5,7},{6,4},{7,5},{8,10},{9,11},{10,... | collective-permute-start | bytes 258056 | tf_op jit(solution)/shard_map/ppermute | solution.py:310
  9.5 0.5 %collective-permute-start.6 = (bf16[24,1792]{1,0:T(8,128)(2,1)S(1)}, bf16[24,1792]{1,0:T(8,128)(2,1)S(1)}, u32[]{:S(2)}, u32[]{:S(2)}) collective-permute-start(bf16[24,1792]{1,0:T(8,128)(2,1)S(1)} %get-tuple-element.32.refs_7_), channel_id=1, source_target_pairs={{0,1},{1,0},{2,3},{3,2},{4,5},{5,4},{6,7},{7,6},{8,9},{9,8},{10,11... | collective-permute-start | bytes 258056 | tf_op jit(solution)/shard_map/ppermute | solution.py:310
  10.0 0.5 %collective-permute-done.refs_6_ = bf16[24,1792]{1,0:T(8,128)(2,1)S(1)} collective-permute-done((bf16[24,1792]{1,0:T(8,128)(2,1)S(1)}, bf16[24,1792]{1,0:T(8,128)(2,1)S(1)}, u32[]{:S(2)}, u32[]{:S(2)}) %collective-permute-start) | collective-permute-done | bytes 86048 | tf_op jit(solution)/shard_map/ppermute | solution.py:307
  10.6 2.2 %collective-permute-start.1 = (bf16[24,1792]{1,0:T(8,128)(2,1)S(1)}, bf16[24,1792]{1,0:T(8,128)(2,1)S(1)}, u32[]{:S(2)}, u32[]{:S(2)}) collective-permute-start(bf16[24,1792]{1,0:T(8,128)(2,1)S(1)} %collective-permute-done.refs_6_), channel_id=1, source_target_pairs={{0,3},{1,2},{2,1},{3,0},{4,7},{5,6},{6,5},{7,4},{8,11},{9,10},{10,... | collective-permute-start | bytes 258056 | tf_op jit(solution)/shard_map/ppermute | solution.py:310
  12.8 1.0 %collective-permute-start.3 = (bf16[24,1792]{1,0:T(8,128)(2,1)S(1)}, bf16[24,1792]{1,0:T(8,128)(2,1)S(1)}, u32[]{:S(2)}, u32[]{:S(2)}) collective-permute-start(bf16[24,1792]{1,0:T(8,128)(2,1)S(1)} %collective-permute-done.refs_6_), channel_id=1, source_target_pairs={{0,2},{1,3},{2,0},{3,1},{4,6},{5,7},{6,4},{7,5},{8,10},{9,11},{10,... | collective-permute-start | bytes 258056 | tf_op jit(solution)/shard_map/ppermute | solution.py:310
  13.8 0.6 %collective-permute-start.5 = (bf16[24,1792]{1,0:T(8,128)(2,1)S(1)}, bf16[24,1792]{1,0:T(8,128)(2,1)S(1)}, u32[]{:S(2)}, u32[]{:S(2)}) collective-permute-start(bf16[24,1792]{1,0:T(8,128)(2,1)S(1)} %collective-permute-done.refs_6_), channel_id=1, source_target_pairs={{0,1},{1,0},{2,3},{3,2},{4,5},{5,4},{6,7},{7,6},{8,9},{9,8},{10,11... | collective-permute-start | bytes 258056 | tf_op jit(solution)/shard_map/ppermute | solution.py:310
  14.4 2.6 %shard_map.95 = (bf16[1792,512]{1,0:T(8,128)(2,1)S(1)}, bf16[1792,512]{1,0:T(8,128)(2,1)S(1)}, bf16[1792,512]{1,0:T(8,128)(2,1)S(1)}) custom-call(bf16[48,256]{1,0:T(8,128)(2,1)S(1)} %get-tuple-element.28.after.refs_0_, bf16[1792,512]{1,0:T(8,128)(2,1)} %refs_0_.1, bf16[1792,512]{1,0:T(8,128)(2,1)} %refs_1_.1, bf16[512,1792]{1,0:T(8,128)(2,1)} %refs_2_.1), custom_call_target="tpu_custom_call" | custom-call | bytes 5505024 | tf_op jit(solution)/shard_map/pallas_call | solution.py:24
  17.1 0.4 collective-permute-done.3.refs_2_
  17.5 0.8 %collective-permute-done.5.refs_4_ = bf16[24,1792]{1,0:T(8,128)(2,1)S(1)} collective-permute-done((bf16[24,1792]{1,0:T(8,128)(2,1)S(1)}, bf16[24,1792]{1,0:T(8,128)(2,1)S(1)}, u32[]{:S(2)}, u32[]{:S(2)}) %collective-permute-start.5) | collective-permute-done | bytes 86048 | tf_op jit(solution)/shard_map/ppermute | solution.py:310
  18.3 0.5 %shard_map.98 = (bf16[96,1792]{1,0:T(8,128)(2,1)S(1)}, bf16[96,512]{1,0:T(8,128)(2,1)S(1)}) custom-call(bf16[1792,512]{1,0:T(8,128)(2,1)S(1)} %get-tuple-element.35.w_gate, bf16[1792,512]{1,0:T(8,128)(2,1)S(1)} %get-tuple-element.36.w_up, bf16[24,1792]{1,0:T(8,128)(2,1)S(1)} %collective-permute-done.1.refs_0_, ...), custom_call_target="tpu_custom_call" | custom-call | flops 176160768 | bytes 3670016 | tf_op jit(solution)/shard_map/pallas_call | solution.py:24
  18.8 0.3 shard_map.96
  19.2 0.6 %collective-permute-start.7 = (bf16[96,256]{1,0:T(8,128)(2,1)S(1)}, bf16[96,256]{1,0:T(8,128)(2,1)S(1)}, u32[]{:S(2)}, u32[]{:S(2)}) collective-permute-start(bf16[96,256]{1,0:T(8,128)(2,1)S(1)} %get-tuple-element.34.after), channel_id=1, source_target_pairs={{0,8},{8,0},{16,24},{24,16},{1,9},{9,1},{17,25},{25,17},{2,10},{10... | collective-permute-start | bytes 147464 | tf_op jit(solution)/shard_map/ppermute | solution.py:313
  19.7 0.4 %shard_map.100 = bf16[96,512]{1,0:T(8,128)(2,1)S(1)} custom-call(bf16[96,256]{1,0:T(8,128)(2,1)S(1)} %get-tuple-element.34.after, bf16[1792,512]{1,0:T(8,128)(2,1)S(1)} %get-tuple-element.35.w_gate, bf16[1792,512]{1,0:T(8,128)(2,1)S(1)} %get-tuple-element.36.w_up, bf16[96,1792]{1,0:T(8,128)(2,1)S(1)} %get-tuple-element.37.rows_ref), custom_call_target="tpu_custom_call" | custom-call | tf_op jit(solution)/shard_map/pallas_call | solution.py:24
  20.5 1.6 %collective-permute-start.9 = (bf16[96,512]{1,0:T(8,128)(2,1)S(1)}, bf16[96,512]{1,0:T(8,128)(2,1)S(1)}, u32[]{:S(2)}, u32[]{:S(2)}) collective-permute-start(bf16[96,512]{1,0:T(8,128)(2,1)S(1)} %add_convert_fusion.pre_own), channel_id=1, source_target_pairs={{0,16},{8,24},{16,0},{24,8},{1,17},{9,25},{17,1},{25,9},{2,18},{10... | collective-permute-start | bytes 294920 | tf_op jit(solution)/shard_map/ppermute | solution.py:313
  22.1 0.6 %collective-permute-start.10 = (bf16[96,256]{1,0:T(8,128)(2,1)S(1)}, bf16[96,256]{1,0:T(8,128)(2,1)S(1)}, u32[]{:S(2)}, u32[]{:S(2)}) collective-permute-start(bf16[96,256]{1,0:T(8,128)(2,1)S(1)} %add_convert_fusion.1.after.hid_own), channel_id=1, source_target_pairs={{0,16},{8,24},{16,0},{24,8},{1,17},{9,25},{17,1},{25,9},{2,18},{10... | collective-permute-start | bytes 147464 | tf_op jit(solution)/shard_map/ppermute | solution.py:313
  22.7 1.1 %shard_map.99 = (bf16[1792,96]{1,0:T(8,128)(2,1)S(1)}, bf16[512,1792]{1,0:T(8,128)(2,1)S(1)}, bf16[512,1792]{1,0:T(8,128)(2,1)S(1)}) custom-call(bf16[96,256]{1,0:T(8,128)(2,1)S(1)} %add_convert_fusion.1.after.hid_own, bf16[96,1792]{1,0:T(8,128)(2,1)S(1)} %get-tuple-element.37.rows_ref, bf16[1792,512]{1,0:T(8,128)(2,1)S(1)} %get-tuple-element.35.w_gate, ...), custom_call_target="tpu_custom_call" | custom-call | tf_op jit(solution)/shard_map/pallas_call | solution.py:24
  23.8 2.5 %collective-permute-done.10.hid_far = bf16[96,256]{1,0:T(8,128)(2,1)S(1)} collective-permute-done((bf16[96,256]{1,0:T(8,128)(2,1)S(1)}, bf16[96,256]{1,0:T(8,128)(2,1)S(1)}, u32[]{:S(2)}, u32[]{:S(2)}) %collective-permute-start.10) | collective-permute-done | bytes 49184 | tf_op jit(solution)/shard_map/ppermute | solution.py:313
  26.5 0.5 %collective-permute-start.11 = (bf16[96,256]{1,0:T(8,128)(2,1)S(1)}, bf16[96,256]{1,0:T(8,128)(2,1)S(1)}, u32[]{:S(2)}, u32[]{:S(2)}) collective-permute-start(bf16[96,256]{1,0:T(8,128)(2,1)S(1)} %get-tuple-element.41.up_acts.acts_own), channel_id=1, source_target_pairs={{0,8},{8,0},{16,24},{24,16},{1,9},{9,1},{17,25},{25,17},{2,10},{10... | collective-permute-start | bytes 147464 | tf_op jit(solution)/shard_map/ppermute | solution.py:313
  27.0 0.4 %shard_map.102.own = f32[96,1792]{1,0:T(8,128)S(1)} custom-call(bf16[512,1792]{1,0:T(8,128)(2,1)S(1)} %get-tuple-element.42.gate_across, bf16[512,1792]{1,0:T(8,128)(2,1)S(1)} %get-tuple-element.38.up_across, bf16[96,256]{1,0:T(8,128)(2,1)S(1)} %get-tuple-element.43.gate_acts.acts_own, bf16[96,256]{1,0:T(8,128)(2,1)S(1)} %get-tuple-element.41.up_acts.acts_own), custom_call_target="tpu_custom_call" | custom-call | flops 176160768 | bytes 1835008 | tf_op jit(solution)/shard_map/pallas_call | solution.py:24
  28.3 1.3 %collective-permute-start.13 = (bf16[24,1792]{1,0:T(8,128)(2,1)S(1)}, bf16[24,1792]{1,0:T(8,128)(2,1)S(1)}, u32[]{:S(2)}, u32[]{:S(2)}) collective-permute-start(bf16[24,1792]{1,0:T(8,128)(2,1)S(1)} %get-tuple-element.46), channel_id=1, source_target_pairs={{0,3},{1,2},{2,1},{3,0},{4,7},{5,6},{6,5},{7,4},{8,11},{9,10},{10,... | collective-permute-start | bytes 258056 | tf_op jit(solution)/shard_map/ppermute | solution.py:310
  29.6 0.9 %collective-permute-start.14 = (bf16[24,1792]{1,0:T(8,128)(2,1)S(1)}, bf16[24,1792]{1,0:T(8,128)(2,1)S(1)}, u32[]{:S(2)}, u32[]{:S(2)}) collective-permute-start(bf16[24,1792]{1,0:T(8,128)(2,1)S(1)} %get-tuple-element.47), channel_id=1, source_target_pairs={{0,2},{1,3},{2,0},{3,1},{4,6},{5,7},{6,4},{7,5},{8,10},{9,11},{10,... | collective-permute-start | bytes 258056 | tf_op jit(solution)/shard_map/ppermute | solution.py:310
  30.5 1.4 %collective-permute-start.15 = (bf16[24,1792]{1,0:T(8,128)(2,1)S(1)}, bf16[24,1792]{1,0:T(8,128)(2,1)S(1)}, u32[]{:S(2)}, u32[]{:S(2)}) collective-permute-start(bf16[24,1792]{1,0:T(8,128)(2,1)S(1)} %get-tuple-element.48), channel_id=1, source_target_pairs={{0,1},{1,0},{2,3},{3,2},{4,5},{5,4},{6,7},{7,6},{8,9},{9,8},{10,11... | collective-permute-start | bytes 258056 | tf_op jit(solution)/shard_map/ppermute | solution.py:310
  31.9 1.5 %shard_map.105 = (bf16[1792,512]{1,0:T(8,128)(2,1)}, f32[8,128]{1,0:T(8,128)S(1)}) custom-call(bf16[24,1792]{1,0:T(8,128)(2,1)S(1)} %get-tuple-element.44.after.refs_3_, bf16[1792,96]{1,0:T(8,128)(2,1)S(1)} %get-tuple-element.39.after.rows_ref, bf16[96,256]{1,0:T(8,128)(2,1)S(1)} %get-tuple-element.43.gate_acts.acts_own, ...), custom_call_target="tpu_custom_call" | custom-call | tf_op jit(solution)/shard_map/pallas_call | solution.py:24
  33.4 1.3 %collective-permute-done.13.refs_0_ = bf16[24,1792]{1,0:T(8,128)(2,1)S(1)} collective-permute-done((bf16[24,1792]{1,0:T(8,128)(2,1)S(1)}, bf16[24,1792]{1,0:T(8,128)(2,1)S(1)}, u32[]{:S(2)}, u32[]{:S(2)}) %collective-permute-start.13) | collective-permute-done | bytes 86048 | tf_op jit(solution)/shard_map/ppermute | solution.py:310
  35.0 0.8 %collective-permute-done.15.refs_2_ = bf16[24,1792]{1,0:T(8,128)(2,1)S(1)} collective-permute-done((bf16[24,1792]{1,0:T(8,128)(2,1)S(1)}, bf16[24,1792]{1,0:T(8,128)(2,1)S(1)}, u32[]{:S(2)}, u32[]{:S(2)}) %collective-permute-start.15) | collective-permute-done | bytes 86048 | tf_op jit(solution)/shard_map/ppermute | solution.py:310
  35.8 2.2 %collective-permute-start.16 = (bf16[24,896]{1,0:T(8,128)(2,1)S(1)}, bf16[24,896]{1,0:T(8,128)(2,1)S(1)}, u32[]{:S(2)}, u32[]{:S(2)}) collective-permute-start(bf16[24,896]{1,0:T(8,128)(2,1)S(1)} %get-tuple-element.50), channel_id=1, source_target_pairs={{0,4},{1,5},{2,6},{3,7},{4,0},{5,1},{6,2},{7,3},{8,12},{9,13},{10,... | collective-permute-start | bytes 129032 | tf_op jit(solution)/shard_map/ppermute | solution.py:307
  38.1 2.1 %shard_map.108 = (bf16[1792,512]{1,0:T(8,128)(2,1)}, f32[8,128]{1,0:T(8,128)}) custom-call(bf16[24,896]{1,0:T(8,128)(2,1)S(1)} %get-tuple-element.49.refs_2_.after, bf16[1792,96]{1,0:T(8,128)(2,1)S(1)} %get-tuple-element.39.after.rows_ref, bf16[96,256]{1,0:T(8,128)(2,1)S(1)} %get-tuple-element.41.up_acts.acts_own, ...), custom_call_target="tpu_custom_call" | custom-call | tf_op jit(solution)/shard_map/pallas_call | solution.py:24
  40.2 0.7 %collective-permute-done.16.refs_3_ = bf16[24,896]{1,0:T(8,128)(2,1)S(1)} collective-permute-done((bf16[24,896]{1,0:T(8,128)(2,1)S(1)}, bf16[24,896]{1,0:T(8,128)(2,1)S(1)}, u32[]{:S(2)}, u32[]{:S(2)}) %collective-permute-start.16) | collective-permute-done | bytes 43040 | tf_op jit(solution)/shard_map/ppermute | solution.py:307
  40.8 1.2 %shard_map.107 = bf16[256,1792]{1,0:T(8,128)(2,1)} custom-call(bf16[48,256]{1,0:T(8,128)(2,1)S(1)} %get-tuple-element.28.after.refs_0_, bf16[48,256]{1,0:T(8,128)(2,1)S(1)} %get-tuple-element.29.refs_1_, bf16[24,896]{1,0:T(8,128)(2,1)S(1)} %get-tuple-element.49.refs_2_.after, bf16[24,896]{1,0:T(8,128)(2,1)S(1)} %collective-permute-done.16.refs_3_), custom_call_target="tpu_custom_call" | custom-call | flops 44040192 | bytes 917504 | tf_op jit(solution)/shard_map/pallas_call | solution.py:24
  (19 shorter events, 1.8 us)
Async XLA Ops:
  2.4 8.1 %collective-permute-start = (bf16[24,1792]{1,0:T(8,128)(2,1)S(1)}, bf16[24,1792]{1,0:T(8,128)(2,1)S(1)}, u32[]{:S(2)}, u32[]{:S(2)}) collective-permute-start(bf16[24,1792]{1,0:T(8,128)(2,1)S(1)} %get-tuple-element.31), channel_id=1, source_target_pairs={{0,4},{1,5},{2,6},{3,7},{4,0},{5,1},{6,2},{7,3},{8,12},{9,13},{10,... | collective-permute-start | bytes 258056 | tf_op jit(solution)/shard_map/ppermute | solution.py:307
  6.5 7.3 %collective-permute-start.2 = (bf16[24,1792]{1,0:T(8,128)(2,1)S(1)}, bf16[24,1792]{1,0:T(8,128)(2,1)S(1)}, u32[]{:S(2)}, u32[]{:S(2)}) collective-permute-start(bf16[24,1792]{1,0:T(8,128)(2,1)S(1)} %get-tuple-element.32.refs_7_), channel_id=1, source_target_pairs={{0,3},{1,2},{2,1},{3,0},{4,7},{5,6},{6,5},{7,4},{8,11},{9,10},{10,... | collective-permute-start | bytes 258056 | tf_op jit(solution)/shard_map/ppermute | solution.py:310
  9.1 8.0 %collective-permute-start.4 = (bf16[24,1792]{1,0:T(8,128)(2,1)S(1)}, bf16[24,1792]{1,0:T(8,128)(2,1)S(1)}, u32[]{:S(2)}, u32[]{:S(2)}) collective-permute-start(bf16[24,1792]{1,0:T(8,128)(2,1)S(1)} %get-tuple-element.32.refs_7_), channel_id=1, source_target_pairs={{0,2},{1,3},{2,0},{3,1},{4,6},{5,7},{6,4},{7,5},{8,10},{9,11},{10,... | collective-permute-start | bytes 258056 | tf_op jit(solution)/shard_map/ppermute | solution.py:310
  9.5 7.6 %collective-permute-start.6 = (bf16[24,1792]{1,0:T(8,128)(2,1)S(1)}, bf16[24,1792]{1,0:T(8,128)(2,1)S(1)}, u32[]{:S(2)}, u32[]{:S(2)}) collective-permute-start(bf16[24,1792]{1,0:T(8,128)(2,1)S(1)} %get-tuple-element.32.refs_7_), channel_id=1, source_target_pairs={{0,1},{1,0},{2,3},{3,2},{4,5},{5,4},{6,7},{7,6},{8,9},{9,8},{10,11... | collective-permute-start | bytes 258056 | tf_op jit(solution)/shard_map/ppermute | solution.py:310
  10.6 6.5 %collective-permute-start.1 = (bf16[24,1792]{1,0:T(8,128)(2,1)S(1)}, bf16[24,1792]{1,0:T(8,128)(2,1)S(1)}, u32[]{:S(2)}, u32[]{:S(2)}) collective-permute-start(bf16[24,1792]{1,0:T(8,128)(2,1)S(1)} %collective-permute-done.refs_6_), channel_id=1, source_target_pairs={{0,3},{1,2},{2,1},{3,0},{4,7},{5,6},{6,5},{7,4},{8,11},{9,10},{10,... | collective-permute-start | bytes 258056 | tf_op jit(solution)/shard_map/ppermute | solution.py:310
  12.8 4.7 %collective-permute-start.3 = (bf16[24,1792]{1,0:T(8,128)(2,1)S(1)}, bf16[24,1792]{1,0:T(8,128)(2,1)S(1)}, u32[]{:S(2)}, u32[]{:S(2)}) collective-permute-start(bf16[24,1792]{1,0:T(8,128)(2,1)S(1)} %collective-permute-done.refs_6_), channel_id=1, source_target_pairs={{0,2},{1,3},{2,0},{3,1},{4,6},{5,7},{6,4},{7,5},{8,10},{9,11},{10,... | collective-permute-start | bytes 258056 | tf_op jit(solution)/shard_map/ppermute | solution.py:310
  13.8 4.5 %collective-permute-start.5 = (bf16[24,1792]{1,0:T(8,128)(2,1)S(1)}, bf16[24,1792]{1,0:T(8,128)(2,1)S(1)}, u32[]{:S(2)}, u32[]{:S(2)}) collective-permute-start(bf16[24,1792]{1,0:T(8,128)(2,1)S(1)} %collective-permute-done.refs_6_), channel_id=1, source_target_pairs={{0,1},{1,0},{2,3},{3,2},{4,5},{5,4},{6,7},{7,6},{8,9},{9,8},{10,11... | collective-permute-start | bytes 258056 | tf_op jit(solution)/shard_map/ppermute | solution.py:310
  18.8 1.7 %collective-permute-start.8 = (bf16[96,512]{1,0:T(8,128)(2,1)S(1)}, bf16[96,512]{1,0:T(8,128)(2,1)S(1)}, u32[]{:S(2)}, u32[]{:S(2)}) collective-permute-start(bf16[96,512]{1,0:T(8,128)(2,1)S(1)} %get-tuple-element.40), channel_id=1, source_target_pairs={{0,8},{8,0},{16,24},{24,16},{1,9},{9,1},{17,25},{25,17},{2,10},{10... | collective-permute-start | bytes 294920 | tf_op jit(solution)/shard_map/ppermute | solution.py:313
  19.2 2.9 %collective-permute-start.7 = (bf16[96,256]{1,0:T(8,128)(2,1)S(1)}, bf16[96,256]{1,0:T(8,128)(2,1)S(1)}, u32[]{:S(2)}, u32[]{:S(2)}) collective-permute-start(bf16[96,256]{1,0:T(8,128)(2,1)S(1)} %get-tuple-element.34.after), channel_id=1, source_target_pairs={{0,8},{8,0},{16,24},{24,16},{1,9},{9,1},{17,25},{25,17},{2,10},{10... | collective-permute-start | bytes 147464 | tf_op jit(solution)/shard_map/ppermute | solution.py:313
  20.5 5.9 %collective-permute-start.9 = (bf16[96,512]{1,0:T(8,128)(2,1)S(1)}, bf16[96,512]{1,0:T(8,128)(2,1)S(1)}, u32[]{:S(2)}, u32[]{:S(2)}) collective-permute-start(bf16[96,512]{1,0:T(8,128)(2,1)S(1)} %add_convert_fusion.pre_own), channel_id=1, source_target_pairs={{0,16},{8,24},{16,0},{24,8},{1,17},{9,25},{17,1},{25,9},{2,18},{10... | collective-permute-start | bytes 294920 | tf_op jit(solution)/shard_map/ppermute | solution.py:313
  22.1 4.3 %collective-permute-start.10 = (bf16[96,256]{1,0:T(8,128)(2,1)S(1)}, bf16[96,256]{1,0:T(8,128)(2,1)S(1)}, u32[]{:S(2)}, u32[]{:S(2)}) collective-permute-start(bf16[96,256]{1,0:T(8,128)(2,1)S(1)} %add_convert_fusion.1.after.hid_own), channel_id=1, source_target_pairs={{0,16},{8,24},{16,0},{24,8},{1,17},{9,25},{17,1},{25,9},{2,18},{10... | collective-permute-start | bytes 147464 | tf_op jit(solution)/shard_map/ppermute | solution.py:313
  26.4 1.3 %collective-permute-start.12 = (bf16[96,256]{1,0:T(8,128)(2,1)S(1)}, bf16[96,256]{1,0:T(8,128)(2,1)S(1)}, u32[]{:S(2)}, u32[]{:S(2)}) collective-permute-start(bf16[96,256]{1,0:T(8,128)(2,1)S(1)} %get-tuple-element.43.gate_acts.acts_own), channel_id=1, source_target_pairs={{0,8},{8,0},{16,24},{24,16},{1,9},{9,1},{17,25},{25,17},{2,10},{10... | collective-permute-start | bytes 147464 | tf_op jit(solution)/shard_map/ppermute | solution.py:313
  26.5 1.5 %collective-permute-start.11 = (bf16[96,256]{1,0:T(8,128)(2,1)S(1)}, bf16[96,256]{1,0:T(8,128)(2,1)S(1)}, u32[]{:S(2)}, u32[]{:S(2)}) collective-permute-start(bf16[96,256]{1,0:T(8,128)(2,1)S(1)} %get-tuple-element.41.up_acts.acts_own), channel_id=1, source_target_pairs={{0,8},{8,0},{16,24},{24,16},{1,9},{9,1},{17,25},{25,17},{2,10},{10... | collective-permute-start | bytes 147464 | tf_op jit(solution)/shard_map/ppermute | solution.py:313
  28.3 6.3 %collective-permute-start.13 = (bf16[24,1792]{1,0:T(8,128)(2,1)S(1)}, bf16[24,1792]{1,0:T(8,128)(2,1)S(1)}, u32[]{:S(2)}, u32[]{:S(2)}) collective-permute-start(bf16[24,1792]{1,0:T(8,128)(2,1)S(1)} %get-tuple-element.46), channel_id=1, source_target_pairs={{0,3},{1,2},{2,1},{3,0},{4,7},{5,6},{6,5},{7,4},{8,11},{9,10},{10,... | collective-permute-start | bytes 258056 | tf_op jit(solution)/shard_map/ppermute | solution.py:310
  29.6 5.3 %collective-permute-start.14 = (bf16[24,1792]{1,0:T(8,128)(2,1)S(1)}, bf16[24,1792]{1,0:T(8,128)(2,1)S(1)}, u32[]{:S(2)}, u32[]{:S(2)}) collective-permute-start(bf16[24,1792]{1,0:T(8,128)(2,1)S(1)} %get-tuple-element.47), channel_id=1, source_target_pairs={{0,2},{1,3},{2,0},{3,1},{4,6},{5,7},{6,4},{7,5},{8,10},{9,11},{10,... | collective-permute-start | bytes 258056 | tf_op jit(solution)/shard_map/ppermute | solution.py:310
  30.5 5.2 %collective-permute-start.15 = (bf16[24,1792]{1,0:T(8,128)(2,1)S(1)}, bf16[24,1792]{1,0:T(8,128)(2,1)S(1)}, u32[]{:S(2)}, u32[]{:S(2)}) collective-permute-start(bf16[24,1792]{1,0:T(8,128)(2,1)S(1)} %get-tuple-element.48), channel_id=1, source_target_pairs={{0,1},{1,0},{2,3},{3,2},{4,5},{5,4},{6,7},{7,6},{8,9},{9,8},{10,11... | collective-permute-start | bytes 258056 | tf_op jit(solution)/shard_map/ppermute | solution.py:310
  35.8 5.0 %collective-permute-start.16 = (bf16[24,896]{1,0:T(8,128)(2,1)S(1)}, bf16[24,896]{1,0:T(8,128)(2,1)S(1)}, u32[]{:S(2)}, u32[]{:S(2)}) collective-permute-start(bf16[24,896]{1,0:T(8,128)(2,1)S(1)} %get-tuple-element.50), channel_id=1, source_target_pairs={{0,4},{1,5},{2,6},{3,7},{4,0},{5,1},{6,2},{7,3},{8,12},{9,13},{10,... | collective-permute-start | bytes 129032 | tf_op jit(solution)/shard_map/ppermute | solution.py:307

commit v9 on v7

--- a/solution.py
+++ b/solution.py
@@ -155,7 +155,8 @@
 
 def take_rows(offset, pieces):
     rows = []
-    for ref in pieces[::-1]:
+    far, near = pieces[:HSPLIT][::-1], pieces[-1:] + pieces[HSPLIT:-1]
+    for ref in [ref for pair in zip(near, far) for ref in pair]:
         piece = ref[...].astype(F32)
         for place in range(offset, piece.shape[0], 2 * CAP):
             rows.append(piece[place : place + CAP])
@@ -332,7 +333,7 @@
     near = [own[0]] + [to_peer(own[0], flip) for flip in range(1, HSPLIT)]
     away = away[0] if len(away) == 1 else jnp.concatenate(away, axis=0)
     far = [away] + [to_peer(away, flip) for flip in range(1, HSPLIT)]
-    pieces = [array for pair in zip(near, far) for array in pair][::-1]
+    pieces = far[::-1] + near[1:] + near[:1]
 
     rows_input, pre_keep, pre_send = run(
         forward_body,

time: 42.2 us -> 42.2 us (level)
  transfers between devices with their start and end apart: 16 -> 16, of which waited for: 8 -> 10; matrix products, arithmetic and copies ran while one was open for 0% -> 0% of each run, Pallas kernels for 18% -> 18%
where the time goes in v9:
time: 42.2 us; the launch traced here: 41.9 us
  starting transfers between devices  19.7 us (47%)
  Pallas kernels  12 us (28%)
  waiting for transfers between devices  9.48 us (22%)
  between operations  0.74 us (2%)
    pallas_call x12, Pallas kernels, run(): pl.pallas_call(body, out_shape=outs, in_specs=specs, out_specs=out_spec i...  12 us
    ppermute x9, starting transfers between devices, to_peer(): lax.ppermute(value, 'expert', [(d, d ^ flip) for d in range(devices)])  10.5 us
    ppermute x2, starting transfers between devices, to_expert(): return lax.ppermute(value, 'expert', pairs)  6.33 us
    ppermute x5, waiting for transfers between devices, to_dp(): return lax.ppermute(value, 'dp', [(d, d ^ flip) for d in range(spread)])  3.78 us
    ppermute x2, waiting for transfers between devices, to_expert(): return lax.ppermute(value, 'expert', pairs)  3.58 us
    ppermute x5, starting transfers between devices, to_dp(): return lax.ppermute(value, 'dp', [(d, d ^ flip) for d in range(spread)])  2.85 us
    ppermute x9, waiting for transfers between devices, to_peer(): lax.ppermute(value, 'expert', [(d, d ^ flip) for d in range(devices)])  2.12 us
  transfers between devices with their start and end apart: 16, of which 10 were waited for; matrix products, arithmetic and copies ran while one was open for 0% of the time, Pallas kernels for 18%

profile of v9, /device:TPU:0, one launch (start us, length us, event | category | flops | bytes accessed | tf_op | source)
XLA Modules:
  0.0 41.9 jit_solution(18080140034905767023)
XLA Ops:
  0.6 1.8 %shard_map.94 = (bf16[48,256]{1,0:T(8,128)(2,1)S(1)}, bf16[48,256]{1,0:T(8,128)(2,1)S(1)}, bf16[24,1792]{1,0:T(8,128)(2,1)S(1)}, bf16[24,1792]{1,0:T(8,128)(2,1)S(1)}) custom-call(s32[8,256]{1,0:T(8,128)} %bitcast.2, f32[8,256]{1,0:T(8,128)} %bitcast.3, bf16[256,1792]{1,0:T(8,128)(2,1)} %grads_hbm.1, bf16[256,1792]{1,0:T(8,128)(2,1)} %inputs_hbm.1), custom_call_target="tpu_custom_call" | custom-call | flops 88080384 | bytes 1835008 | tf_op jit(solution)/shard_map/pallas_call | solution.py:24
  2.4 4.1 %collective-permute-start = (bf16[24,1792]{1,0:T(8,128)(2,1)S(1)}, bf16[24,1792]{1,0:T(8,128)(2,1)S(1)}, u32[]{:S(2)}, u32[]{:S(2)}) collective-permute-start(bf16[24,1792]{1,0:T(8,128)(2,1)S(1)} %get-tuple-element.31), channel_id=1, source_target_pairs={{0,4},{1,5},{2,6},{3,7},{4,0},{5,1},{6,2},{7,3},{8,12},{9,13},{10,... | collective-permute-start | bytes 258056 | tf_op jit(solution)/shard_map/ppermute | solution.py:296
  6.5 1.5 %collective-permute-start.4 = (bf16[24,1792]{1,0:T(8,128)(2,1)S(1)}, bf16[24,1792]{1,0:T(8,128)(2,1)S(1)}, u32[]{:S(2)}, u32[]{:S(2)}) collective-permute-start(bf16[24,1792]{1,0:T(8,128)(2,1)S(1)} %get-tuple-element.32.refs_7_), channel_id=1, source_target_pairs={{0,1},{1,0},{2,3},{3,2},{4,5},{5,4},{6,7},{7,6},{8,9},{9,8},{10,11... | collective-permute-start | bytes 258056 | tf_op jit(solution)/shard_map/ppermute | solution.py:299
  8.1 1.6 %collective-permute-start.5 = (bf16[24,1792]{1,0:T(8,128)(2,1)S(1)}, bf16[24,1792]{1,0:T(8,128)(2,1)S(1)}, u32[]{:S(2)}, u32[]{:S(2)}) collective-permute-start(bf16[24,1792]{1,0:T(8,128)(2,1)S(1)} %get-tuple-element.32.refs_7_), channel_id=1, source_target_pairs={{0,2},{1,3},{2,0},{3,1},{4,6},{5,7},{6,4},{7,5},{8,10},{9,11},{10,... | collective-permute-start | bytes 258056 | tf_op jit(solution)/shard_map/ppermute | solution.py:299
  9.6 0.4 collective-permute-start.6
  10.0 0.8 %collective-permute-done.refs_3_ = bf16[24,1792]{1,0:T(8,128)(2,1)S(1)} collective-permute-done((bf16[24,1792]{1,0:T(8,128)(2,1)S(1)}, bf16[24,1792]{1,0:T(8,128)(2,1)S(1)}, u32[]{:S(2)}, u32[]{:S(2)}) %collective-permute-start) | collective-permute-done | bytes 86048 | tf_op jit(solution)/shard_map/ppermute | solution.py:296
  10.9 1.7 %collective-permute-start.1 = (bf16[24,1792]{1,0:T(8,128)(2,1)S(1)}, bf16[24,1792]{1,0:T(8,128)(2,1)S(1)}, u32[]{:S(2)}, u32[]{:S(2)}) collective-permute-start(bf16[24,1792]{1,0:T(8,128)(2,1)S(1)} %collective-permute-done.refs_3_), channel_id=1, source_target_pairs={{0,3},{1,2},{2,1},{3,0},{4,7},{5,6},{6,5},{7,4},{8,11},{9,10},{10,... | collective-permute-start | bytes 258056 | tf_op jit(solution)/shard_map/ppermute | solution.py:299
  12.6 1.2 %collective-permute-start.2 = (bf16[24,1792]{1,0:T(8,128)(2,1)S(1)}, bf16[24,1792]{1,0:T(8,128)(2,1)S(1)}, u32[]{:S(2)}, u32[]{:S(2)}) collective-permute-start(bf16[24,1792]{1,0:T(8,128)(2,1)S(1)} %collective-permute-done.refs_3_), channel_id=1, source_target_pairs={{0,2},{1,3},{2,0},{3,1},{4,6},{5,7},{6,4},{7,5},{8,10},{9,11},{10,... | collective-permute-start | bytes 258056 | tf_op jit(solution)/shard_map/ppermute | solution.py:299
  13.8 0.5 %collective-permute-start.3 = (bf16[24,1792]{1,0:T(8,128)(2,1)S(1)}, bf16[24,1792]{1,0:T(8,128)(2,1)S(1)}, u32[]{:S(2)}, u32[]{:S(2)}) collective-permute-start(bf16[24,1792]{1,0:T(8,128)(2,1)S(1)} %collective-permute-done.refs_3_), channel_id=1, source_target_pairs={{0,1},{1,0},{2,3},{3,2},{4,5},{5,4},{6,7},{7,6},{8,9},{9,8},{10,11... | collective-permute-start | bytes 258056 | tf_op jit(solution)/shard_map/ppermute | solution.py:299
  14.4 2.6 %shard_map.95 = (bf16[1792,512]{1,0:T(8,128)(2,1)S(1)}, bf16[1792,512]{1,0:T(8,128)(2,1)S(1)}, bf16[1792,512]{1,0:T(8,128)(2,1)S(1)}) custom-call(bf16[48,256]{1,0:T(8,128)(2,1)S(1)} %get-tuple-element.28.after.refs_0_, bf16[1792,512]{1,0:T(8,128)(2,1)} %refs_0_.1, bf16[1792,512]{1,0:T(8,128)(2,1)} %refs_1_.1, bf16[512,1792]{1,0:T(8,128)(2,1)} %refs_2_.1), custom_call_target="tpu_custom_call" | custom-call | bytes 5505024 | tf_op jit(solution)/shard_map/pallas_call | solution.py:24
  17.2 0.6 %collective-permute-done.2.refs_1_ = bf16[24,1792]{1,0:T(8,128)(2,1)S(1)} collective-permute-done((bf16[24,1792]{1,0:T(8,128)(2,1)S(1)}, bf16[24,1792]{1,0:T(8,128)(2,1)S(1)}, u32[]{:S(2)}, u32[]{:S(2)}) %collective-permute-start.2) | collective-permute-done | bytes 86048 | tf_op jit(solution)/shard_map/ppermute | solution.py:299
  17.8 0.5 %collective-permute-done.3.refs_2_ = bf16[24,1792]{1,0:T(8,128)(2,1)S(1)} collective-permute-done((bf16[24,1792]{1,0:T(8,128)(2,1)S(1)}, bf16[24,1792]{1,0:T(8,128)(2,1)S(1)}, u32[]{:S(2)}, u32[]{:S(2)}) %collective-permute-start.3) | collective-permute-done | bytes 86048 | tf_op jit(solution)/shard_map/ppermute | solution.py:299
  18.3 0.7 %shard_map.97 = (bf16[96,1792]{1,0:T(8,128)(2,1)S(1)}, bf16[96,512]{1,0:T(8,128)(2,1)S(1)}, bf16[96,512]{1,0:T(8,128)(2,1)S(1)}) custom-call(bf16[1792,512]{1,0:T(8,128)(2,1)S(1)} %get-tuple-element.35.w_gate, bf16[1792,512]{1,0:T(8,128)(2,1)S(1)} %get-tuple-element.36.w_up, bf16[24,1792]{1,0:T(8,128)(2,1)S(1)} %collective-permute-done.1.refs_0_, ...), custom_call_target="tpu_custom_call" | custom-call | flops 352321536 | bytes 3670016 | tf_op jit(solution)/shard_map/pallas_call | solution.py:24
  19.1 0.5 %shard_map.96 = (bf16[96,256]{1,0:T(8,128)(2,1)S(1)}, bf16[96,256]{1,0:T(8,128)(2,1)S(1)}) custom-call(bf16[1792,512]{1,0:T(8,128)(2,1)S(1)} %get-tuple-element.30.down_across, bf16[24,1792]{1,0:T(8,128)(2,1)S(1)} %collective-permute-done.1.refs_0_, bf16[24,1792]{1,0:T(8,128)(2,1)S(1)} %collective-permute-done.2.refs_1_, ...), custom_call_target="tpu_custom_call" | custom-call | flops 176160768 | bytes 1835008 | tf_op jit(solution)/shard_map/pallas_call | solution.py:24
  19.6 0.6 %collective-permute-start.7 = (bf16[96,256]{1,0:T(8,128)(2,1)S(1)}, bf16[96,256]{1,0:T(8,128)(2,1)S(1)}, u32[]{:S(2)}, u32[]{:S(2)}) collective-permute-start(bf16[96,256]{1,0:T(8,128)(2,1)S(1)} %get-tuple-element.34), channel_id=1, source_target_pairs={{0,8},{8,0},{16,24},{24,16},{1,9},{9,1},{17,25},{25,17},{2,10},{10... | collective-permute-start | bytes 147464 | tf_op jit(solution)/shard_map/ppermute | solution.py:302
  20.4 1.6 %collective-permute-start.9 = (bf16[96,512]{1,0:T(8,128)(2,1)S(1)}, bf16[96,512]{1,0:T(8,128)(2,1)S(1)}, u32[]{:S(2)}, u32[]{:S(2)}) collective-permute-start(bf16[96,512]{1,0:T(8,128)(2,1)S(1)} %add_convert_fusion.pre_own), channel_id=1, source_target_pairs={{0,16},{8,24},{16,0},{24,8},{1,17},{9,25},{17,1},{25,9},{2,18},{10... | collective-permute-start | bytes 294920 | tf_op jit(solution)/shard_map/ppermute | solution.py:302
  22.0 0.6 %collective-permute-start.10 = (bf16[96,256]{1,0:T(8,128)(2,1)S(1)}, bf16[96,256]{1,0:T(8,128)(2,1)S(1)}, u32[]{:S(2)}, u32[]{:S(2)}) collective-permute-start(bf16[96,256]{1,0:T(8,128)(2,1)S(1)} %add_convert_fusion.1.after.hid_own), channel_id=1, source_target_pairs={{0,16},{8,24},{16,0},{24,8},{1,17},{9,25},{17,1},{25,9},{2,18},{10... | collective-permute-start | bytes 147464 | tf_op jit(solution)/shard_map/ppermute | solution.py:302
  22.6 1.1 %shard_map.98 = (bf16[1792,96]{1,0:T(8,128)(2,1)S(1)}, bf16[512,1792]{1,0:T(8,128)(2,1)S(1)}, bf16[512,1792]{1,0:T(8,128)(2,1)S(1)}) custom-call(bf16[96,256]{1,0:T(8,128)(2,1)S(1)} %add_convert_fusion.1.after.hid_own, bf16[96,1792]{1,0:T(8,128)(2,1)S(1)} %get-tuple-element.37.rows_ref, bf16[1792,512]{1,0:T(8,128)(2,1)S(1)} %get-tuple-element.35.w_gate, ...), custom_call_target="tpu_custom_call" | custom-call | tf_op jit(solution)/shard_map/pallas_call | solution.py:24
  23.8 2.6 %collective-permute-done.10.hid_far = bf16[96,256]{1,0:T(8,128)(2,1)S(1)} collective-permute-done((bf16[96,256]{1,0:T(8,128)(2,1)S(1)}, bf16[96,256]{1,0:T(8,128)(2,1)S(1)}, u32[]{:S(2)}, u32[]{:S(2)}) %collective-permute-start.10) | collective-permute-done | bytes 49184 | tf_op jit(solution)/shard_map/ppermute | solution.py:302
  26.6 0.4 %shard_map.100.own = f32[96,1792]{1,0:T(8,128)S(1)} custom-call(bf16[512,1792]{1,0:T(8,128)(2,1)S(1)} %get-tuple-element.38.gate_across, bf16[512,1792]{1,0:T(8,128)(2,1)S(1)} %get-tuple-element.39.up_across, bf16[96,512]{1,0:T(8,128)(2,1)S(1)} %shard_map.99.acts.acts_own), custom_call_target="tpu_custom_call" | custom-call | flops 176160768 | bytes 1835008 | tf_op jit(solution)/shard_map/pallas_call | solution.py:24
  27.0 0.8 %collective-permute-done.11.acts.acts_far = bf16[96,512]{1,0:T(8,128)(2,1)S(1)} collective-permute-done((bf16[96,512]{1,0:T(8,128)(2,1)S(1)}, bf16[96,512]{1,0:T(8,128)(2,1)S(1)}, u32[]{:S(2)}, u32[]{:S(2)}) %collective-permute-start.11) | collective-permute-done | bytes 98336 | tf_op jit(solution)/shard_map/ppermute | solution.py:302
  27.9 0.4 %shard_map.101 = (bf16[24,1792]{1,0:T(8,128)(2,1)S(1)}, bf16[24,1792]{1,0:T(8,128)(2,1)S(1)}, bf16[24,1792]{1,0:T(8,128)(2,1)S(1)}, bf16[24,1792]{1,0:T(8,128)(2,1)S(1)}) custom-call(bf16[512,1792]{1,0:T(8,128)(2,1)S(1)} %get-tuple-element.38.gate_across, bf16[512,1792]{1,0:T(8,128)(2,1)S(1)} %get-tuple-element.39.up_across, ...), custom_call_target="tpu_custom_call" | custom-call | flops 176160768 | bytes 1835008 | tf_op jit(solution)/shard_map/pallas_call | solution.py:24
  28.3 1.5 %collective-permute-start.12 = (bf16[24,1792]{1,0:T(8,128)(2,1)S(1)}, bf16[24,1792]{1,0:T(8,128)(2,1)S(1)}, u32[]{:S(2)}, u32[]{:S(2)}) collective-permute-start(bf16[24,1792]{1,0:T(8,128)(2,1)S(1)} %get-tuple-element.46), channel_id=1, source_target_pairs={{0,3},{1,2},{2,1},{3,0},{4,7},{5,6},{6,5},{7,4},{8,11},{9,10},{10,... | collective-permute-start | bytes 258056 | tf_op jit(solution)/shard_map/ppermute | solution.py:299
  29.8 0.9 %collective-permute-start.13 = (bf16[24,1792]{1,0:T(8,128)(2,1)S(1)}, bf16[24,1792]{1,0:T(8,128)(2,1)S(1)}, u32[]{:S(2)}, u32[]{:S(2)}) collective-permute-start(bf16[24,1792]{1,0:T(8,128)(2,1)S(1)} %get-tuple-element.47), channel_id=1, source_target_pairs={{0,2},{1,3},{2,0},{3,1},{4,6},{5,7},{6,4},{7,5},{8,10},{9,11},{10,... | collective-permute-start | bytes 258056 | tf_op jit(solution)/shard_map/ppermute | solution.py:299
  30.7 1.1 %collective-permute-start.14 = (bf16[24,1792]{1,0:T(8,128)(2,1)S(1)}, bf16[24,1792]{1,0:T(8,128)(2,1)S(1)}, u32[]{:S(2)}, u32[]{:S(2)}) collective-permute-start(bf16[24,1792]{1,0:T(8,128)(2,1)S(1)} %get-tuple-element.48), channel_id=1, source_target_pairs={{0,1},{1,0},{2,3},{3,2},{4,5},{5,4},{6,7},{7,6},{8,9},{9,8},{10,11... | collective-permute-start | bytes 258056 | tf_op jit(solution)/shard_map/ppermute | solution.py:299
  31.8 1.5 %shard_map.102 = (bf16[1792,512]{1,0:T(8,128)(2,1)}, f32[8,128]{1,0:T(8,128)S(1)}) custom-call(bf16[24,1792]{1,0:T(8,128)(2,1)S(1)} %get-tuple-element.43.after.refs_3_, bf16[1792,96]{1,0:T(8,128)(2,1)S(1)} %get-tuple-element.40.after.rows_ref, bf16[96,512]{1,0:T(8,128)(2,1)S(1)} %shard_map.99.acts.acts_own, ...), custom_call_target="tpu_custom_call" | custom-call | tf_op jit(solution)/shard_map/pallas_call | solution.py:24
  33.3 1.5 %shard_map.103 = (bf16[1792,512]{1,0:T(8,128)(2,1)}, f32[8,128]{1,0:T(8,128)S(1)}) custom-call(f32[8,128]{1,0:T(8,128)S(1)} %get-tuple-element.44.after, bf16[1792,96]{1,0:T(8,128)(2,1)S(1)} %get-tuple-element.40.after.rows_ref, bf16[96,512]{1,0:T(8,128)(2,1)S(1)} %shard_map.99.acts.acts_own, bf16[96,512]{1,0:T(8,128)(2,1)S(1)} %collective-permute-done.11.acts.acts_far), custom_call_target="tpu_custom_call" | custom-call | tf_op jit(solution)/shard_map/pallas_call | solution.py:24
  34.9 0.3 collective-permute-done.13.refs_1_
  35.1 0.5 %collective-permute-done.14.refs_2_ = bf16[24,1792]{1,0:T(8,128)(2,1)S(1)} collective-permute-done((bf16[24,1792]{1,0:T(8,128)(2,1)S(1)}, bf16[24,1792]{1,0:T(8,128)(2,1)S(1)}, u32[]{:S(2)}, u32[]{:S(2)}) %collective-permute-start.14) | collective-permute-done | bytes 86048 | tf_op jit(solution)/shard_map/ppermute | solution.py:299
  35.7 2.2 %collective-permute-start.15 = (bf16[24,896]{1,0:T(8,128)(2,1)S(1)}, bf16[24,896]{1,0:T(8,128)(2,1)S(1)}, u32[]{:S(2)}, u32[]{:S(2)}) collective-permute-start(bf16[24,896]{1,0:T(8,128)(2,1)S(1)} %get-tuple-element.50), channel_id=1, source_target_pairs={{0,4},{1,5},{2,6},{3,7},{4,0},{5,1},{6,2},{7,3},{8,12},{9,13},{10,... | collective-permute-start | bytes 129032 | tf_op jit(solution)/shard_map/ppermute | solution.py:296
  38.0 2.8 %collective-permute-done.15.refs_3_ = bf16[24,896]{1,0:T(8,128)(2,1)S(1)} collective-permute-done((bf16[24,896]{1,0:T(8,128)(2,1)S(1)}, bf16[24,896]{1,0:T(8,128)(2,1)S(1)}, u32[]{:S(2)}, u32[]{:S(2)}) %collective-permute-start.15) | collective-permute-done | bytes 43040 | tf_op jit(solution)/shard_map/ppermute | solution.py:296
  40.7 1.2 %shard_map.105 = bf16[256,1792]{1,0:T(8,128)(2,1)} custom-call(bf16[48,256]{1,0:T(8,128)(2,1)S(1)} %get-tuple-element.28.after.refs_0_, bf16[48,256]{1,0:T(8,128)(2,1)S(1)} %get-tuple-element.29.refs_1_, bf16[24,896]{1,0:T(8,128)(2,1)S(1)} %get-tuple-element.49.refs_2_, bf16[24,896]{1,0:T(8,128)(2,1)S(1)} %collective-permute-done.15.refs_3_), custom_call_target="tpu_custom_call" | custom-call | flops 44040192 | bytes 917504 | tf_op jit(solution)/shard_map/pallas_call | solution.py:24
  (14 shorter events, 0.8 us)
Async XLA Ops:
  2.4 8.4 %collective-permute-start = (bf16[24,1792]{1,0:T(8,128)(2,1)S(1)}, bf16[24,1792]{1,0:T(8,128)(2,1)S(1)}, u32[]{:S(2)}, u32[]{:S(2)}) collective-permute-start(bf16[24,1792]{1,0:T(8,128)(2,1)S(1)} %get-tuple-element.31), channel_id=1, source_target_pairs={{0,4},{1,5},{2,6},{3,7},{4,0},{5,1},{6,2},{7,3},{8,12},{9,13},{10,... | collective-permute-start | bytes 258056 | tf_op jit(solution)/shard_map/ppermute | solution.py:296
  6.5 7.3 %collective-permute-start.4 = (bf16[24,1792]{1,0:T(8,128)(2,1)S(1)}, bf16[24,1792]{1,0:T(8,128)(2,1)S(1)}, u32[]{:S(2)}, u32[]{:S(2)}) collective-permute-start(bf16[24,1792]{1,0:T(8,128)(2,1)S(1)} %get-tuple-element.32.refs_7_), channel_id=1, source_target_pairs={{0,1},{1,0},{2,3},{3,2},{4,5},{5,4},{6,7},{7,6},{8,9},{9,8},{10,11... | collective-permute-start | bytes 258056 | tf_op jit(solution)/shard_map/ppermute | solution.py:299
  8.1 8.9 %collective-permute-start.5 = (bf16[24,1792]{1,0:T(8,128)(2,1)S(1)}, bf16[24,1792]{1,0:T(8,128)(2,1)S(1)}, u32[]{:S(2)}, u32[]{:S(2)}) collective-permute-start(bf16[24,1792]{1,0:T(8,128)(2,1)S(1)} %get-tuple-element.32.refs_7_), channel_id=1, source_target_pairs={{0,2},{1,3},{2,0},{3,1},{4,6},{5,7},{6,4},{7,5},{8,10},{9,11},{10,... | collective-permute-start | bytes 258056 | tf_op jit(solution)/shard_map/ppermute | solution.py:299
  9.6 7.4 %collective-permute-start.6 = (bf16[24,1792]{1,0:T(8,128)(2,1)S(1)}, bf16[24,1792]{1,0:T(8,128)(2,1)S(1)}, u32[]{:S(2)}, u32[]{:S(2)}) collective-permute-start(bf16[24,1792]{1,0:T(8,128)(2,1)S(1)} %get-tuple-element.32.refs_7_), channel_id=1, source_target_pairs={{0,3},{1,2},{2,1},{3,0},{4,7},{5,6},{6,5},{7,4},{8,11},{9,10},{10,... | collective-permute-start | bytes 258056 | tf_op jit(solution)/shard_map/ppermute | solution.py:299
  10.9 6.4 %collective-permute-start.1 = (bf16[24,1792]{1,0:T(8,128)(2,1)S(1)}, bf16[24,1792]{1,0:T(8,128)(2,1)S(1)}, u32[]{:S(2)}, u32[]{:S(2)}) collective-permute-start(bf16[24,1792]{1,0:T(8,128)(2,1)S(1)} %collective-permute-done.refs_3_), channel_id=1, source_target_pairs={{0,3},{1,2},{2,1},{3,0},{4,7},{5,6},{6,5},{7,4},{8,11},{9,10},{10,... | collective-permute-start | bytes 258056 | tf_op jit(solution)/shard_map/ppermute | solution.py:299
  12.6 5.2 %collective-permute-start.2 = (bf16[24,1792]{1,0:T(8,128)(2,1)S(1)}, bf16[24,1792]{1,0:T(8,128)(2,1)S(1)}, u32[]{:S(2)}, u32[]{:S(2)}) collective-permute-start(bf16[24,1792]{1,0:T(8,128)(2,1)S(1)} %collective-permute-done.refs_3_), channel_id=1, source_target_pairs={{0,2},{1,3},{2,0},{3,1},{4,6},{5,7},{6,4},{7,5},{8,10},{9,11},{10,... | collective-permute-start | bytes 258056 | tf_op jit(solution)/shard_map/ppermute | solution.py:299
  13.8 4.5 %collective-permute-start.3 = (bf16[24,1792]{1,0:T(8,128)(2,1)S(1)}, bf16[24,1792]{1,0:T(8,128)(2,1)S(1)}, u32[]{:S(2)}, u32[]{:S(2)}) collective-permute-start(bf16[24,1792]{1,0:T(8,128)(2,1)S(1)} %collective-permute-done.refs_3_), channel_id=1, source_target_pairs={{0,1},{1,0},{2,3},{3,2},{4,5},{5,4},{6,7},{7,6},{8,9},{9,8},{10,11... | collective-permute-start | bytes 258056 | tf_op jit(solution)/shard_map/ppermute | solution.py:299
  19.0 1.4 %collective-permute-start.8 = (bf16[96,512]{1,0:T(8,128)(2,1)S(1)}, bf16[96,512]{1,0:T(8,128)(2,1)S(1)}, u32[]{:S(2)}, u32[]{:S(2)}) collective-permute-start(bf16[96,512]{1,0:T(8,128)(2,1)S(1)} %get-tuple-element.42), channel_id=1, source_target_pairs={{0,8},{8,0},{16,24},{24,16},{1,9},{9,1},{17,25},{25,17},{2,10},{10... | collective-permute-start | bytes 294920 | tf_op jit(solution)/shard_map/ppermute | solution.py:302
  19.6 2.4 %collective-permute-start.7 = (bf16[96,256]{1,0:T(8,128)(2,1)S(1)}, bf16[96,256]{1,0:T(8,128)(2,1)S(1)}, u32[]{:S(2)}, u32[]{:S(2)}) collective-permute-start(bf16[96,256]{1,0:T(8,128)(2,1)S(1)} %get-tuple-element.34), channel_id=1, source_target_pairs={{0,8},{8,0},{16,24},{24,16},{1,9},{9,1},{17,25},{25,17},{2,10},{10... | collective-permute-start | bytes 147464 | tf_op jit(solution)/shard_map/ppermute | solution.py:302
  20.4 6.0 %collective-permute-start.9 = (bf16[96,512]{1,0:T(8,128)(2,1)S(1)}, bf16[96,512]{1,0:T(8,128)(2,1)S(1)}, u32[]{:S(2)}, u32[]{:S(2)}) collective-permute-start(bf16[96,512]{1,0:T(8,128)(2,1)S(1)} %add_convert_fusion.pre_own), channel_id=1, source_target_pairs={{0,16},{8,24},{16,0},{24,8},{1,17},{9,25},{17,1},{25,9},{2,18},{10... | collective-permute-start | bytes 294920 | tf_op jit(solution)/shard_map/ppermute | solution.py:302
  22.0 4.4 %collective-permute-start.10 = (bf16[96,256]{1,0:T(8,128)(2,1)S(1)}, bf16[96,256]{1,0:T(8,128)(2,1)S(1)}, u32[]{:S(2)}, u32[]{:S(2)}) collective-permute-start(bf16[96,256]{1,0:T(8,128)(2,1)S(1)} %add_convert_fusion.1.after.hid_own), channel_id=1, source_target_pairs={{0,16},{8,24},{16,0},{24,8},{1,17},{9,25},{17,1},{25,9},{2,18},{10... | collective-permute-start | bytes 147464 | tf_op jit(solution)/shard_map/ppermute | solution.py:302
  26.5 1.4 %collective-permute-start.11 = (bf16[96,512]{1,0:T(8,128)(2,1)S(1)}, bf16[96,512]{1,0:T(8,128)(2,1)S(1)}, u32[]{:S(2)}, u32[]{:S(2)}) collective-permute-start(bf16[96,512]{1,0:T(8,128)(2,1)S(1)} %shard_map.99.acts.acts_own), channel_id=1, source_target_pairs={{0,8},{8,0},{16,24},{24,16},{1,9},{9,1},{17,25},{25,17},{2,10},{10... | collective-permute-start | bytes 294920 | tf_op jit(solution)/shard_map/ppermute | solution.py:302
  28.3 6.6 %collective-permute-start.12 = (bf16[24,1792]{1,0:T(8,128)(2,1)S(1)}, bf16[24,1792]{1,0:T(8,128)(2,1)S(1)}, u32[]{:S(2)}, u32[]{:S(2)}) collective-permute-start(bf16[24,1792]{1,0:T(8,128)(2,1)S(1)} %get-tuple-element.46), channel_id=1, source_target_pairs={{0,3},{1,2},{2,1},{3,0},{4,7},{5,6},{6,5},{7,4},{8,11},{9,10},{10,... | collective-permute-start | bytes 258056 | tf_op jit(solution)/shard_map/ppermute | solution.py:299
  29.8 5.3 %collective-permute-start.13 = (bf16[24,1792]{1,0:T(8,128)(2,1)S(1)}, bf16[24,1792]{1,0:T(8,128)(2,1)S(1)}, u32[]{:S(2)}, u32[]{:S(2)}) collective-permute-start(bf16[24,1792]{1,0:T(8,128)(2,1)S(1)} %get-tuple-element.47), channel_id=1, source_target_pairs={{0,2},{1,3},{2,0},{3,1},{4,6},{5,7},{6,4},{7,5},{8,10},{9,11},{10,... | collective-permute-start | bytes 258056 | tf_op jit(solution)/shard_map/ppermute | solution.py:299
  30.7 4.9 %collective-permute-start.14 = (bf16[24,1792]{1,0:T(8,128)(2,1)S(1)}, bf16[24,1792]{1,0:T(8,128)(2,1)S(1)}, u32[]{:S(2)}, u32[]{:S(2)}) collective-permute-start(bf16[24,1792]{1,0:T(8,128)(2,1)S(1)} %get-tuple-element.48), channel_id=1, source_target_pairs={{0,1},{1,0},{2,3},{3,2},{4,5},{5,4},{6,7},{7,6},{8,9},{9,8},{10,11... | collective-permute-start | bytes 258056 | tf_op jit(solution)/shard_map/ppermute | solution.py:299
  35.7 5.0 %collective-permute-start.15 = (bf16[24,896]{1,0:T(8,128)(2,1)S(1)}, bf16[24,896]{1,0:T(8,128)(2,1)S(1)}, u32[]{:S(2)}, u32[]{:S(2)}) collective-permute-start(bf16[24,896]{1,0:T(8,128)(2,1)S(1)} %get-tuple-element.50), channel_id=1, source_target_pairs={{0,4},{1,5},{2,6},{3,7},{4,0},{5,1},{6,2},{7,3},{8,12},{9,13},{10,... | collective-permute-start | bytes 129032 | tf_op jit(solution)/shard_map/ppermute | solution.py:296

commit v10 on v9

--- a/solution.py
+++ b/solution.py
@@ -182,7 +182,11 @@
         target[...] = dot(rows, down_across[:, core_columns(half, far)]).astype(BF16)
 
 
-def transpose_body(after, rows_ref, w_gate, w_up, rows_across, gate_across, up_across):
+def transpose_body(after, rows_ref, w_gate, w_up, *refs):
+    count = (len(refs) - 3) // 2
+    picks, (rows_across, gate_across, up_across) = refs[:count], refs[count : count + 3]
+    for pick, across in zip(picks, refs[count + 3 :]):
+        across[...] = pick[...].astype(F32).T.astype(BF16)
     rows = rows_ref[...]
     count = rows.shape[0]
     same = (iota((count, count), 0) == iota((count, count), 1)).astype(F32).astype(BF16)
@@ -268,7 +272,7 @@
     for part in range(fold):
         for span in column_spans(width):
             target = slice(part * width + span.start, part * width + span.stop)
-            tile[:, target] = dot(picks[part][...], returned[:, span], 0, 0).astype(BF16)
+            tile[:, target] = dot(picks[part][...], returned[:, span]).astype(BF16)
             store = pltpu.make_async_copy(
                 tile.at[:, target], out.at[:, target], sems.at[len(stores)]
             )
@@ -368,16 +372,19 @@
         *pieces,
     )
     hid_own, hid_far = spread_sum(hid_keep, hid_send)
-    rows_across, gate_across, up_across = run(
+    rows_across, gate_across, up_across, *picks_across = run(
         transpose_body,
-        (shape((features, count)),) + (shape((hidden, features)),) * 2,
-        [ANY] + [VMEM] * 3,
+        (shape((features, count)),)
+        + (shape((hidden, features)),) * 2
+        + tuple(shape(pick.shape[::-1]) for pick in picks),
+        [ANY] + [VMEM] * (3 + fold),
         0,
         0,
         hid_own,
         rows_input,
         gate_here,
         up_here,
+        *picks,
     )
     acts = run(
         activate_body,
@@ -449,7 +456,7 @@
         [VMEM] * (fold + experts),
         4 * experts * CAP * tokens * features,
         2 * tokens * features,
-        *picks,
+        *picks_across,
         *returned,
         out_spec=HBM,
         scratch=(

time: 42.2 us -> 42.1 us (level)
  no operation moved by 1% of the time
where the time goes in v10:
time: 42.1 us; the launch traced here: 41.9 us
  starting transfers between devices  19.7 us (47%)
  Pallas kernels  12 us (29%)
  waiting for transfers between devices  9.43 us (22%)
  between operations  0.74 us (2%)
    pallas_call x12, Pallas kernels, run(): pl.pallas_call(body, out_shape=outs, in_specs=specs, out_specs=out_spec i...  12 us
    ppermute x9, starting transfers between devices, to_peer(): lax.ppermute(value, 'expert', [(d, d ^ flip) for d in range(devices)])  10.5 us
    ppermute x2, starting transfers between devices, to_expert(): return lax.ppermute(value, 'expert', pairs)  6.33 us
    ppermute x5, waiting for transfers between devices, to_dp(): return lax.ppermute(value, 'dp', [(d, d ^ flip) for d in range(spread)])  3.72 us
    ppermute x2, waiting for transfers between devices, to_expert(): return lax.ppermute(value, 'expert', pairs)  3.58 us
    ppermute x5, starting transfers between devices, to_dp(): return lax.ppermute(value, 'dp', [(d, d ^ flip) for d in range(spread)])  2.85 us
    ppermute x9, waiting for transfers between devices, to_peer(): lax.ppermute(value, 'expert', [(d, d ^ flip) for d in range(devices)])  2.12 us
  transfers between devices with their start and end apart: 16, of which 10 were waited for; matrix products, arithmetic and copies ran while one was open for 0% of the time, Pallas kernels for 18%

profile of v10, /device:TPU:0, one launch (start us, length us, event | category | flops | bytes accessed | tf_op | source)
XLA Modules:
  0.0 41.9 jit_solution(2939070076241172847)
XLA Ops:
  0.6 1.8 %shard_map.94 = (bf16[48,256]{1,0:T(8,128)(2,1)S(1)}, bf16[48,256]{1,0:T(8,128)(2,1)S(1)}, bf16[24,1792]{1,0:T(8,128)(2,1)S(1)}, bf16[24,1792]{1,0:T(8,128)(2,1)S(1)}) custom-call(s32[8,256]{1,0:T(8,128)} %bitcast.2, f32[8,256]{1,0:T(8,128)} %bitcast.3, bf16[256,1792]{1,0:T(8,128)(2,1)} %grads_hbm.1, bf16[256,1792]{1,0:T(8,128)(2,1)} %inputs_hbm.1), custom_call_target="tpu_custom_call" | custom-call | flops 88080384 | bytes 1835008 | tf_op jit(solution)/shard_map/pallas_call | solution.py:24
  2.4 4.1 %collective-permute-start = (bf16[24,1792]{1,0:T(8,128)(2,1)S(1)}, bf16[24,1792]{1,0:T(8,128)(2,1)S(1)}, u32[]{:S(2)}, u32[]{:S(2)}) collective-permute-start(bf16[24,1792]{1,0:T(8,128)(2,1)S(1)} %get-tuple-element.32), channel_id=1, source_target_pairs={{0,4},{1,5},{2,6},{3,7},{4,0},{5,1},{6,2},{7,3},{8,12},{9,13},{10,... | collective-permute-start | bytes 258056 | tf_op jit(solution)/shard_map/ppermute | solution.py:300
  6.5 1.5 %collective-permute-start.4 = (bf16[24,1792]{1,0:T(8,128)(2,1)S(1)}, bf16[24,1792]{1,0:T(8,128)(2,1)S(1)}, u32[]{:S(2)}, u32[]{:S(2)}) collective-permute-start(bf16[24,1792]{1,0:T(8,128)(2,1)S(1)} %get-tuple-element.33.refs_7_), channel_id=1, source_target_pairs={{0,1},{1,0},{2,3},{3,2},{4,5},{5,4},{6,7},{7,6},{8,9},{9,8},{10,11... | collective-permute-start | bytes 258056 | tf_op jit(solution)/shard_map/ppermute | solution.py:303
  8.1 1.6 %collective-permute-start.5 = (bf16[24,1792]{1,0:T(8,128)(2,1)S(1)}, bf16[24,1792]{1,0:T(8,128)(2,1)S(1)}, u32[]{:S(2)}, u32[]{:S(2)}) collective-permute-start(bf16[24,1792]{1,0:T(8,128)(2,1)S(1)} %get-tuple-element.33.refs_7_), channel_id=1, source_target_pairs={{0,2},{1,3},{2,0},{3,1},{4,6},{5,7},{6,4},{7,5},{8,10},{9,11},{10,... | collective-permute-start | bytes 258056 | tf_op jit(solution)/shard_map/ppermute | solution.py:303
  9.6 0.4 collective-permute-start.6
  10.0 0.8 %collective-permute-done.refs_3_ = bf16[24,1792]{1,0:T(8,128)(2,1)S(1)} collective-permute-done((bf16[24,1792]{1,0:T(8,128)(2,1)S(1)}, bf16[24,1792]{1,0:T(8,128)(2,1)S(1)}, u32[]{:S(2)}, u32[]{:S(2)}) %collective-permute-start) | collective-permute-done | bytes 86048 | tf_op jit(solution)/shard_map/ppermute | solution.py:300
  10.9 1.7 %collective-permute-start.1 = (bf16[24,1792]{1,0:T(8,128)(2,1)S(1)}, bf16[24,1792]{1,0:T(8,128)(2,1)S(1)}, u32[]{:S(2)}, u32[]{:S(2)}) collective-permute-start(bf16[24,1792]{1,0:T(8,128)(2,1)S(1)} %collective-permute-done.refs_3_), channel_id=1, source_target_pairs={{0,3},{1,2},{2,1},{3,0},{4,7},{5,6},{6,5},{7,4},{8,11},{9,10},{10,... | collective-permute-start | bytes 258056 | tf_op jit(solution)/shard_map/ppermute | solution.py:303
  12.6 1.2 %collective-permute-start.2 = (bf16[24,1792]{1,0:T(8,128)(2,1)S(1)}, bf16[24,1792]{1,0:T(8,128)(2,1)S(1)}, u32[]{:S(2)}, u32[]{:S(2)}) collective-permute-start(bf16[24,1792]{1,0:T(8,128)(2,1)S(1)} %collective-permute-done.refs_3_), channel_id=1, source_target_pairs={{0,2},{1,3},{2,0},{3,1},{4,6},{5,7},{6,4},{7,5},{8,10},{9,11},{10,... | collective-permute-start | bytes 258056 | tf_op jit(solution)/shard_map/ppermute | solution.py:303
  13.8 0.5 %collective-permute-start.3 = (bf16[24,1792]{1,0:T(8,128)(2,1)S(1)}, bf16[24,1792]{1,0:T(8,128)(2,1)S(1)}, u32[]{:S(2)}, u32[]{:S(2)}) collective-permute-start(bf16[24,1792]{1,0:T(8,128)(2,1)S(1)} %collective-permute-done.refs_3_), channel_id=1, source_target_pairs={{0,1},{1,0},{2,3},{3,2},{4,5},{5,4},{6,7},{7,6},{8,9},{9,8},{10,11... | collective-permute-start | bytes 258056 | tf_op jit(solution)/shard_map/ppermute | solution.py:303
  14.4 2.6 %shard_map.95 = (bf16[1792,512]{1,0:T(8,128)(2,1)S(1)}, bf16[1792,512]{1,0:T(8,128)(2,1)S(1)}, bf16[1792,512]{1,0:T(8,128)(2,1)S(1)}) custom-call(bf16[48,256]{1,0:T(8,128)(2,1)S(1)} %get-tuple-element.30.after.refs_0_, bf16[1792,512]{1,0:T(8,128)(2,1)} %refs_0_.1, bf16[1792,512]{1,0:T(8,128)(2,1)} %refs_1_.1, bf16[512,1792]{1,0:T(8,128)(2,1)} %refs_2_.1), custom_call_target="tpu_custom_call" | custom-call | bytes 5505024 | tf_op jit(solution)/shard_map/pallas_call | solution.py:24
  17.2 0.6 %collective-permute-done.2.refs_1_ = bf16[24,1792]{1,0:T(8,128)(2,1)S(1)} collective-permute-done((bf16[24,1792]{1,0:T(8,128)(2,1)S(1)}, bf16[24,1792]{1,0:T(8,128)(2,1)S(1)}, u32[]{:S(2)}, u32[]{:S(2)}) %collective-permute-start.2) | collective-permute-done | bytes 86048 | tf_op jit(solution)/shard_map/ppermute | solution.py:303
  17.8 0.5 %collective-permute-done.3.refs_2_ = bf16[24,1792]{1,0:T(8,128)(2,1)S(1)} collective-permute-done((bf16[24,1792]{1,0:T(8,128)(2,1)S(1)}, bf16[24,1792]{1,0:T(8,128)(2,1)S(1)}, u32[]{:S(2)}, u32[]{:S(2)}) %collective-permute-start.3) | collective-permute-done | bytes 86048 | tf_op jit(solution)/shard_map/ppermute | solution.py:303
  18.3 0.7 %shard_map.97 = (bf16[96,1792]{1,0:T(8,128)(2,1)S(1)}, bf16[96,512]{1,0:T(8,128)(2,1)S(1)}, bf16[96,512]{1,0:T(8,128)(2,1)S(1)}) custom-call(bf16[1792,512]{1,0:T(8,128)(2,1)S(1)} %get-tuple-element.36.w_gate, bf16[1792,512]{1,0:T(8,128)(2,1)S(1)} %get-tuple-element.37.w_up, bf16[24,1792]{1,0:T(8,128)(2,1)S(1)} %collective-permute-done.1.refs_0_, ...), custom_call_target="tpu_custom_call" | custom-call | flops 352321536 | bytes 3670016 | tf_op jit(solution)/shard_map/pallas_call | solution.py:24
  19.1 0.5 %shard_map.96 = (bf16[96,256]{1,0:T(8,128)(2,1)S(1)}, bf16[96,256]{1,0:T(8,128)(2,1)S(1)}) custom-call(bf16[1792,512]{1,0:T(8,128)(2,1)S(1)} %get-tuple-element.31.down_across, bf16[24,1792]{1,0:T(8,128)(2,1)S(1)} %collective-permute-done.1.refs_0_, bf16[24,1792]{1,0:T(8,128)(2,1)S(1)} %collective-permute-done.2.refs_1_, ...), custom_call_target="tpu_custom_call" | custom-call | flops 176160768 | bytes 1835008 | tf_op jit(solution)/shard_map/pallas_call | solution.py:24
  19.6 0.6 %collective-permute-start.7 = (bf16[96,256]{1,0:T(8,128)(2,1)S(1)}, bf16[96,256]{1,0:T(8,128)(2,1)S(1)}, u32[]{:S(2)}, u32[]{:S(2)}) collective-permute-start(bf16[96,256]{1,0:T(8,128)(2,1)S(1)} %get-tuple-element.35), channel_id=1, source_target_pairs={{0,8},{8,0},{16,24},{24,16},{1,9},{9,1},{17,25},{25,17},{2,10},{10... | collective-permute-start | bytes 147464 | tf_op jit(solution)/shard_map/ppermute | solution.py:306
  20.4 1.6 %collective-permute-start.9 = (bf16[96,512]{1,0:T(8,128)(2,1)S(1)}, bf16[96,512]{1,0:T(8,128)(2,1)S(1)}, u32[]{:S(2)}, u32[]{:S(2)}) collective-permute-start(bf16[96,512]{1,0:T(8,128)(2,1)S(1)} %add_convert_fusion.pre_own), channel_id=1, source_target_pairs={{0,16},{8,24},{16,0},{24,8},{1,17},{9,25},{17,1},{25,9},{2,18},{10... | collective-permute-start | bytes 294920 | tf_op jit(solution)/shard_map/ppermute | solution.py:306
  22.0 0.6 %collective-permute-start.10 = (bf16[96,256]{1,0:T(8,128)(2,1)S(1)}, bf16[96,256]{1,0:T(8,128)(2,1)S(1)}, u32[]{:S(2)}, u32[]{:S(2)}) collective-permute-start(bf16[96,256]{1,0:T(8,128)(2,1)S(1)} %add_convert_fusion.1.after.hid_own), channel_id=1, source_target_pairs={{0,16},{8,24},{16,0},{24,8},{1,17},{9,25},{17,1},{25,9},{2,18},{10... | collective-permute-start | bytes 147464 | tf_op jit(solution)/shard_map/ppermute | solution.py:306
  22.6 1.2 %shard_map.98 = (bf16[1792,96]{1,0:T(8,128)(2,1)S(1)}, bf16[512,1792]{1,0:T(8,128)(2,1)S(1)}, bf16[512,1792]{1,0:T(8,128)(2,1)S(1)}, bf16[256,48]{1,0:T(8,128)(2,1)S(1)}, bf16[256,48]{1,0:T(8,128)(2,1)S(1)}) custom-call(bf16[96,256]{1,0:T(8,128)(2,1)S(1)} %add_convert_fusion.1.after.hid_own, bf16[96,1792]{1,0:T(8,128)(2,1)S(1)} %get-tuple-element.38.rows_ref, ...), custom_call_target="tpu_custom_call" | custom-call | tf_op jit(solution)/shard_map/pallas_call | solution.py:24
  23.8 2.6 %collective-permute-done.10.hid_far = bf16[96,256]{1,0:T(8,128)(2,1)S(1)} collective-permute-done((bf16[96,256]{1,0:T(8,128)(2,1)S(1)}, bf16[96,256]{1,0:T(8,128)(2,1)S(1)}, u32[]{:S(2)}, u32[]{:S(2)}) %collective-permute-start.10) | collective-permute-done | bytes 49184 | tf_op jit(solution)/shard_map/ppermute | solution.py:306
  26.6 0.4 %shard_map.100.own = f32[96,1792]{1,0:T(8,128)S(1)} custom-call(bf16[512,1792]{1,0:T(8,128)(2,1)S(1)} %get-tuple-element.42.gate_across, bf16[512,1792]{1,0:T(8,128)(2,1)S(1)} %get-tuple-element.43.up_across, bf16[96,512]{1,0:T(8,128)(2,1)S(1)} %shard_map.99.acts.acts_own), custom_call_target="tpu_custom_call" | custom-call | flops 176160768 | bytes 1835008 | tf_op jit(solution)/shard_map/pallas_call | solution.py:24
  27.0 0.8 %collective-permute-done.11.acts.acts_far = bf16[96,512]{1,0:T(8,128)(2,1)S(1)} collective-permute-done((bf16[96,512]{1,0:T(8,128)(2,1)S(1)}, bf16[96,512]{1,0:T(8,128)(2,1)S(1)}, u32[]{:S(2)}, u32[]{:S(2)}) %collective-permute-start.11) | collective-permute-done | bytes 98336 | tf_op jit(solution)/shard_map/ppermute | solution.py:306
  27.9 0.4 %shard_map.101 = (bf16[24,1792]{1,0:T(8,128)(2,1)S(1)}, bf16[24,1792]{1,0:T(8,128)(2,1)S(1)}, bf16[24,1792]{1,0:T(8,128)(2,1)S(1)}, bf16[24,1792]{1,0:T(8,128)(2,1)S(1)}) custom-call(bf16[512,1792]{1,0:T(8,128)(2,1)S(1)} %get-tuple-element.42.gate_across, bf16[512,1792]{1,0:T(8,128)(2,1)S(1)} %get-tuple-element.43.up_across, ...), custom_call_target="tpu_custom_call" | custom-call | flops 176160768 | bytes 1835008 | tf_op jit(solution)/shard_map/pallas_call | solution.py:24
  28.3 1.5 %collective-permute-start.12 = (bf16[24,1792]{1,0:T(8,128)(2,1)S(1)}, bf16[24,1792]{1,0:T(8,128)(2,1)S(1)}, u32[]{:S(2)}, u32[]{:S(2)}) collective-permute-start(bf16[24,1792]{1,0:T(8,128)(2,1)S(1)} %get-tuple-element.50), channel_id=1, source_target_pairs={{0,3},{1,2},{2,1},{3,0},{4,7},{5,6},{6,5},{7,4},{8,11},{9,10},{10,... | collective-permute-start | bytes 258056 | tf_op jit(solution)/shard_map/ppermute | solution.py:303
  29.8 0.9 %collective-permute-start.13 = (bf16[24,1792]{1,0:T(8,128)(2,1)S(1)}, bf16[24,1792]{1,0:T(8,128)(2,1)S(1)}, u32[]{:S(2)}, u32[]{:S(2)}) collective-permute-start(bf16[24,1792]{1,0:T(8,128)(2,1)S(1)} %get-tuple-element.51), channel_id=1, source_target_pairs={{0,2},{1,3},{2,0},{3,1},{4,6},{5,7},{6,4},{7,5},{8,10},{9,11},{10,... | collective-permute-start | bytes 258056 | tf_op jit(solution)/shard_map/ppermute | solution.py:303
  30.7 1.1 %collective-permute-start.14 = (bf16[24,1792]{1,0:T(8,128)(2,1)S(1)}, bf16[24,1792]{1,0:T(8,128)(2,1)S(1)}, u32[]{:S(2)}, u32[]{:S(2)}) collective-permute-start(bf16[24,1792]{1,0:T(8,128)(2,1)S(1)} %get-tuple-element.52), channel_id=1, source_target_pairs={{0,1},{1,0},{2,3},{3,2},{4,5},{5,4},{6,7},{7,6},{8,9},{9,8},{10,11... | collective-permute-start | bytes 258056 | tf_op jit(solution)/shard_map/ppermute | solution.py:303
  31.8 1.5 %shard_map.102 = (bf16[1792,512]{1,0:T(8,128)(2,1)}, f32[8,128]{1,0:T(8,128)S(1)}) custom-call(bf16[24,1792]{1,0:T(8,128)(2,1)S(1)} %get-tuple-element.47.after.refs_3_, bf16[1792,96]{1,0:T(8,128)(2,1)S(1)} %get-tuple-element.44.after.rows_ref, bf16[96,512]{1,0:T(8,128)(2,1)S(1)} %shard_map.99.acts.acts_own, ...), custom_call_target="tpu_custom_call" | custom-call | tf_op jit(solution)/shard_map/pallas_call | solution.py:24
  33.3 1.5 %shard_map.103 = (bf16[1792,512]{1,0:T(8,128)(2,1)}, f32[8,128]{1,0:T(8,128)S(1)}) custom-call(f32[8,128]{1,0:T(8,128)S(1)} %get-tuple-element.48.after, bf16[1792,96]{1,0:T(8,128)(2,1)S(1)} %get-tuple-element.44.after.rows_ref, bf16[96,512]{1,0:T(8,128)(2,1)S(1)} %shard_map.99.acts.acts_own, bf16[96,512]{1,0:T(8,128)(2,1)S(1)} %collective-permute-done.11.acts.acts_far), custom_call_target="tpu_custom_call" | custom-call | tf_op jit(solution)/shard_map/pallas_call | solution.py:24
  34.9 0.3 collective-permute-done.13.refs_1_
  35.1 0.5 %collective-permute-done.14.refs_2_ = bf16[24,1792]{1,0:T(8,128)(2,1)S(1)} collective-permute-done((bf16[24,1792]{1,0:T(8,128)(2,1)S(1)}, bf16[24,1792]{1,0:T(8,128)(2,1)S(1)}, u32[]{:S(2)}, u32[]{:S(2)}) %collective-permute-start.14) | collective-permute-done | bytes 86048 | tf_op jit(solution)/shard_map/ppermute | solution.py:303
  35.7 2.2 %collective-permute-start.15 = (bf16[24,896]{1,0:T(8,128)(2,1)S(1)}, bf16[24,896]{1,0:T(8,128)(2,1)S(1)}, u32[]{:S(2)}, u32[]{:S(2)}) collective-permute-start(bf16[24,896]{1,0:T(8,128)(2,1)S(1)} %get-tuple-element.54), channel_id=1, source_target_pairs={{0,4},{1,5},{2,6},{3,7},{4,0},{5,1},{6,2},{7,3},{8,12},{9,13},{10,... | collective-permute-start | bytes 129032 | tf_op jit(solution)/shard_map/ppermute | solution.py:300
  38.0 2.8 %collective-permute-done.15.refs_3_ = bf16[24,896]{1,0:T(8,128)(2,1)S(1)} collective-permute-done((bf16[24,896]{1,0:T(8,128)(2,1)S(1)}, bf16[24,896]{1,0:T(8,128)(2,1)S(1)}, u32[]{:S(2)}, u32[]{:S(2)}) %collective-permute-start.15) | collective-permute-done | bytes 43040 | tf_op jit(solution)/shard_map/ppermute | solution.py:300
  40.7 1.2 %shard_map.105 = bf16[256,1792]{1,0:T(8,128)(2,1)} custom-call(bf16[256,48]{1,0:T(8,128)(2,1)S(1)} %get-tuple-element.40.refs_0_, bf16[256,48]{1,0:T(8,128)(2,1)S(1)} %get-tuple-element.41.refs_1_, bf16[24,896]{1,0:T(8,128)(2,1)S(1)} %get-tuple-element.53.refs_2_, bf16[24,896]{1,0:T(8,128)(2,1)S(1)} %collective-permute-done.15.refs_3_), custom_call_target="tpu_custom_call" | custom-call | flops 44040192 | bytes 917504 | tf_op jit(solution)/shard_map/pallas_call | solution.py:24
  (14 shorter events, 0.8 us)
Async XLA Ops:
  2.4 8.4 %collective-permute-start = (bf16[24,1792]{1,0:T(8,128)(2,1)S(1)}, bf16[24,1792]{1,0:T(8,128)(2,1)S(1)}, u32[]{:S(2)}, u32[]{:S(2)}) collective-permute-start(bf16[24,1792]{1,0:T(8,128)(2,1)S(1)} %get-tuple-element.32), channel_id=1, source_target_pairs={{0,4},{1,5},{2,6},{3,7},{4,0},{5,1},{6,2},{7,3},{8,12},{9,13},{10,... | collective-permute-start | bytes 258056 | tf_op jit(solution)/shard_map/ppermute | solution.py:300
  6.5 7.3 %collective-permute-start.4 = (bf16[24,1792]{1,0:T(8,128)(2,1)S(1)}, bf16[24,1792]{1,0:T(8,128)(2,1)S(1)}, u32[]{:S(2)}, u32[]{:S(2)}) collective-permute-start(bf16[24,1792]{1,0:T(8,128)(2,1)S(1)} %get-tuple-element.33.refs_7_), channel_id=1, source_target_pairs={{0,1},{1,0},{2,3},{3,2},{4,5},{5,4},{6,7},{7,6},{8,9},{9,8},{10,11... | collective-permute-start | bytes 258056 | tf_op jit(solution)/shard_map/ppermute | solution.py:303
  8.1 8.9 %collective-permute-start.5 = (bf16[24,1792]{1,0:T(8,128)(2,1)S(1)}, bf16[24,1792]{1,0:T(8,128)(2,1)S(1)}, u32[]{:S(2)}, u32[]{:S(2)}) collective-permute-start(bf16[24,1792]{1,0:T(8,128)(2,1)S(1)} %get-tuple-element.33.refs_7_), channel_id=1, source_target_pairs={{0,2},{1,3},{2,0},{3,1},{4,6},{5,7},{6,4},{7,5},{8,10},{9,11},{10,... | collective-permute-start | bytes 258056 | tf_op jit(solution)/shard_map/ppermute | solution.py:303
  9.6 7.4 %collective-permute-start.6 = (bf16[24,1792]{1,0:T(8,128)(2,1)S(1)}, bf16[24,1792]{1,0:T(8,128)(2,1)S(1)}, u32[]{:S(2)}, u32[]{:S(2)}) collective-permute-start(bf16[24,1792]{1,0:T(8,128)(2,1)S(1)} %get-tuple-element.33.refs_7_), channel_id=1, source_target_pairs={{0,3},{1,2},{2,1},{3,0},{4,7},{5,6},{6,5},{7,4},{8,11},{9,10},{10,... | collective-permute-start | bytes 258056 | tf_op jit(solution)/shard_map/ppermute | solution.py:303
  10.9 6.4 %collective-permute-start.1 = (bf16[24,1792]{1,0:T(8,128)(2,1)S(1)}, bf16[24,1792]{1,0:T(8,128)(2,1)S(1)}, u32[]{:S(2)}, u32[]{:S(2)}) collective-permute-start(bf16[24,1792]{1,0:T(8,128)(2,1)S(1)} %collective-permute-done.refs_3_), channel_id=1, source_target_pairs={{0,3},{1,2},{2,1},{3,0},{4,7},{5,6},{6,5},{7,4},{8,11},{9,10},{10,... | collective-permute-start | bytes 258056 | tf_op jit(solution)/shard_map/ppermute | solution.py:303
  12.6 5.2 %collective-permute-start.2 = (bf16[24,1792]{1,0:T(8,128)(2,1)S(1)}, bf16[24,1792]{1,0:T(8,128)(2,1)S(1)}, u32[]{:S(2)}, u32[]{:S(2)}) collective-permute-start(bf16[24,1792]{1,0:T(8,128)(2,1)S(1)} %collective-permute-done.refs_3_), channel_id=1, source_target_pairs={{0,2},{1,3},{2,0},{3,1},{4,6},{5,7},{6,4},{7,5},{8,10},{9,11},{10,... | collective-permute-start | bytes 258056 | tf_op jit(solution)/shard_map/ppermute | solution.py:303
  13.8 4.5 %collective-permute-start.3 = (bf16[24,1792]{1,0:T(8,128)(2,1)S(1)}, bf16[24,1792]{1,0:T(8,128)(2,1)S(1)}, u32[]{:S(2)}, u32[]{:S(2)}) collective-permute-start(bf16[24,1792]{1,0:T(8,128)(2,1)S(1)} %collective-permute-done.refs_3_), channel_id=1, source_target_pairs={{0,1},{1,0},{2,3},{3,2},{4,5},{5,4},{6,7},{7,6},{8,9},{9,8},{10,11... | collective-permute-start | bytes 258056 | tf_op jit(solution)/shard_map/ppermute | solution.py:303
  19.0 1.4 %collective-permute-start.8 = (bf16[96,512]{1,0:T(8,128)(2,1)S(1)}, bf16[96,512]{1,0:T(8,128)(2,1)S(1)}, u32[]{:S(2)}, u32[]{:S(2)}) collective-permute-start(bf16[96,512]{1,0:T(8,128)(2,1)S(1)} %get-tuple-element.46), channel_id=1, source_target_pairs={{0,8},{8,0},{16,24},{24,16},{1,9},{9,1},{17,25},{25,17},{2,10},{10... | collective-permute-start | bytes 294920 | tf_op jit(solution)/shard_map/ppermute | solution.py:306
  19.6 2.4 %collective-permute-start.7 = (bf16[96,256]{1,0:T(8,128)(2,1)S(1)}, bf16[96,256]{1,0:T(8,128)(2,1)S(1)}, u32[]{:S(2)}, u32[]{:S(2)}) collective-permute-start(bf16[96,256]{1,0:T(8,128)(2,1)S(1)} %get-tuple-element.35), channel_id=1, source_target_pairs={{0,8},{8,0},{16,24},{24,16},{1,9},{9,1},{17,25},{25,17},{2,10},{10... | collective-permute-start | bytes 147464 | tf_op jit(solution)/shard_map/ppermute | solution.py:306
  20.4 6.0 %collective-permute-start.9 = (bf16[96,512]{1,0:T(8,128)(2,1)S(1)}, bf16[96,512]{1,0:T(8,128)(2,1)S(1)}, u32[]{:S(2)}, u32[]{:S(2)}) collective-permute-start(bf16[96,512]{1,0:T(8,128)(2,1)S(1)} %add_convert_fusion.pre_own), channel_id=1, source_target_pairs={{0,16},{8,24},{16,0},{24,8},{1,17},{9,25},{17,1},{25,9},{2,18},{10... | collective-permute-start | bytes 294920 | tf_op jit(solution)/shard_map/ppermute | solution.py:306
  22.0 4.4 %collective-permute-start.10 = (bf16[96,256]{1,0:T(8,128)(2,1)S(1)}, bf16[96,256]{1,0:T(8,128)(2,1)S(1)}, u32[]{:S(2)}, u32[]{:S(2)}) collective-permute-start(bf16[96,256]{1,0:T(8,128)(2,1)S(1)} %add_convert_fusion.1.after.hid_own), channel_id=1, source_target_pairs={{0,16},{8,24},{16,0},{24,8},{1,17},{9,25},{17,1},{25,9},{2,18},{10... | collective-permute-start | bytes 147464 | tf_op jit(solution)/shard_map/ppermute | solution.py:306
  26.5 1.4 %collective-permute-start.11 = (bf16[96,512]{1,0:T(8,128)(2,1)S(1)}, bf16[96,512]{1,0:T(8,128)(2,1)S(1)}, u32[]{:S(2)}, u32[]{:S(2)}) collective-permute-start(bf16[96,512]{1,0:T(8,128)(2,1)S(1)} %shard_map.99.acts.acts_own), channel_id=1, source_target_pairs={{0,8},{8,0},{16,24},{24,16},{1,9},{9,1},{17,25},{25,17},{2,10},{10... | collective-permute-start | bytes 294920 | tf_op jit(solution)/shard_map/ppermute | solution.py:306
  28.3 6.6 %collective-permute-start.12 = (bf16[24,1792]{1,0:T(8,128)(2,1)S(1)}, bf16[24,1792]{1,0:T(8,128)(2,1)S(1)}, u32[]{:S(2)}, u32[]{:S(2)}) collective-permute-start(bf16[24,1792]{1,0:T(8,128)(2,1)S(1)} %get-tuple-element.50), channel_id=1, source_target_pairs={{0,3},{1,2},{2,1},{3,0},{4,7},{5,6},{6,5},{7,4},{8,11},{9,10},{10,... | collective-permute-start | bytes 258056 | tf_op jit(solution)/shard_map/ppermute | solution.py:303
  29.8 5.3 %collective-permute-start.13 = (bf16[24,1792]{1,0:T(8,128)(2,1)S(1)}, bf16[24,1792]{1,0:T(8,128)(2,1)S(1)}, u32[]{:S(2)}, u32[]{:S(2)}) collective-permute-start(bf16[24,1792]{1,0:T(8,128)(2,1)S(1)} %get-tuple-element.51), channel_id=1, source_target_pairs={{0,2},{1,3},{2,0},{3,1},{4,6},{5,7},{6,4},{7,5},{8,10},{9,11},{10,... | collective-permute-start | bytes 258056 | tf_op jit(solution)/shard_map/ppermute | solution.py:303
  30.7 4.9 %collective-permute-start.14 = (bf16[24,1792]{1,0:T(8,128)(2,1)S(1)}, bf16[24,1792]{1,0:T(8,128)(2,1)S(1)}, u32[]{:S(2)}, u32[]{:S(2)}) collective-permute-start(bf16[24,1792]{1,0:T(8,128)(2,1)S(1)} %get-tuple-element.52), channel_id=1, source_target_pairs={{0,1},{1,0},{2,3},{3,2},{4,5},{5,4},{6,7},{7,6},{8,9},{9,8},{10,11... | collective-permute-start | bytes 258056 | tf_op jit(solution)/shard_map/ppermute | solution.py:303
  35.7 5.0 %collective-permute-start.15 = (bf16[24,896]{1,0:T(8,128)(2,1)S(1)}, bf16[24,896]{1,0:T(8,128)(2,1)S(1)}, u32[]{:S(2)}, u32[]{:S(2)}) collective-permute-start(bf16[24,896]{1,0:T(8,128)(2,1)S(1)} %get-tuple-element.54), channel_id=1, source_target_pairs={{0,4},{1,5},{2,6},{3,7},{4,0},{5,1},{6,2},{7,3},{8,12},{9,13},{10,... | collective-permute-start | bytes 129032 | tf_op jit(solution)/shard_map/ppermute | solution.py:300
